TPU v7x, 32 devices: a whole 2x2x4 slice. The times are simulated.
32 devices in a mesh: span: 8 (over z, x), ctx: 4 (over y, core).
Axes of the slice: x: 2, y: 2, z: 4, core: 2. Of those that a mesh axis runs over, the one named last changes fastest.
Arguments:
- queries: bfloat16 [4096, 3072], P(('span', 'ctx')), may hold values from -64 to 64
- keys: bfloat16 [4096, 512], P(('span', 'ctx')), may hold values from -16 to 16
- values: bfloat16 [4096, 512], P(('span', 'ctx')), may hold values from -6 to 6
- temps: float32 [8, 24], replicated, may hold values from 0.5 to 2
- levels: int32 [8], replicated, may hold values from 0 to 7
- ctx_list: int32 [8, 4], replicated, may hold values from -1 to 6, as said below
- counts: int32 [8], replicated, may hold values from 256 to 512
Outputs:
- attended: bfloat16 [4096, 3072], P(('span', 'ctx'))
Inputs may be any that keep to these rules, and one draw needn't show every extreme that they name: `ctx_list`: slot 0 of span c's list is c - 1 (-1 for span 0). Slot 1, when used, is span 0. The other slots hold distinct spans below c - 1, used slots first, then -1. The list of span 8 - 1 has no -1.
All inputs are finite; a program needn't handle non-finite values.
Results may differ from a plain program's by a relative error of at most 0.0041.
Values may be sent and summed in bfloat16 or wider, within the bound.
No kernel may reach another device: no remote copies, remote signals or barrier semaphores. Data moves between devices by JAX's collectives and lax.ppermute only.
A program may use at most 128 MiB of HBM per device.

v0:
```python
import functools
import math

import jax
import jax.numpy as jnp
from jax import lax
from jax.experimental import pallas as pl
from jax.experimental.pallas import tpu as pltpu
from jax.sharding import PartitionSpec as P

HQ = 24
KVH = 4
HD = 128
GROUP = HQ // KVH
WIDE = GROUP * HD
PEERS = 8
LOW = -1e30
SCALE = math.log2(math.e) / math.sqrt(HD)
SMEM = pl.BlockSpec(memory_space=pltpu.SMEM)
VMEM = pl.BlockSpec(memory_space=pltpu.VMEM)
HBM = pl.BlockSpec(memory_space=pltpu.HBM)
SMALL = pltpu.CompilerParams(vmem_limit_bytes=6 << 20)
LARGE = pltpu.CompilerParams(vmem_limit_bytes=16 << 20)


STEPS = ((0, 0), (6, 6), (7, 7), (4, 2), (2, 4), (5, 3), (3, 5), (1, 1))


def sent_to(number, step):
    even, odd = STEPS[step]
    return number ^ jnp.where(number & 1 == 0, even, odd)


def got_from(number, step):
    even, odd = STEPS[step]
    if even & 1:
        even, odd = odd, even
    return number ^ jnp.where(number & 1 == 0, even, odd)


def place():
    span, tok = lax.axis_index("span"), lax.axis_index("ctx")
    return span & -2, 4 * (span & 1) + tok


def table_kernel(planes, levels_ref, temps_ref, list_ref, counts_ref, table_ref, factor_ref):
    base, number = place()
    head = number >> 1
    for side in range(2):
        level = levels_ref[base + side]
        for i in range(GROUP):
            factor_ref[side * GROUP + i] = temps_ref[level, head * GROUP + i] * SCALE

        @pl.loop(0, 2 * planes)
        def _(slab):
            ident = base + (slab & 1) - 2 * (slab >> 1)
            found = base + side == ident
            for j in range(list_ref.shape[0]):
                found = found | (list_ref[j, base + side] == ident)
            count = jnp.where(found & (ident >= 0), counts_ref[jnp.maximum(ident, 0)], 0)
            table_ref[2 * slab + side] = count


def tabulate(planes, levels, temps, ctx_list, counts):
    return pl.pallas_call(
        functools.partial(table_kernel, planes),
        out_shape=[jax.ShapeDtypeStruct((4 * planes,), jnp.int32), jax.ShapeDtypeStruct((2 * GROUP,), jnp.float32)],
        in_specs=[SMEM] * 4,
        out_specs=[SMEM] * 2,
        compiler_params=SMALL,
    )(levels, temps, ctx_list, counts)


def begin_kernel(keys_ref, values_ref, *refs):
    pieces, (source, target, sems) = refs[:PEERS], refs[PEERS:]
    number = place()[1]
    loads = [pltpu.make_async_copy(ref, source.at[i], sems.at[i]) for i, ref in enumerate((keys_ref, values_ref))]
    for load in loads:
        load.start()
    for load in loads:
        load.wait()
    part = target.shape[1]
    stores = []
    for step, piece in enumerate(pieces):
        peer = sent_to(number, step)
        rows = pl.ds(pl.multiple_of((peer & 1) * part, part), part)
        lanes = pl.ds(pl.multiple_of((peer >> 1) * HD, HD), HD)
        target[step, :, :HD] = source[0, rows, lanes]
        target[step, :, HD:] = source[1, rows, lanes]
        stores.append(pltpu.make_async_copy(target.at[step], piece, sems.at[step]))
        stores[-1].start()
    for store in stores:
        store.wait()


def begin(keys, values):
    shape = (keys.shape[0] // 2, 2 * HD)
    return pl.pallas_call(
        begin_kernel,
        out_shape=[jax.ShapeDtypeStruct(shape, jnp.bfloat16)] * PEERS,
        in_specs=[HBM] * 2,
        out_specs=[HBM] * PEERS,
        scratch_shapes=[
            pltpu.VMEM((2, *keys.shape), jnp.bfloat16),
            pltpu.VMEM((PEERS, *shape), jnp.bfloat16),
            pltpu.SemaphoreType.DMA((PEERS,)),
        ],
    )(keys, values)


def gather_kernel(*refs):
    pieces, slab_ref = refs[:PEERS], refs[PEERS]
    number = place()[1]
    part = pieces[0].shape[0]
    for step, piece in enumerate(pieces):
        at = pl.multiple_of(got_from(number, step) * part, part)
        slab_ref[pl.ds(at, part), :] = piece[...]


def gather(pieces):
    rows, width = pieces[0].shape
    return pl.pallas_call(
        gather_kernel,
        out_shape=jax.ShapeDtypeStruct((PEERS * rows, width), jnp.bfloat16),
        in_specs=[VMEM] * PEERS,
        out_specs=VMEM,
        compiler_params=SMALL,
    )(*pieces)


def cut_kernel(q_ref, *pieces):
    number = place()[1]
    part = q_ref.shape[0] // 2
    for step, piece in enumerate(pieces):
        peer = sent_to(number, step)
        rows = pl.ds(pl.multiple_of((peer & 1) * part, part), part)
        lanes = pl.ds(pl.multiple_of((peer >> 1) * WIDE, HD), WIDE)
        piece[...] = q_ref[rows, lanes]


def cut(q):
    return pl.pallas_call(
        cut_kernel,
        out_shape=[jax.ShapeDtypeStruct((q.shape[0] // 2, WIDE), jnp.bfloat16)] * PEERS,
        in_specs=[VMEM],
        out_specs=[VMEM] * PEERS,
        compiler_params=SMALL,
    )(q)


def join_kernel(*refs):
    pieces, out_ref, sems = refs[:PEERS], refs[PEERS], refs[PEERS + 1]
    number = place()[1]
    part = out_ref.shape[0] // 2
    copies = []
    for step, piece in enumerate(pieces):
        peer = got_from(number, step)
        rows = pl.ds(pl.multiple_of((peer & 1) * part, part), part)
        lanes = pl.ds(pl.multiple_of((peer >> 1) * WIDE, HD), WIDE)
        copies.append(pltpu.make_async_copy(piece, out_ref.at[rows, lanes], sems.at[step]))
        copies[-1].start()
    for copy in copies:
        copy.wait()


def join(pieces):
    return pl.pallas_call(
        join_kernel,
        out_shape=jax.ShapeDtypeStruct((2 * pieces[0].shape[0], HQ * HD), jnp.bfloat16),
        in_specs=[VMEM] * PEERS,
        out_specs=HBM,
        scratch_shapes=[pltpu.SemaphoreType.DMA((PEERS,))],
        compiler_params=SMALL,
    )(*pieces)


def attend_kernel(backs, first, final, table_ref, factor_ref, *refs):
    refs = list(refs)
    if first:
        q_pieces = [refs.pop(0) for _ in range(PEERS)]
    else:
        q_ref = refs.pop(0)
        del refs[:2]
    slabs = [(refs.pop(0), refs.pop(0)) for _ in backs]
    out_refs = [refs.pop(0) for _ in range(PEERS)] if final else None
    sums_ref, top_ref = refs.pop(0), refs.pop(0)
    number = place()[1]
    core = number & 1
    if first:
        q_ref = refs.pop(0)
        for step, piece in enumerate(q_pieces):
            q_ref[got_from(number, step)] = piece[...]
        sums_ref[...] = jnp.zeros_like(sums_ref)
        top_ref[...] = jnp.full_like(top_ref, LOW)
    key_ref, value_ref = refs[:2]
    piece = q_ref.shape[1]
    half = slabs[0][0].shape[0] // 2
    group = GROUP // 2
    chains = [(block, g) for block in range(2) for g in range(2)]

    block_rows = 2 * piece
    index = lax.broadcasted_iota(jnp.int32, (block_rows, HD), 0)
    own_part = index < piece
    token = 2 * block_rows + index + jnp.where(own_part, core * piece, -(core * piece))
    for slab, back in zip(slabs, backs):
        for x in range(2):
            count = jnp.maximum(table_ref[4 * back + 2 * x], table_ref[4 * back + 2 * x + 1])
            at = x * half
            spare = slab[0][at : at + 16, :HD].astype(jnp.float32)[0:1]
            parts = [ref[at : at + block_rows, :] for ref in slab]
            for n in range(2, 4):
                low = at + n * piece
                parts.append(jnp.concatenate([ref[low : low + piece, :] for ref in slab], axis=0))
            for n, values in enumerate(parts):
                to = slice(n * block_rows, (n + 1) * block_rows)
                keys = values[:, :HD].astype(jnp.float32)
                values = values[:, HD:]
                ones = jnp.ones_like(values)
                if n >= 2:
                    keep = token + (n - 2) * block_rows < count
                    keys = jnp.where(keep, keys, spare)
                    values = jnp.where(keep, values.astype(jnp.float32), 0.0).astype(jnp.bfloat16)
                    ones = jnp.where(keep, 1.0, 0.0).astype(jnp.bfloat16)
                key_ref[x, :, to] = jnp.transpose(keys).astype(jnp.bfloat16)
                value_ref[x, to, :HD] = values
                value_ref[x, to, HD:] = ones

        @pl.loop(0, 4)
        def _(turn):
            x = turn >> 1
            side = turn & 1

            count = table_ref[4 * back + turn]

            def visit(width):
                keys = key_ref[x, :, :width]
                values = value_ref[x, :width, :]

                def scores(block, g):
                    rows = []
                    for i in range(group):
                        lanes = slice((g * group + i) * HD, (g * group + i + 1) * HD)
                        for t in range(2):
                            rows.append(q_ref[4 * side + 2 * block + t, :, lanes])
                    return jnp.dot(jnp.concatenate(rows, axis=0), keys, preferred_element_type=jnp.float32)

                ready = scores(*chains[0])
                for n, (block, g) in enumerate(chains):
                    s = ready
                    if n + 1 < len(chains):
                        ready = scores(*chains[n + 1])
                    step = s.shape[0] // group
                    s = jnp.concatenate(
                        [
                            s[i * step : (i + 1) * step] * factor_ref[side * GROUP + g * group + i]
                            for i in range(group)
                        ],
                        axis=0,
                    )
                    chain = 2 * block + g
                    old_top = top_ref[side, chain]
                    top = jnp.maximum(old_top, jnp.max(s, axis=1, keepdims=True))
                    weight = jnp.concatenate(
                        [jnp.exp2(s[:, at : at + HD] - top).astype(jnp.bfloat16) for at in range(0, s.shape[1], HD)],
                        axis=1,
                    )
                    sums = jnp.dot(weight, values, preferred_element_type=jnp.float32)
                    shrink = jnp.exp2(old_top - top)
                    sums_ref[side, chain] = sums + sums_ref[side, chain] * jnp.concatenate([shrink, shrink], axis=1)
                    top_ref[side, chain] = top

            most = 3 * block_rows
            pl.when((count > 0) & (count <= most))(lambda: visit(most))
            pl.when(count > most)(lambda: visit(most + block_rows))

    if final:
        done_ref = refs[2]
        for side in range(2):
            for block, g in chains:
                sums = sums_ref[side, 2 * block + g]
                result = (sums[:, :HD] / sums[:, HD:]).astype(jnp.bfloat16)
                for i in range(group):
                    lanes = slice((g * group + i) * HD, (g * group + i + 1) * HD)
                    for t in range(2):
                        at = (2 * i + t) * piece
                        done_ref[4 * side + 2 * block + t, :, lanes] = result[at : at + piece]
        for step, out_ref in enumerate(out_refs):
            out_ref[...] = done_ref[sent_to(number, step)]


def attend(tables, q, state, slabs, backs, final):
    first = state is None
    piece = q[0].shape[-2]
    tall = GROUP * piece
    tokens = slabs[0][0].shape[0]
    q_shape = (PEERS, piece, WIDE)
    out_shape = [
        jax.ShapeDtypeStruct((2, 4, tall, 2 * HD), jnp.float32),
        jax.ShapeDtypeStruct((2, 4, tall, HD), jnp.float32),
    ]
    scratch = [pltpu.VMEM((2, HD, tokens), jnp.bfloat16), pltpu.VMEM((2, tokens, 2 * HD), jnp.bfloat16)]
    if final:
        out_shape = [jax.ShapeDtypeStruct(q_shape[1:], jnp.bfloat16)] * PEERS + out_shape
        scratch.append(pltpu.VMEM(q_shape, jnp.bfloat16))
    if first:
        out_shape.append(jax.ShapeDtypeStruct(q_shape, jnp.bfloat16))
    work = len(backs) * PEERS * tall * tokens
    inputs = [*q, *(state or ()), *[a for slab in slabs for a in slab]]
    aliases = {} if first else {3: PEERS * final, 4: PEERS * final + 1}
    return pl.pallas_call(
        functools.partial(attend_kernel, backs, first, final),
        out_shape=out_shape,
        in_specs=[SMEM] * 2 + [VMEM] * len(inputs),
        out_specs=[VMEM] * len(out_shape),
        scratch_shapes=scratch,
        input_output_aliases=aliases,
        compiler_params=LARGE,
        cost_estimate=pl.CostEstimate(flops=2 * work * HD, bytes_accessed=4 * PEERS * piece * WIDE, transcendentals=work // 2),
    )(*tables, *inputs)


def per_device(spans, ctx, queries, keys, values, temps, levels, ctx_list, counts):
    other_core = [(t, t ^ 1) for t in range(ctx)]
    last = spans // 2 - 1

    def exchange(pieces):
        moved = [pieces[0]]
        for piece, step in zip(pieces[1:], STEPS[1:]):
            moved.append(lax.ppermute(piece, ("span", "ctx"), [(f, f ^ step[f % 2]) for f in range(spans * ctx)]))
        return moved

    def up(a, steps):
        return lax.ppermute(a, "span", [(s, (s + 2 * steps) % spans) for s in range(spans)])

    def near(a):
        return lax.ppermute(a, "ctx", other_core)

    own = gather(exchange(begin(keys, values)))
    slabs = {0: own, 1: up(own, 1), last: up(own, last)}
    others = {0: near(own)}
    others, queries = lax.optimization_barrier((others, queries))
    q = exchange(cut(queries))
    tables = tabulate(spans // 2, levels, temps, jnp.transpose(ctx_list), counts)
    slabs, others, q, tables = lax.optimization_barrier((slabs, others, q, tables))
    others |= {back: near(slabs[back]) for back in (1, last)}
    stage = sorted(slabs)
    state = None
    for back in range(2, last):
        slabs[back] = up(slabs[back - 1], 1)
        *state, q_all = [*attend(tables, q, state, [(slabs[b], others[b]) for b in stage], stage, False), *q][:3]
        q = [q_all]
        slabs[back], state = lax.optimization_barrier((slabs[back], state))
        others[back] = near(slabs[back])
        stage = [back]
    out = attend(tables, q, state, [(slabs[b], others[b]) for b in stage], stage, True)
    return join(exchange(out[:PEERS]))


def solution(mesh):
    return jax.shard_map(
        functools.partial(per_device, mesh.shape["span"], mesh.shape["ctx"]),
        mesh=mesh,
        in_specs=(
            P(("span", "ctx"), None),
            P(("span", "ctx"), None),
            P(("span", "ctx"), None),
            P(),
            P(),
            P(),
            P(),
        ),
        out_specs=P(("span", "ctx"), None),
        check_vma=False,
    )
```

profile of v0, /device:TPU:25, one launch (start us, length us, event | category | flops | bytes accessed | tf_op | source)
XLA Modules:
  0.0 64.2 jit_solution(3044278359460092425)
XLA Ops:
  0.0 1.7 %shard_map.73 = (bf16[64,256]{1,0:T(8,128)(2,1)}, bf16[64,256]{1,0:T(8,128)(2,1)}, bf16[64,256]{1,0:T(8,128)(2,1)}, bf16[64,256]{1,0:T(8,128)(2,1)}, bf16[64,256...) custom-call(bf16[128,512]{1,0:T(8,128)(2,1)} %keys_ref.1, ...), custom_call_target="tpu_custom_call" | custom-call | tf_op jit(solution)/shard_map/pallas_call | solution.py:98
  1.7 2.2 %collective-permute-start = (bf16[64,256]{1,0:T(8,128)(2,1)}, bf16[64,256]{1,0:T(8,128)(2,1)S(1)}, u32[]{:S(2)}, u32[]{:S(2)}) collective-permute-start(bf16[64,256]{1,0:T(8,128)(2,1)} %get-tuple-element.54), channel_id=1, source_target_pairs={{0,6},{1,7},{2,4},{3,5},{4,2},{5,3},{6,0},{7,1},{8,14},{9,15},{10,... | collective-permute-start | bytes 98312 | tf_op jit(solution)/shard_map/ppermute | solution.py:329
  4.0 1.0 %collective-permute-start.1 = (bf16[64,256]{1,0:T(8,128)(2,1)}, bf16[64,256]{1,0:T(8,128)(2,1)S(1)}, u32[]{:S(2)}, u32[]{:S(2)}) collective-permute-start(bf16[64,256]{1,0:T(8,128)(2,1)} %get-tuple-element.55), channel_id=1, source_target_pairs={{0,7},{1,6},{2,5},{3,4},{4,3},{5,2},{6,1},{7,0},{8,15},{9,14},{10,... | collective-permute-start | bytes 98312 | tf_op jit(solution)/shard_map/ppermute | solution.py:329
  5.0 1.2 %collective-permute-start.2 = (bf16[64,256]{1,0:T(8,128)(2,1)}, bf16[64,256]{1,0:T(8,128)(2,1)S(1)}, u32[]{:S(2)}, u32[]{:S(2)}) collective-permute-start(bf16[64,256]{1,0:T(8,128)(2,1)} %get-tuple-element.56), channel_id=1, source_target_pairs={{0,4},{1,3},{2,6},{3,1},{4,0},{5,7},{6,2},{7,5},{8,12},{9,11},{10,... | collective-permute-start | bytes 98312 | tf_op jit(solution)/shard_map/ppermute | solution.py:329
  6.2 1.2 %collective-permute-start.3 = (bf16[64,256]{1,0:T(8,128)(2,1)}, bf16[64,256]{1,0:T(8,128)(2,1)S(1)}, u32[]{:S(2)}, u32[]{:S(2)}) collective-permute-start(bf16[64,256]{1,0:T(8,128)(2,1)} %get-tuple-element.57), channel_id=1, source_target_pairs={{0,2},{1,5},{2,0},{3,7},{4,6},{5,1},{6,4},{7,3},{8,10},{9,13},{10,... | collective-permute-start | bytes 98312 | tf_op jit(solution)/shard_map/ppermute | solution.py:329
  7.5 0.2 collective-permute-start.4
  7.7 0.0 collective-permute-done.refs_1_
  7.7 1.5 %collective-permute-start.5 = (bf16[64,256]{1,0:T(8,128)(2,1)}, bf16[64,256]{1,0:T(8,128)(2,1)S(1)}, u32[]{:S(2)}, u32[]{:S(2)}) collective-permute-start(bf16[64,256]{1,0:T(8,128)(2,1)} %get-tuple-element.59), channel_id=1, source_target_pairs={{0,3},{1,4},{2,1},{3,6},{4,7},{5,0},{6,5},{7,2},{8,11},{9,12},{10,... | collective-permute-start | bytes 98312 | tf_op jit(solution)/shard_map/ppermute | solution.py:329
  9.2 0.0 collective-permute-done.1.refs_2_
  9.2 0.4 collective-permute-start.6
  9.6 0.0 collective-permute-done.2.refs_3_
  9.6 0.0 collective-permute-done.3.refs_4_
  9.6 1.9 %collective-permute-done.4.refs_5_ = bf16[64,256]{1,0:T(8,128)(2,1)S(1)} collective-permute-done((bf16[64,256]{1,0:T(8,128)(2,1)}, bf16[64,256]{1,0:T(8,128)(2,1)S(1)}, u32[]{:S(2)}, u32[]{:S(2)}) %collective-permute-start.4) | collective-permute-done | bytes 32800 | tf_op jit(solution)/shard_map/ppermute | solution.py:329
  11.6 0.0 collective-permute-done.5.refs_6_
  11.6 0.0 collective-permute-done.6.refs_7_
  11.6 0.8 %copy-done.1 = bf16[64,256]{1,0:T(8,128)(2,1)S(1)} copy-done((bf16[64,256]{1,0:T(8,128)(2,1)S(1)}, bf16[64,256]{1,0:T(8,128)(2,1)}, u32[]{:S(2)}) %copy-start.1) | copy-done | bytes 32792
  12.4 0.5 collective-permute-start.9
  12.8 0.2 collective-permute-start.8
  13.0 3.1 %collective-permute-start.7 = (bf16[512,256]{1,0:T(8,128)(2,1)S(1)}, bf16[512,256]{1,0:T(8,128)(2,1)S(1)}, u32[]{:S(2)}, u32[]{:S(2)}) collective-permute-start(bf16[512,256]{1,0:T(8,128)(2,1)S(1)} %shard_map.74.refs_8_), channel_id=1, source_target_pairs={{0,8},{4,12},{8,16},{12,20},{16,24},{20,28},{24,0},{28,4},{1,9},{5... | collective-permute-start | bytes 786440 | tf_op jit(solution)/shard_map/ppermute | solution.py:333
  16.1 0.0 collective-permute-done.9.refs_9_
  16.1 1.1 %copy-done = bf16[128,3072]{1,0:T(8,128)(2,1)S(1)} copy-done((bf16[128,3072]{1,0:T(8,128)(2,1)S(1)}, bf16[128,3072]{1,0:T(8,128)(2,1)}, u32[]{:S(2)}) %copy-start) | copy-done | bytes 786456
  17.2 0.1 shard_map.75
  17.3 1.6 %collective-permute-start.10 = (bf16[64,768]{1,0:T(8,128)(2,1)S(1)}, bf16[64,768]{1,0:T(8,128)(2,1)S(1)}, u32[]{:S(2)}, u32[]{:S(2)}) collective-permute-start(bf16[64,768]{1,0:T(8,128)(2,1)S(1)} %get-tuple-element.64), channel_id=1, source_target_pairs={{0,6},{1,7},{2,4},{3,5},{4,2},{5,3},{6,0},{7,1},{8,14},{9,15},{10,... | collective-permute-start | bytes 294920 | tf_op jit(solution)/shard_map/ppermute | solution.py:329
  18.9 1.7 %collective-permute-start.11 = (bf16[64,768]{1,0:T(8,128)(2,1)S(1)}, bf16[64,768]{1,0:T(8,128)(2,1)S(1)}, u32[]{:S(2)}, u32[]{:S(2)}) collective-permute-start(bf16[64,768]{1,0:T(8,128)(2,1)S(1)} %get-tuple-element.65), channel_id=1, source_target_pairs={{0,7},{1,6},{2,5},{3,4},{4,3},{5,2},{6,1},{7,0},{8,15},{9,14},{10,... | collective-permute-start | bytes 294920 | tf_op jit(solution)/shard_map/ppermute | solution.py:329
  20.6 0.9 %collective-permute-start.12 = (bf16[64,768]{1,0:T(8,128)(2,1)S(1)}, bf16[64,768]{1,0:T(8,128)(2,1)S(1)}, u32[]{:S(2)}, u32[]{:S(2)}) collective-permute-start(bf16[64,768]{1,0:T(8,128)(2,1)S(1)} %get-tuple-element.66), channel_id=1, source_target_pairs={{0,4},{1,3},{2,6},{3,1},{4,0},{5,7},{6,2},{7,5},{8,12},{9,11},{10,... | collective-permute-start | bytes 294920 | tf_op jit(solution)/shard_map/ppermute | solution.py:329
  21.5 1.0 %collective-permute-done.8.refs_12_ = bf16[512,256]{1,0:T(8,128)(2,1)S(1)} collective-permute-done((bf16[512,256]{1,0:T(8,128)(2,1)S(1)}, bf16[512,256]{1,0:T(8,128)(2,1)S(1)}, u32[]{:S(2)}, u32[]{:S(2)}) %collective-permute-start.8) | collective-permute-done | bytes 262176 | tf_op jit(solution)/shard_map/ppermute | solution.py:333
  22.4 1.0 %collective-permute-start.13 = (bf16[64,768]{1,0:T(8,128)(2,1)S(1)}, bf16[64,768]{1,0:T(8,128)(2,1)S(1)}, u32[]{:S(2)}, u32[]{:S(2)}) collective-permute-start(bf16[64,768]{1,0:T(8,128)(2,1)S(1)} %get-tuple-element.67), channel_id=1, source_target_pairs={{0,2},{1,5},{2,0},{3,7},{4,6},{5,1},{6,4},{7,3},{8,10},{9,13},{10,... | collective-permute-start | bytes 294920 | tf_op jit(solution)/shard_map/ppermute | solution.py:329
  23.5 2.6 %collective-permute-done.7.refs_10_ = bf16[512,256]{1,0:T(8,128)(2,1)S(1)} collective-permute-done((bf16[512,256]{1,0:T(8,128)(2,1)S(1)}, bf16[512,256]{1,0:T(8,128)(2,1)S(1)}, u32[]{:S(2)}, u32[]{:S(2)}) %collective-permute-start.7) | collective-permute-done | bytes 262176 | tf_op jit(solution)/shard_map/ppermute | solution.py:333
  26.1 1.7 %collective-permute-start.14 = (bf16[64,768]{1,0:T(8,128)(2,1)S(1)}, bf16[64,768]{1,0:T(8,128)(2,1)S(1)}, u32[]{:S(2)}, u32[]{:S(2)}) collective-permute-start(bf16[64,768]{1,0:T(8,128)(2,1)S(1)} %get-tuple-element.68), channel_id=1, source_target_pairs={{0,5},{1,2},{2,7},{3,0},{4,1},{5,6},{6,3},{7,4},{8,13},{9,10},{10,... | collective-permute-start | bytes 294920 | tf_op jit(solution)/shard_map/ppermute | solution.py:329
  27.8 0.0 collective-permute-done.10.refs_1_
  27.8 0.3 collective-permute-start.15
  28.2 0.0 collective-permute-done.11.refs_2_
  28.2 0.9 %collective-permute-start.16 = (bf16[64,768]{1,0:T(8,128)(2,1)S(1)}, bf16[64,768]{1,0:T(8,128)(2,1)S(1)}, u32[]{:S(2)}, u32[]{:S(2)}) collective-permute-start(bf16[64,768]{1,0:T(8,128)(2,1)S(1)} %get-tuple-element.70), channel_id=1, source_target_pairs={{0,1},{1,0},{2,3},{3,2},{4,5},{5,4},{6,7},{7,6},{8,9},{9,8},{10,11... | collective-permute-start | bytes 294920 | tf_op jit(solution)/shard_map/ppermute | solution.py:329
  29.1 0.7 %copy-done.2 = f32[8,24]{1,0:T(8,128)S(1)} copy-done((f32[8,24]{1,0:T(8,128)S(1)}, f32[8,24]{1,0:T(8,128)}, u32[]{:S(2)}) %copy-start.2) | copy-done | bytes 792
  29.8 0.7 %copy-done.3 = s32[8,4]{0,1:T(4,128)S(1)} copy-done((s32[8,4]{0,1:T(4,128)S(1)}, s32[8,4]{0,1:T(4,128)}, u32[]{:S(2)}) %copy-start.3) | copy-done | bytes 152
  30.5 0.7 %copy-done.4 = s32[8]{0:T(128)S(1)} copy-done((s32[8]{0:T(128)S(1)}, s32[8]{0:T(128)}, u32[]{:S(2)}) %copy-start.4) | copy-done | bytes 56
  31.1 0.7 %copy-done.5 = s32[8]{0:T(128)S(1)} copy-done((s32[8]{0:T(128)S(1)}, s32[8]{0:T(128)}, u32[]{:S(2)}) %copy-start.5) | copy-done | bytes 56
  31.8 1.5 %shard_map.76 = (s32[16]{0:T(128)S(1)}, f32[12]{0:T(128)S(1)}) custom-call(s32[8]{0:T(128)S(1)} %copy-done.4, f32[8,24]{1,0:T(8,128)S(1)} %copy-done.2, s32[4,8]{1,0:T(4,128)S(1)} %bitcast.1, s32[8]{0:T(128)S(1)} %copy-done.5), custom_call_target="tpu_custom_call" | custom-call | tf_op jit(solution)/shard_map/pallas_call | solution.py:65
  33.3 0.0 collective-permute-done.12.refs_3_
  33.3 0.0 collective-permute-done.15.refs_6_
  33.3 0.0 collective-permute-done.16.refs_7_
  33.4 0.1 collective-permute-start.18
  33.4 0.5 collective-permute-start.17
  33.9 1.8 %collective-permute-start.19 = (bf16[512,256]{1,0:T(8,128)(2,1)S(1)}, bf16[512,256]{1,0:T(8,128)(2,1)S(1)}, u32[]{:S(2)}, u32[]{:S(2)}) collective-permute-start(bf16[512,256]{1,0:T(8,128)(2,1)S(1)} %collective-permute-done.7.refs_10_), channel_id=1, source_target_pairs={{0,8},{4,12},{8,16},{12,20},{16,24},{20,28},{24,0},{28,4},{1,9},{5... | collective-permute-start | bytes 786440 | tf_op jit(solution)/shard_map/ppermute | solution.py:333
  35.7 10.4 %shard_map.77 = (f32[2,4,384,256]{3,2,1,0:T(8,128)S(1)}, f32[2,4,384,128]{3,2,1,0:T(8,128)S(1)}, bf16[8,64,768]{2,1,0:T(8,128)(2,1)S(1)}) custom-call(s32[16]{0:T(128)S(1)} %get-tuple-element.73.table_ref, f32[12]{0:T(128)S(1)} %get-tuple-element.74.factor_ref, bf16[64,768]{1,0:T(8,128)(2,1)S(1)} %get-tuple-element.75.refs_0_, ...), custom_call_target="tpu_custom_call" | custom-call | flops 1207959552 | bytes 1572864 | tf_op jit(solution)/shard_map/pallas_call | solution.py:310
  46.2 0.0 collective-permute-done.19.refs_3_
  46.2 0.4 collective-permute-start.20
  46.6 1.2 %collective-permute-done.20.refs_4_ = bf16[512,256]{1,0:T(8,128)(2,1)S(1)} collective-permute-done((bf16[512,256]{1,0:T(8,128)(2,1)S(1)}, bf16[512,256]{1,0:T(8,128)(2,1)S(1)}, u32[]{:S(2)}, u32[]{:S(2)}) %collective-permute-start.20) | collective-permute-done | bytes 262176 | tf_op jit(solution)/shard_map/ppermute | solution.py:336
  47.8 3.5 %shard_map.78 = (bf16[64,768]{1,0:T(8,128)(2,1)S(1)}, bf16[64,768]{1,0:T(8,128)(2,1)S(1)}, bf16[64,768]{1,0:T(8,128)(2,1)S(1)}, bf16[64,768]{1,0:T(8,128)(2,1)S(...) custom-call(s32[16]{0:T(128)S(1)} %get-tuple-element.73.table_ref, ...), custom_call_target="tpu_custom_call", output_to_operand_aliasing={{8}: (3, {}), {9}: (4, {})} | custom-call | flops 402653184 | bytes 1572864 | tf_op jit(solution)/shard_map/pallas_call | solution.py:310
  51.3 1.6 %collective-permute-start.21 = (bf16[64,768]{1,0:T(8,128)(2,1)S(1)}, bf16[64,768]{1,0:T(8,128)(2,1)S(1)}, u32[]{:S(2)}, u32[]{:S(2)}) collective-permute-start(bf16[64,768]{1,0:T(8,128)(2,1)S(1)} %get-tuple-element.94), channel_id=1, source_target_pairs={{0,6},{1,7},{2,4},{3,5},{4,2},{5,3},{6,0},{7,1},{8,14},{9,15},{10,... | collective-permute-start | bytes 294920 | tf_op jit(solution)/shard_map/ppermute | solution.py:329
  52.9 1.4 %collective-permute-start.22 = (bf16[64,768]{1,0:T(8,128)(2,1)S(1)}, bf16[64,768]{1,0:T(8,128)(2,1)S(1)}, u32[]{:S(2)}, u32[]{:S(2)}) collective-permute-start(bf16[64,768]{1,0:T(8,128)(2,1)S(1)} %get-tuple-element.95), channel_id=1, source_target_pairs={{0,7},{1,6},{2,5},{3,4},{4,3},{5,2},{6,1},{7,0},{8,15},{9,14},{10,... | collective-permute-start | bytes 294920 | tf_op jit(solution)/shard_map/ppermute | solution.py:329
  54.2 0.6 collective-permute-start.23
  54.8 1.2 %collective-permute-start.24 = (bf16[64,768]{1,0:T(8,128)(2,1)S(1)}, bf16[64,768]{1,0:T(8,128)(2,1)S(1)}, u32[]{:S(2)}, u32[]{:S(2)}) collective-permute-start(bf16[64,768]{1,0:T(8,128)(2,1)S(1)} %get-tuple-element.97), channel_id=1, source_target_pairs={{0,2},{1,5},{2,0},{3,7},{4,6},{5,1},{6,4},{7,3},{8,10},{9,13},{10,... | collective-permute-start | bytes 294920 | tf_op jit(solution)/shard_map/ppermute | solution.py:329
  56.0 0.9 %collective-permute-start.25 = (bf16[64,768]{1,0:T(8,128)(2,1)S(1)}, bf16[64,768]{1,0:T(8,128)(2,1)S(1)}, u32[]{:S(2)}, u32[]{:S(2)}) collective-permute-start(bf16[64,768]{1,0:T(8,128)(2,1)S(1)} %get-tuple-element.98), channel_id=1, source_target_pairs={{0,5},{1,2},{2,7},{3,0},{4,1},{5,6},{6,3},{7,4},{8,13},{9,10},{10,... | collective-permute-start | bytes 294920 | tf_op jit(solution)/shard_map/ppermute | solution.py:329
  57.0 0.0 collective-permute-done.21.refs_1_
  57.0 2.2 %collective-permute-start.26 = (bf16[64,768]{1,0:T(8,128)(2,1)S(1)}, bf16[64,768]{1,0:T(8,128)(2,1)S(1)}, u32[]{:S(2)}, u32[]{:S(2)}) collective-permute-start(bf16[64,768]{1,0:T(8,128)(2,1)S(1)} %get-tuple-element.99), channel_id=1, source_target_pairs={{0,3},{1,4},{2,1},{3,6},{4,7},{5,0},{6,5},{7,2},{8,11},{9,12},{10,... | collective-permute-start | bytes 294920 | tf_op jit(solution)/shard_map/ppermute | solution.py:329
  59.1 0.0 collective-permute-done.22.refs_2_
  59.2 0.5 collective-permute-start.27
  59.6 1.6 %collective-permute-done.23.refs_3_ = bf16[64,768]{1,0:T(8,128)(2,1)S(1)} collective-permute-done((bf16[64,768]{1,0:T(8,128)(2,1)S(1)}, bf16[64,768]{1,0:T(8,128)(2,1)S(1)}, u32[]{:S(2)}, u32[]{:S(2)}) %collective-permute-start.23) | collective-permute-done | bytes 98336 | tf_op jit(solution)/shard_map/ppermute | solution.py:329
  61.2 0.0 collective-permute-done.24.refs_4_
  61.2 1.6 %collective-permute-done.25.refs_5_ = bf16[64,768]{1,0:T(8,128)(2,1)S(1)} collective-permute-done((bf16[64,768]{1,0:T(8,128)(2,1)S(1)}, bf16[64,768]{1,0:T(8,128)(2,1)S(1)}, u32[]{:S(2)}, u32[]{:S(2)}) %collective-permute-start.25) | collective-permute-done | bytes 98336 | tf_op jit(solution)/shard_map/ppermute | solution.py:329
  62.8 0.5 collective-permute-done.26.refs_6_
  63.3 0.0 collective-permute-done.27.refs_7_
  63.3 0.9 %shard_map.79 = bf16[128,3072]{1,0:T(8,128)(2,1)} custom-call(bf16[64,768]{1,0:T(8,128)(2,1)S(1)} %get-tuple-element.93.refs_0_, bf16[64,768]{1,0:T(8,128)(2,1)S(1)} %collective-permute-done.21.refs_1_, bf16[64,768]{1,0:T(8,128)(2,1)S(1)} %collective-permute-done.22.refs_2_, bf16[64,768]{1,0:T(8,128)(2,1)S(1)} %collective-permute-done.23.refs_3_, ...), custom_call_target="tpu_custom_call" | custom-call | tf_op jit(solution)/shard_map/pallas_call | solution.py:167
  (11 shorter events, 0.0 us)
Async XLA Ops:
  1.7 6.0 %collective-permute-start = (bf16[64,256]{1,0:T(8,128)(2,1)}, bf16[64,256]{1,0:T(8,128)(2,1)S(1)}, u32[]{:S(2)}, u32[]{:S(2)}) collective-permute-start(bf16[64,256]{1,0:T(8,128)(2,1)} %get-tuple-element.54), channel_id=1, source_target_pairs={{0,6},{1,7},{2,4},{3,5},{4,2},{5,3},{6,0},{7,1},{8,14},{9,15},{10,... | collective-permute-start | bytes 98312 | tf_op jit(solution)/shard_map/ppermute | solution.py:329
  4.0 5.3 %collective-permute-start.1 = (bf16[64,256]{1,0:T(8,128)(2,1)}, bf16[64,256]{1,0:T(8,128)(2,1)S(1)}, u32[]{:S(2)}, u32[]{:S(2)}) collective-permute-start(bf16[64,256]{1,0:T(8,128)(2,1)} %get-tuple-element.55), channel_id=1, source_target_pairs={{0,7},{1,6},{2,5},{3,4},{4,3},{5,2},{6,1},{7,0},{8,15},{9,14},{10,... | collective-permute-start | bytes 98312 | tf_op jit(solution)/shard_map/ppermute | solution.py:329
  5.0 4.6 %collective-permute-start.2 = (bf16[64,256]{1,0:T(8,128)(2,1)}, bf16[64,256]{1,0:T(8,128)(2,1)S(1)}, u32[]{:S(2)}, u32[]{:S(2)}) collective-permute-start(bf16[64,256]{1,0:T(8,128)(2,1)} %get-tuple-element.56), channel_id=1, source_target_pairs={{0,4},{1,3},{2,6},{3,1},{4,0},{5,7},{6,2},{7,5},{8,12},{9,11},{10,... | collective-permute-start | bytes 98312 | tf_op jit(solution)/shard_map/ppermute | solution.py:329
  6.2 3.4 %collective-permute-start.3 = (bf16[64,256]{1,0:T(8,128)(2,1)}, bf16[64,256]{1,0:T(8,128)(2,1)S(1)}, u32[]{:S(2)}, u32[]{:S(2)}) collective-permute-start(bf16[64,256]{1,0:T(8,128)(2,1)} %get-tuple-element.57), channel_id=1, source_target_pairs={{0,2},{1,5},{2,0},{3,7},{4,6},{5,1},{6,4},{7,3},{8,10},{9,13},{10,... | collective-permute-start | bytes 98312 | tf_op jit(solution)/shard_map/ppermute | solution.py:329
  7.5 4.1 %collective-permute-start.4 = (bf16[64,256]{1,0:T(8,128)(2,1)}, bf16[64,256]{1,0:T(8,128)(2,1)S(1)}, u32[]{:S(2)}, u32[]{:S(2)}) collective-permute-start(bf16[64,256]{1,0:T(8,128)(2,1)} %get-tuple-element.58), channel_id=1, source_target_pairs={{0,5},{1,2},{2,7},{3,0},{4,1},{5,6},{6,3},{7,4},{8,13},{9,10},{10,... | collective-permute-start | bytes 98312 | tf_op jit(solution)/shard_map/ppermute | solution.py:329
  7.7 3.9 %collective-permute-start.5 = (bf16[64,256]{1,0:T(8,128)(2,1)}, bf16[64,256]{1,0:T(8,128)(2,1)S(1)}, u32[]{:S(2)}, u32[]{:S(2)}) collective-permute-start(bf16[64,256]{1,0:T(8,128)(2,1)} %get-tuple-element.59), channel_id=1, source_target_pairs={{0,3},{1,4},{2,1},{3,6},{4,7},{5,0},{6,5},{7,2},{8,11},{9,12},{10,... | collective-permute-start | bytes 98312 | tf_op jit(solution)/shard_map/ppermute | solution.py:329
  9.2 2.3 %collective-permute-start.6 = (bf16[64,256]{1,0:T(8,128)(2,1)}, bf16[64,256]{1,0:T(8,128)(2,1)S(1)}, u32[]{:S(2)}, u32[]{:S(2)}) collective-permute-start(bf16[64,256]{1,0:T(8,128)(2,1)} %get-tuple-element.60), channel_id=1, source_target_pairs={{0,1},{1,0},{2,3},{3,2},{4,5},{5,4},{6,7},{7,6},{8,9},{9,8},{10,11... | collective-permute-start | bytes 98312 | tf_op jit(solution)/shard_map/ppermute | solution.py:329
  11.6 0.8 %copy-start.1 = (bf16[64,256]{1,0:T(8,128)(2,1)S(1)}, bf16[64,256]{1,0:T(8,128)(2,1)}, u32[]{:S(2)}) copy-start(bf16[64,256]{1,0:T(8,128)(2,1)} %get-tuple-element.53.refs_0_) | copy-start | bytes 98308
  12.4 3.7 %collective-permute-start.9 = (bf16[512,256]{1,0:T(8,128)(2,1)S(1)}, bf16[512,256]{1,0:T(8,128)(2,1)S(1)}, u32[]{:S(2)}, u32[]{:S(2)}) collective-permute-start(bf16[512,256]{1,0:T(8,128)(2,1)S(1)} %shard_map.74.refs_8_), channel_id=1, source_target_pairs={{0,1},{1,0},{2,3},{3,2},{4,5},{5,4},{6,7},{7,6},{8,9},{9,8},{10,11... | collective-permute-start | bytes 786440 | tf_op jit(solution)/shard_map/ppermute | solution.py:336
  12.8 9.6 %collective-permute-start.8 = (bf16[512,256]{1,0:T(8,128)(2,1)S(1)}, bf16[512,256]{1,0:T(8,128)(2,1)S(1)}, u32[]{:S(2)}, u32[]{:S(2)}) collective-permute-start(bf16[512,256]{1,0:T(8,128)(2,1)S(1)} %shard_map.74.refs_8_), channel_id=1, source_target_pairs={{0,24},{4,28},{8,0},{12,4},{16,8},{20,12},{24,16},{28,20},{1,25},{... | collective-permute-start | bytes 786440 | tf_op jit(solution)/shard_map/ppermute | solution.py:333
  13.0 13.1 %collective-permute-start.7 = (bf16[512,256]{1,0:T(8,128)(2,1)S(1)}, bf16[512,256]{1,0:T(8,128)(2,1)S(1)}, u32[]{:S(2)}, u32[]{:S(2)}) collective-permute-start(bf16[512,256]{1,0:T(8,128)(2,1)S(1)} %shard_map.74.refs_8_), channel_id=1, source_target_pairs={{0,8},{4,12},{8,16},{12,20},{16,24},{20,28},{24,0},{28,4},{1,9},{5... | collective-permute-start | bytes 786440 | tf_op jit(solution)/shard_map/ppermute | solution.py:333
  16.1 1.1 %copy-start = (bf16[128,3072]{1,0:T(8,128)(2,1)S(1)}, bf16[128,3072]{1,0:T(8,128)(2,1)}, u32[]{:S(2)}) copy-start(bf16[128,3072]{1,0:T(8,128)(2,1)} %q_ref) | copy-start | bytes 2359300
  17.3 10.5 %collective-permute-start.10 = (bf16[64,768]{1,0:T(8,128)(2,1)S(1)}, bf16[64,768]{1,0:T(8,128)(2,1)S(1)}, u32[]{:S(2)}, u32[]{:S(2)}) collective-permute-start(bf16[64,768]{1,0:T(8,128)(2,1)S(1)} %get-tuple-element.64), channel_id=1, source_target_pairs={{0,6},{1,7},{2,4},{3,5},{4,2},{5,3},{6,0},{7,1},{8,14},{9,15},{10,... | collective-permute-start | bytes 294920 | tf_op jit(solution)/shard_map/ppermute | solution.py:329
  18.9 9.3 %collective-permute-start.11 = (bf16[64,768]{1,0:T(8,128)(2,1)S(1)}, bf16[64,768]{1,0:T(8,128)(2,1)S(1)}, u32[]{:S(2)}, u32[]{:S(2)}) collective-permute-start(bf16[64,768]{1,0:T(8,128)(2,1)S(1)} %get-tuple-element.65), channel_id=1, source_target_pairs={{0,7},{1,6},{2,5},{3,4},{4,3},{5,2},{6,1},{7,0},{8,15},{9,14},{10,... | collective-permute-start | bytes 294920 | tf_op jit(solution)/shard_map/ppermute | solution.py:329
  20.6 12.7 %collective-permute-start.12 = (bf16[64,768]{1,0:T(8,128)(2,1)S(1)}, bf16[64,768]{1,0:T(8,128)(2,1)S(1)}, u32[]{:S(2)}, u32[]{:S(2)}) collective-permute-start(bf16[64,768]{1,0:T(8,128)(2,1)S(1)} %get-tuple-element.66), channel_id=1, source_target_pairs={{0,4},{1,3},{2,6},{3,1},{4,0},{5,7},{6,2},{7,5},{8,12},{9,11},{10,... | collective-permute-start | bytes 294920 | tf_op jit(solution)/shard_map/ppermute | solution.py:329
  22.4 10.9 %collective-permute-start.13 = (bf16[64,768]{1,0:T(8,128)(2,1)S(1)}, bf16[64,768]{1,0:T(8,128)(2,1)S(1)}, u32[]{:S(2)}, u32[]{:S(2)}) collective-permute-start(bf16[64,768]{1,0:T(8,128)(2,1)S(1)} %get-tuple-element.67), channel_id=1, source_target_pairs={{0,2},{1,5},{2,0},{3,7},{4,6},{5,1},{6,4},{7,3},{8,10},{9,13},{10,... | collective-permute-start | bytes 294920 | tf_op jit(solution)/shard_map/ppermute | solution.py:329
  26.1 7.3 %collective-permute-start.14 = (bf16[64,768]{1,0:T(8,128)(2,1)S(1)}, bf16[64,768]{1,0:T(8,128)(2,1)S(1)}, u32[]{:S(2)}, u32[]{:S(2)}) collective-permute-start(bf16[64,768]{1,0:T(8,128)(2,1)S(1)} %get-tuple-element.68), channel_id=1, source_target_pairs={{0,5},{1,2},{2,7},{3,0},{4,1},{5,6},{6,3},{7,4},{8,13},{9,10},{10,... | collective-permute-start | bytes 294920 | tf_op jit(solution)/shard_map/ppermute | solution.py:329
  27.8 5.5 %collective-permute-start.15 = (bf16[64,768]{1,0:T(8,128)(2,1)S(1)}, bf16[64,768]{1,0:T(8,128)(2,1)S(1)}, u32[]{:S(2)}, u32[]{:S(2)}) collective-permute-start(bf16[64,768]{1,0:T(8,128)(2,1)S(1)} %get-tuple-element.69), channel_id=1, source_target_pairs={{0,3},{1,4},{2,1},{3,6},{4,7},{5,0},{6,5},{7,2},{8,11},{9,12},{10,... | collective-permute-start | bytes 294920 | tf_op jit(solution)/shard_map/ppermute | solution.py:329
  28.2 5.2 %collective-permute-start.16 = (bf16[64,768]{1,0:T(8,128)(2,1)S(1)}, bf16[64,768]{1,0:T(8,128)(2,1)S(1)}, u32[]{:S(2)}, u32[]{:S(2)}) collective-permute-start(bf16[64,768]{1,0:T(8,128)(2,1)S(1)} %get-tuple-element.70), channel_id=1, source_target_pairs={{0,1},{1,0},{2,3},{3,2},{4,5},{5,4},{6,7},{7,6},{8,9},{9,8},{10,11... | collective-permute-start | bytes 294920 | tf_op jit(solution)/shard_map/ppermute | solution.py:329
  29.1 0.7 %copy-start.2 = (f32[8,24]{1,0:T(8,128)S(1)}, f32[8,24]{1,0:T(8,128)}, u32[]{:S(2)}) copy-start(f32[8,24]{1,0:T(8,128)} %temps_ref.1) | copy-start | bytes 2308
  29.8 0.7 %copy-start.3 = (s32[8,4]{0,1:T(4,128)S(1)}, s32[8,4]{0,1:T(4,128)}, u32[]{:S(2)}) copy-start(s32[8,4]{0,1:T(4,128)} %param.12) | copy-start | bytes 388
  30.5 0.7 %copy-start.4 = (s32[8]{0:T(128)S(1)}, s32[8]{0:T(128)}, u32[]{:S(2)}) copy-start(s32[8]{0:T(128)} %levels_ref.1) | copy-start | bytes 100
  31.1 0.7 %copy-start.5 = (s32[8]{0:T(128)S(1)}, s32[8]{0:T(128)}, u32[]{:S(2)}) copy-start(s32[8]{0:T(128)} %counts_ref.1) | copy-start | bytes 100
  33.4 2.4 %collective-permute-start.18 = (bf16[512,256]{1,0:T(8,128)(2,1)S(1)}, bf16[512,256]{1,0:T(8,128)(2,1)S(1)}, u32[]{:S(2)}, u32[]{:S(2)}) collective-permute-start(bf16[512,256]{1,0:T(8,128)(2,1)S(1)} %collective-permute-done.8.refs_12_), channel_id=1, source_target_pairs={{0,1},{1,0},{2,3},{3,2},{4,5},{5,4},{6,7},{7,6},{8,9},{9,8},{10,11... | collective-permute-start | bytes 786440 | tf_op jit(solution)/shard_map/ppermute | solution.py:336
  33.4 2.3 %collective-permute-start.17 = (bf16[512,256]{1,0:T(8,128)(2,1)S(1)}, bf16[512,256]{1,0:T(8,128)(2,1)S(1)}, u32[]{:S(2)}, u32[]{:S(2)}) collective-permute-start(bf16[512,256]{1,0:T(8,128)(2,1)S(1)} %collective-permute-done.7.refs_10_), channel_id=1, source_target_pairs={{0,1},{1,0},{2,3},{3,2},{4,5},{5,4},{6,7},{7,6},{8,9},{9,8},{10,11... | collective-permute-start | bytes 786440 | tf_op jit(solution)/shard_map/ppermute | solution.py:336
  33.9 12.2 %collective-permute-start.19 = (bf16[512,256]{1,0:T(8,128)(2,1)S(1)}, bf16[512,256]{1,0:T(8,128)(2,1)S(1)}, u32[]{:S(2)}, u32[]{:S(2)}) collective-permute-start(bf16[512,256]{1,0:T(8,128)(2,1)S(1)} %collective-permute-done.7.refs_10_), channel_id=1, source_target_pairs={{0,8},{4,12},{8,16},{12,20},{16,24},{20,28},{24,0},{28,4},{1,9},{5... | collective-permute-start | bytes 786440 | tf_op jit(solution)/shard_map/ppermute | solution.py:333
  46.2 1.6 %collective-permute-start.20 = (bf16[512,256]{1,0:T(8,128)(2,1)S(1)}, bf16[512,256]{1,0:T(8,128)(2,1)S(1)}, u32[]{:S(2)}, u32[]{:S(2)}) collective-permute-start(bf16[512,256]{1,0:T(8,128)(2,1)S(1)} %collective-permute-done.19.refs_3_), channel_id=1, source_target_pairs={{0,1},{1,0},{2,3},{3,2},{4,5},{5,4},{6,7},{7,6},{8,9},{9,8},{10,11... | collective-permute-start | bytes 786440 | tf_op jit(solution)/shard_map/ppermute | solution.py:336
  51.3 5.7 %collective-permute-start.21 = (bf16[64,768]{1,0:T(8,128)(2,1)S(1)}, bf16[64,768]{1,0:T(8,128)(2,1)S(1)}, u32[]{:S(2)}, u32[]{:S(2)}) collective-permute-start(bf16[64,768]{1,0:T(8,128)(2,1)S(1)} %get-tuple-element.94), channel_id=1, source_target_pairs={{0,6},{1,7},{2,4},{3,5},{4,2},{5,3},{6,0},{7,1},{8,14},{9,15},{10,... | collective-permute-start | bytes 294920 | tf_op jit(solution)/shard_map/ppermute | solution.py:329
  52.9 6.3 %collective-permute-start.22 = (bf16[64,768]{1,0:T(8,128)(2,1)S(1)}, bf16[64,768]{1,0:T(8,128)(2,1)S(1)}, u32[]{:S(2)}, u32[]{:S(2)}) collective-permute-start(bf16[64,768]{1,0:T(8,128)(2,1)S(1)} %get-tuple-element.95), channel_id=1, source_target_pairs={{0,7},{1,6},{2,5},{3,4},{4,3},{5,2},{6,1},{7,0},{8,15},{9,14},{10,... | collective-permute-start | bytes 294920 | tf_op jit(solution)/shard_map/ppermute | solution.py:329
  54.2 7.0 %collective-permute-start.23 = (bf16[64,768]{1,0:T(8,128)(2,1)S(1)}, bf16[64,768]{1,0:T(8,128)(2,1)S(1)}, u32[]{:S(2)}, u32[]{:S(2)}) collective-permute-start(bf16[64,768]{1,0:T(8,128)(2,1)S(1)} %get-tuple-element.96), channel_id=1, source_target_pairs={{0,4},{1,3},{2,6},{3,1},{4,0},{5,7},{6,2},{7,5},{8,12},{9,11},{10,... | collective-permute-start | bytes 294920 | tf_op jit(solution)/shard_map/ppermute | solution.py:329
  54.8 6.4 %collective-permute-start.24 = (bf16[64,768]{1,0:T(8,128)(2,1)S(1)}, bf16[64,768]{1,0:T(8,128)(2,1)S(1)}, u32[]{:S(2)}, u32[]{:S(2)}) collective-permute-start(bf16[64,768]{1,0:T(8,128)(2,1)S(1)} %get-tuple-element.97), channel_id=1, source_target_pairs={{0,2},{1,5},{2,0},{3,7},{4,6},{5,1},{6,4},{7,3},{8,10},{9,13},{10,... | collective-permute-start | bytes 294920 | tf_op jit(solution)/shard_map/ppermute | solution.py:329
  56.0 6.8 %collective-permute-start.25 = (bf16[64,768]{1,0:T(8,128)(2,1)S(1)}, bf16[64,768]{1,0:T(8,128)(2,1)S(1)}, u32[]{:S(2)}, u32[]{:S(2)}) collective-permute-start(bf16[64,768]{1,0:T(8,128)(2,1)S(1)} %get-tuple-element.98), channel_id=1, source_target_pairs={{0,5},{1,2},{2,7},{3,0},{4,1},{5,6},{6,3},{7,4},{8,13},{9,10},{10,... | collective-permute-start | bytes 294920 | tf_op jit(solution)/shard_map/ppermute | solution.py:329
  57.0 6.3 %collective-permute-start.26 = (bf16[64,768]{1,0:T(8,128)(2,1)S(1)}, bf16[64,768]{1,0:T(8,128)(2,1)S(1)}, u32[]{:S(2)}, u32[]{:S(2)}) collective-permute-start(bf16[64,768]{1,0:T(8,128)(2,1)S(1)} %get-tuple-element.99), channel_id=1, source_target_pairs={{0,3},{1,4},{2,1},{3,6},{4,7},{5,0},{6,5},{7,2},{8,11},{9,12},{10,... | collective-permute-start | bytes 294920 | tf_op jit(solution)/shard_map/ppermute | solution.py:329
  59.2 4.1 %collective-permute-start.27 = (bf16[64,768]{1,0:T(8,128)(2,1)S(1)}, bf16[64,768]{1,0:T(8,128)(2,1)S(1)}, u32[]{:S(2)}, u32[]{:S(2)}) collective-permute-start(bf16[64,768]{1,0:T(8,128)(2,1)S(1)} %get-tuple-element.100), channel_id=1, source_target_pairs={{0,1},{1,0},{2,3},{3,2},{4,5},{5,4},{6,7},{7,6},{8,9},{9,8},{10,11... | collective-permute-start | bytes 294920 | tf_op jit(solution)/shard_map/ppermute | solution.py:329
where the time goes:
time: 64.4 us; the launch traced here: 64.2 us
  starting transfers between devices  30.9 us (48%)
  Pallas kernels  18.2 us (28%)
  waiting for transfers between devices  10.5 us (16%)
  local copies, waits for them, and re-layouts  4.57 us (7%)
    ppermute x21, starting transfers between devices, exchange(): lax.ppermute(piece, ('span', 'ctx'), [(f, f ^ step[f % 2]) for f in range...  24.4 us
    pallas_call x2, Pallas kernels, attend(): pl.pallas_call(functools.partial(attend_kernel, backs, first, final), out...  13.9 us
    ppermute x21, waiting for transfers between devices, exchange(): lax.ppermute(piece, ('span', 'ctx'), [(f, f ^ step[f % 2]) for f in range...  5.69 us
    ppermute x3, starting transfers between devices, up(): lax.ppermute(a, 'span', [(s, (s + 2 * steps) % spans) for s in range(span...  5.08 us
    unnamed x12, local copies, waits for them, and re-layouts  4.57 us
    ppermute x3, waiting for transfers between devices, up(): lax.ppermute(a, 'span', [(s, (s + 2 * steps) % spans) for s in range(span...  3.57 us
    pallas_call x1, Pallas kernels, begin(): pl.pallas_call(begin_kernel, out_shape=[jax.ShapeDtypeStruct(shape, jnp.b...  1.73 us
    pallas_call x1, Pallas kernels, tabulate(): pl.pallas_call(functools.partial(table_kernel, planes), out_shape=[jax.Sh...  1.52 us
  transfers between devices with their start and end apart: 28, of which 7 were waited for; matrix products, arithmetic and copies ran while one was open for 0% of the time, Pallas kernels for 19%

commit v1 on v0

--- a/solution.py
+++ b/solution.py
@@ -335,14 +335,15 @@
     def near(a):
         return lax.ppermute(a, "ctx", other_core)
 
-    own = gather(exchange(begin(keys, values)))
+    tables = tabulate(spans // 2, levels, temps, jnp.transpose(ctx_list), counts)
+    kv, tables = lax.optimization_barrier((exchange(begin(keys, values)), tables))
+    own = gather(kv)
     slabs = {0: own, 1: up(own, 1), last: up(own, last)}
     others = {0: near(own)}
     others, queries = lax.optimization_barrier((others, queries))
     q = exchange(cut(queries))
-    tables = tabulate(spans // 2, levels, temps, jnp.transpose(ctx_list), counts)
-    slabs, others, q, tables = lax.optimization_barrier((slabs, others, q, tables))
     others |= {back: near(slabs[back]) for back in (1, last)}
+    slabs, others, q = lax.optimization_barrier((slabs, others, q))
     stage = sorted(slabs)
     state = None
     for back in range(2, last):

time: 64.4 us -> 72.8 us (1.13); the launches traced: 64.2 us -> 71.5 us
  waiting for transfers between devices: 10.5 us -> 19.8 us
  starting transfers between devices: 30.9 us -> 28.9 us
    ppermute x21, waiting for transfers between devices: 5.69 us -> 12.8 us  [exchange(): lax.ppermute(piece, ('span', 'ctx'), [(f, f ^ step[f % 2]) for f in range...]
    ppermute x21, starting transfers between devices: 24.4 us -> 18.7 us  [exchange(): lax.ppermute(piece, ('span', 'ctx'), [(f, f ^ step[f % 2]) for f in range...]
    ppermute x4, starting transfers between devices: 1.43 us -> 5.11 us  [near(): return lax.ppermute(a, 'ctx', other_core)]
    ppermute x3, waiting for transfers between devices: 3.57 us -> 5.79 us  [up(): lax.ppermute(a, 'span', [(s, (s + 2 * steps) % spans) for s in range(span...]
  transfers between devices with their start and end apart: 28 -> 28, of which waited for: 7 -> 12; matrix products, arithmetic and copies ran while one was open for 0% -> 0% of each run, Pallas kernels for 19% -> 17%
where the time goes in v1:
time: 72.8 us; the launch traced here: 71.5 us
  starting transfers between devices  28.9 us (40%)
  waiting for transfers between devices  19.8 us (27%)
  Pallas kernels  18.1 us (25%)
  local copies, waits for them, and re-layouts  4.56 us (6%)
    ppermute x21, starting transfers between devices, exchange(): lax.ppermute(piece, ('span', 'ctx'), [(f, f ^ step[f % 2]) for f in range...  18.7 us
    pallas_call x2, Pallas kernels, attend(): pl.pallas_call(functools.partial(attend_kernel, backs, first, final), out...  13.9 us
    ppermute x21, waiting for transfers between devices, exchange(): lax.ppermute(piece, ('span', 'ctx'), [(f, f ^ step[f % 2]) for f in range...  12.8 us
    ppermute x3, waiting for transfers between devices, up(): lax.ppermute(a, 'span', [(s, (s + 2 * steps) % spans) for s in range(span...  5.79 us
    ppermute x3, starting transfers between devices, up(): lax.ppermute(a, 'span', [(s, (s + 2 * steps) % spans) for s in range(span...  5.11 us
    ppermute x4, starting transfers between devices, near(): return lax.ppermute(a, 'ctx', other_core)  5.11 us
    unnamed x12, local copies, waits for them, and re-layouts  4.56 us
    pallas_call x1, Pallas kernels, begin(): pl.pallas_call(begin_kernel, out_shape=[jax.ShapeDtypeStruct(shape, jnp.b...  1.73 us
  transfers between devices with their start and end apart: 28, of which 12 were waited for; matrix products, arithmetic and copies ran while one was open for 0% of the time, Pallas kernels for 17%

profile of v1, /device:TPU:25, one launch (start us, length us, event | category | flops | bytes accessed | tf_op | source)
XLA Modules:
  0.0 71.5 jit_solution(13083408287722625714)
XLA Ops:
  0.0 1.7 %shard_map.73 = (bf16[64,256]{1,0:T(8,128)(2,1)}, bf16[64,256]{1,0:T(8,128)(2,1)}, bf16[64,256]{1,0:T(8,128)(2,1)}, bf16[64,256]{1,0:T(8,128)(2,1)}, bf16[64,256...) custom-call(bf16[128,512]{1,0:T(8,128)(2,1)} %keys_ref.1, ...), custom_call_target="tpu_custom_call" | custom-call | tf_op jit(solution)/shard_map/pallas_call | solution.py:98
  1.7 2.2 %collective-permute-start = (bf16[64,256]{1,0:T(8,128)(2,1)}, bf16[64,256]{1,0:T(8,128)(2,1)S(1)}, u32[]{:S(2)}, u32[]{:S(2)}) collective-permute-start(bf16[64,256]{1,0:T(8,128)(2,1)} %get-tuple-element.64), channel_id=1, source_target_pairs={{0,6},{1,7},{2,4},{3,5},{4,2},{5,3},{6,0},{7,1},{8,14},{9,15},{10,... | collective-permute-start | bytes 98312 | tf_op jit(solution)/shard_map/ppermute | solution.py:329
  4.0 1.0 %collective-permute-start.1 = (bf16[64,256]{1,0:T(8,128)(2,1)}, bf16[64,256]{1,0:T(8,128)(2,1)S(1)}, u32[]{:S(2)}, u32[]{:S(2)}) collective-permute-start(bf16[64,256]{1,0:T(8,128)(2,1)} %get-tuple-element.65), channel_id=1, source_target_pairs={{0,7},{1,6},{2,5},{3,4},{4,3},{5,2},{6,1},{7,0},{8,15},{9,14},{10,... | collective-permute-start | bytes 98312 | tf_op jit(solution)/shard_map/ppermute | solution.py:329
  5.0 1.2 %collective-permute-start.2 = (bf16[64,256]{1,0:T(8,128)(2,1)}, bf16[64,256]{1,0:T(8,128)(2,1)S(1)}, u32[]{:S(2)}, u32[]{:S(2)}) collective-permute-start(bf16[64,256]{1,0:T(8,128)(2,1)} %get-tuple-element.66), channel_id=1, source_target_pairs={{0,4},{1,3},{2,6},{3,1},{4,0},{5,7},{6,2},{7,5},{8,12},{9,11},{10,... | collective-permute-start | bytes 98312 | tf_op jit(solution)/shard_map/ppermute | solution.py:329
  6.2 1.2 %collective-permute-start.3 = (bf16[64,256]{1,0:T(8,128)(2,1)}, bf16[64,256]{1,0:T(8,128)(2,1)S(1)}, u32[]{:S(2)}, u32[]{:S(2)}) collective-permute-start(bf16[64,256]{1,0:T(8,128)(2,1)} %get-tuple-element.67), channel_id=1, source_target_pairs={{0,2},{1,5},{2,0},{3,7},{4,6},{5,1},{6,4},{7,3},{8,10},{9,13},{10,... | collective-permute-start | bytes 98312 | tf_op jit(solution)/shard_map/ppermute | solution.py:329
  7.5 0.2 collective-permute-start.4
  7.7 0.0 collective-permute-done.refs_1_
  7.7 1.5 %collective-permute-start.5 = (bf16[64,256]{1,0:T(8,128)(2,1)}, bf16[64,256]{1,0:T(8,128)(2,1)S(1)}, u32[]{:S(2)}, u32[]{:S(2)}) collective-permute-start(bf16[64,256]{1,0:T(8,128)(2,1)} %get-tuple-element.69), channel_id=1, source_target_pairs={{0,3},{1,4},{2,1},{3,6},{4,7},{5,0},{6,5},{7,2},{8,11},{9,12},{10,... | collective-permute-start | bytes 98312 | tf_op jit(solution)/shard_map/ppermute | solution.py:329
  9.2 0.0 collective-permute-done.1.refs_2_
  9.2 0.4 collective-permute-start.6
  9.6 0.7 copy-done.2
  10.3 0.7 copy-done.3
  11.0 0.7 copy-done.4
  11.6 0.7 copy-done.5
  12.3 1.5 %shard_map.74 = (s32[16]{0:T(128)S(1)}, f32[12]{0:T(128)S(1)}) custom-call(s32[8]{0:T(128)S(1)} %copy-done.4, f32[8,24]{1,0:T(8,128)S(1)} %copy-done.2, s32[4,8]{1,0:T(4,128)S(1)} %bitcast.1, s32[8]{0:T(128)S(1)} %copy-done.5), custom_call_target="tpu_custom_call" | custom-call | tf_op jit(solution)/shard_map/pallas_call | solution.py:65
  13.8 0.0 collective-permute-done.2.refs_3_
  13.8 0.0 collective-permute-done.3.refs_4_
  13.9 0.0 collective-permute-done.4.refs_5_
  13.9 0.0 collective-permute-done.5.refs_6_
  13.9 0.0 collective-permute-done.6.refs_7_
  13.9 0.0 copy-start.1
  13.9 0.7 %copy-done.1 = bf16[64,256]{1,0:T(8,128)(2,1)S(1)} copy-done((bf16[64,256]{1,0:T(8,128)(2,1)S(1)}, bf16[64,256]{1,0:T(8,128)(2,1)}, u32[]{:S(2)}) %copy-start.1) | copy-done | bytes 32792
  14.7 0.2 collective-permute-start.9
  14.9 0.2 collective-permute-start.8
  15.0 3.1 %collective-permute-start.7 = (bf16[512,256]{1,0:T(8,128)(2,1)S(1)}, bf16[512,256]{1,0:T(8,128)(2,1)S(1)}, u32[]{:S(2)}, u32[]{:S(2)}) collective-permute-start(bf16[512,256]{1,0:T(8,128)(2,1)S(1)} %shard_map.75.refs_8_), channel_id=1, source_target_pairs={{0,8},{4,12},{8,16},{12,20},{16,24},{20,28},{24,0},{28,4},{1,9},{5... | collective-permute-start | bytes 786440 | tf_op jit(solution)/shard_map/ppermute | solution.py:333
  18.1 0.0 collective-permute-done.9.refs_9_
  18.1 1.1 %copy-done = bf16[128,3072]{1,0:T(8,128)(2,1)S(1)} copy-done((bf16[128,3072]{1,0:T(8,128)(2,1)S(1)}, bf16[128,3072]{1,0:T(8,128)(2,1)}, u32[]{:S(2)}) %copy-start) | copy-done | bytes 786456
  19.3 0.1 shard_map.76
  19.3 0.7 collective-permute-start.12
  20.0 4.2 %collective-permute-done.8.refs_12_ = bf16[512,256]{1,0:T(8,128)(2,1)S(1)} collective-permute-done((bf16[512,256]{1,0:T(8,128)(2,1)S(1)}, bf16[512,256]{1,0:T(8,128)(2,1)S(1)}, u32[]{:S(2)}, u32[]{:S(2)}) %collective-permute-start.8) | collective-permute-done | bytes 262176 | tf_op jit(solution)/shard_map/ppermute | solution.py:333
  24.2 2.1 %collective-permute-start.11 = (bf16[512,256]{1,0:T(8,128)(2,1)S(1)}, bf16[512,256]{1,0:T(8,128)(2,1)S(1)}, u32[]{:S(2)}, u32[]{:S(2)}) collective-permute-start(bf16[512,256]{1,0:T(8,128)(2,1)S(1)} %collective-permute-done.8.refs_12_), channel_id=1, source_target_pairs={{0,1},{1,0},{2,3},{3,2},{4,5},{5,4},{6,7},{7,6},{8,9},{9,8},{10,11... | collective-permute-start | bytes 786440 | tf_op jit(solution)/shard_map/ppermute | solution.py:336
  26.3 1.6 %collective-permute-done.7.refs_10_ = bf16[512,256]{1,0:T(8,128)(2,1)S(1)} collective-permute-done((bf16[512,256]{1,0:T(8,128)(2,1)S(1)}, bf16[512,256]{1,0:T(8,128)(2,1)S(1)}, u32[]{:S(2)}, u32[]{:S(2)}) %collective-permute-start.7) | collective-permute-done | bytes 262176 | tf_op jit(solution)/shard_map/ppermute | solution.py:333
  27.8 1.6 %collective-permute-start.10 = (bf16[512,256]{1,0:T(8,128)(2,1)S(1)}, bf16[512,256]{1,0:T(8,128)(2,1)S(1)}, u32[]{:S(2)}, u32[]{:S(2)}) collective-permute-start(bf16[512,256]{1,0:T(8,128)(2,1)S(1)} %collective-permute-done.7.refs_10_), channel_id=1, source_target_pairs={{0,1},{1,0},{2,3},{3,2},{4,5},{5,4},{6,7},{7,6},{8,9},{9,8},{10,11... | collective-permute-start | bytes 786440 | tf_op jit(solution)/shard_map/ppermute | solution.py:336
  29.4 0.5 collective-permute-start.13
  29.8 0.8 %collective-permute-start.14 = (bf16[64,768]{1,0:T(8,128)(2,1)S(1)}, bf16[64,768]{1,0:T(8,128)(2,1)S(1)}, u32[]{:S(2)}, u32[]{:S(2)}) collective-permute-start(bf16[64,768]{1,0:T(8,128)(2,1)S(1)} %get-tuple-element.88), channel_id=1, source_target_pairs={{0,4},{1,3},{2,6},{3,1},{4,0},{5,7},{6,2},{7,5},{8,12},{9,11},{10,... | collective-permute-start | bytes 294920 | tf_op jit(solution)/shard_map/ppermute | solution.py:329
  30.7 1.2 %collective-permute-start.15 = (bf16[64,768]{1,0:T(8,128)(2,1)S(1)}, bf16[64,768]{1,0:T(8,128)(2,1)S(1)}, u32[]{:S(2)}, u32[]{:S(2)}) collective-permute-start(bf16[64,768]{1,0:T(8,128)(2,1)S(1)} %get-tuple-element.89), channel_id=1, source_target_pairs={{0,2},{1,5},{2,0},{3,7},{4,6},{5,1},{6,4},{7,3},{8,10},{9,13},{10,... | collective-permute-start | bytes 294920 | tf_op jit(solution)/shard_map/ppermute | solution.py:329
  31.9 3.5 %collective-permute-done.13.refs_2_ = bf16[64,768]{1,0:T(8,128)(2,1)S(1)} collective-permute-done((bf16[64,768]{1,0:T(8,128)(2,1)S(1)}, bf16[64,768]{1,0:T(8,128)(2,1)S(1)}, u32[]{:S(2)}, u32[]{:S(2)}) %collective-permute-start.13) | collective-permute-done | bytes 98336 | tf_op jit(solution)/shard_map/ppermute | solution.py:329
  35.4 0.2 collective-permute-start.16
  35.6 0.3 collective-permute-done.14.refs_3_
  35.9 1.2 %collective-permute-start.17 = (bf16[64,768]{1,0:T(8,128)(2,1)S(1)}, bf16[64,768]{1,0:T(8,128)(2,1)S(1)}, u32[]{:S(2)}, u32[]{:S(2)}) collective-permute-start(bf16[64,768]{1,0:T(8,128)(2,1)S(1)} %get-tuple-element.91), channel_id=1, source_target_pairs={{0,3},{1,4},{2,1},{3,6},{4,7},{5,0},{6,5},{7,2},{8,11},{9,12},{10,... | collective-permute-start | bytes 294920 | tf_op jit(solution)/shard_map/ppermute | solution.py:329
  37.1 0.0 collective-permute-done.15.refs_4_
  37.1 0.1 collective-permute-start.18
  37.2 2.2 %collective-permute-done.16.refs_5_ = bf16[64,768]{1,0:T(8,128)(2,1)S(1)} collective-permute-done((bf16[64,768]{1,0:T(8,128)(2,1)S(1)}, bf16[64,768]{1,0:T(8,128)(2,1)S(1)}, u32[]{:S(2)}, u32[]{:S(2)}) %collective-permute-start.16) | collective-permute-done | bytes 98336 | tf_op jit(solution)/shard_map/ppermute | solution.py:329
  39.4 0.9 %collective-permute-done.17.refs_6_ = bf16[64,768]{1,0:T(8,128)(2,1)S(1)} collective-permute-done((bf16[64,768]{1,0:T(8,128)(2,1)S(1)}, bf16[64,768]{1,0:T(8,128)(2,1)S(1)}, u32[]{:S(2)}, u32[]{:S(2)}) %collective-permute-start.17) | collective-permute-done | bytes 98336 | tf_op jit(solution)/shard_map/ppermute | solution.py:329
  40.3 0.0 collective-permute-done.18.refs_7_
  40.3 1.9 %collective-permute-start.19 = (bf16[512,256]{1,0:T(8,128)(2,1)S(1)}, bf16[512,256]{1,0:T(8,128)(2,1)S(1)}, u32[]{:S(2)}, u32[]{:S(2)}) collective-permute-start(bf16[512,256]{1,0:T(8,128)(2,1)S(1)} %collective-permute-done.7.refs_10_), channel_id=1, source_target_pairs={{0,8},{4,12},{8,16},{12,20},{16,24},{20,28},{24,0},{28,4},{1,9},{5... | collective-permute-start | bytes 786440 | tf_op jit(solution)/shard_map/ppermute | solution.py:333
  42.2 10.3 %shard_map.77 = (f32[2,4,384,256]{3,2,1,0:T(8,128)S(1)}, f32[2,4,384,128]{3,2,1,0:T(8,128)S(1)}, bf16[8,64,768]{2,1,0:T(8,128)(2,1)S(1)}) custom-call(s32[16]{0:T(128)S(1)} %get-tuple-element.73.table_ref, f32[12]{0:T(128)S(1)} %get-tuple-element.74.factor_ref, bf16[64,768]{1,0:T(8,128)(2,1)S(1)} %get-tuple-element.93.refs_0_, ...), custom_call_target="tpu_custom_call" | custom-call | flops 1207959552 | bytes 1572864 | tf_op jit(solution)/shard_map/pallas_call | solution.py:310
  52.5 0.0 collective-permute-done.19.refs_3_
  52.5 1.3 %collective-permute-start.20 = (bf16[512,256]{1,0:T(8,128)(2,1)S(1)}, bf16[512,256]{1,0:T(8,128)(2,1)S(1)}, u32[]{:S(2)}, u32[]{:S(2)}) collective-permute-start(bf16[512,256]{1,0:T(8,128)(2,1)S(1)} %collective-permute-done.19.refs_3_), channel_id=1, source_target_pairs={{0,1},{1,0},{2,3},{3,2},{4,5},{5,4},{6,7},{7,6},{8,9},{9,8},{10,11... | collective-permute-start | bytes 786440 | tf_op jit(solution)/shard_map/ppermute | solution.py:336
  53.8 1.2 %collective-permute-done.20.refs_4_ = bf16[512,256]{1,0:T(8,128)(2,1)S(1)} collective-permute-done((bf16[512,256]{1,0:T(8,128)(2,1)S(1)}, bf16[512,256]{1,0:T(8,128)(2,1)S(1)}, u32[]{:S(2)}, u32[]{:S(2)}) %collective-permute-start.20) | collective-permute-done | bytes 262176 | tf_op jit(solution)/shard_map/ppermute | solution.py:336
  55.0 3.5 %shard_map.78 = (bf16[64,768]{1,0:T(8,128)(2,1)S(1)}, bf16[64,768]{1,0:T(8,128)(2,1)S(1)}, bf16[64,768]{1,0:T(8,128)(2,1)S(1)}, bf16[64,768]{1,0:T(8,128)(2,1)S(...) custom-call(s32[16]{0:T(128)S(1)} %get-tuple-element.73.table_ref, ...), custom_call_target="tpu_custom_call", output_to_operand_aliasing={{8}: (3, {}), {9}: (4, {})} | custom-call | flops 402653184 | bytes 1572864 | tf_op jit(solution)/shard_map/pallas_call | solution.py:310
  58.5 0.7 collective-permute-start.21
  59.2 2.3 %collective-permute-start.22 = (bf16[64,768]{1,0:T(8,128)(2,1)S(1)}, bf16[64,768]{1,0:T(8,128)(2,1)S(1)}, u32[]{:S(2)}, u32[]{:S(2)}) collective-permute-start(bf16[64,768]{1,0:T(8,128)(2,1)S(1)} %get-tuple-element.115), channel_id=1, source_target_pairs={{0,7},{1,6},{2,5},{3,4},{4,3},{5,2},{6,1},{7,0},{8,15},{9,14},{10,... | collective-permute-start | bytes 294920 | tf_op jit(solution)/shard_map/ppermute | solution.py:329
  61.5 0.8 %collective-permute-start.23 = (bf16[64,768]{1,0:T(8,128)(2,1)S(1)}, bf16[64,768]{1,0:T(8,128)(2,1)S(1)}, u32[]{:S(2)}, u32[]{:S(2)}) collective-permute-start(bf16[64,768]{1,0:T(8,128)(2,1)S(1)} %get-tuple-element.116), channel_id=1, source_target_pairs={{0,4},{1,3},{2,6},{3,1},{4,0},{5,7},{6,2},{7,5},{8,12},{9,11},{10,... | collective-permute-start | bytes 294920 | tf_op jit(solution)/shard_map/ppermute | solution.py:329
  62.3 0.1 collective-permute-start.24
  62.4 1.0 %collective-permute-start.25 = (bf16[64,768]{1,0:T(8,128)(2,1)S(1)}, bf16[64,768]{1,0:T(8,128)(2,1)S(1)}, u32[]{:S(2)}, u32[]{:S(2)}) collective-permute-start(bf16[64,768]{1,0:T(8,128)(2,1)S(1)} %get-tuple-element.118), channel_id=1, source_target_pairs={{0,5},{1,2},{2,7},{3,0},{4,1},{5,6},{6,3},{7,4},{8,13},{9,10},{10,... | collective-permute-start | bytes 294920 | tf_op jit(solution)/shard_map/ppermute | solution.py:329
  63.4 0.1 collective-permute-done.21.refs_1_
  63.5 1.2 %collective-permute-start.26 = (bf16[64,768]{1,0:T(8,128)(2,1)S(1)}, bf16[64,768]{1,0:T(8,128)(2,1)S(1)}, u32[]{:S(2)}, u32[]{:S(2)}) collective-permute-start(bf16[64,768]{1,0:T(8,128)(2,1)S(1)} %get-tuple-element.119), channel_id=1, source_target_pairs={{0,3},{1,4},{2,1},{3,6},{4,7},{5,0},{6,5},{7,2},{8,11},{9,12},{10,... | collective-permute-start | bytes 294920 | tf_op jit(solution)/shard_map/ppermute | solution.py:329
  64.7 2.2 %collective-permute-done.22.refs_2_ = bf16[64,768]{1,0:T(8,128)(2,1)S(1)} collective-permute-done((bf16[64,768]{1,0:T(8,128)(2,1)S(1)}, bf16[64,768]{1,0:T(8,128)(2,1)S(1)}, u32[]{:S(2)}, u32[]{:S(2)}) %collective-permute-start.22) | collective-permute-done | bytes 98336 | tf_op jit(solution)/shard_map/ppermute | solution.py:329
  66.9 0.0 collective-permute-start.27
  66.9 1.5 %collective-permute-done.23.refs_3_ = bf16[64,768]{1,0:T(8,128)(2,1)S(1)} collective-permute-done((bf16[64,768]{1,0:T(8,128)(2,1)S(1)}, bf16[64,768]{1,0:T(8,128)(2,1)S(1)}, u32[]{:S(2)}, u32[]{:S(2)}) %collective-permute-start.23) | collective-permute-done | bytes 98336 | tf_op jit(solution)/shard_map/ppermute | solution.py:329
  68.5 1.6 %collective-permute-done.25.refs_5_ = bf16[64,768]{1,0:T(8,128)(2,1)S(1)} collective-permute-done((bf16[64,768]{1,0:T(8,128)(2,1)S(1)}, bf16[64,768]{1,0:T(8,128)(2,1)S(1)}, u32[]{:S(2)}, u32[]{:S(2)}) %collective-permute-start.25) | collective-permute-done | bytes 98336 | tf_op jit(solution)/shard_map/ppermute | solution.py:329
  70.0 0.5 collective-permute-done.26.refs_6_
  70.6 0.9 %shard_map.79 = bf16[128,3072]{1,0:T(8,128)(2,1)} custom-call(bf16[64,768]{1,0:T(8,128)(2,1)S(1)} %get-tuple-element.113.refs_0_, bf16[64,768]{1,0:T(8,128)(2,1)S(1)} %collective-permute-done.21.refs_1_, bf16[64,768]{1,0:T(8,128)(2,1)S(1)} %collective-permute-done.22.refs_2_, bf16[64,768]{1,0:T(8,128)(2,1)S(1)} %collective-permute-done.23.refs_3_, ...), custom_call_target="tpu_custom_call" | custom-call | tf_op jit(solution)/shard_map/pallas_call | solution.py:167
  (11 shorter events, 0.0 us)
Async XLA Ops:
  1.7 6.0 %collective-permute-start = (bf16[64,256]{1,0:T(8,128)(2,1)}, bf16[64,256]{1,0:T(8,128)(2,1)S(1)}, u32[]{:S(2)}, u32[]{:S(2)}) collective-permute-start(bf16[64,256]{1,0:T(8,128)(2,1)} %get-tuple-element.64), channel_id=1, source_target_pairs={{0,6},{1,7},{2,4},{3,5},{4,2},{5,3},{6,0},{7,1},{8,14},{9,15},{10,... | collective-permute-start | bytes 98312 | tf_op jit(solution)/shard_map/ppermute | solution.py:329
  4.0 5.3 %collective-permute-start.1 = (bf16[64,256]{1,0:T(8,128)(2,1)}, bf16[64,256]{1,0:T(8,128)(2,1)S(1)}, u32[]{:S(2)}, u32[]{:S(2)}) collective-permute-start(bf16[64,256]{1,0:T(8,128)(2,1)} %get-tuple-element.65), channel_id=1, source_target_pairs={{0,7},{1,6},{2,5},{3,4},{4,3},{5,2},{6,1},{7,0},{8,15},{9,14},{10,... | collective-permute-start | bytes 98312 | tf_op jit(solution)/shard_map/ppermute | solution.py:329
  5.0 8.8 %collective-permute-start.2 = (bf16[64,256]{1,0:T(8,128)(2,1)}, bf16[64,256]{1,0:T(8,128)(2,1)S(1)}, u32[]{:S(2)}, u32[]{:S(2)}) collective-permute-start(bf16[64,256]{1,0:T(8,128)(2,1)} %get-tuple-element.66), channel_id=1, source_target_pairs={{0,4},{1,3},{2,6},{3,1},{4,0},{5,7},{6,2},{7,5},{8,12},{9,11},{10,... | collective-permute-start | bytes 98312 | tf_op jit(solution)/shard_map/ppermute | solution.py:329
  6.2 7.6 %collective-permute-start.3 = (bf16[64,256]{1,0:T(8,128)(2,1)}, bf16[64,256]{1,0:T(8,128)(2,1)S(1)}, u32[]{:S(2)}, u32[]{:S(2)}) collective-permute-start(bf16[64,256]{1,0:T(8,128)(2,1)} %get-tuple-element.67), channel_id=1, source_target_pairs={{0,2},{1,5},{2,0},{3,7},{4,6},{5,1},{6,4},{7,3},{8,10},{9,13},{10,... | collective-permute-start | bytes 98312 | tf_op jit(solution)/shard_map/ppermute | solution.py:329
  7.5 6.4 %collective-permute-start.4 = (bf16[64,256]{1,0:T(8,128)(2,1)}, bf16[64,256]{1,0:T(8,128)(2,1)S(1)}, u32[]{:S(2)}, u32[]{:S(2)}) collective-permute-start(bf16[64,256]{1,0:T(8,128)(2,1)} %get-tuple-element.68), channel_id=1, source_target_pairs={{0,5},{1,2},{2,7},{3,0},{4,1},{5,6},{6,3},{7,4},{8,13},{9,10},{10,... | collective-permute-start | bytes 98312 | tf_op jit(solution)/shard_map/ppermute | solution.py:329
  7.7 6.2 %collective-permute-start.5 = (bf16[64,256]{1,0:T(8,128)(2,1)}, bf16[64,256]{1,0:T(8,128)(2,1)S(1)}, u32[]{:S(2)}, u32[]{:S(2)}) collective-permute-start(bf16[64,256]{1,0:T(8,128)(2,1)} %get-tuple-element.69), channel_id=1, source_target_pairs={{0,3},{1,4},{2,1},{3,6},{4,7},{5,0},{6,5},{7,2},{8,11},{9,12},{10,... | collective-permute-start | bytes 98312 | tf_op jit(solution)/shard_map/ppermute | solution.py:329
  9.2 4.7 %collective-permute-start.6 = (bf16[64,256]{1,0:T(8,128)(2,1)}, bf16[64,256]{1,0:T(8,128)(2,1)S(1)}, u32[]{:S(2)}, u32[]{:S(2)}) collective-permute-start(bf16[64,256]{1,0:T(8,128)(2,1)} %get-tuple-element.70), channel_id=1, source_target_pairs={{0,1},{1,0},{2,3},{3,2},{4,5},{5,4},{6,7},{7,6},{8,9},{9,8},{10,11... | collective-permute-start | bytes 98312 | tf_op jit(solution)/shard_map/ppermute | solution.py:329
  9.6 0.7 copy-start.2
  10.3 0.7 copy-start.3
  11.0 0.7 copy-start.4
  11.6 0.7 copy-start.5
  13.9 0.8 %copy-start.1 = (bf16[64,256]{1,0:T(8,128)(2,1)S(1)}, bf16[64,256]{1,0:T(8,128)(2,1)}, u32[]{:S(2)}) copy-start(bf16[64,256]{1,0:T(8,128)(2,1)} %get-tuple-element.75.refs_0_) | copy-start | bytes 98308
  14.7 3.4 %collective-permute-start.9 = (bf16[512,256]{1,0:T(8,128)(2,1)S(1)}, bf16[512,256]{1,0:T(8,128)(2,1)S(1)}, u32[]{:S(2)}, u32[]{:S(2)}) collective-permute-start(bf16[512,256]{1,0:T(8,128)(2,1)S(1)} %shard_map.75.refs_8_), channel_id=1, source_target_pairs={{0,1},{1,0},{2,3},{3,2},{4,5},{5,4},{6,7},{7,6},{8,9},{9,8},{10,11... | collective-permute-start | bytes 786440 | tf_op jit(solution)/shard_map/ppermute | solution.py:336
  14.9 9.3 %collective-permute-start.8 = (bf16[512,256]{1,0:T(8,128)(2,1)S(1)}, bf16[512,256]{1,0:T(8,128)(2,1)S(1)}, u32[]{:S(2)}, u32[]{:S(2)}) collective-permute-start(bf16[512,256]{1,0:T(8,128)(2,1)S(1)} %shard_map.75.refs_8_), channel_id=1, source_target_pairs={{0,24},{4,28},{8,0},{12,4},{16,8},{20,12},{24,16},{28,20},{1,25},{... | collective-permute-start | bytes 786440 | tf_op jit(solution)/shard_map/ppermute | solution.py:333
  15.0 12.8 %collective-permute-start.7 = (bf16[512,256]{1,0:T(8,128)(2,1)S(1)}, bf16[512,256]{1,0:T(8,128)(2,1)S(1)}, u32[]{:S(2)}, u32[]{:S(2)}) collective-permute-start(bf16[512,256]{1,0:T(8,128)(2,1)S(1)} %shard_map.75.refs_8_), channel_id=1, source_target_pairs={{0,8},{4,12},{8,16},{12,20},{16,24},{20,28},{24,0},{28,4},{1,9},{5... | collective-permute-start | bytes 786440 | tf_op jit(solution)/shard_map/ppermute | solution.py:333
  18.1 1.1 %copy-start = (bf16[128,3072]{1,0:T(8,128)(2,1)S(1)}, bf16[128,3072]{1,0:T(8,128)(2,1)}, u32[]{:S(2)}) copy-start(bf16[128,3072]{1,0:T(8,128)(2,1)} %q_ref) | copy-start | bytes 2359300
  19.3 11.4 %collective-permute-start.12 = (bf16[64,768]{1,0:T(8,128)(2,1)S(1)}, bf16[64,768]{1,0:T(8,128)(2,1)S(1)}, u32[]{:S(2)}, u32[]{:S(2)}) collective-permute-start(bf16[64,768]{1,0:T(8,128)(2,1)S(1)} %get-tuple-element.86), channel_id=1, source_target_pairs={{0,6},{1,7},{2,4},{3,5},{4,2},{5,3},{6,0},{7,1},{8,14},{9,15},{10,... | collective-permute-start | bytes 294920 | tf_op jit(solution)/shard_map/ppermute | solution.py:329
  24.2 16.1 %collective-permute-start.11 = (bf16[512,256]{1,0:T(8,128)(2,1)S(1)}, bf16[512,256]{1,0:T(8,128)(2,1)S(1)}, u32[]{:S(2)}, u32[]{:S(2)}) collective-permute-start(bf16[512,256]{1,0:T(8,128)(2,1)S(1)} %collective-permute-done.8.refs_12_), channel_id=1, source_target_pairs={{0,1},{1,0},{2,3},{3,2},{4,5},{5,4},{6,7},{7,6},{8,9},{9,8},{10,11... | collective-permute-start | bytes 786440 | tf_op jit(solution)/shard_map/ppermute | solution.py:336
  27.8 12.5 %collective-permute-start.10 = (bf16[512,256]{1,0:T(8,128)(2,1)S(1)}, bf16[512,256]{1,0:T(8,128)(2,1)S(1)}, u32[]{:S(2)}, u32[]{:S(2)}) collective-permute-start(bf16[512,256]{1,0:T(8,128)(2,1)S(1)} %collective-permute-done.7.refs_10_), channel_id=1, source_target_pairs={{0,1},{1,0},{2,3},{3,2},{4,5},{5,4},{6,7},{7,6},{8,9},{9,8},{10,11... | collective-permute-start | bytes 786440 | tf_op jit(solution)/shard_map/ppermute | solution.py:336
  29.4 6.0 %collective-permute-start.13 = (bf16[64,768]{1,0:T(8,128)(2,1)S(1)}, bf16[64,768]{1,0:T(8,128)(2,1)S(1)}, u32[]{:S(2)}, u32[]{:S(2)}) collective-permute-start(bf16[64,768]{1,0:T(8,128)(2,1)S(1)} %get-tuple-element.87), channel_id=1, source_target_pairs={{0,7},{1,6},{2,5},{3,4},{4,3},{5,2},{6,1},{7,0},{8,15},{9,14},{10,... | collective-permute-start | bytes 294920 | tf_op jit(solution)/shard_map/ppermute | solution.py:329
  29.8 6.0 %collective-permute-start.14 = (bf16[64,768]{1,0:T(8,128)(2,1)S(1)}, bf16[64,768]{1,0:T(8,128)(2,1)S(1)}, u32[]{:S(2)}, u32[]{:S(2)}) collective-permute-start(bf16[64,768]{1,0:T(8,128)(2,1)S(1)} %get-tuple-element.88), channel_id=1, source_target_pairs={{0,4},{1,3},{2,6},{3,1},{4,0},{5,7},{6,2},{7,5},{8,12},{9,11},{10,... | collective-permute-start | bytes 294920 | tf_op jit(solution)/shard_map/ppermute | solution.py:329
  30.7 6.4 %collective-permute-start.15 = (bf16[64,768]{1,0:T(8,128)(2,1)S(1)}, bf16[64,768]{1,0:T(8,128)(2,1)S(1)}, u32[]{:S(2)}, u32[]{:S(2)}) collective-permute-start(bf16[64,768]{1,0:T(8,128)(2,1)S(1)} %get-tuple-element.89), channel_id=1, source_target_pairs={{0,2},{1,5},{2,0},{3,7},{4,6},{5,1},{6,4},{7,3},{8,10},{9,13},{10,... | collective-permute-start | bytes 294920 | tf_op jit(solution)/shard_map/ppermute | solution.py:329
  35.4 4.0 %collective-permute-start.16 = (bf16[64,768]{1,0:T(8,128)(2,1)S(1)}, bf16[64,768]{1,0:T(8,128)(2,1)S(1)}, u32[]{:S(2)}, u32[]{:S(2)}) collective-permute-start(bf16[64,768]{1,0:T(8,128)(2,1)S(1)} %get-tuple-element.90), channel_id=1, source_target_pairs={{0,5},{1,2},{2,7},{3,0},{4,1},{5,6},{6,3},{7,4},{8,13},{9,10},{10,... | collective-permute-start | bytes 294920 | tf_op jit(solution)/shard_map/ppermute | solution.py:329
  35.9 4.4 %collective-permute-start.17 = (bf16[64,768]{1,0:T(8,128)(2,1)S(1)}, bf16[64,768]{1,0:T(8,128)(2,1)S(1)}, u32[]{:S(2)}, u32[]{:S(2)}) collective-permute-start(bf16[64,768]{1,0:T(8,128)(2,1)S(1)} %get-tuple-element.91), channel_id=1, source_target_pairs={{0,3},{1,4},{2,1},{3,6},{4,7},{5,0},{6,5},{7,2},{8,11},{9,12},{10,... | collective-permute-start | bytes 294920 | tf_op jit(solution)/shard_map/ppermute | solution.py:329
  37.1 3.2 %collective-permute-start.18 = (bf16[64,768]{1,0:T(8,128)(2,1)S(1)}, bf16[64,768]{1,0:T(8,128)(2,1)S(1)}, u32[]{:S(2)}, u32[]{:S(2)}) collective-permute-start(bf16[64,768]{1,0:T(8,128)(2,1)S(1)} %get-tuple-element.92), channel_id=1, source_target_pairs={{0,1},{1,0},{2,3},{3,2},{4,5},{5,4},{6,7},{7,6},{8,9},{9,8},{10,11... | collective-permute-start | bytes 294920 | tf_op jit(solution)/shard_map/ppermute | solution.py:329
  40.3 12.2 %collective-permute-start.19 = (bf16[512,256]{1,0:T(8,128)(2,1)S(1)}, bf16[512,256]{1,0:T(8,128)(2,1)S(1)}, u32[]{:S(2)}, u32[]{:S(2)}) collective-permute-start(bf16[512,256]{1,0:T(8,128)(2,1)S(1)} %collective-permute-done.7.refs_10_), channel_id=1, source_target_pairs={{0,8},{4,12},{8,16},{12,20},{16,24},{20,28},{24,0},{28,4},{1,9},{5... | collective-permute-start | bytes 786440 | tf_op jit(solution)/shard_map/ppermute | solution.py:333
  52.5 2.5 %collective-permute-start.20 = (bf16[512,256]{1,0:T(8,128)(2,1)S(1)}, bf16[512,256]{1,0:T(8,128)(2,1)S(1)}, u32[]{:S(2)}, u32[]{:S(2)}) collective-permute-start(bf16[512,256]{1,0:T(8,128)(2,1)S(1)} %collective-permute-done.19.refs_3_), channel_id=1, source_target_pairs={{0,1},{1,0},{2,3},{3,2},{4,5},{5,4},{6,7},{7,6},{8,9},{9,8},{10,11... | collective-permute-start | bytes 786440 | tf_op jit(solution)/shard_map/ppermute | solution.py:336
  58.5 5.0 %collective-permute-start.21 = (bf16[64,768]{1,0:T(8,128)(2,1)S(1)}, bf16[64,768]{1,0:T(8,128)(2,1)S(1)}, u32[]{:S(2)}, u32[]{:S(2)}) collective-permute-start(bf16[64,768]{1,0:T(8,128)(2,1)S(1)} %get-tuple-element.114), channel_id=1, source_target_pairs={{0,6},{1,7},{2,4},{3,5},{4,2},{5,3},{6,0},{7,1},{8,14},{9,15},{10,... | collective-permute-start | bytes 294920 | tf_op jit(solution)/shard_map/ppermute | solution.py:329
  59.2 7.7 %collective-permute-start.22 = (bf16[64,768]{1,0:T(8,128)(2,1)S(1)}, bf16[64,768]{1,0:T(8,128)(2,1)S(1)}, u32[]{:S(2)}, u32[]{:S(2)}) collective-permute-start(bf16[64,768]{1,0:T(8,128)(2,1)S(1)} %get-tuple-element.115), channel_id=1, source_target_pairs={{0,7},{1,6},{2,5},{3,4},{4,3},{5,2},{6,1},{7,0},{8,15},{9,14},{10,... | collective-permute-start | bytes 294920 | tf_op jit(solution)/shard_map/ppermute | solution.py:329
  61.5 7.0 %collective-permute-start.23 = (bf16[64,768]{1,0:T(8,128)(2,1)S(1)}, bf16[64,768]{1,0:T(8,128)(2,1)S(1)}, u32[]{:S(2)}, u32[]{:S(2)}) collective-permute-start(bf16[64,768]{1,0:T(8,128)(2,1)S(1)} %get-tuple-element.116), channel_id=1, source_target_pairs={{0,4},{1,3},{2,6},{3,1},{4,0},{5,7},{6,2},{7,5},{8,12},{9,11},{10,... | collective-permute-start | bytes 294920 | tf_op jit(solution)/shard_map/ppermute | solution.py:329
  62.3 6.2 %collective-permute-start.24 = (bf16[64,768]{1,0:T(8,128)(2,1)S(1)}, bf16[64,768]{1,0:T(8,128)(2,1)S(1)}, u32[]{:S(2)}, u32[]{:S(2)}) collective-permute-start(bf16[64,768]{1,0:T(8,128)(2,1)S(1)} %get-tuple-element.117), channel_id=1, source_target_pairs={{0,2},{1,5},{2,0},{3,7},{4,6},{5,1},{6,4},{7,3},{8,10},{9,13},{10,... | collective-permute-start | bytes 294920 | tf_op jit(solution)/shard_map/ppermute | solution.py:329
  62.4 7.7 %collective-permute-start.25 = (bf16[64,768]{1,0:T(8,128)(2,1)S(1)}, bf16[64,768]{1,0:T(8,128)(2,1)S(1)}, u32[]{:S(2)}, u32[]{:S(2)}) collective-permute-start(bf16[64,768]{1,0:T(8,128)(2,1)S(1)} %get-tuple-element.118), channel_id=1, source_target_pairs={{0,5},{1,2},{2,7},{3,0},{4,1},{5,6},{6,3},{7,4},{8,13},{9,10},{10,... | collective-permute-start | bytes 294920 | tf_op jit(solution)/shard_map/ppermute | solution.py:329
  63.5 7.1 %collective-permute-start.26 = (bf16[64,768]{1,0:T(8,128)(2,1)S(1)}, bf16[64,768]{1,0:T(8,128)(2,1)S(1)}, u32[]{:S(2)}, u32[]{:S(2)}) collective-permute-start(bf16[64,768]{1,0:T(8,128)(2,1)S(1)} %get-tuple-element.119), channel_id=1, source_target_pairs={{0,3},{1,4},{2,1},{3,6},{4,7},{5,0},{6,5},{7,2},{8,11},{9,12},{10,... | collective-permute-start | bytes 294920 | tf_op jit(solution)/shard_map/ppermute | solution.py:329
  66.9 3.6 %collective-permute-start.27 = (bf16[64,768]{1,0:T(8,128)(2,1)S(1)}, bf16[64,768]{1,0:T(8,128)(2,1)S(1)}, u32[]{:S(2)}, u32[]{:S(2)}) collective-permute-start(bf16[64,768]{1,0:T(8,128)(2,1)S(1)} %get-tuple-element.120), channel_id=1, source_target_pairs={{0,1},{1,0},{2,3},{3,2},{4,5},{5,4},{6,7},{7,6},{8,9},{9,8},{10,11... | collective-permute-start | bytes 294920 | tf_op jit(solution)/shard_map/ppermute | solution.py:329

commit v2 on v0

--- a/solution.py
+++ b/solution.py
@@ -43,7 +43,12 @@
     return span & -2, 4 * (span & 1) + tok
 
 
-def table_kernel(planes, levels_ref, temps_ref, list_ref, counts_ref, table_ref, factor_ref):
+def begin_kernel(planes, levels_ref, temps_ref, list_ref, counts_ref, keys_ref, values_ref, q_ref, *refs):
+    pieces, (table_ref, factor_ref, source, q_source, target, sems) = refs[:PEERS], refs[PEERS:]
+    loads = [pltpu.make_async_copy(ref, source.at[i], sems.at[i]) for i, ref in enumerate((keys_ref, values_ref))]
+    loads.append(pltpu.make_async_copy(q_ref, q_source, sems.at[2]))
+    for load in loads:
+        load.start()
     base, number = place()
     head = number >> 1
     for side in range(2):
@@ -60,23 +65,6 @@
             count = jnp.where(found & (ident >= 0), counts_ref[jnp.maximum(ident, 0)], 0)
             table_ref[2 * slab + side] = count
 
-
-def tabulate(planes, levels, temps, ctx_list, counts):
-    return pl.pallas_call(
-        functools.partial(table_kernel, planes),
-        out_shape=[jax.ShapeDtypeStruct((4 * planes,), jnp.int32), jax.ShapeDtypeStruct((2 * GROUP,), jnp.float32)],
-        in_specs=[SMEM] * 4,
-        out_specs=[SMEM] * 2,
-        compiler_params=SMALL,
-    )(levels, temps, ctx_list, counts)
-
-
-def begin_kernel(keys_ref, values_ref, *refs):
-    pieces, (source, target, sems) = refs[:PEERS], refs[PEERS:]
-    number = place()[1]
-    loads = [pltpu.make_async_copy(ref, source.at[i], sems.at[i]) for i, ref in enumerate((keys_ref, values_ref))]
-    for load in loads:
-        load.start()
     for load in loads:
         load.wait()
     part = target.shape[1]
@@ -86,66 +74,54 @@
         rows = pl.ds(pl.multiple_of((peer & 1) * part, part), part)
         lanes = pl.ds(pl.multiple_of((peer >> 1) * HD, HD), HD)
         target[step, :, :HD] = source[0, rows, lanes]
-        target[step, :, HD:] = source[1, rows, lanes]
+        target[step, :, HD : 2 * HD] = source[1, rows, lanes]
+        target[step, :, 2 * HD :] = q_source[rows, pl.ds(pl.multiple_of((peer >> 1) * WIDE, HD), WIDE)]
         stores.append(pltpu.make_async_copy(target.at[step], piece, sems.at[step]))
         stores[-1].start()
     for store in stores:
         store.wait()
 
 
-def begin(keys, values):
-    shape = (keys.shape[0] // 2, 2 * HD)
-    return pl.pallas_call(
-        begin_kernel,
-        out_shape=[jax.ShapeDtypeStruct(shape, jnp.bfloat16)] * PEERS,
-        in_specs=[HBM] * 2,
-        out_specs=[HBM] * PEERS,
+def begin(planes, levels, temps, ctx_list, counts, keys, values, queries):
+    shape = (keys.shape[0] // 2, 2 * HD + WIDE)
+    out = pl.pallas_call(
+        functools.partial(begin_kernel, planes),
+        out_shape=[jax.ShapeDtypeStruct(shape, jnp.bfloat16)] * PEERS
+        + [jax.ShapeDtypeStruct((4 * planes,), jnp.int32), jax.ShapeDtypeStruct((2 * GROUP,), jnp.float32)],
+        in_specs=[SMEM] * 4 + [HBM] * 3,
+        out_specs=[HBM] * PEERS + [SMEM] * 2,
         scratch_shapes=[
             pltpu.VMEM((2, *keys.shape), jnp.bfloat16),
+            pltpu.VMEM(queries.shape, jnp.bfloat16),
             pltpu.VMEM((PEERS, *shape), jnp.bfloat16),
             pltpu.SemaphoreType.DMA((PEERS,)),
         ],
-    )(keys, values)
+    )(levels, temps, ctx_list, counts, keys, values, queries)
+    return out[:PEERS], out[PEERS:]
 
 
 def gather_kernel(*refs):
-    pieces, slab_ref = refs[:PEERS], refs[PEERS]
+    pieces, slab_ref, q_ref = refs[:PEERS], refs[PEERS], refs[PEERS + 1]
     number = place()[1]
     part = pieces[0].shape[0]
     for step, piece in enumerate(pieces):
-        at = pl.multiple_of(got_from(number, step) * part, part)
-        slab_ref[pl.ds(at, part), :] = piece[...]
+        peer = got_from(number, step)
+        slab_ref[pl.ds(pl.multiple_of(peer * part, part), part), :] = piece[:, : 2 * HD]
+        q_ref[peer] = piece[:, 2 * HD :]
 
 
 def gather(pieces):
-    rows, width = pieces[0].shape
+    rows = pieces[0].shape[0]
     return pl.pallas_call(
         gather_kernel,
-        out_shape=jax.ShapeDtypeStruct((PEERS * rows, width), jnp.bfloat16),
+        out_shape=[
+            jax.ShapeDtypeStruct((PEERS * rows, 2 * HD), jnp.bfloat16),
+            jax.ShapeDtypeStruct((PEERS, rows, WIDE), jnp.bfloat16),
+        ],
         in_specs=[VMEM] * PEERS,
-        out_specs=VMEM,
+        out_specs=[VMEM] * 2,
         compiler_params=SMALL,
     )(*pieces)
-
-
-def cut_kernel(q_ref, *pieces):
-    number = place()[1]
-    part = q_ref.shape[0] // 2
-    for step, piece in enumerate(pieces):
-        peer = sent_to(number, step)
-        rows = pl.ds(pl.multiple_of((peer & 1) * part, part), part)
-        lanes = pl.ds(pl.multiple_of((peer >> 1) * WIDE, HD), WIDE)
-        piece[...] = q_ref[rows, lanes]
-
-
-def cut(q):
-    return pl.pallas_call(
-        cut_kernel,
-        out_shape=[jax.ShapeDtypeStruct((q.shape[0] // 2, WIDE), jnp.bfloat16)] * PEERS,
-        in_specs=[VMEM],
-        out_specs=[VMEM] * PEERS,
-        compiler_params=SMALL,
-    )(q)
 
 
 def join_kernel(*refs):
@@ -176,10 +152,8 @@
 
 def attend_kernel(backs, first, final, table_ref, factor_ref, *refs):
     refs = list(refs)
-    if first:
-        q_pieces = [refs.pop(0) for _ in range(PEERS)]
-    else:
-        q_ref = refs.pop(0)
+    q_ref = refs.pop(0)
+    if not first:
         del refs[:2]
     slabs = [(refs.pop(0), refs.pop(0)) for _ in backs]
     out_refs = [refs.pop(0) for _ in range(PEERS)] if final else None
@@ -187,9 +161,6 @@
     number = place()[1]
     core = number & 1
     if first:
-        q_ref = refs.pop(0)
-        for step, piece in enumerate(q_pieces):
-            q_ref[got_from(number, step)] = piece[...]
         sums_ref[...] = jnp.zeros_like(sums_ref)
         top_ref[...] = jnp.full_like(top_ref, LOW)
     key_ref, value_ref = refs[:2]
@@ -290,22 +261,19 @@
 
 def attend(tables, q, state, slabs, backs, final):
     first = state is None
-    piece = q[0].shape[-2]
+    piece = q.shape[1]
     tall = GROUP * piece
     tokens = slabs[0][0].shape[0]
-    q_shape = (PEERS, piece, WIDE)
     out_shape = [
         jax.ShapeDtypeStruct((2, 4, tall, 2 * HD), jnp.float32),
         jax.ShapeDtypeStruct((2, 4, tall, HD), jnp.float32),
     ]
     scratch = [pltpu.VMEM((2, HD, tokens), jnp.bfloat16), pltpu.VMEM((2, tokens, 2 * HD), jnp.bfloat16)]
     if final:
-        out_shape = [jax.ShapeDtypeStruct(q_shape[1:], jnp.bfloat16)] * PEERS + out_shape
-        scratch.append(pltpu.VMEM(q_shape, jnp.bfloat16))
-    if first:
-        out_shape.append(jax.ShapeDtypeStruct(q_shape, jnp.bfloat16))
+        out_shape = [jax.ShapeDtypeStruct(q.shape[1:], jnp.bfloat16)] * PEERS + out_shape
+        scratch.append(pltpu.VMEM(q.shape, jnp.bfloat16))
     work = len(backs) * PEERS * tall * tokens
-    inputs = [*q, *(state or ()), *[a for slab in slabs for a in slab]]
+    inputs = [q, *(state or ()), *[a for slab in slabs for a in slab]]
     aliases = {} if first else {3: PEERS * final, 4: PEERS * final + 1}
     return pl.pallas_call(
         functools.partial(attend_kernel, backs, first, final),
@@ -315,7 +283,7 @@
         scratch_shapes=scratch,
         input_output_aliases=aliases,
         compiler_params=LARGE,
-        cost_estimate=pl.CostEstimate(flops=2 * work * HD, bytes_accessed=4 * PEERS * piece * WIDE, transcendentals=work // 2),
+        cost_estimate=pl.CostEstimate(flops=2 * work * HD, bytes_accessed=4 * q.size, transcendentals=work // 2),
     )(*tables, *inputs)
 
 
@@ -335,20 +303,17 @@
     def near(a):
         return lax.ppermute(a, "ctx", other_core)
 
-    own = gather(exchange(begin(keys, values)))
+    pieces, tables = begin(spans // 2, levels, temps, jnp.transpose(ctx_list), counts, keys, values, queries)
+    own, q = gather(exchange(pieces))
     slabs = {0: own, 1: up(own, 1), last: up(own, last)}
     others = {0: near(own)}
-    others, queries = lax.optimization_barrier((others, queries))
-    q = exchange(cut(queries))
-    tables = tabulate(spans // 2, levels, temps, jnp.transpose(ctx_list), counts)
-    slabs, others, q, tables = lax.optimization_barrier((slabs, others, q, tables))
-    others |= {back: near(slabs[back]) for back in (1, last)}
-    stage = sorted(slabs)
-    state = None
+    state = attend(tables, q, None, [(own, others[0])], [0], False)
+    slabs, state = lax.optimization_barrier((slabs, state))
+    stage = [1, last]
+    others |= {back: near(slabs[back]) for back in stage}
     for back in range(2, last):
         slabs[back] = up(slabs[back - 1], 1)
-        *state, q_all = [*attend(tables, q, state, [(slabs[b], others[b]) for b in stage], stage, False), *q][:3]
-        q = [q_all]
+        state = attend(tables, q, state, [(slabs[b], others[b]) for b in stage], stage, False)
         slabs[back], state = lax.optimization_barrier((slabs[back], state))
         others[back] = near(slabs[back])
         stage = [back]

time: 64.4 us -> 63.5 us (0.986)
  the two profiles are of different devices: /device:TPU:25 before, /device:TPU:0 now
where the time goes in v2:
time: 63.5 us; the launch traced here: 63.3 us
  waiting for transfers between devices  28.6 us (45%)
  starting transfers between devices  20.8 us (33%)
  Pallas kernels  11.5 us (18%)
  local copies, waits for them, and re-layouts  2.14 us (3%)
    ppermute x14, starting transfers between devices, exchange(): lax.ppermute(piece, ('span', 'ctx'), [(f, f ^ step[f % 2]) for f in range...  14.6 us
    ppermute x3, waiting for transfers between devices, up(): lax.ppermute(a, 'span', [(s, (s + 2 * steps) % spans) for s in range(span...  13.9 us
    ppermute x14, waiting for transfers between devices, exchange(): lax.ppermute(piece, ('span', 'ctx'), [(f, f ^ step[f % 2]) for f in range...  13.1 us
    pallas_call x3, Pallas kernels, attend(): pl.pallas_call(functools.partial(attend_kernel, backs, first, final), out...  6.91 us
    ppermute x3, starting transfers between devices, up(): lax.ppermute(a, 'span', [(s, (s + 2 * steps) % spans) for s in range(span...  5.36 us
    pallas_call x1, Pallas kernels, begin(): pl.pallas_call(functools.partial(begin_kernel, planes), out_shape=[jax.Sh...  3.6 us
    unnamed x6, local copies, waits for them, and re-layouts  2.14 us
    ppermute x4, waiting for transfers between devices, near(): return lax.ppermute(a, 'ctx', other_core)  1.54 us
  transfers between devices with their start and end apart: 21, of which 14 were waited for; matrix products, arithmetic and copies ran while one was open for 0% of the time, Pallas kernels for 9%

profile of v2, /device:TPU:0, one launch (start us, length us, event | category | flops | bytes accessed | tf_op | source)
XLA Modules:
  0.0 63.3 jit_solution(7480364102778420527)
XLA Ops:
  0.0 3.6 %shard_map.73 = (bf16[64,1024]{1,0:T(8,128)(2,1)}, bf16[64,1024]{1,0:T(8,128)(2,1)}, bf16[64,1024]{1,0:T(8,128)(2,1)}, bf16[64,1024]{1,0:T(8,128)(2,1)}, bf16[64...) custom-call(s32[8]{0:T(128)} %levels_ref.1, ...), custom_call_target="tpu_custom_call" | custom-call | tf_op jit(solution)/shard_map/pallas_call | solution.py:87
  3.6 4.0 %collective-permute-start = (bf16[64,1024]{1,0:T(8,128)(2,1)}, bf16[64,1024]{1,0:T(8,128)(2,1)S(1)}, u32[]{:S(2)}, u32[]{:S(2)}) collective-permute-start(bf16[64,1024]{1,0:T(8,128)(2,1)} %get-tuple-element.39), channel_id=1, source_target_pairs={{0,6},{1,7},{2,4},{3,5},{4,2},{5,3},{6,0},{7,1},{8,14},{9,15},{10,... | collective-permute-start | bytes 393224 | tf_op jit(solution)/shard_map/ppermute | solution.py:297
  7.6 0.0 collective-permute-start.1
  7.6 1.1 %collective-permute-start.2 = (bf16[64,1024]{1,0:T(8,128)(2,1)}, bf16[64,1024]{1,0:T(8,128)(2,1)S(1)}, u32[]{:S(2)}, u32[]{:S(2)}) collective-permute-start(bf16[64,1024]{1,0:T(8,128)(2,1)} %get-tuple-element.41), channel_id=1, source_target_pairs={{0,4},{1,3},{2,6},{3,1},{4,0},{5,7},{6,2},{7,5},{8,12},{9,11},{10,... | collective-permute-start | bytes 393224 | tf_op jit(solution)/shard_map/ppermute | solution.py:297
  8.7 1.5 %collective-permute-start.3 = (bf16[64,1024]{1,0:T(8,128)(2,1)}, bf16[64,1024]{1,0:T(8,128)(2,1)S(1)}, u32[]{:S(2)}, u32[]{:S(2)}) collective-permute-start(bf16[64,1024]{1,0:T(8,128)(2,1)} %get-tuple-element.42), channel_id=1, source_target_pairs={{0,2},{1,5},{2,0},{3,7},{4,6},{5,1},{6,4},{7,3},{8,10},{9,13},{10,... | collective-permute-start | bytes 393224 | tf_op jit(solution)/shard_map/ppermute | solution.py:297
  10.2 0.5 collective-permute-start.4
  10.8 1.0 %collective-permute-done.refs_1_ = bf16[64,1024]{1,0:T(8,128)(2,1)S(1)} collective-permute-done((bf16[64,1024]{1,0:T(8,128)(2,1)}, bf16[64,1024]{1,0:T(8,128)(2,1)S(1)}, u32[]{:S(2)}, u32[]{:S(2)}) %collective-permute-start) | collective-permute-done | bytes 131104 | tf_op jit(solution)/shard_map/ppermute | solution.py:297
  11.8 0.2 collective-permute-start.5
  12.0 2.7 %collective-permute-done.1.refs_2_ = bf16[64,1024]{1,0:T(8,128)(2,1)S(1)} collective-permute-done((bf16[64,1024]{1,0:T(8,128)(2,1)}, bf16[64,1024]{1,0:T(8,128)(2,1)S(1)}, u32[]{:S(2)}, u32[]{:S(2)}) %collective-permute-start.1) | collective-permute-done | bytes 131104 | tf_op jit(solution)/shard_map/ppermute | solution.py:297
  14.6 0.0 collective-permute-start.6
  14.6 3.4 %collective-permute-done.2.refs_3_ = bf16[64,1024]{1,0:T(8,128)(2,1)S(1)} collective-permute-done((bf16[64,1024]{1,0:T(8,128)(2,1)}, bf16[64,1024]{1,0:T(8,128)(2,1)S(1)}, u32[]{:S(2)}, u32[]{:S(2)}) %collective-permute-start.2) | collective-permute-done | bytes 131104 | tf_op jit(solution)/shard_map/ppermute | solution.py:297
  18.0 0.0 collective-permute-done.3.refs_4_
  18.0 1.5 %collective-permute-done.4.refs_5_ = bf16[64,1024]{1,0:T(8,128)(2,1)S(1)} collective-permute-done((bf16[64,1024]{1,0:T(8,128)(2,1)}, bf16[64,1024]{1,0:T(8,128)(2,1)S(1)}, u32[]{:S(2)}, u32[]{:S(2)}) %collective-permute-start.4) | collective-permute-done | bytes 131104 | tf_op jit(solution)/shard_map/ppermute | solution.py:297
  19.5 0.0 collective-permute-done.5.refs_6_
  19.5 0.0 collective-permute-done.6.refs_7_
  19.5 0.0 copy-start
  19.5 0.9 %copy-done = bf16[64,1024]{1,0:T(8,128)(2,1)S(1)} copy-done((bf16[64,1024]{1,0:T(8,128)(2,1)S(1)}, bf16[64,1024]{1,0:T(8,128)(2,1)}, u32[]{:S(2)}) %copy-start) | copy-done | bytes 131096
  20.4 0.1 shard_map.74
  20.5 0.4 collective-permute-start.9
  20.9 3.7 %collective-permute-start.8 = (bf16[512,256]{1,0:T(8,128)(2,1)S(1)}, bf16[512,256]{1,0:T(8,128)(2,1)S(1)}, u32[]{:S(2)}, u32[]{:S(2)}) collective-permute-start(bf16[512,256]{1,0:T(8,128)(2,1)S(1)} %get-tuple-element.47.refs_1_), channel_id=1, source_target_pairs={{0,24},{4,28},{8,0},{12,4},{16,8},{20,12},{24,16},{28,20},{1,25},{... | collective-permute-start | bytes 786440 | tf_op jit(solution)/shard_map/ppermute | solution.py:301
  24.6 0.0 collective-permute-start.7
  24.6 0.0 collective-permute-done.9.refs_2_
  24.6 0.0 copy-start.1
  24.6 0.7 %copy-done.1 = s32[16]{0:T(128)S(1)} copy-done((s32[16]{0:T(128)S(1)}, s32[16]{0:T(128)}, u32[]{:S(2)}) %copy-start.1) | copy-done | bytes 88
  25.3 0.0 copy-start.2
  25.3 0.6 copy-done.2
  25.9 4.8 %shard_map.75 = (f32[2,4,384,256]{3,2,1,0:T(8,128)S(1)}, f32[2,4,384,128]{3,2,1,0:T(8,128)S(1)}) custom-call(s32[16]{0:T(128)S(1)} %copy-done.1, f32[12]{0:T(128)S(1)} %copy-done.2, bf16[8,64,768]{2,1,0:T(8,128)(2,1)S(1)} %get-tuple-element.46.refs_0_, bf16[512,256]{1,0:T(8,128)(2,1)S(1)} %get-tuple-element.47.refs_1_, ...), custom_call_target="tpu_custom_call" | custom-call | flops 402653184 | bytes 1572864 | tf_op jit(solution)/shard_map/pallas_call | solution.py:278
  30.7 0.6 collective-permute-done.8.refs_5_
  31.3 5.9 %collective-permute-done.7.refs_3_ = bf16[512,256]{1,0:T(8,128)(2,1)S(1)} collective-permute-done((bf16[512,256]{1,0:T(8,128)(2,1)S(1)}, bf16[512,256]{1,0:T(8,128)(2,1)S(1)}, u32[]{:S(2)}, u32[]{:S(2)}) %collective-permute-start.7) | collective-permute-done | bytes 262176 | tf_op jit(solution)/shard_map/ppermute | solution.py:301
  37.2 0.0 collective-permute-start.12
  37.2 0.5 collective-permute-start.11
  37.7 1.6 %collective-permute-start.10 = (bf16[512,256]{1,0:T(8,128)(2,1)S(1)}, bf16[512,256]{1,0:T(8,128)(2,1)S(1)}, u32[]{:S(2)}, u32[]{:S(2)}) collective-permute-start(bf16[512,256]{1,0:T(8,128)(2,1)S(1)} %collective-permute-done.7.refs_3_), channel_id=1, source_target_pairs={{0,8},{4,12},{8,16},{12,20},{16,24},{20,28},{24,0},{28,4},{1,9},{5... | collective-permute-start | bytes 786440 | tf_op jit(solution)/shard_map/ppermute | solution.py:301
  39.4 0.0 collective-permute-done.12.refs_6_
  39.4 0.0 collective-permute-done.11.refs_4_
  39.4 1.0 %shard_map.76 = (f32[2,4,384,256]{3,2,1,0:T(8,128)S(1)}, f32[2,4,384,128]{3,2,1,0:T(8,128)S(1)}) custom-call(s32[16]{0:T(128)S(1)} %copy-done.1, f32[12]{0:T(128)S(1)} %copy-done.2, bf16[8,64,768]{2,1,0:T(8,128)(2,1)S(1)} %get-tuple-element.46.refs_0_, ...), custom_call_target="tpu_custom_call", output_to_operand_aliasing={{0}: (3, {}), {1}: (4, {})} | custom-call | flops 805306368 | bytes 1572864 | tf_op jit(solution)/shard_map/pallas_call | solution.py:278
  40.4 7.3 %collective-permute-done.10.refs_3_ = bf16[512,256]{1,0:T(8,128)(2,1)S(1)} collective-permute-done((bf16[512,256]{1,0:T(8,128)(2,1)S(1)}, bf16[512,256]{1,0:T(8,128)(2,1)S(1)}, u32[]{:S(2)}, u32[]{:S(2)}) %collective-permute-start.10) | collective-permute-done | bytes 262176 | tf_op jit(solution)/shard_map/ppermute | solution.py:301
  47.8 0.0 collective-permute-start.13
  47.8 1.5 %collective-permute-done.13.refs_4_ = bf16[512,256]{1,0:T(8,128)(2,1)S(1)} collective-permute-done((bf16[512,256]{1,0:T(8,128)(2,1)S(1)}, bf16[512,256]{1,0:T(8,128)(2,1)S(1)}, u32[]{:S(2)}, u32[]{:S(2)}) %collective-permute-start.13) | collective-permute-done | bytes 262176 | tf_op jit(solution)/shard_map/ppermute | solution.py:304
  49.3 1.1 %shard_map.77 = (bf16[64,768]{1,0:T(8,128)(2,1)S(1)}, bf16[64,768]{1,0:T(8,128)(2,1)S(1)}, bf16[64,768]{1,0:T(8,128)(2,1)S(1)}, bf16[64,768]{1,0:T(8,128)(2,1)S(...) custom-call(s32[16]{0:T(128)S(1)} %copy-done.1, ...), custom_call_target="tpu_custom_call", output_to_operand_aliasing={{8}: (3, {}), {9}: (4, {})} | custom-call | flops 402653184 | bytes 1572864 | tf_op jit(solution)/shard_map/pallas_call | solution.py:278
  50.4 2.6 %collective-permute-start.14 = (bf16[64,768]{1,0:T(8,128)(2,1)S(1)}, bf16[64,768]{1,0:T(8,128)(2,1)S(1)}, u32[]{:S(2)}, u32[]{:S(2)}) collective-permute-start(bf16[64,768]{1,0:T(8,128)(2,1)S(1)} %get-tuple-element.60), channel_id=1, source_target_pairs={{0,6},{1,7},{2,4},{3,5},{4,2},{5,3},{6,0},{7,1},{8,14},{9,15},{10,... | collective-permute-start | bytes 294920 | tf_op jit(solution)/shard_map/ppermute | solution.py:297
  52.9 0.0 collective-permute-start.15
  53.0 1.4 %collective-permute-start.16 = (bf16[64,768]{1,0:T(8,128)(2,1)S(1)}, bf16[64,768]{1,0:T(8,128)(2,1)S(1)}, u32[]{:S(2)}, u32[]{:S(2)}) collective-permute-start(bf16[64,768]{1,0:T(8,128)(2,1)S(1)} %get-tuple-element.62), channel_id=1, source_target_pairs={{0,4},{1,3},{2,6},{3,1},{4,0},{5,7},{6,2},{7,5},{8,12},{9,11},{10,... | collective-permute-start | bytes 294920 | tf_op jit(solution)/shard_map/ppermute | solution.py:297
  54.3 1.6 %collective-permute-start.17 = (bf16[64,768]{1,0:T(8,128)(2,1)S(1)}, bf16[64,768]{1,0:T(8,128)(2,1)S(1)}, u32[]{:S(2)}, u32[]{:S(2)}) collective-permute-start(bf16[64,768]{1,0:T(8,128)(2,1)S(1)} %get-tuple-element.63), channel_id=1, source_target_pairs={{0,2},{1,5},{2,0},{3,7},{4,6},{5,1},{6,4},{7,3},{8,10},{9,13},{10,... | collective-permute-start | bytes 294920 | tf_op jit(solution)/shard_map/ppermute | solution.py:297
  55.9 0.2 collective-permute-start.18
  56.1 0.1 collective-permute-done.14.refs_1_
  56.2 1.5 %collective-permute-start.19 = (bf16[64,768]{1,0:T(8,128)(2,1)S(1)}, bf16[64,768]{1,0:T(8,128)(2,1)S(1)}, u32[]{:S(2)}, u32[]{:S(2)}) collective-permute-start(bf16[64,768]{1,0:T(8,128)(2,1)S(1)} %get-tuple-element.65), channel_id=1, source_target_pairs={{0,3},{1,4},{2,1},{3,6},{4,7},{5,0},{6,5},{7,2},{8,11},{9,12},{10,... | collective-permute-start | bytes 294920 | tf_op jit(solution)/shard_map/ppermute | solution.py:297
  57.6 1.4 %collective-permute-done.15.refs_2_ = bf16[64,768]{1,0:T(8,128)(2,1)S(1)} collective-permute-done((bf16[64,768]{1,0:T(8,128)(2,1)S(1)}, bf16[64,768]{1,0:T(8,128)(2,1)S(1)}, u32[]{:S(2)}, u32[]{:S(2)}) %collective-permute-start.15) | collective-permute-done | bytes 98336 | tf_op jit(solution)/shard_map/ppermute | solution.py:297
  59.0 0.1 collective-permute-start.20
  59.1 1.8 %collective-permute-done.16.refs_3_ = bf16[64,768]{1,0:T(8,128)(2,1)S(1)} collective-permute-done((bf16[64,768]{1,0:T(8,128)(2,1)S(1)}, bf16[64,768]{1,0:T(8,128)(2,1)S(1)}, u32[]{:S(2)}, u32[]{:S(2)}) %collective-permute-start.16) | collective-permute-done | bytes 98336 | tf_op jit(solution)/shard_map/ppermute | solution.py:297
  60.9 0.3 collective-permute-done.17.refs_4_
  61.2 0.4 collective-permute-done.18.refs_5_
  61.6 0.5 collective-permute-done.19.refs_6_
  62.2 0.0 collective-permute-done.20.refs_7_
  62.2 0.9 %shard_map.78 = bf16[128,3072]{1,0:T(8,128)(2,1)} custom-call(bf16[64,768]{1,0:T(8,128)(2,1)S(1)} %get-tuple-element.59.refs_0_, bf16[64,768]{1,0:T(8,128)(2,1)S(1)} %collective-permute-done.14.refs_1_, bf16[64,768]{1,0:T(8,128)(2,1)S(1)} %collective-permute-done.15.refs_2_, bf16[64,768]{1,0:T(8,128)(2,1)S(1)} %collective-permute-done.16.refs_3_, ...), custom_call_target="tpu_custom_call" | custom-call | tf_op jit(solution)/shard_map/pallas_call | solution.py:143
Async XLA Ops:
  3.6 8.2 %collective-permute-start = (bf16[64,1024]{1,0:T(8,128)(2,1)}, bf16[64,1024]{1,0:T(8,128)(2,1)S(1)}, u32[]{:S(2)}, u32[]{:S(2)}) collective-permute-start(bf16[64,1024]{1,0:T(8,128)(2,1)} %get-tuple-element.39), channel_id=1, source_target_pairs={{0,6},{1,7},{2,4},{3,5},{4,2},{5,3},{6,0},{7,1},{8,14},{9,15},{10,... | collective-permute-start | bytes 393224 | tf_op jit(solution)/shard_map/ppermute | solution.py:297
  7.6 7.1 %collective-permute-start.1 = (bf16[64,1024]{1,0:T(8,128)(2,1)}, bf16[64,1024]{1,0:T(8,128)(2,1)S(1)}, u32[]{:S(2)}, u32[]{:S(2)}) collective-permute-start(bf16[64,1024]{1,0:T(8,128)(2,1)} %get-tuple-element.40), channel_id=1, source_target_pairs={{0,7},{1,6},{2,5},{3,4},{4,3},{5,2},{6,1},{7,0},{8,15},{9,14},{10,... | collective-permute-start | bytes 393224 | tf_op jit(solution)/shard_map/ppermute | solution.py:297
  7.6 10.4 %collective-permute-start.2 = (bf16[64,1024]{1,0:T(8,128)(2,1)}, bf16[64,1024]{1,0:T(8,128)(2,1)S(1)}, u32[]{:S(2)}, u32[]{:S(2)}) collective-permute-start(bf16[64,1024]{1,0:T(8,128)(2,1)} %get-tuple-element.41), channel_id=1, source_target_pairs={{0,4},{1,3},{2,6},{3,1},{4,0},{5,7},{6,2},{7,5},{8,12},{9,11},{10,... | collective-permute-start | bytes 393224 | tf_op jit(solution)/shard_map/ppermute | solution.py:297
  8.7 9.3 %collective-permute-start.3 = (bf16[64,1024]{1,0:T(8,128)(2,1)}, bf16[64,1024]{1,0:T(8,128)(2,1)S(1)}, u32[]{:S(2)}, u32[]{:S(2)}) collective-permute-start(bf16[64,1024]{1,0:T(8,128)(2,1)} %get-tuple-element.42), channel_id=1, source_target_pairs={{0,2},{1,5},{2,0},{3,7},{4,6},{5,1},{6,4},{7,3},{8,10},{9,13},{10,... | collective-permute-start | bytes 393224 | tf_op jit(solution)/shard_map/ppermute | solution.py:297
  10.2 9.3 %collective-permute-start.4 = (bf16[64,1024]{1,0:T(8,128)(2,1)}, bf16[64,1024]{1,0:T(8,128)(2,1)S(1)}, u32[]{:S(2)}, u32[]{:S(2)}) collective-permute-start(bf16[64,1024]{1,0:T(8,128)(2,1)} %get-tuple-element.43), channel_id=1, source_target_pairs={{0,5},{1,2},{2,7},{3,0},{4,1},{5,6},{6,3},{7,4},{8,13},{9,10},{10,... | collective-permute-start | bytes 393224 | tf_op jit(solution)/shard_map/ppermute | solution.py:297
  11.8 7.7 %collective-permute-start.5 = (bf16[64,1024]{1,0:T(8,128)(2,1)}, bf16[64,1024]{1,0:T(8,128)(2,1)S(1)}, u32[]{:S(2)}, u32[]{:S(2)}) collective-permute-start(bf16[64,1024]{1,0:T(8,128)(2,1)} %get-tuple-element.44), channel_id=1, source_target_pairs={{0,3},{1,4},{2,1},{3,6},{4,7},{5,0},{6,5},{7,2},{8,11},{9,12},{10,... | collective-permute-start | bytes 393224 | tf_op jit(solution)/shard_map/ppermute | solution.py:297
  14.6 4.9 %collective-permute-start.6 = (bf16[64,1024]{1,0:T(8,128)(2,1)}, bf16[64,1024]{1,0:T(8,128)(2,1)S(1)}, u32[]{:S(2)}, u32[]{:S(2)}) collective-permute-start(bf16[64,1024]{1,0:T(8,128)(2,1)} %get-tuple-element.45), channel_id=1, source_target_pairs={{0,1},{1,0},{2,3},{3,2},{4,5},{5,4},{6,7},{7,6},{8,9},{9,8},{10,11... | collective-permute-start | bytes 393224 | tf_op jit(solution)/shard_map/ppermute | solution.py:297
  19.5 0.9 %copy-start = (bf16[64,1024]{1,0:T(8,128)(2,1)S(1)}, bf16[64,1024]{1,0:T(8,128)(2,1)}, u32[]{:S(2)}) copy-start(bf16[64,1024]{1,0:T(8,128)(2,1)} %get-tuple-element.38.refs_0_) | copy-start | bytes 393220
  20.5 4.1 %collective-permute-start.9 = (bf16[512,256]{1,0:T(8,128)(2,1)S(1)}, bf16[512,256]{1,0:T(8,128)(2,1)S(1)}, u32[]{:S(2)}, u32[]{:S(2)}) collective-permute-start(bf16[512,256]{1,0:T(8,128)(2,1)S(1)} %get-tuple-element.47.refs_1_), channel_id=1, source_target_pairs={{0,1},{1,0},{2,3},{3,2},{4,5},{5,4},{6,7},{7,6},{8,9},{9,8},{10,11... | collective-permute-start | bytes 786440 | tf_op jit(solution)/shard_map/ppermute | solution.py:304
  20.9 10.4 %collective-permute-start.8 = (bf16[512,256]{1,0:T(8,128)(2,1)S(1)}, bf16[512,256]{1,0:T(8,128)(2,1)S(1)}, u32[]{:S(2)}, u32[]{:S(2)}) collective-permute-start(bf16[512,256]{1,0:T(8,128)(2,1)S(1)} %get-tuple-element.47.refs_1_), channel_id=1, source_target_pairs={{0,24},{4,28},{8,0},{12,4},{16,8},{20,12},{24,16},{28,20},{1,25},{... | collective-permute-start | bytes 786440 | tf_op jit(solution)/shard_map/ppermute | solution.py:301
  24.6 12.6 %collective-permute-start.7 = (bf16[512,256]{1,0:T(8,128)(2,1)S(1)}, bf16[512,256]{1,0:T(8,128)(2,1)S(1)}, u32[]{:S(2)}, u32[]{:S(2)}) collective-permute-start(bf16[512,256]{1,0:T(8,128)(2,1)S(1)} %get-tuple-element.47.refs_1_), channel_id=1, source_target_pairs={{0,8},{4,12},{8,16},{12,20},{16,24},{20,28},{24,0},{28,4},{1,9},{5... | collective-permute-start | bytes 786440 | tf_op jit(solution)/shard_map/ppermute | solution.py:301
  24.6 0.7 %copy-start.1 = (s32[16]{0:T(128)S(1)}, s32[16]{0:T(128)}, u32[]{:S(2)}) copy-start(s32[16]{0:T(128)} %get-tuple-element.36.table_ref) | copy-start | bytes 196
  25.3 0.6 copy-start.2
  37.2 2.1 %collective-permute-start.12 = (bf16[512,256]{1,0:T(8,128)(2,1)S(1)}, bf16[512,256]{1,0:T(8,128)(2,1)S(1)}, u32[]{:S(2)}, u32[]{:S(2)}) collective-permute-start(bf16[512,256]{1,0:T(8,128)(2,1)S(1)} %collective-permute-done.8.refs_5_), channel_id=1, source_target_pairs={{0,1},{1,0},{2,3},{3,2},{4,5},{5,4},{6,7},{7,6},{8,9},{9,8},{10,11... | collective-permute-start | bytes 786440 | tf_op jit(solution)/shard_map/ppermute | solution.py:304
  37.2 2.1 %collective-permute-start.11 = (bf16[512,256]{1,0:T(8,128)(2,1)S(1)}, bf16[512,256]{1,0:T(8,128)(2,1)S(1)}, u32[]{:S(2)}, u32[]{:S(2)}) collective-permute-start(bf16[512,256]{1,0:T(8,128)(2,1)S(1)} %collective-permute-done.7.refs_3_), channel_id=1, source_target_pairs={{0,1},{1,0},{2,3},{3,2},{4,5},{5,4},{6,7},{7,6},{8,9},{9,8},{10,11... | collective-permute-start | bytes 786440 | tf_op jit(solution)/shard_map/ppermute | solution.py:304
  37.7 10.0 %collective-permute-start.10 = (bf16[512,256]{1,0:T(8,128)(2,1)S(1)}, bf16[512,256]{1,0:T(8,128)(2,1)S(1)}, u32[]{:S(2)}, u32[]{:S(2)}) collective-permute-start(bf16[512,256]{1,0:T(8,128)(2,1)S(1)} %collective-permute-done.7.refs_3_), channel_id=1, source_target_pairs={{0,8},{4,12},{8,16},{12,20},{16,24},{20,28},{24,0},{28,4},{1,9},{5... | collective-permute-start | bytes 786440 | tf_op jit(solution)/shard_map/ppermute | solution.py:301
  47.8 1.5 %collective-permute-start.13 = (bf16[512,256]{1,0:T(8,128)(2,1)S(1)}, bf16[512,256]{1,0:T(8,128)(2,1)S(1)}, u32[]{:S(2)}, u32[]{:S(2)}) collective-permute-start(bf16[512,256]{1,0:T(8,128)(2,1)S(1)} %collective-permute-done.10.refs_3_), channel_id=1, source_target_pairs={{0,1},{1,0},{2,3},{3,2},{4,5},{5,4},{6,7},{7,6},{8,9},{9,8},{10,11... | collective-permute-start | bytes 786440 | tf_op jit(solution)/shard_map/ppermute | solution.py:304
  50.4 5.8 %collective-permute-start.14 = (bf16[64,768]{1,0:T(8,128)(2,1)S(1)}, bf16[64,768]{1,0:T(8,128)(2,1)S(1)}, u32[]{:S(2)}, u32[]{:S(2)}) collective-permute-start(bf16[64,768]{1,0:T(8,128)(2,1)S(1)} %get-tuple-element.60), channel_id=1, source_target_pairs={{0,6},{1,7},{2,4},{3,5},{4,2},{5,3},{6,0},{7,1},{8,14},{9,15},{10,... | collective-permute-start | bytes 294920 | tf_op jit(solution)/shard_map/ppermute | solution.py:297
  52.9 6.1 %collective-permute-start.15 = (bf16[64,768]{1,0:T(8,128)(2,1)S(1)}, bf16[64,768]{1,0:T(8,128)(2,1)S(1)}, u32[]{:S(2)}, u32[]{:S(2)}) collective-permute-start(bf16[64,768]{1,0:T(8,128)(2,1)S(1)} %get-tuple-element.61), channel_id=1, source_target_pairs={{0,7},{1,6},{2,5},{3,4},{4,3},{5,2},{6,1},{7,0},{8,15},{9,14},{10,... | collective-permute-start | bytes 294920 | tf_op jit(solution)/shard_map/ppermute | solution.py:297
  53.0 8.0 %collective-permute-start.16 = (bf16[64,768]{1,0:T(8,128)(2,1)S(1)}, bf16[64,768]{1,0:T(8,128)(2,1)S(1)}, u32[]{:S(2)}, u32[]{:S(2)}) collective-permute-start(bf16[64,768]{1,0:T(8,128)(2,1)S(1)} %get-tuple-element.62), channel_id=1, source_target_pairs={{0,4},{1,3},{2,6},{3,1},{4,0},{5,7},{6,2},{7,5},{8,12},{9,11},{10,... | collective-permute-start | bytes 294920 | tf_op jit(solution)/shard_map/ppermute | solution.py:297
  54.3 6.9 %collective-permute-start.17 = (bf16[64,768]{1,0:T(8,128)(2,1)S(1)}, bf16[64,768]{1,0:T(8,128)(2,1)S(1)}, u32[]{:S(2)}, u32[]{:S(2)}) collective-permute-start(bf16[64,768]{1,0:T(8,128)(2,1)S(1)} %get-tuple-element.63), channel_id=1, source_target_pairs={{0,2},{1,5},{2,0},{3,7},{4,6},{5,1},{6,4},{7,3},{8,10},{9,13},{10,... | collective-permute-start | bytes 294920 | tf_op jit(solution)/shard_map/ppermute | solution.py:297
  55.9 5.7 %collective-permute-start.18 = (bf16[64,768]{1,0:T(8,128)(2,1)S(1)}, bf16[64,768]{1,0:T(8,128)(2,1)S(1)}, u32[]{:S(2)}, u32[]{:S(2)}) collective-permute-start(bf16[64,768]{1,0:T(8,128)(2,1)S(1)} %get-tuple-element.64), channel_id=1, source_target_pairs={{0,5},{1,2},{2,7},{3,0},{4,1},{5,6},{6,3},{7,4},{8,13},{9,10},{10,... | collective-permute-start | bytes 294920 | tf_op jit(solution)/shard_map/ppermute | solution.py:297
  56.2 6.0 %collective-permute-start.19 = (bf16[64,768]{1,0:T(8,128)(2,1)S(1)}, bf16[64,768]{1,0:T(8,128)(2,1)S(1)}, u32[]{:S(2)}, u32[]{:S(2)}) collective-permute-start(bf16[64,768]{1,0:T(8,128)(2,1)S(1)} %get-tuple-element.65), channel_id=1, source_target_pairs={{0,3},{1,4},{2,1},{3,6},{4,7},{5,0},{6,5},{7,2},{8,11},{9,12},{10,... | collective-permute-start | bytes 294920 | tf_op jit(solution)/shard_map/ppermute | solution.py:297
  59.0 3.2 %collective-permute-start.20 = (bf16[64,768]{1,0:T(8,128)(2,1)S(1)}, bf16[64,768]{1,0:T(8,128)(2,1)S(1)}, u32[]{:S(2)}, u32[]{:S(2)}) collective-permute-start(bf16[64,768]{1,0:T(8,128)(2,1)S(1)} %get-tuple-element.66), channel_id=1, source_target_pairs={{0,1},{1,0},{2,3},{3,2},{4,5},{5,4},{6,7},{7,6},{8,9},{9,8},{10,11... | collective-permute-start | bytes 294920 | tf_op jit(solution)/shard_map/ppermute | solution.py:297

commit v3 on v2

--- a/solution.py
+++ b/solution.py
@@ -23,7 +23,7 @@
 LARGE = pltpu.CompilerParams(vmem_limit_bytes=16 << 20)
 
 
-STEPS = ((0, 0), (6, 6), (7, 7), (4, 2), (2, 4), (5, 3), (3, 5), (1, 1))
+STEPS = ((0, 0), (1, 1), (6, 6), (7, 7), (4, 2), (2, 4), (5, 3), (3, 5))
 
 
 def sent_to(number, step):
@@ -43,12 +43,7 @@
     return span & -2, 4 * (span & 1) + tok
 
 
-def begin_kernel(planes, levels_ref, temps_ref, list_ref, counts_ref, keys_ref, values_ref, q_ref, *refs):
-    pieces, (table_ref, factor_ref, source, q_source, target, sems) = refs[:PEERS], refs[PEERS:]
-    loads = [pltpu.make_async_copy(ref, source.at[i], sems.at[i]) for i, ref in enumerate((keys_ref, values_ref))]
-    loads.append(pltpu.make_async_copy(q_ref, q_source, sems.at[2]))
-    for load in loads:
-        load.start()
+def table_kernel(planes, levels_ref, temps_ref, list_ref, counts_ref, table_ref, factor_ref):
     base, number = place()
     head = number >> 1
     for side in range(2):
@@ -65,39 +60,69 @@
             count = jnp.where(found & (ident >= 0), counts_ref[jnp.maximum(ident, 0)], 0)
             table_ref[2 * slab + side] = count
 
+
+def tabulate(planes, levels, temps, ctx_list, counts):
+    return pl.pallas_call(
+        functools.partial(table_kernel, planes),
+        out_shape=[jax.ShapeDtypeStruct((4 * planes,), jnp.int32), jax.ShapeDtypeStruct((2 * GROUP,), jnp.float32)],
+        in_specs=[SMEM] * 4,
+        out_specs=[SMEM] * 2,
+        compiler_params=SMALL,
+    )(levels, temps, ctx_list, counts)
+
+
+def begin_kernel(keys_ref, values_ref, q_ref, *refs):
+    pieces, (source, q_source, target, sems) = refs[:PEERS], refs[PEERS:]
+    loads = [pltpu.make_async_copy(ref, source.at[i], sems.at[i]) for i, ref in enumerate((keys_ref, values_ref))]
+    loads.append(pltpu.make_async_copy(q_ref, q_source, sems.at[2]))
+    for load in loads:
+        load.start()
+    number = place()[1]
     for load in loads:
         load.wait()
     part = target.shape[1]
     stores = []
-    for step, piece in enumerate(pieces):
+    for step in [*range(1, PEERS), 0]:
         peer = sent_to(number, step)
         rows = pl.ds(pl.multiple_of((peer & 1) * part, part), part)
         lanes = pl.ds(pl.multiple_of((peer >> 1) * HD, HD), HD)
         target[step, :, :HD] = source[0, rows, lanes]
         target[step, :, HD : 2 * HD] = source[1, rows, lanes]
         target[step, :, 2 * HD :] = q_source[rows, pl.ds(pl.multiple_of((peer >> 1) * WIDE, HD), WIDE)]
-        stores.append(pltpu.make_async_copy(target.at[step], piece, sems.at[step]))
+        stores.append(pltpu.make_async_copy(target.at[step], pieces[step], sems.at[step]))
         stores[-1].start()
     for store in stores:
         store.wait()
 
 
-def begin(planes, levels, temps, ctx_list, counts, keys, values, queries):
+def begin(keys, values, queries):
     shape = (keys.shape[0] // 2, 2 * HD + WIDE)
-    out = pl.pallas_call(
-        functools.partial(begin_kernel, planes),
-        out_shape=[jax.ShapeDtypeStruct(shape, jnp.bfloat16)] * PEERS
-        + [jax.ShapeDtypeStruct((4 * planes,), jnp.int32), jax.ShapeDtypeStruct((2 * GROUP,), jnp.float32)],
-        in_specs=[SMEM] * 4 + [HBM] * 3,
-        out_specs=[HBM] * PEERS + [SMEM] * 2,
+    return pl.pallas_call(
+        begin_kernel,
+        out_shape=[jax.ShapeDtypeStruct(shape, jnp.bfloat16)] * PEERS,
+        in_specs=[HBM] * 3,
+        out_specs=[HBM] * PEERS,
         scratch_shapes=[
             pltpu.VMEM((2, *keys.shape), jnp.bfloat16),
             pltpu.VMEM(queries.shape, jnp.bfloat16),
             pltpu.VMEM((PEERS, *shape), jnp.bfloat16),
             pltpu.SemaphoreType.DMA((PEERS,)),
         ],
-    )(levels, temps, ctx_list, counts, keys, values, queries)
-    return out[:PEERS], out[PEERS:]
+    )(keys, values, queries)
+
+
+def hold_kernel(piece_ref, out_ref):
+    out_ref[...] = piece_ref[...]
+
+
+def hold(piece):
+    return pl.pallas_call(
+        hold_kernel,
+        out_shape=jax.ShapeDtypeStruct(piece.shape, piece.dtype),
+        in_specs=[VMEM],
+        out_specs=VMEM,
+        compiler_params=SMALL,
+    )(piece)
 
 
 def gather_kernel(*refs):
@@ -303,21 +328,18 @@
     def near(a):
         return lax.ppermute(a, "ctx", other_core)
 
-    pieces, tables = begin(spans // 2, levels, temps, jnp.transpose(ctx_list), counts, keys, values, queries)
-    own, q = gather(exchange(pieces))
+    pieces = begin(keys, values, queries)
+    tables = tabulate(spans // 2, levels, temps, jnp.transpose(ctx_list), counts)
+    moved, mine, tables = lax.optimization_barrier((exchange(pieces)[1:], hold(pieces[0]), tables))
+    own, q = gather([mine, *moved])
     slabs = {0: own, 1: up(own, 1), last: up(own, last)}
-    others = {0: near(own)}
-    state = attend(tables, q, None, [(own, others[0])], [0], False)
-    slabs, state = lax.optimization_barrier((slabs, state))
-    stage = [1, last]
-    others |= {back: near(slabs[back]) for back in stage}
     for back in range(2, last):
         slabs[back] = up(slabs[back - 1], 1)
-        state = attend(tables, q, state, [(slabs[b], others[b]) for b in stage], stage, False)
-        slabs[back], state = lax.optimization_barrier((slabs[back], state))
-        others[back] = near(slabs[back])
-        stage = [back]
-    out = attend(tables, q, state, [(slabs[b], others[b]) for b in stage], stage, True)
+    order = [1, last, *range(2, last)]
+    out = attend(tables, q, None, [(own, near(own))], [0], False)
+    for back in order:
+        slab, state = lax.optimization_barrier((slabs[back], out))
+        out = attend(tables, q, state, [(slab, near(slab))], [back], back == order[-1])
     return join(exchange(out[:PEERS]))
 
 

time: 63.5 us -> 65.2 us (1.027)
  the two profiles are of different devices: /device:TPU:0 before, /device:TPU:25 now
where the time goes in v3:
time: 65.2 us; the launch traced here: 64.7 us
  Pallas kernels  20.9 us (32%)
  starting transfers between devices  20.6 us (32%)
  waiting for transfers between devices  19.3 us (30%)
  local copies, waits for them, and re-layouts  3.58 us (5%)
    ppermute x14, starting transfers between devices, exchange(): lax.ppermute(piece, ('span', 'ctx'), [(f, f ^ step[f % 2]) for f in range...  17.5 us
    pallas_call x4, Pallas kernels, attend(): pl.pallas_call(functools.partial(attend_kernel, backs, first, final), out...  16.1 us
    ppermute x3, waiting for transfers between devices, up(): lax.ppermute(a, 'span', [(s, (s + 2 * steps) % spans) for s in range(span...  9.45 us
    ppermute x14, waiting for transfers between devices, exchange(): lax.ppermute(piece, ('span', 'ctx'), [(f, f ^ step[f % 2]) for f in range...  5.4 us
    ppermute x4, waiting for transfers between devices, near(): return lax.ppermute(a, 'ctx', other_core)  4.47 us
    unnamed x10, local copies, waits for them, and re-layouts  3.58 us
    ppermute x4, starting transfers between devices, near(): return lax.ppermute(a, 'ctx', other_core)  2.98 us
    pallas_call x1, Pallas kernels, begin(): pl.pallas_call(begin_kernel, out_shape=[jax.ShapeDtypeStruct(shape, jnp.b...  2.31 us
  transfers between devices with their start and end apart: 21, of which 13 were waited for; matrix products, arithmetic and copies ran while one was open for 0% of the time, Pallas kernels for 22%

profile of v3, /device:TPU:25, one launch (start us, length us, event | category | flops | bytes accessed | tf_op | source)
XLA Modules:
  0.0 64.7 jit_solution(15682717212248459712)
XLA Ops:
  0.0 2.3 %shard_map.73 = (bf16[64,1024]{1,0:T(8,128)(2,1)}, bf16[64,1024]{1,0:T(8,128)(2,1)}, bf16[64,1024]{1,0:T(8,128)(2,1)}, bf16[64,1024]{1,0:T(8,128)(2,1)}, bf16[64...) custom-call(bf16[128,512]{1,0:T(8,128)(2,1)} %keys_ref.1, ...), custom_call_target="tpu_custom_call" | custom-call | tf_op jit(solution)/shard_map/pallas_call | solution.py:100
  2.3 0.7 %collective-permute-start = (bf16[64,1024]{1,0:T(8,128)(2,1)}, bf16[64,1024]{1,0:T(8,128)(2,1)S(1)}, u32[]{:S(2)}, u32[]{:S(2)}) collective-permute-start(bf16[64,1024]{1,0:T(8,128)(2,1)} %get-tuple-element.50), channel_id=1, source_target_pairs={{0,1},{1,0},{2,3},{3,2},{4,5},{5,4},{6,7},{7,6},{8,9},{9,8},{10,11... | collective-permute-start | bytes 393224 | tf_op jit(solution)/shard_map/ppermute | solution.py:322
  3.1 2.2 %collective-permute-start.1 = (bf16[64,1024]{1,0:T(8,128)(2,1)}, bf16[64,1024]{1,0:T(8,128)(2,1)S(1)}, u32[]{:S(2)}, u32[]{:S(2)}) collective-permute-start(bf16[64,1024]{1,0:T(8,128)(2,1)} %get-tuple-element.51), channel_id=1, source_target_pairs={{0,6},{1,7},{2,4},{3,5},{4,2},{5,3},{6,0},{7,1},{8,14},{9,15},{10,... | collective-permute-start | bytes 393224 | tf_op jit(solution)/shard_map/ppermute | solution.py:322
  5.2 0.4 collective-permute-start.2
  5.7 1.2 %collective-permute-start.3 = (bf16[64,1024]{1,0:T(8,128)(2,1)}, bf16[64,1024]{1,0:T(8,128)(2,1)S(1)}, u32[]{:S(2)}, u32[]{:S(2)}) collective-permute-start(bf16[64,1024]{1,0:T(8,128)(2,1)} %get-tuple-element.53), channel_id=1, source_target_pairs={{0,4},{1,3},{2,6},{3,1},{4,0},{5,7},{6,2},{7,5},{8,12},{9,11},{10,... | collective-permute-start | bytes 393224 | tf_op jit(solution)/shard_map/ppermute | solution.py:322
  6.9 1.2 %collective-permute-start.4 = (bf16[64,1024]{1,0:T(8,128)(2,1)}, bf16[64,1024]{1,0:T(8,128)(2,1)S(1)}, u32[]{:S(2)}, u32[]{:S(2)}) collective-permute-start(bf16[64,1024]{1,0:T(8,128)(2,1)} %get-tuple-element.54), channel_id=1, source_target_pairs={{0,2},{1,5},{2,0},{3,7},{4,6},{5,1},{6,4},{7,3},{8,10},{9,13},{10,... | collective-permute-start | bytes 393224 | tf_op jit(solution)/shard_map/ppermute | solution.py:322
  8.1 0.0 collective-permute-done.refs_1_
  8.1 0.8 %collective-permute-start.5 = (bf16[64,1024]{1,0:T(8,128)(2,1)}, bf16[64,1024]{1,0:T(8,128)(2,1)S(1)}, u32[]{:S(2)}, u32[]{:S(2)}) collective-permute-start(bf16[64,1024]{1,0:T(8,128)(2,1)} %get-tuple-element.55), channel_id=1, source_target_pairs={{0,5},{1,2},{2,7},{3,0},{4,1},{5,6},{6,3},{7,4},{8,13},{9,10},{10,... | collective-permute-start | bytes 393224 | tf_op jit(solution)/shard_map/ppermute | solution.py:322
  9.0 0.3 collective-permute-done.1.refs_2_
  9.2 2.5 %collective-permute-start.6 = (bf16[64,1024]{1,0:T(8,128)(2,1)}, bf16[64,1024]{1,0:T(8,128)(2,1)S(1)}, u32[]{:S(2)}, u32[]{:S(2)}) collective-permute-start(bf16[64,1024]{1,0:T(8,128)(2,1)} %get-tuple-element.56), channel_id=1, source_target_pairs={{0,3},{1,4},{2,1},{3,6},{4,7},{5,0},{6,5},{7,2},{8,11},{9,12},{10,... | collective-permute-start | bytes 393224 | tf_op jit(solution)/shard_map/ppermute | solution.py:322
  11.7 0.0 copy-start
  11.7 0.9 %copy-done = bf16[64,1024]{1,0:T(8,128)(2,1)S(1)} copy-done((bf16[64,1024]{1,0:T(8,128)(2,1)S(1)}, bf16[64,1024]{1,0:T(8,128)(2,1)}, u32[]{:S(2)}) %copy-start) | copy-done | bytes 131096
  12.7 0.0 copy-start.1
  12.7 0.7 %copy-done.1 = f32[8,24]{1,0:T(8,128)S(1)} copy-done((f32[8,24]{1,0:T(8,128)S(1)}, f32[8,24]{1,0:T(8,128)}, u32[]{:S(2)}) %copy-start.1) | copy-done | bytes 792
  13.3 0.0 copy-start.2
  13.3 0.7 %copy-done.2 = s32[8,4]{0,1:T(4,128)S(1)} copy-done((s32[8,4]{0,1:T(4,128)S(1)}, s32[8,4]{0,1:T(4,128)}, u32[]{:S(2)}) %copy-start.2) | copy-done | bytes 152
  14.0 0.0 copy-start.3
  14.0 0.7 %copy-done.3 = s32[8]{0:T(128)S(1)} copy-done((s32[8]{0:T(128)S(1)}, s32[8]{0:T(128)}, u32[]{:S(2)}) %copy-start.3) | copy-done | bytes 56
  14.7 0.0 copy-start.4
  14.7 0.7 %copy-done.4 = s32[8]{0:T(128)S(1)} copy-done((s32[8]{0:T(128)S(1)}, s32[8]{0:T(128)}, u32[]{:S(2)}) %copy-start.4) | copy-done | bytes 56
  15.3 1.5 %shard_map.75 = (s32[16]{0:T(128)S(1)}, f32[12]{0:T(128)S(1)}) custom-call(s32[8]{0:T(128)S(1)} %copy-done.3, f32[8,24]{1,0:T(8,128)S(1)} %copy-done.1, s32[4,8]{1,0:T(4,128)S(1)} %bitcast.1, s32[8]{0:T(128)S(1)} %copy-done.4), custom_call_target="tpu_custom_call" | custom-call | tf_op jit(solution)/shard_map/pallas_call | solution.py:65
  16.9 0.0 collective-permute-done.2.refs_3_
  16.9 0.0 collective-permute-done.3.refs_4_
  16.9 0.0 collective-permute-done.4.refs_5_
  16.9 1.1 %collective-permute-done.5.refs_6_ = bf16[64,1024]{1,0:T(8,128)(2,1)S(1)} collective-permute-done((bf16[64,1024]{1,0:T(8,128)(2,1)}, bf16[64,1024]{1,0:T(8,128)(2,1)S(1)}, u32[]{:S(2)}, u32[]{:S(2)}) %collective-permute-start.5) | collective-permute-done | bytes 131104 | tf_op jit(solution)/shard_map/ppermute | solution.py:322
  18.0 0.0 collective-permute-done.6.refs_7_
  18.0 0.1 shard_map.76
  18.1 0.5 collective-permute-start.10
  18.6 0.0 collective-permute-start.7
  18.6 1.2 %collective-permute-done.10.refs_2_ = bf16[512,256]{1,0:T(8,128)(2,1)S(1)} collective-permute-done((bf16[512,256]{1,0:T(8,128)(2,1)S(1)}, bf16[512,256]{1,0:T(8,128)(2,1)S(1)}, u32[]{:S(2)}, u32[]{:S(2)}) %collective-permute-start.10) | collective-permute-done | bytes 262176 | tf_op jit(solution)/shard_map/ppermute | solution.py:329
  19.7 4.7 %shard_map.77 = (f32[2,4,384,256]{3,2,1,0:T(8,128)S(1)}, f32[2,4,384,128]{3,2,1,0:T(8,128)S(1)}) custom-call(s32[16]{0:T(128)S(1)} %get-tuple-element.60.table_ref, f32[12]{0:T(128)S(1)} %get-tuple-element.61.factor_ref, bf16[8,64,768]{2,1,0:T(8,128)(2,1)S(1)} %get-tuple-element.70.refs_0_, bf16[512,256]{1,0:T(8,128)(2,1)S(1)} %get-tuple-element.71.refs_1_, ...), custom_call_target="tpu_custom_call" | custom-call | flops 402653184 | bytes 1572864 | tf_op jit(solution)/shard_map/pallas_call | solution.py:303
  24.5 1.9 %collective-permute-done.7.refs_3_ = bf16[512,256]{1,0:T(8,128)(2,1)S(1)} collective-permute-done((bf16[512,256]{1,0:T(8,128)(2,1)S(1)}, bf16[512,256]{1,0:T(8,128)(2,1)S(1)}, u32[]{:S(2)}, u32[]{:S(2)}) %collective-permute-start.7) | collective-permute-done | bytes 262176 | tf_op jit(solution)/shard_map/ppermute | solution.py:326
  26.4 0.9 %collective-permute-start.11 = (bf16[512,256]{1,0:T(8,128)(2,1)S(1)}, bf16[512,256]{1,0:T(8,128)(2,1)S(1)}, u32[]{:S(2)}, u32[]{:S(2)}) collective-permute-start(bf16[512,256]{1,0:T(8,128)(2,1)S(1)} %collective-permute-done.7.refs_3_), channel_id=1, source_target_pairs={{0,1},{1,0},{2,3},{3,2},{4,5},{5,4},{6,7},{7,6},{8,9},{9,8},{10,11... | collective-permute-start | bytes 786440 | tf_op jit(solution)/shard_map/ppermute | solution.py:329
  27.3 0.2 collective-permute-start.9
  27.5 1.0 %collective-permute-done.11.refs_4_ = bf16[512,256]{1,0:T(8,128)(2,1)S(1)} collective-permute-done((bf16[512,256]{1,0:T(8,128)(2,1)S(1)}, bf16[512,256]{1,0:T(8,128)(2,1)S(1)}, u32[]{:S(2)}, u32[]{:S(2)}) %collective-permute-start.11) | collective-permute-done | bytes 262176 | tf_op jit(solution)/shard_map/ppermute | solution.py:329
  28.5 2.0 %shard_map.78 = (f32[2,4,384,256]{3,2,1,0:T(8,128)S(1)}, f32[2,4,384,128]{3,2,1,0:T(8,128)S(1)}) custom-call(s32[16]{0:T(128)S(1)} %get-tuple-element.60.table_ref, f32[12]{0:T(128)S(1)} %get-tuple-element.61.factor_ref, bf16[8,64,768]{2,1,0:T(8,128)(2,1)S(1)} %get-tuple-element.70.refs_0_, ...), custom_call_target="tpu_custom_call", output_to_operand_aliasing={{0}: (3, {}), {1}: (4, {})} | custom-call | flops 402653184 | bytes 1572864 | tf_op jit(solution)/shard_map/pallas_call | solution.py:303
  30.5 6.6 %collective-permute-done.9.refs_3_ = bf16[512,256]{1,0:T(8,128)(2,1)S(1)} collective-permute-done((bf16[512,256]{1,0:T(8,128)(2,1)S(1)}, bf16[512,256]{1,0:T(8,128)(2,1)S(1)}, u32[]{:S(2)}, u32[]{:S(2)}) %collective-permute-start.9) | collective-permute-done | bytes 262176 | tf_op jit(solution)/shard_map/ppermute | solution.py:326
  37.0 0.8 %collective-permute-start.12 = (bf16[512,256]{1,0:T(8,128)(2,1)S(1)}, bf16[512,256]{1,0:T(8,128)(2,1)S(1)}, u32[]{:S(2)}, u32[]{:S(2)}) collective-permute-start(bf16[512,256]{1,0:T(8,128)(2,1)S(1)} %collective-permute-done.9.refs_3_), channel_id=1, source_target_pairs={{0,1},{1,0},{2,3},{3,2},{4,5},{5,4},{6,7},{7,6},{8,9},{9,8},{10,11... | collective-permute-start | bytes 786440 | tf_op jit(solution)/shard_map/ppermute | solution.py:329
  37.8 0.0 collective-permute-start.8
  37.8 1.2 %collective-permute-done.12.refs_4_ = bf16[512,256]{1,0:T(8,128)(2,1)S(1)} collective-permute-done((bf16[512,256]{1,0:T(8,128)(2,1)S(1)}, bf16[512,256]{1,0:T(8,128)(2,1)S(1)}, u32[]{:S(2)}, u32[]{:S(2)}) %collective-permute-start.12) | collective-permute-done | bytes 262176 | tf_op jit(solution)/shard_map/ppermute | solution.py:329
  39.0 5.7 %shard_map.79 = (f32[2,4,384,256]{3,2,1,0:T(8,128)S(1)}, f32[2,4,384,128]{3,2,1,0:T(8,128)S(1)}) custom-call(s32[16]{0:T(128)S(1)} %get-tuple-element.60.table_ref, f32[12]{0:T(128)S(1)} %get-tuple-element.61.factor_ref, bf16[8,64,768]{2,1,0:T(8,128)(2,1)S(1)} %get-tuple-element.70.refs_0_, ...), custom_call_target="tpu_custom_call", output_to_operand_aliasing={{0}: (3, {}), {1}: (4, {})} | custom-call | flops 402653184 | bytes 1572864 | tf_op jit(solution)/shard_map/pallas_call | solution.py:303
  44.7 1.0 %collective-permute-done.8.refs_3_ = bf16[512,256]{1,0:T(8,128)(2,1)S(1)} collective-permute-done((bf16[512,256]{1,0:T(8,128)(2,1)S(1)}, bf16[512,256]{1,0:T(8,128)(2,1)S(1)}, u32[]{:S(2)}, u32[]{:S(2)}) %collective-permute-start.8) | collective-permute-done | bytes 262176 | tf_op jit(solution)/shard_map/ppermute | solution.py:326
  45.8 0.8 %collective-permute-start.13 = (bf16[512,256]{1,0:T(8,128)(2,1)S(1)}, bf16[512,256]{1,0:T(8,128)(2,1)S(1)}, u32[]{:S(2)}, u32[]{:S(2)}) collective-permute-start(bf16[512,256]{1,0:T(8,128)(2,1)S(1)} %collective-permute-done.8.refs_3_), channel_id=1, source_target_pairs={{0,1},{1,0},{2,3},{3,2},{4,5},{5,4},{6,7},{7,6},{8,9},{9,8},{10,11... | collective-permute-start | bytes 786440 | tf_op jit(solution)/shard_map/ppermute | solution.py:329
  46.5 1.2 %collective-permute-done.13.refs_4_ = bf16[512,256]{1,0:T(8,128)(2,1)S(1)} collective-permute-done((bf16[512,256]{1,0:T(8,128)(2,1)S(1)}, bf16[512,256]{1,0:T(8,128)(2,1)S(1)}, u32[]{:S(2)}, u32[]{:S(2)}) %collective-permute-start.13) | collective-permute-done | bytes 262176 | tf_op jit(solution)/shard_map/ppermute | solution.py:329
  47.7 3.6 %shard_map.80 = (bf16[64,768]{1,0:T(8,128)(2,1)S(1)}, bf16[64,768]{1,0:T(8,128)(2,1)S(1)}, bf16[64,768]{1,0:T(8,128)(2,1)S(1)}, bf16[64,768]{1,0:T(8,128)(2,1)S(...) custom-call(s32[16]{0:T(128)S(1)} %get-tuple-element.60.table_ref, ...), custom_call_target="tpu_custom_call", output_to_operand_aliasing={{8}: (3, {}), {9}: (4, {})} | custom-call | flops 402653184 | bytes 1572864 | tf_op jit(solution)/shard_map/pallas_call | solution.py:303
  51.3 0.4 collective-permute-start.14
  51.7 2.2 %collective-permute-start.15 = (bf16[64,768]{1,0:T(8,128)(2,1)S(1)}, bf16[64,768]{1,0:T(8,128)(2,1)S(1)}, u32[]{:S(2)}, u32[]{:S(2)}) collective-permute-start(bf16[64,768]{1,0:T(8,128)(2,1)S(1)} %get-tuple-element.89), channel_id=1, source_target_pairs={{0,6},{1,7},{2,4},{3,5},{4,2},{5,3},{6,0},{7,1},{8,14},{9,15},{10,... | collective-permute-start | bytes 294920 | tf_op jit(solution)/shard_map/ppermute | solution.py:322
  53.9 0.5 collective-permute-start.16
  54.4 1.3 %collective-permute-start.17 = (bf16[64,768]{1,0:T(8,128)(2,1)S(1)}, bf16[64,768]{1,0:T(8,128)(2,1)S(1)}, u32[]{:S(2)}, u32[]{:S(2)}) collective-permute-start(bf16[64,768]{1,0:T(8,128)(2,1)S(1)} %get-tuple-element.91), channel_id=1, source_target_pairs={{0,4},{1,3},{2,6},{3,1},{4,0},{5,7},{6,2},{7,5},{8,12},{9,11},{10,... | collective-permute-start | bytes 294920 | tf_op jit(solution)/shard_map/ppermute | solution.py:322
  55.7 1.2 %collective-permute-start.18 = (bf16[64,768]{1,0:T(8,128)(2,1)S(1)}, bf16[64,768]{1,0:T(8,128)(2,1)S(1)}, u32[]{:S(2)}, u32[]{:S(2)}) collective-permute-start(bf16[64,768]{1,0:T(8,128)(2,1)S(1)} %get-tuple-element.92), channel_id=1, source_target_pairs={{0,2},{1,5},{2,0},{3,7},{4,6},{5,1},{6,4},{7,3},{8,10},{9,13},{10,... | collective-permute-start | bytes 294920 | tf_op jit(solution)/shard_map/ppermute | solution.py:322
  56.9 0.0 collective-permute-done.14.refs_1_
  56.9 0.8 %collective-permute-start.19 = (bf16[64,768]{1,0:T(8,128)(2,1)S(1)}, bf16[64,768]{1,0:T(8,128)(2,1)S(1)}, u32[]{:S(2)}, u32[]{:S(2)}) collective-permute-start(bf16[64,768]{1,0:T(8,128)(2,1)S(1)} %get-tuple-element.93), channel_id=1, source_target_pairs={{0,5},{1,2},{2,7},{3,0},{4,1},{5,6},{6,3},{7,4},{8,13},{9,10},{10,... | collective-permute-start | bytes 294920 | tf_op jit(solution)/shard_map/ppermute | solution.py:322
  57.7 0.0 collective-permute-done.15.refs_2_
  57.7 2.0 %collective-permute-start.20 = (bf16[64,768]{1,0:T(8,128)(2,1)S(1)}, bf16[64,768]{1,0:T(8,128)(2,1)S(1)}, u32[]{:S(2)}, u32[]{:S(2)}) collective-permute-start(bf16[64,768]{1,0:T(8,128)(2,1)S(1)} %get-tuple-element.94), channel_id=1, source_target_pairs={{0,3},{1,4},{2,1},{3,6},{4,7},{5,0},{6,5},{7,2},{8,11},{9,12},{10,... | collective-permute-start | bytes 294920 | tf_op jit(solution)/shard_map/ppermute | solution.py:322
  59.6 0.3 collective-permute-done.16.refs_3_
  59.9 1.2 %collective-permute-done.17.refs_4_ = bf16[64,768]{1,0:T(8,128)(2,1)S(1)} collective-permute-done((bf16[64,768]{1,0:T(8,128)(2,1)S(1)}, bf16[64,768]{1,0:T(8,128)(2,1)S(1)}, u32[]{:S(2)}, u32[]{:S(2)}) %collective-permute-start.17) | collective-permute-done | bytes 98336 | tf_op jit(solution)/shard_map/ppermute | solution.py:322
  61.1 0.1 collective-permute-done.18.refs_5_
  61.2 2.4 %collective-permute-done.19.refs_6_ = bf16[64,768]{1,0:T(8,128)(2,1)S(1)} collective-permute-done((bf16[64,768]{1,0:T(8,128)(2,1)S(1)}, bf16[64,768]{1,0:T(8,128)(2,1)S(1)}, u32[]{:S(2)}, u32[]{:S(2)}) %collective-permute-start.19) | collective-permute-done | bytes 98336 | tf_op jit(solution)/shard_map/ppermute | solution.py:322
  63.6 0.0 collective-permute-done.20.refs_7_
  63.6 0.9 %shard_map.81 = bf16[128,3072]{1,0:T(8,128)(2,1)} custom-call(bf16[64,768]{1,0:T(8,128)(2,1)S(1)} %get-tuple-element.87.refs_0_, bf16[64,768]{1,0:T(8,128)(2,1)S(1)} %collective-permute-done.14.refs_1_, bf16[64,768]{1,0:T(8,128)(2,1)S(1)} %collective-permute-done.15.refs_2_, bf16[64,768]{1,0:T(8,128)(2,1)S(1)} %collective-permute-done.16.refs_3_, ...), custom_call_target="tpu_custom_call" | custom-call | tf_op jit(solution)/shard_map/pallas_call | solution.py:168
  (1 shorter events, 0.0 us)
Async XLA Ops:
  2.3 5.8 %collective-permute-start = (bf16[64,1024]{1,0:T(8,128)(2,1)}, bf16[64,1024]{1,0:T(8,128)(2,1)S(1)}, u32[]{:S(2)}, u32[]{:S(2)}) collective-permute-start(bf16[64,1024]{1,0:T(8,128)(2,1)} %get-tuple-element.50), channel_id=1, source_target_pairs={{0,1},{1,0},{2,3},{3,2},{4,5},{5,4},{6,7},{7,6},{8,9},{9,8},{10,11... | collective-permute-start | bytes 393224 | tf_op jit(solution)/shard_map/ppermute | solution.py:322
  3.1 6.2 %collective-permute-start.1 = (bf16[64,1024]{1,0:T(8,128)(2,1)}, bf16[64,1024]{1,0:T(8,128)(2,1)S(1)}, u32[]{:S(2)}, u32[]{:S(2)}) collective-permute-start(bf16[64,1024]{1,0:T(8,128)(2,1)} %get-tuple-element.51), channel_id=1, source_target_pairs={{0,6},{1,7},{2,4},{3,5},{4,2},{5,3},{6,0},{7,1},{8,14},{9,15},{10,... | collective-permute-start | bytes 393224 | tf_op jit(solution)/shard_map/ppermute | solution.py:322
  5.2 11.6 %collective-permute-start.2 = (bf16[64,1024]{1,0:T(8,128)(2,1)}, bf16[64,1024]{1,0:T(8,128)(2,1)S(1)}, u32[]{:S(2)}, u32[]{:S(2)}) collective-permute-start(bf16[64,1024]{1,0:T(8,128)(2,1)} %get-tuple-element.52), channel_id=1, source_target_pairs={{0,7},{1,6},{2,5},{3,4},{4,3},{5,2},{6,1},{7,0},{8,15},{9,14},{10,... | collective-permute-start | bytes 393224 | tf_op jit(solution)/shard_map/ppermute | solution.py:322
  5.7 11.2 %collective-permute-start.3 = (bf16[64,1024]{1,0:T(8,128)(2,1)}, bf16[64,1024]{1,0:T(8,128)(2,1)S(1)}, u32[]{:S(2)}, u32[]{:S(2)}) collective-permute-start(bf16[64,1024]{1,0:T(8,128)(2,1)} %get-tuple-element.53), channel_id=1, source_target_pairs={{0,4},{1,3},{2,6},{3,1},{4,0},{5,7},{6,2},{7,5},{8,12},{9,11},{10,... | collective-permute-start | bytes 393224 | tf_op jit(solution)/shard_map/ppermute | solution.py:322
  6.9 10.0 %collective-permute-start.4 = (bf16[64,1024]{1,0:T(8,128)(2,1)}, bf16[64,1024]{1,0:T(8,128)(2,1)S(1)}, u32[]{:S(2)}, u32[]{:S(2)}) collective-permute-start(bf16[64,1024]{1,0:T(8,128)(2,1)} %get-tuple-element.54), channel_id=1, source_target_pairs={{0,2},{1,5},{2,0},{3,7},{4,6},{5,1},{6,4},{7,3},{8,10},{9,13},{10,... | collective-permute-start | bytes 393224 | tf_op jit(solution)/shard_map/ppermute | solution.py:322
  8.1 9.9 %collective-permute-start.5 = (bf16[64,1024]{1,0:T(8,128)(2,1)}, bf16[64,1024]{1,0:T(8,128)(2,1)S(1)}, u32[]{:S(2)}, u32[]{:S(2)}) collective-permute-start(bf16[64,1024]{1,0:T(8,128)(2,1)} %get-tuple-element.55), channel_id=1, source_target_pairs={{0,5},{1,2},{2,7},{3,0},{4,1},{5,6},{6,3},{7,4},{8,13},{9,10},{10,... | collective-permute-start | bytes 393224 | tf_op jit(solution)/shard_map/ppermute | solution.py:322
  9.2 8.8 %collective-permute-start.6 = (bf16[64,1024]{1,0:T(8,128)(2,1)}, bf16[64,1024]{1,0:T(8,128)(2,1)S(1)}, u32[]{:S(2)}, u32[]{:S(2)}) collective-permute-start(bf16[64,1024]{1,0:T(8,128)(2,1)} %get-tuple-element.56), channel_id=1, source_target_pairs={{0,3},{1,4},{2,1},{3,6},{4,7},{5,0},{6,5},{7,2},{8,11},{9,12},{10,... | collective-permute-start | bytes 393224 | tf_op jit(solution)/shard_map/ppermute | solution.py:322
  11.7 0.9 %copy-start = (bf16[64,1024]{1,0:T(8,128)(2,1)S(1)}, bf16[64,1024]{1,0:T(8,128)(2,1)}, u32[]{:S(2)}) copy-start(bf16[64,1024]{1,0:T(8,128)(2,1)} %get-tuple-element.57.piece_ref) | copy-start | bytes 393220
  12.7 0.7 %copy-start.1 = (f32[8,24]{1,0:T(8,128)S(1)}, f32[8,24]{1,0:T(8,128)}, u32[]{:S(2)}) copy-start(f32[8,24]{1,0:T(8,128)} %temps_ref.1) | copy-start | bytes 2308
  13.3 0.7 %copy-start.2 = (s32[8,4]{0,1:T(4,128)S(1)}, s32[8,4]{0,1:T(4,128)}, u32[]{:S(2)}) copy-start(s32[8,4]{0,1:T(4,128)} %param.12) | copy-start | bytes 388
  14.0 0.7 %copy-start.3 = (s32[8]{0:T(128)S(1)}, s32[8]{0:T(128)}, u32[]{:S(2)}) copy-start(s32[8]{0:T(128)} %levels_ref.1) | copy-start | bytes 100
  14.7 0.7 %copy-start.4 = (s32[8]{0:T(128)S(1)}, s32[8]{0:T(128)}, u32[]{:S(2)}) copy-start(s32[8]{0:T(128)} %counts_ref.1) | copy-start | bytes 100
  18.1 1.6 %collective-permute-start.10 = (bf16[512,256]{1,0:T(8,128)(2,1)S(1)}, bf16[512,256]{1,0:T(8,128)(2,1)S(1)}, u32[]{:S(2)}, u32[]{:S(2)}) collective-permute-start(bf16[512,256]{1,0:T(8,128)(2,1)S(1)} %get-tuple-element.71.refs_1_), channel_id=1, source_target_pairs={{0,1},{1,0},{2,3},{3,2},{4,5},{5,4},{6,7},{7,6},{8,9},{9,8},{10,11... | collective-permute-start | bytes 786440 | tf_op jit(solution)/shard_map/ppermute | solution.py:329
  18.6 7.8 %collective-permute-start.7 = (bf16[512,256]{1,0:T(8,128)(2,1)S(1)}, bf16[512,256]{1,0:T(8,128)(2,1)S(1)}, u32[]{:S(2)}, u32[]{:S(2)}) collective-permute-start(bf16[512,256]{1,0:T(8,128)(2,1)S(1)} %get-tuple-element.71.refs_1_), channel_id=1, source_target_pairs={{0,8},{4,12},{8,16},{12,20},{16,24},{20,28},{24,0},{28,4},{1,9},{5... | collective-permute-start | bytes 786440 | tf_op jit(solution)/shard_map/ppermute | solution.py:326
  26.4 2.1 %collective-permute-start.11 = (bf16[512,256]{1,0:T(8,128)(2,1)S(1)}, bf16[512,256]{1,0:T(8,128)(2,1)S(1)}, u32[]{:S(2)}, u32[]{:S(2)}) collective-permute-start(bf16[512,256]{1,0:T(8,128)(2,1)S(1)} %collective-permute-done.7.refs_3_), channel_id=1, source_target_pairs={{0,1},{1,0},{2,3},{3,2},{4,5},{5,4},{6,7},{7,6},{8,9},{9,8},{10,11... | collective-permute-start | bytes 786440 | tf_op jit(solution)/shard_map/ppermute | solution.py:329
  27.3 9.7 %collective-permute-start.9 = (bf16[512,256]{1,0:T(8,128)(2,1)S(1)}, bf16[512,256]{1,0:T(8,128)(2,1)S(1)}, u32[]{:S(2)}, u32[]{:S(2)}) collective-permute-start(bf16[512,256]{1,0:T(8,128)(2,1)S(1)} %get-tuple-element.71.refs_1_), channel_id=1, source_target_pairs={{0,24},{4,28},{8,0},{12,4},{16,8},{20,12},{24,16},{28,20},{1,25},{... | collective-permute-start | bytes 786440 | tf_op jit(solution)/shard_map/ppermute | solution.py:326
  37.0 1.9 %collective-permute-start.12 = (bf16[512,256]{1,0:T(8,128)(2,1)S(1)}, bf16[512,256]{1,0:T(8,128)(2,1)S(1)}, u32[]{:S(2)}, u32[]{:S(2)}) collective-permute-start(bf16[512,256]{1,0:T(8,128)(2,1)S(1)} %collective-permute-done.9.refs_3_), channel_id=1, source_target_pairs={{0,1},{1,0},{2,3},{3,2},{4,5},{5,4},{6,7},{7,6},{8,9},{9,8},{10,11... | collective-permute-start | bytes 786440 | tf_op jit(solution)/shard_map/ppermute | solution.py:329
  37.8 7.9 %collective-permute-start.8 = (bf16[512,256]{1,0:T(8,128)(2,1)S(1)}, bf16[512,256]{1,0:T(8,128)(2,1)S(1)}, u32[]{:S(2)}, u32[]{:S(2)}) collective-permute-start(bf16[512,256]{1,0:T(8,128)(2,1)S(1)} %collective-permute-done.7.refs_3_), channel_id=1, source_target_pairs={{0,8},{4,12},{8,16},{12,20},{16,24},{20,28},{24,0},{28,4},{1,9},{5... | collective-permute-start | bytes 786440 | tf_op jit(solution)/shard_map/ppermute | solution.py:326
  45.8 1.9 %collective-permute-start.13 = (bf16[512,256]{1,0:T(8,128)(2,1)S(1)}, bf16[512,256]{1,0:T(8,128)(2,1)S(1)}, u32[]{:S(2)}, u32[]{:S(2)}) collective-permute-start(bf16[512,256]{1,0:T(8,128)(2,1)S(1)} %collective-permute-done.8.refs_3_), channel_id=1, source_target_pairs={{0,1},{1,0},{2,3},{3,2},{4,5},{5,4},{6,7},{7,6},{8,9},{9,8},{10,11... | collective-permute-start | bytes 786440 | tf_op jit(solution)/shard_map/ppermute | solution.py:329
  51.3 5.6 %collective-permute-start.14 = (bf16[64,768]{1,0:T(8,128)(2,1)S(1)}, bf16[64,768]{1,0:T(8,128)(2,1)S(1)}, u32[]{:S(2)}, u32[]{:S(2)}) collective-permute-start(bf16[64,768]{1,0:T(8,128)(2,1)S(1)} %get-tuple-element.88), channel_id=1, source_target_pairs={{0,1},{1,0},{2,3},{3,2},{4,5},{5,4},{6,7},{7,6},{8,9},{9,8},{10,11... | collective-permute-start | bytes 294920 | tf_op jit(solution)/shard_map/ppermute | solution.py:322
  51.7 5.9 %collective-permute-start.15 = (bf16[64,768]{1,0:T(8,128)(2,1)S(1)}, bf16[64,768]{1,0:T(8,128)(2,1)S(1)}, u32[]{:S(2)}, u32[]{:S(2)}) collective-permute-start(bf16[64,768]{1,0:T(8,128)(2,1)S(1)} %get-tuple-element.89), channel_id=1, source_target_pairs={{0,6},{1,7},{2,4},{3,5},{4,2},{5,3},{6,0},{7,1},{8,14},{9,15},{10,... | collective-permute-start | bytes 294920 | tf_op jit(solution)/shard_map/ppermute | solution.py:322
  53.9 6.0 %collective-permute-start.16 = (bf16[64,768]{1,0:T(8,128)(2,1)S(1)}, bf16[64,768]{1,0:T(8,128)(2,1)S(1)}, u32[]{:S(2)}, u32[]{:S(2)}) collective-permute-start(bf16[64,768]{1,0:T(8,128)(2,1)S(1)} %get-tuple-element.90), channel_id=1, source_target_pairs={{0,7},{1,6},{2,5},{3,4},{4,3},{5,2},{6,1},{7,0},{8,15},{9,14},{10,... | collective-permute-start | bytes 294920 | tf_op jit(solution)/shard_map/ppermute | solution.py:322
  54.4 6.7 %collective-permute-start.17 = (bf16[64,768]{1,0:T(8,128)(2,1)S(1)}, bf16[64,768]{1,0:T(8,128)(2,1)S(1)}, u32[]{:S(2)}, u32[]{:S(2)}) collective-permute-start(bf16[64,768]{1,0:T(8,128)(2,1)S(1)} %get-tuple-element.91), channel_id=1, source_target_pairs={{0,4},{1,3},{2,6},{3,1},{4,0},{5,7},{6,2},{7,5},{8,12},{9,11},{10,... | collective-permute-start | bytes 294920 | tf_op jit(solution)/shard_map/ppermute | solution.py:322
  55.7 5.5 %collective-permute-start.18 = (bf16[64,768]{1,0:T(8,128)(2,1)S(1)}, bf16[64,768]{1,0:T(8,128)(2,1)S(1)}, u32[]{:S(2)}, u32[]{:S(2)}) collective-permute-start(bf16[64,768]{1,0:T(8,128)(2,1)S(1)} %get-tuple-element.92), channel_id=1, source_target_pairs={{0,2},{1,5},{2,0},{3,7},{4,6},{5,1},{6,4},{7,3},{8,10},{9,13},{10,... | collective-permute-start | bytes 294920 | tf_op jit(solution)/shard_map/ppermute | solution.py:322
  56.9 6.7 %collective-permute-start.19 = (bf16[64,768]{1,0:T(8,128)(2,1)S(1)}, bf16[64,768]{1,0:T(8,128)(2,1)S(1)}, u32[]{:S(2)}, u32[]{:S(2)}) collective-permute-start(bf16[64,768]{1,0:T(8,128)(2,1)S(1)} %get-tuple-element.93), channel_id=1, source_target_pairs={{0,5},{1,2},{2,7},{3,0},{4,1},{5,6},{6,3},{7,4},{8,13},{9,10},{10,... | collective-permute-start | bytes 294920 | tf_op jit(solution)/shard_map/ppermute | solution.py:322
  57.7 5.9 %collective-permute-start.20 = (bf16[64,768]{1,0:T(8,128)(2,1)S(1)}, bf16[64,768]{1,0:T(8,128)(2,1)S(1)}, u32[]{:S(2)}, u32[]{:S(2)}) collective-permute-start(bf16[64,768]{1,0:T(8,128)(2,1)S(1)} %get-tuple-element.94), channel_id=1, source_target_pairs={{0,3},{1,4},{2,1},{3,6},{4,7},{5,0},{6,5},{7,2},{8,11},{9,12},{10,... | collective-permute-start | bytes 294920 | tf_op jit(solution)/shard_map/ppermute | solution.py:322

commit v4 on v3

--- a/solution.py
+++ b/solution.py
@@ -175,16 +175,16 @@
     )(*pieces)
 
 
-def attend_kernel(backs, first, final, table_ref, factor_ref, *refs):
+def attend_kernel(backs, sides, far_side, first, final, table_ref, factor_ref, *refs):
     refs = list(refs)
     q_ref = refs.pop(0)
     if not first:
         del refs[:2]
-    slabs = [(refs.pop(0), refs.pop(0)) for _ in backs]
+    slabs = [[refs.pop(0) for _ in range(sides)] for _ in backs]
     out_refs = [refs.pop(0) for _ in range(PEERS)] if final else None
     sums_ref, top_ref = refs.pop(0), refs.pop(0)
     number = place()[1]
-    core = number & 1
+    core = (number & 1) ^ far_side
     if first:
         sums_ref[...] = jnp.zeros_like(sums_ref)
         top_ref[...] = jnp.full_like(top_ref, LOW)
@@ -197,23 +197,29 @@
     block_rows = 2 * piece
     index = lax.broadcasted_iota(jnp.int32, (block_rows, HD), 0)
     own_part = index < piece
-    token = 2 * block_rows + index + jnp.where(own_part, core * piece, -(core * piece))
+    if sides == 2:
+        token = 2 * block_rows + index + jnp.where(own_part, core * piece, -(core * piece))
+    else:
+        token = 2 * block_rows + index + jnp.where(own_part, core * piece, (core + 1) * piece)
     for slab, back in zip(slabs, backs):
         for x in range(2):
             count = jnp.maximum(table_ref[4 * back + 2 * x], table_ref[4 * back + 2 * x + 1])
             at = x * half
             spare = slab[0][at : at + 16, :HD].astype(jnp.float32)[0:1]
             parts = [ref[at : at + block_rows, :] for ref in slab]
-            for n in range(2, 4):
-                low = at + n * piece
-                parts.append(jnp.concatenate([ref[low : low + piece, :] for ref in slab], axis=0))
+            if sides == 2:
+                for n in range(2, 4):
+                    low = at + n * piece
+                    parts.append(jnp.concatenate([ref[low : low + piece, :] for ref in slab], axis=0))
+            else:
+                parts.append(slab[0][at + block_rows : at + 2 * block_rows, :])
             for n, values in enumerate(parts):
                 to = slice(n * block_rows, (n + 1) * block_rows)
                 keys = values[:, :HD].astype(jnp.float32)
                 values = values[:, HD:]
                 ones = jnp.ones_like(values)
-                if n >= 2:
-                    keep = token + (n - 2) * block_rows < count
+                if n >= sides:
+                    keep = token + (n - sides) * block_rows < count
                     keys = jnp.where(keep, keys, spare)
                     values = jnp.where(keep, values.astype(jnp.float32), 0.0).astype(jnp.bfloat16)
                     ones = jnp.where(keep, 1.0, 0.0).astype(jnp.bfloat16)
@@ -266,8 +272,11 @@
                     top_ref[side, chain] = top
 
             most = 3 * block_rows
-            pl.when((count > 0) & (count <= most))(lambda: visit(most))
-            pl.when(count > most)(lambda: visit(most + block_rows))
+            if sides == 2:
+                pl.when((count > 0) & (count <= most))(lambda: visit(most))
+                pl.when(count > most)(lambda: visit(most + block_rows))
+            else:
+                pl.when(count > 0)(lambda: visit(2 * block_rows))
 
     if final:
         done_ref = refs[2]
@@ -284,11 +293,11 @@
             out_ref[...] = done_ref[sent_to(number, step)]
 
 
-def attend(tables, q, state, slabs, backs, final):
+def attend(tables, q, state, slabs, backs, final, far_side=False):
     first = state is None
     piece = q.shape[1]
     tall = GROUP * piece
-    tokens = slabs[0][0].shape[0]
+    tokens = slabs[0][0].shape[0] * len(slabs[0]) // 2
     out_shape = [
         jax.ShapeDtypeStruct((2, 4, tall, 2 * HD), jnp.float32),
         jax.ShapeDtypeStruct((2, 4, tall, HD), jnp.float32),
@@ -301,7 +310,7 @@
     inputs = [q, *(state or ()), *[a for slab in slabs for a in slab]]
     aliases = {} if first else {3: PEERS * final, 4: PEERS * final + 1}
     return pl.pallas_call(
-        functools.partial(attend_kernel, backs, first, final),
+        functools.partial(attend_kernel, backs, len(slabs[0]), far_side, first, final),
         out_shape=out_shape,
         in_specs=[SMEM] * 2 + [VMEM] * len(inputs),
         out_specs=[VMEM] * len(out_shape),
@@ -333,13 +342,20 @@
     moved, mine, tables = lax.optimization_barrier((exchange(pieces)[1:], hold(pieces[0]), tables))
     own, q = gather([mine, *moved])
     slabs = {0: own, 1: up(own, 1), last: up(own, last)}
+    state = attend(tables, q, None, [(own, near(own))], [0], False)
+    slabs, state = lax.optimization_barrier((slabs, state))
+    stage = [1, last]
+    sides = [(slabs[b], near(slabs[b])) for b in stage]
     for back in range(2, last):
-        slabs[back] = up(slabs[back - 1], 1)
-    order = [1, last, *range(2, last)]
-    out = attend(tables, q, None, [(own, near(own))], [0], False)
-    for back in order:
-        slab, state = lax.optimization_barrier((slabs[back], out))
-        out = attend(tables, q, state, [(slab, near(slab))], [back], back == order[-1])
+        slab = up(slabs[back - 1], 1)
+        state = attend(tables, q, state, sides, stage, False)
+        slabs[back], state = lax.optimization_barrier((slab, state))
+        stage = [back]
+        sides = [(slabs[back], near(slabs[back]))]
+    mine, other = sides[0]
+    state = attend(tables, q, state, [(mine,)], stage, False)
+    other, state = lax.optimization_barrier((other, state))
+    out = attend(tables, q, state, [(other,)], stage, True, True)
     return join(exchange(out[:PEERS]))
 
 

time: 65.2 us -> 62.2 us (0.954); the launches traced: 64.7 us -> 60.9 us
  waiting for transfers between devices: 19.3 us -> 11 us
  starting transfers between devices: 20.6 us -> 24.5 us
  Pallas kernels: 20.9 us -> 21.8 us
    ppermute x3, starting transfers between devices: 0.18 us -> 5.06 us  [up(): lax.ppermute(a, 'span', [(s, (s + 2 * steps) % spans) for s in range(span...]
    ppermute x4, waiting for transfers between devices: 4.47 us -> 0.01 us  [near(): return lax.ppermute(a, 'ctx', other_core)]
    ppermute x3, waiting for transfers between devices: 9.45 us -> 5.27 us  [up(): lax.ppermute(a, 'span', [(s, (s + 2 * steps) % spans) for s in range(span...]
    pallas_call x4, Pallas kernels: 16.1 us -> 16.9 us  [attend(): pl.pallas_call(functools.partial(attend_kernel, backs, len(slabs[0]), far...]
  transfers between devices with their start and end apart: 21 -> 21, of which waited for: 13 -> 8; matrix products, arithmetic and copies ran while one was open for 0% -> 0% of each run, Pallas kernels for 22% -> 26%
where the time goes in v4:
time: 62.2 us; the launch traced here: 60.9 us
  starting transfers between devices  24.5 us (39%)
  Pallas kernels  21.8 us (35%)
  waiting for transfers between devices  11 us (18%)
  local copies, waits for them, and re-layouts  3.58 us (6%)
    pallas_call x4, Pallas kernels, attend(): pl.pallas_call(functools.partial(attend_kernel, backs, len(slabs[0]), far...  16.9 us
    ppermute x14, starting transfers between devices, exchange(): lax.ppermute(piece, ('span', 'ctx'), [(f, f ^ step[f % 2]) for f in range...  16.9 us
    ppermute x14, waiting for transfers between devices, exchange(): lax.ppermute(piece, ('span', 'ctx'), [(f, f ^ step[f % 2]) for f in range...  5.68 us
    ppermute x3, waiting for transfers between devices, up(): lax.ppermute(a, 'span', [(s, (s + 2 * steps) % spans) for s in range(span...  5.27 us
    ppermute x3, starting transfers between devices, up(): lax.ppermute(a, 'span', [(s, (s + 2 * steps) % spans) for s in range(span...  5.06 us
    unnamed x10, local copies, waits for them, and re-layouts  3.58 us
    ppermute x4, starting transfers between devices, near(): return lax.ppermute(a, 'ctx', other_core)  2.59 us
    pallas_call x1, Pallas kernels, begin(): pl.pallas_call(begin_kernel, out_shape=[jax.ShapeDtypeStruct(shape, jnp.b...  2.31 us
  transfers between devices with their start and end apart: 21, of which 8 were waited for; matrix products, arithmetic and copies ran while one was open for 0% of the time, Pallas kernels for 26%

profile of v4, /device:TPU:25, one launch (start us, length us, event | category | flops | bytes accessed | tf_op | source)
XLA Modules:
  0.0 60.9 jit_solution(14155367601369940626)
XLA Ops:
  0.0 2.3 %shard_map.73 = (bf16[64,1024]{1,0:T(8,128)(2,1)}, bf16[64,1024]{1,0:T(8,128)(2,1)}, bf16[64,1024]{1,0:T(8,128)(2,1)}, bf16[64,1024]{1,0:T(8,128)(2,1)}, bf16[64...) custom-call(bf16[128,512]{1,0:T(8,128)(2,1)} %keys_ref.1, ...), custom_call_target="tpu_custom_call" | custom-call | tf_op jit(solution)/shard_map/pallas_call | solution.py:100
  2.3 0.7 %collective-permute-start = (bf16[64,1024]{1,0:T(8,128)(2,1)}, bf16[64,1024]{1,0:T(8,128)(2,1)S(1)}, u32[]{:S(2)}, u32[]{:S(2)}) collective-permute-start(bf16[64,1024]{1,0:T(8,128)(2,1)} %get-tuple-element.51), channel_id=1, source_target_pairs={{0,1},{1,0},{2,3},{3,2},{4,5},{5,4},{6,7},{7,6},{8,9},{9,8},{10,11... | collective-permute-start | bytes 393224 | tf_op jit(solution)/shard_map/ppermute | solution.py:331
  3.1 2.2 %collective-permute-start.1 = (bf16[64,1024]{1,0:T(8,128)(2,1)}, bf16[64,1024]{1,0:T(8,128)(2,1)S(1)}, u32[]{:S(2)}, u32[]{:S(2)}) collective-permute-start(bf16[64,1024]{1,0:T(8,128)(2,1)} %get-tuple-element.52), channel_id=1, source_target_pairs={{0,6},{1,7},{2,4},{3,5},{4,2},{5,3},{6,0},{7,1},{8,14},{9,15},{10,... | collective-permute-start | bytes 393224 | tf_op jit(solution)/shard_map/ppermute | solution.py:331
  5.2 0.4 collective-permute-start.2
  5.7 1.2 %collective-permute-start.3 = (bf16[64,1024]{1,0:T(8,128)(2,1)}, bf16[64,1024]{1,0:T(8,128)(2,1)S(1)}, u32[]{:S(2)}, u32[]{:S(2)}) collective-permute-start(bf16[64,1024]{1,0:T(8,128)(2,1)} %get-tuple-element.54), channel_id=1, source_target_pairs={{0,4},{1,3},{2,6},{3,1},{4,0},{5,7},{6,2},{7,5},{8,12},{9,11},{10,... | collective-permute-start | bytes 393224 | tf_op jit(solution)/shard_map/ppermute | solution.py:331
  6.9 1.2 %collective-permute-start.4 = (bf16[64,1024]{1,0:T(8,128)(2,1)}, bf16[64,1024]{1,0:T(8,128)(2,1)S(1)}, u32[]{:S(2)}, u32[]{:S(2)}) collective-permute-start(bf16[64,1024]{1,0:T(8,128)(2,1)} %get-tuple-element.55), channel_id=1, source_target_pairs={{0,2},{1,5},{2,0},{3,7},{4,6},{5,1},{6,4},{7,3},{8,10},{9,13},{10,... | collective-permute-start | bytes 393224 | tf_op jit(solution)/shard_map/ppermute | solution.py:331
  8.1 0.0 collective-permute-done.refs_1_
  8.1 0.8 %collective-permute-start.5 = (bf16[64,1024]{1,0:T(8,128)(2,1)}, bf16[64,1024]{1,0:T(8,128)(2,1)S(1)}, u32[]{:S(2)}, u32[]{:S(2)}) collective-permute-start(bf16[64,1024]{1,0:T(8,128)(2,1)} %get-tuple-element.56), channel_id=1, source_target_pairs={{0,5},{1,2},{2,7},{3,0},{4,1},{5,6},{6,3},{7,4},{8,13},{9,10},{10,... | collective-permute-start | bytes 393224 | tf_op jit(solution)/shard_map/ppermute | solution.py:331
  9.0 0.3 collective-permute-done.1.refs_2_
  9.2 2.5 %collective-permute-start.6 = (bf16[64,1024]{1,0:T(8,128)(2,1)}, bf16[64,1024]{1,0:T(8,128)(2,1)S(1)}, u32[]{:S(2)}, u32[]{:S(2)}) collective-permute-start(bf16[64,1024]{1,0:T(8,128)(2,1)} %get-tuple-element.57), channel_id=1, source_target_pairs={{0,3},{1,4},{2,1},{3,6},{4,7},{5,0},{6,5},{7,2},{8,11},{9,12},{10,... | collective-permute-start | bytes 393224 | tf_op jit(solution)/shard_map/ppermute | solution.py:331
  11.7 0.0 copy-start
  11.7 0.9 %copy-done = bf16[64,1024]{1,0:T(8,128)(2,1)S(1)} copy-done((bf16[64,1024]{1,0:T(8,128)(2,1)S(1)}, bf16[64,1024]{1,0:T(8,128)(2,1)}, u32[]{:S(2)}) %copy-start) | copy-done | bytes 131096
  12.7 0.0 copy-start.1
  12.7 0.7 %copy-done.1 = f32[8,24]{1,0:T(8,128)S(1)} copy-done((f32[8,24]{1,0:T(8,128)S(1)}, f32[8,24]{1,0:T(8,128)}, u32[]{:S(2)}) %copy-start.1) | copy-done | bytes 792
  13.3 0.0 copy-start.2
  13.3 0.7 %copy-done.2 = s32[8,4]{0,1:T(4,128)S(1)} copy-done((s32[8,4]{0,1:T(4,128)S(1)}, s32[8,4]{0,1:T(4,128)}, u32[]{:S(2)}) %copy-start.2) | copy-done | bytes 152
  14.0 0.0 copy-start.3
  14.0 0.7 %copy-done.3 = s32[8]{0:T(128)S(1)} copy-done((s32[8]{0:T(128)S(1)}, s32[8]{0:T(128)}, u32[]{:S(2)}) %copy-start.3) | copy-done | bytes 56
  14.7 0.0 copy-start.4
  14.7 0.7 %copy-done.4 = s32[8]{0:T(128)S(1)} copy-done((s32[8]{0:T(128)S(1)}, s32[8]{0:T(128)}, u32[]{:S(2)}) %copy-start.4) | copy-done | bytes 56
  15.3 1.5 %shard_map.75 = (s32[16]{0:T(128)S(1)}, f32[12]{0:T(128)S(1)}) custom-call(s32[8]{0:T(128)S(1)} %copy-done.3, f32[8,24]{1,0:T(8,128)S(1)} %copy-done.1, s32[4,8]{1,0:T(4,128)S(1)} %bitcast.1, s32[8]{0:T(128)S(1)} %copy-done.4), custom_call_target="tpu_custom_call" | custom-call | tf_op jit(solution)/shard_map/pallas_call | solution.py:65
  16.9 0.0 collective-permute-done.2.refs_3_
  16.9 0.0 collective-permute-done.3.refs_4_
  16.9 0.0 collective-permute-done.4.refs_5_
  16.9 1.1 %collective-permute-done.5.refs_6_ = bf16[64,1024]{1,0:T(8,128)(2,1)S(1)} collective-permute-done((bf16[64,1024]{1,0:T(8,128)(2,1)}, bf16[64,1024]{1,0:T(8,128)(2,1)S(1)}, u32[]{:S(2)}, u32[]{:S(2)}) %collective-permute-start.5) | collective-permute-done | bytes 131104 | tf_op jit(solution)/shard_map/ppermute | solution.py:331
  18.0 0.0 collective-permute-done.6.refs_7_
  18.0 0.1 shard_map.76
  18.1 0.5 collective-permute-start.9
  18.6 0.2 collective-permute-start.8
  18.7 3.1 %collective-permute-start.7 = (bf16[512,256]{1,0:T(8,128)(2,1)S(1)}, bf16[512,256]{1,0:T(8,128)(2,1)S(1)}, u32[]{:S(2)}, u32[]{:S(2)}) collective-permute-start(bf16[512,256]{1,0:T(8,128)(2,1)S(1)} %get-tuple-element.72.refs_1_), channel_id=1, source_target_pairs={{0,8},{4,12},{8,16},{12,20},{16,24},{20,28},{24,0},{28,4},{1,9},{5... | collective-permute-start | bytes 786440 | tf_op jit(solution)/shard_map/ppermute | solution.py:335
  21.8 0.0 collective-permute-done.9.refs_2_
  21.8 4.7 %shard_map.77 = (f32[2,4,384,256]{3,2,1,0:T(8,128)S(1)}, f32[2,4,384,128]{3,2,1,0:T(8,128)S(1)}) custom-call(s32[16]{0:T(128)S(1)} %get-tuple-element.61.table_ref, f32[12]{0:T(128)S(1)} %get-tuple-element.62.factor_ref, bf16[8,64,768]{2,1,0:T(8,128)(2,1)S(1)} %get-tuple-element.71.refs_0_, bf16[512,256]{1,0:T(8,128)(2,1)S(1)} %get-tuple-element.72.refs_1_, ...), custom_call_target="tpu_custom_call" | custom-call | flops 402653184 | bytes 1572864 | tf_op jit(solution)/shard_map/pallas_call | solution.py:312
  26.6 1.6 %collective-permute-done.8.refs_5_ = bf16[512,256]{1,0:T(8,128)(2,1)S(1)} collective-permute-done((bf16[512,256]{1,0:T(8,128)(2,1)S(1)}, bf16[512,256]{1,0:T(8,128)(2,1)S(1)}, u32[]{:S(2)}, u32[]{:S(2)}) %collective-permute-start.8) | collective-permute-done | bytes 262176 | tf_op jit(solution)/shard_map/ppermute | solution.py:335
  28.2 3.6 %collective-permute-done.7.refs_3_ = bf16[512,256]{1,0:T(8,128)(2,1)S(1)} collective-permute-done((bf16[512,256]{1,0:T(8,128)(2,1)S(1)}, bf16[512,256]{1,0:T(8,128)(2,1)S(1)}, u32[]{:S(2)}, u32[]{:S(2)}) %collective-permute-start.7) | collective-permute-done | bytes 262176 | tf_op jit(solution)/shard_map/ppermute | solution.py:335
  31.8 1.3 %collective-permute-start.12 = (bf16[512,256]{1,0:T(8,128)(2,1)S(1)}, bf16[512,256]{1,0:T(8,128)(2,1)S(1)}, u32[]{:S(2)}, u32[]{:S(2)}) collective-permute-start(bf16[512,256]{1,0:T(8,128)(2,1)S(1)} %collective-permute-done.8.refs_5_), channel_id=1, source_target_pairs={{0,1},{1,0},{2,3},{3,2},{4,5},{5,4},{6,7},{7,6},{8,9},{9,8},{10,11... | collective-permute-start | bytes 786440 | tf_op jit(solution)/shard_map/ppermute | solution.py:338
  33.1 0.0 collective-permute-start.11
  33.1 1.8 %collective-permute-start.10 = (bf16[512,256]{1,0:T(8,128)(2,1)S(1)}, bf16[512,256]{1,0:T(8,128)(2,1)S(1)}, u32[]{:S(2)}, u32[]{:S(2)}) collective-permute-start(bf16[512,256]{1,0:T(8,128)(2,1)S(1)} %collective-permute-done.7.refs_3_), channel_id=1, source_target_pairs={{0,8},{4,12},{8,16},{12,20},{16,24},{20,28},{24,0},{28,4},{1,9},{5... | collective-permute-start | bytes 786440 | tf_op jit(solution)/shard_map/ppermute | solution.py:335
  34.9 0.0 collective-permute-done.12.refs_6_
  34.9 0.0 collective-permute-done.11.refs_4_
  34.9 7.2 %shard_map.78 = (f32[2,4,384,256]{3,2,1,0:T(8,128)S(1)}, f32[2,4,384,128]{3,2,1,0:T(8,128)S(1)}) custom-call(s32[16]{0:T(128)S(1)} %get-tuple-element.61.table_ref, f32[12]{0:T(128)S(1)} %get-tuple-element.62.factor_ref, bf16[8,64,768]{2,1,0:T(8,128)(2,1)S(1)} %get-tuple-element.71.refs_0_, ...), custom_call_target="tpu_custom_call", output_to_operand_aliasing={{0}: (3, {}), {1}: (4, {})} | custom-call | flops 805306368 | bytes 1572864 | tf_op jit(solution)/shard_map/pallas_call | solution.py:312
  42.1 0.0 collective-permute-done.10.refs_3_
  42.2 0.9 %collective-permute-start.13 = (bf16[512,256]{1,0:T(8,128)(2,1)S(1)}, bf16[512,256]{1,0:T(8,128)(2,1)S(1)}, u32[]{:S(2)}, u32[]{:S(2)}) collective-permute-start(bf16[512,256]{1,0:T(8,128)(2,1)S(1)} %collective-permute-done.10.refs_3_), channel_id=1, source_target_pairs={{0,1},{1,0},{2,3},{3,2},{4,5},{5,4},{6,7},{7,6},{8,9},{9,8},{10,11... | collective-permute-start | bytes 786440 | tf_op jit(solution)/shard_map/ppermute | solution.py:338
  43.0 2.4 %shard_map.79 = (f32[2,4,384,256]{3,2,1,0:T(8,128)S(1)}, f32[2,4,384,128]{3,2,1,0:T(8,128)S(1)}) custom-call(s32[16]{0:T(128)S(1)} %get-tuple-element.61.table_ref, f32[12]{0:T(128)S(1)} %get-tuple-element.62.factor_ref, bf16[8,64,768]{2,1,0:T(8,128)(2,1)S(1)} %get-tuple-element.71.refs_0_, ...), custom_call_target="tpu_custom_call", output_to_operand_aliasing={{0}: (3, {}), {1}: (4, {})} | custom-call | flops 201326592 | bytes 1572864 | tf_op jit(solution)/shard_map/pallas_call | solution.py:312
  45.4 0.0 collective-permute-done.13.refs_3_
  45.4 2.6 %shard_map.80 = (bf16[64,768]{1,0:T(8,128)(2,1)S(1)}, bf16[64,768]{1,0:T(8,128)(2,1)S(1)}, bf16[64,768]{1,0:T(8,128)(2,1)S(1)}, bf16[64,768]{1,0:T(8,128)(2,1)S(...) custom-call(s32[16]{0:T(128)S(1)} %get-tuple-element.61.table_ref, ...), custom_call_target="tpu_custom_call", output_to_operand_aliasing={{8}: (3, {}), {9}: (4, {})} | custom-call | flops 201326592 | bytes 1572864 | tf_op jit(solution)/shard_map/pallas_call | solution.py:312
  48.0 0.1 collective-permute-start.14
  48.1 2.3 %collective-permute-start.15 = (bf16[64,768]{1,0:T(8,128)(2,1)S(1)}, bf16[64,768]{1,0:T(8,128)(2,1)S(1)}, u32[]{:S(2)}, u32[]{:S(2)}) collective-permute-start(bf16[64,768]{1,0:T(8,128)(2,1)S(1)} %get-tuple-element.91), channel_id=1, source_target_pairs={{0,6},{1,7},{2,4},{3,5},{4,2},{5,3},{6,0},{7,1},{8,14},{9,15},{10,... | collective-permute-start | bytes 294920 | tf_op jit(solution)/shard_map/ppermute | solution.py:331
  50.3 0.8 %collective-permute-start.16 = (bf16[64,768]{1,0:T(8,128)(2,1)S(1)}, bf16[64,768]{1,0:T(8,128)(2,1)S(1)}, u32[]{:S(2)}, u32[]{:S(2)}) collective-permute-start(bf16[64,768]{1,0:T(8,128)(2,1)S(1)} %get-tuple-element.92), channel_id=1, source_target_pairs={{0,7},{1,6},{2,5},{3,4},{4,3},{5,2},{6,1},{7,0},{8,15},{9,14},{10,... | collective-permute-start | bytes 294920 | tf_op jit(solution)/shard_map/ppermute | solution.py:331
  51.1 1.3 %collective-permute-start.17 = (bf16[64,768]{1,0:T(8,128)(2,1)S(1)}, bf16[64,768]{1,0:T(8,128)(2,1)S(1)}, u32[]{:S(2)}, u32[]{:S(2)}) collective-permute-start(bf16[64,768]{1,0:T(8,128)(2,1)S(1)} %get-tuple-element.93), channel_id=1, source_target_pairs={{0,4},{1,3},{2,6},{3,1},{4,0},{5,7},{6,2},{7,5},{8,12},{9,11},{10,... | collective-permute-start | bytes 294920 | tf_op jit(solution)/shard_map/ppermute | solution.py:331
  52.4 1.2 %collective-permute-start.18 = (bf16[64,768]{1,0:T(8,128)(2,1)S(1)}, bf16[64,768]{1,0:T(8,128)(2,1)S(1)}, u32[]{:S(2)}, u32[]{:S(2)}) collective-permute-start(bf16[64,768]{1,0:T(8,128)(2,1)S(1)} %get-tuple-element.94), channel_id=1, source_target_pairs={{0,2},{1,5},{2,0},{3,7},{4,6},{5,1},{6,4},{7,3},{8,10},{9,13},{10,... | collective-permute-start | bytes 294920 | tf_op jit(solution)/shard_map/ppermute | solution.py:331
  53.6 0.0 collective-permute-done.14.refs_1_
  53.6 0.5 collective-permute-start.19
  54.1 0.0 collective-permute-done.15.refs_2_
  54.1 1.7 %collective-permute-start.20 = (bf16[64,768]{1,0:T(8,128)(2,1)S(1)}, bf16[64,768]{1,0:T(8,128)(2,1)S(1)}, u32[]{:S(2)}, u32[]{:S(2)}) collective-permute-start(bf16[64,768]{1,0:T(8,128)(2,1)S(1)} %get-tuple-element.96), channel_id=1, source_target_pairs={{0,3},{1,4},{2,1},{3,6},{4,7},{5,0},{6,5},{7,2},{8,11},{9,12},{10,... | collective-permute-start | bytes 294920 | tf_op jit(solution)/shard_map/ppermute | solution.py:331
  55.7 0.9 %collective-permute-done.16.refs_3_ = bf16[64,768]{1,0:T(8,128)(2,1)S(1)} collective-permute-done((bf16[64,768]{1,0:T(8,128)(2,1)S(1)}, bf16[64,768]{1,0:T(8,128)(2,1)S(1)}, u32[]{:S(2)}, u32[]{:S(2)}) %collective-permute-start.16) | collective-permute-done | bytes 98336 | tf_op jit(solution)/shard_map/ppermute | solution.py:331
  56.7 0.6 collective-permute-done.17.refs_4_
  57.2 0.6 collective-permute-done.18.refs_5_
  57.8 2.2 %collective-permute-done.19.refs_6_ = bf16[64,768]{1,0:T(8,128)(2,1)S(1)} collective-permute-done((bf16[64,768]{1,0:T(8,128)(2,1)S(1)}, bf16[64,768]{1,0:T(8,128)(2,1)S(1)}, u32[]{:S(2)}, u32[]{:S(2)}) %collective-permute-start.19) | collective-permute-done | bytes 98336 | tf_op jit(solution)/shard_map/ppermute | solution.py:331
  60.0 0.0 collective-permute-done.20.refs_7_
  60.0 0.9 %shard_map.81 = bf16[128,3072]{1,0:T(8,128)(2,1)} custom-call(bf16[64,768]{1,0:T(8,128)(2,1)S(1)} %get-tuple-element.89.refs_0_, bf16[64,768]{1,0:T(8,128)(2,1)S(1)} %collective-permute-done.14.refs_1_, bf16[64,768]{1,0:T(8,128)(2,1)S(1)} %collective-permute-done.15.refs_2_, bf16[64,768]{1,0:T(8,128)(2,1)S(1)} %collective-permute-done.16.refs_3_, ...), custom_call_target="tpu_custom_call" | custom-call | tf_op jit(solution)/shard_map/pallas_call | solution.py:168
  (1 shorter events, 0.0 us)
Async XLA Ops:
  2.3 5.8 %collective-permute-start = (bf16[64,1024]{1,0:T(8,128)(2,1)}, bf16[64,1024]{1,0:T(8,128)(2,1)S(1)}, u32[]{:S(2)}, u32[]{:S(2)}) collective-permute-start(bf16[64,1024]{1,0:T(8,128)(2,1)} %get-tuple-element.51), channel_id=1, source_target_pairs={{0,1},{1,0},{2,3},{3,2},{4,5},{5,4},{6,7},{7,6},{8,9},{9,8},{10,11... | collective-permute-start | bytes 393224 | tf_op jit(solution)/shard_map/ppermute | solution.py:331
  3.1 6.2 %collective-permute-start.1 = (bf16[64,1024]{1,0:T(8,128)(2,1)}, bf16[64,1024]{1,0:T(8,128)(2,1)S(1)}, u32[]{:S(2)}, u32[]{:S(2)}) collective-permute-start(bf16[64,1024]{1,0:T(8,128)(2,1)} %get-tuple-element.52), channel_id=1, source_target_pairs={{0,6},{1,7},{2,4},{3,5},{4,2},{5,3},{6,0},{7,1},{8,14},{9,15},{10,... | collective-permute-start | bytes 393224 | tf_op jit(solution)/shard_map/ppermute | solution.py:331
  5.2 11.6 %collective-permute-start.2 = (bf16[64,1024]{1,0:T(8,128)(2,1)}, bf16[64,1024]{1,0:T(8,128)(2,1)S(1)}, u32[]{:S(2)}, u32[]{:S(2)}) collective-permute-start(bf16[64,1024]{1,0:T(8,128)(2,1)} %get-tuple-element.53), channel_id=1, source_target_pairs={{0,7},{1,6},{2,5},{3,4},{4,3},{5,2},{6,1},{7,0},{8,15},{9,14},{10,... | collective-permute-start | bytes 393224 | tf_op jit(solution)/shard_map/ppermute | solution.py:331
  5.7 11.2 %collective-permute-start.3 = (bf16[64,1024]{1,0:T(8,128)(2,1)}, bf16[64,1024]{1,0:T(8,128)(2,1)S(1)}, u32[]{:S(2)}, u32[]{:S(2)}) collective-permute-start(bf16[64,1024]{1,0:T(8,128)(2,1)} %get-tuple-element.54), channel_id=1, source_target_pairs={{0,4},{1,3},{2,6},{3,1},{4,0},{5,7},{6,2},{7,5},{8,12},{9,11},{10,... | collective-permute-start | bytes 393224 | tf_op jit(solution)/shard_map/ppermute | solution.py:331
  6.9 10.0 %collective-permute-start.4 = (bf16[64,1024]{1,0:T(8,128)(2,1)}, bf16[64,1024]{1,0:T(8,128)(2,1)S(1)}, u32[]{:S(2)}, u32[]{:S(2)}) collective-permute-start(bf16[64,1024]{1,0:T(8,128)(2,1)} %get-tuple-element.55), channel_id=1, source_target_pairs={{0,2},{1,5},{2,0},{3,7},{4,6},{5,1},{6,4},{7,3},{8,10},{9,13},{10,... | collective-permute-start | bytes 393224 | tf_op jit(solution)/shard_map/ppermute | solution.py:331
  8.1 9.9 %collective-permute-start.5 = (bf16[64,1024]{1,0:T(8,128)(2,1)}, bf16[64,1024]{1,0:T(8,128)(2,1)S(1)}, u32[]{:S(2)}, u32[]{:S(2)}) collective-permute-start(bf16[64,1024]{1,0:T(8,128)(2,1)} %get-tuple-element.56), channel_id=1, source_target_pairs={{0,5},{1,2},{2,7},{3,0},{4,1},{5,6},{6,3},{7,4},{8,13},{9,10},{10,... | collective-permute-start | bytes 393224 | tf_op jit(solution)/shard_map/ppermute | solution.py:331
  9.2 8.8 %collective-permute-start.6 = (bf16[64,1024]{1,0:T(8,128)(2,1)}, bf16[64,1024]{1,0:T(8,128)(2,1)S(1)}, u32[]{:S(2)}, u32[]{:S(2)}) collective-permute-start(bf16[64,1024]{1,0:T(8,128)(2,1)} %get-tuple-element.57), channel_id=1, source_target_pairs={{0,3},{1,4},{2,1},{3,6},{4,7},{5,0},{6,5},{7,2},{8,11},{9,12},{10,... | collective-permute-start | bytes 393224 | tf_op jit(solution)/shard_map/ppermute | solution.py:331
  11.7 0.9 %copy-start = (bf16[64,1024]{1,0:T(8,128)(2,1)S(1)}, bf16[64,1024]{1,0:T(8,128)(2,1)}, u32[]{:S(2)}) copy-start(bf16[64,1024]{1,0:T(8,128)(2,1)} %get-tuple-element.58.piece_ref) | copy-start | bytes 393220
  12.7 0.7 %copy-start.1 = (f32[8,24]{1,0:T(8,128)S(1)}, f32[8,24]{1,0:T(8,128)}, u32[]{:S(2)}) copy-start(f32[8,24]{1,0:T(8,128)} %temps_ref.1) | copy-start | bytes 2308
  13.3 0.7 %copy-start.2 = (s32[8,4]{0,1:T(4,128)S(1)}, s32[8,4]{0,1:T(4,128)}, u32[]{:S(2)}) copy-start(s32[8,4]{0,1:T(4,128)} %param.12) | copy-start | bytes 388
  14.0 0.7 %copy-start.3 = (s32[8]{0:T(128)S(1)}, s32[8]{0:T(128)}, u32[]{:S(2)}) copy-start(s32[8]{0:T(128)} %levels_ref.1) | copy-start | bytes 100
  14.7 0.7 %copy-start.4 = (s32[8]{0:T(128)S(1)}, s32[8]{0:T(128)}, u32[]{:S(2)}) copy-start(s32[8]{0:T(128)} %counts_ref.1) | copy-start | bytes 100
  18.1 3.7 %collective-permute-start.9 = (bf16[512,256]{1,0:T(8,128)(2,1)S(1)}, bf16[512,256]{1,0:T(8,128)(2,1)S(1)}, u32[]{:S(2)}, u32[]{:S(2)}) collective-permute-start(bf16[512,256]{1,0:T(8,128)(2,1)S(1)} %get-tuple-element.72.refs_1_), channel_id=1, source_target_pairs={{0,1},{1,0},{2,3},{3,2},{4,5},{5,4},{6,7},{7,6},{8,9},{9,8},{10,11... | collective-permute-start | bytes 786440 | tf_op jit(solution)/shard_map/ppermute | solution.py:338
  18.6 9.6 %collective-permute-start.8 = (bf16[512,256]{1,0:T(8,128)(2,1)S(1)}, bf16[512,256]{1,0:T(8,128)(2,1)S(1)}, u32[]{:S(2)}, u32[]{:S(2)}) collective-permute-start(bf16[512,256]{1,0:T(8,128)(2,1)S(1)} %get-tuple-element.72.refs_1_), channel_id=1, source_target_pairs={{0,24},{4,28},{8,0},{12,4},{16,8},{20,12},{24,16},{28,20},{1,25},{... | collective-permute-start | bytes 786440 | tf_op jit(solution)/shard_map/ppermute | solution.py:335
  18.7 13.1 %collective-permute-start.7 = (bf16[512,256]{1,0:T(8,128)(2,1)S(1)}, bf16[512,256]{1,0:T(8,128)(2,1)S(1)}, u32[]{:S(2)}, u32[]{:S(2)}) collective-permute-start(bf16[512,256]{1,0:T(8,128)(2,1)S(1)} %get-tuple-element.72.refs_1_), channel_id=1, source_target_pairs={{0,8},{4,12},{8,16},{12,20},{16,24},{20,28},{24,0},{28,4},{1,9},{5... | collective-permute-start | bytes 786440 | tf_op jit(solution)/shard_map/ppermute | solution.py:335
  31.8 3.1 %collective-permute-start.12 = (bf16[512,256]{1,0:T(8,128)(2,1)S(1)}, bf16[512,256]{1,0:T(8,128)(2,1)S(1)}, u32[]{:S(2)}, u32[]{:S(2)}) collective-permute-start(bf16[512,256]{1,0:T(8,128)(2,1)S(1)} %collective-permute-done.8.refs_5_), channel_id=1, source_target_pairs={{0,1},{1,0},{2,3},{3,2},{4,5},{5,4},{6,7},{7,6},{8,9},{9,8},{10,11... | collective-permute-start | bytes 786440 | tf_op jit(solution)/shard_map/ppermute | solution.py:338
  33.1 1.8 %collective-permute-start.11 = (bf16[512,256]{1,0:T(8,128)(2,1)S(1)}, bf16[512,256]{1,0:T(8,128)(2,1)S(1)}, u32[]{:S(2)}, u32[]{:S(2)}) collective-permute-start(bf16[512,256]{1,0:T(8,128)(2,1)S(1)} %collective-permute-done.7.refs_3_), channel_id=1, source_target_pairs={{0,1},{1,0},{2,3},{3,2},{4,5},{5,4},{6,7},{7,6},{8,9},{9,8},{10,11... | collective-permute-start | bytes 786440 | tf_op jit(solution)/shard_map/ppermute | solution.py:338
  33.1 9.1 %collective-permute-start.10 = (bf16[512,256]{1,0:T(8,128)(2,1)S(1)}, bf16[512,256]{1,0:T(8,128)(2,1)S(1)}, u32[]{:S(2)}, u32[]{:S(2)}) collective-permute-start(bf16[512,256]{1,0:T(8,128)(2,1)S(1)} %collective-permute-done.7.refs_3_), channel_id=1, source_target_pairs={{0,8},{4,12},{8,16},{12,20},{16,24},{20,28},{24,0},{28,4},{1,9},{5... | collective-permute-start | bytes 786440 | tf_op jit(solution)/shard_map/ppermute | solution.py:335
  42.2 3.2 %collective-permute-start.13 = (bf16[512,256]{1,0:T(8,128)(2,1)S(1)}, bf16[512,256]{1,0:T(8,128)(2,1)S(1)}, u32[]{:S(2)}, u32[]{:S(2)}) collective-permute-start(bf16[512,256]{1,0:T(8,128)(2,1)S(1)} %collective-permute-done.10.refs_3_), channel_id=1, source_target_pairs={{0,1},{1,0},{2,3},{3,2},{4,5},{5,4},{6,7},{7,6},{8,9},{9,8},{10,11... | collective-permute-start | bytes 786440 | tf_op jit(solution)/shard_map/ppermute | solution.py:338
  48.0 5.6 %collective-permute-start.14 = (bf16[64,768]{1,0:T(8,128)(2,1)S(1)}, bf16[64,768]{1,0:T(8,128)(2,1)S(1)}, u32[]{:S(2)}, u32[]{:S(2)}) collective-permute-start(bf16[64,768]{1,0:T(8,128)(2,1)S(1)} %get-tuple-element.90), channel_id=1, source_target_pairs={{0,1},{1,0},{2,3},{3,2},{4,5},{5,4},{6,7},{7,6},{8,9},{9,8},{10,11... | collective-permute-start | bytes 294920 | tf_op jit(solution)/shard_map/ppermute | solution.py:331
  48.1 6.0 %collective-permute-start.15 = (bf16[64,768]{1,0:T(8,128)(2,1)S(1)}, bf16[64,768]{1,0:T(8,128)(2,1)S(1)}, u32[]{:S(2)}, u32[]{:S(2)}) collective-permute-start(bf16[64,768]{1,0:T(8,128)(2,1)S(1)} %get-tuple-element.91), channel_id=1, source_target_pairs={{0,6},{1,7},{2,4},{3,5},{4,2},{5,3},{6,0},{7,1},{8,14},{9,15},{10,... | collective-permute-start | bytes 294920 | tf_op jit(solution)/shard_map/ppermute | solution.py:331
  50.3 6.3 %collective-permute-start.16 = (bf16[64,768]{1,0:T(8,128)(2,1)S(1)}, bf16[64,768]{1,0:T(8,128)(2,1)S(1)}, u32[]{:S(2)}, u32[]{:S(2)}) collective-permute-start(bf16[64,768]{1,0:T(8,128)(2,1)S(1)} %get-tuple-element.92), channel_id=1, source_target_pairs={{0,7},{1,6},{2,5},{3,4},{4,3},{5,2},{6,1},{7,0},{8,15},{9,14},{10,... | collective-permute-start | bytes 294920 | tf_op jit(solution)/shard_map/ppermute | solution.py:331
  51.1 6.1 %collective-permute-start.17 = (bf16[64,768]{1,0:T(8,128)(2,1)S(1)}, bf16[64,768]{1,0:T(8,128)(2,1)S(1)}, u32[]{:S(2)}, u32[]{:S(2)}) collective-permute-start(bf16[64,768]{1,0:T(8,128)(2,1)S(1)} %get-tuple-element.93), channel_id=1, source_target_pairs={{0,4},{1,3},{2,6},{3,1},{4,0},{5,7},{6,2},{7,5},{8,12},{9,11},{10,... | collective-permute-start | bytes 294920 | tf_op jit(solution)/shard_map/ppermute | solution.py:331
  52.4 5.4 %collective-permute-start.18 = (bf16[64,768]{1,0:T(8,128)(2,1)S(1)}, bf16[64,768]{1,0:T(8,128)(2,1)S(1)}, u32[]{:S(2)}, u32[]{:S(2)}) collective-permute-start(bf16[64,768]{1,0:T(8,128)(2,1)S(1)} %get-tuple-element.94), channel_id=1, source_target_pairs={{0,2},{1,5},{2,0},{3,7},{4,6},{5,1},{6,4},{7,3},{8,10},{9,13},{10,... | collective-permute-start | bytes 294920 | tf_op jit(solution)/shard_map/ppermute | solution.py:331
  53.6 6.4 %collective-permute-start.19 = (bf16[64,768]{1,0:T(8,128)(2,1)S(1)}, bf16[64,768]{1,0:T(8,128)(2,1)S(1)}, u32[]{:S(2)}, u32[]{:S(2)}) collective-permute-start(bf16[64,768]{1,0:T(8,128)(2,1)S(1)} %get-tuple-element.95), channel_id=1, source_target_pairs={{0,5},{1,2},{2,7},{3,0},{4,1},{5,6},{6,3},{7,4},{8,13},{9,10},{10,... | collective-permute-start | bytes 294920 | tf_op jit(solution)/shard_map/ppermute | solution.py:331
  54.1 5.9 %collective-permute-start.20 = (bf16[64,768]{1,0:T(8,128)(2,1)S(1)}, bf16[64,768]{1,0:T(8,128)(2,1)S(1)}, u32[]{:S(2)}, u32[]{:S(2)}) collective-permute-start(bf16[64,768]{1,0:T(8,128)(2,1)S(1)} %get-tuple-element.96), channel_id=1, source_target_pairs={{0,3},{1,4},{2,1},{3,6},{4,7},{5,0},{6,5},{7,2},{8,11},{9,12},{10,... | collective-permute-start | bytes 294920 | tf_op jit(solution)/shard_map/ppermute | solution.py:331

commit v5 on v4

--- a/solution.py
+++ b/solution.py
@@ -13,7 +13,7 @@
 HD = 128
 GROUP = HQ // KVH
 WIDE = GROUP * HD
-PEERS = 8
+PEERS = 4
 LOW = -1e30
 SCALE = math.log2(math.e) / math.sqrt(HD)
 SMEM = pl.BlockSpec(memory_space=pltpu.SMEM)
@@ -23,29 +23,21 @@
 LARGE = pltpu.CompilerParams(vmem_limit_bytes=16 << 20)
 
 
-STEPS = ((0, 0), (1, 1), (6, 6), (7, 7), (4, 2), (2, 4), (5, 3), (3, 5))
-
-
-def sent_to(number, step):
-    even, odd = STEPS[step]
-    return number ^ jnp.where(number & 1 == 0, even, odd)
-
-
-def got_from(number, step):
-    even, odd = STEPS[step]
-    if even & 1:
-        even, odd = odd, even
-    return number ^ jnp.where(number & 1 == 0, even, odd)
+STEPS = ((0, 0), (3, 3), (2, 1), (1, 2))
 
 
 def place():
     span, tok = lax.axis_index("span"), lax.axis_index("ctx")
-    return span & -2, 4 * (span & 1) + tok
+    return span & -2, 2 * (span & 1) + (tok >> 1), tok & 1
+
+
+def peer_of(chip, core, step):
+    even, odd = STEPS[step]
+    return chip ^ jnp.where(core == 0, even, odd)
 
 
 def table_kernel(planes, levels_ref, temps_ref, list_ref, counts_ref, table_ref, factor_ref):
-    base, number = place()
-    head = number >> 1
+    base, head, _ = place()
     for side in range(2):
         level = levels_ref[base + side]
         for i in range(GROUP):
@@ -77,18 +69,16 @@
     loads.append(pltpu.make_async_copy(q_ref, q_source, sems.at[2]))
     for load in loads:
         load.start()
-    number = place()[1]
+    _, chip, core = place()
     for load in loads:
         load.wait()
-    part = target.shape[1]
     stores = []
     for step in [*range(1, PEERS), 0]:
-        peer = sent_to(number, step)
-        rows = pl.ds(pl.multiple_of((peer & 1) * part, part), part)
-        lanes = pl.ds(pl.multiple_of((peer >> 1) * HD, HD), HD)
-        target[step, :, :HD] = source[0, rows, lanes]
-        target[step, :, HD : 2 * HD] = source[1, rows, lanes]
-        target[step, :, 2 * HD :] = q_source[rows, pl.ds(pl.multiple_of((peer >> 1) * WIDE, HD), WIDE)]
+        peer = peer_of(chip, core, step)
+        lanes = pl.ds(pl.multiple_of(peer * HD, HD), HD)
+        target[step, :, :HD] = source[0, :, lanes]
+        target[step, :, HD : 2 * HD] = source[1, :, lanes]
+        target[step, :, 2 * HD :] = q_source[:, pl.ds(pl.multiple_of(peer * WIDE, HD), WIDE)]
         stores.append(pltpu.make_async_copy(target.at[step], pieces[step], sems.at[step]))
         stores[-1].start()
     for store in stores:
@@ -96,7 +86,7 @@
 
 
 def begin(keys, values, queries):
-    shape = (keys.shape[0] // 2, 2 * HD + WIDE)
+    shape = (keys.shape[0], 2 * HD + WIDE)
     return pl.pallas_call(
         begin_kernel,
         out_shape=[jax.ShapeDtypeStruct(shape, jnp.bfloat16)] * PEERS,
@@ -127,10 +117,10 @@
 
 def gather_kernel(*refs):
     pieces, slab_ref, q_ref = refs[:PEERS], refs[PEERS], refs[PEERS + 1]
-    number = place()[1]
+    _, chip, core = place()
     part = pieces[0].shape[0]
     for step, piece in enumerate(pieces):
-        peer = got_from(number, step)
+        peer = peer_of(chip, core, step)
         slab_ref[pl.ds(pl.multiple_of(peer * part, part), part), :] = piece[:, : 2 * HD]
         q_ref[peer] = piece[:, 2 * HD :]
 
@@ -151,14 +141,11 @@
 
 def join_kernel(*refs):
     pieces, out_ref, sems = refs[:PEERS], refs[PEERS], refs[PEERS + 1]
-    number = place()[1]
-    part = out_ref.shape[0] // 2
+    _, chip, core = place()
     copies = []
     for step, piece in enumerate(pieces):
-        peer = got_from(number, step)
-        rows = pl.ds(pl.multiple_of((peer & 1) * part, part), part)
-        lanes = pl.ds(pl.multiple_of((peer >> 1) * WIDE, HD), WIDE)
-        copies.append(pltpu.make_async_copy(piece, out_ref.at[rows, lanes], sems.at[step]))
+        lanes = pl.ds(pl.multiple_of(peer_of(chip, core, step) * WIDE, HD), WIDE)
+        copies.append(pltpu.make_async_copy(piece, out_ref.at[:, lanes], sems.at[step]))
         copies[-1].start()
     for copy in copies:
         copy.wait()
@@ -167,7 +154,7 @@
 def join(pieces):
     return pl.pallas_call(
         join_kernel,
-        out_shape=jax.ShapeDtypeStruct((2 * pieces[0].shape[0], HQ * HD), jnp.bfloat16),
+        out_shape=jax.ShapeDtypeStruct((pieces[0].shape[0], HQ * HD), jnp.bfloat16),
         in_specs=[VMEM] * PEERS,
         out_specs=HBM,
         scratch_shapes=[pltpu.SemaphoreType.DMA((PEERS,))],
@@ -183,8 +170,8 @@
     slabs = [[refs.pop(0) for _ in range(sides)] for _ in backs]
     out_refs = [refs.pop(0) for _ in range(PEERS)] if final else None
     sums_ref, top_ref = refs.pop(0), refs.pop(0)
-    number = place()[1]
-    core = (number & 1) ^ far_side
+    _, chip, this_core = place()
+    core = this_core ^ far_side
     if first:
         sums_ref[...] = jnp.zeros_like(sums_ref)
         top_ref[...] = jnp.full_like(top_ref, LOW)
@@ -194,38 +181,31 @@
     group = GROUP // 2
     chains = [(block, g) for block in range(2) for g in range(2)]
 
-    block_rows = 2 * piece
+    block_rows = half // 2
     index = lax.broadcasted_iota(jnp.int32, (block_rows, HD), 0)
-    own_part = index < piece
-    if sides == 2:
-        token = 2 * block_rows + index + jnp.where(own_part, core * piece, -(core * piece))
-    else:
-        token = 2 * block_rows + index + jnp.where(own_part, core * piece, (core + 1) * piece)
     for slab, back in zip(slabs, backs):
         for x in range(2):
             count = jnp.maximum(table_ref[4 * back + 2 * x], table_ref[4 * back + 2 * x + 1])
             at = x * half
             spare = slab[0][at : at + 16, :HD].astype(jnp.float32)[0:1]
-            parts = [ref[at : at + block_rows, :] for ref in slab]
-            if sides == 2:
-                for n in range(2, 4):
-                    low = at + n * piece
-                    parts.append(jnp.concatenate([ref[low : low + piece, :] for ref in slab], axis=0))
-            else:
-                parts.append(slab[0][at + block_rows : at + 2 * block_rows, :])
-            for n, values in enumerate(parts):
-                to = slice(n * block_rows, (n + 1) * block_rows)
-                keys = values[:, :HD].astype(jnp.float32)
-                values = values[:, HD:]
-                ones = jnp.ones_like(values)
-                if n >= sides:
-                    keep = token + (n - sides) * block_rows < count
-                    keys = jnp.where(keep, keys, spare)
-                    values = jnp.where(keep, values.astype(jnp.float32), 0.0).astype(jnp.bfloat16)
-                    ones = jnp.where(keep, 1.0, 0.0).astype(jnp.bfloat16)
-                key_ref[x, :, to] = jnp.transpose(keys).astype(jnp.bfloat16)
-                value_ref[x, to, :HD] = values
-                value_ref[x, to, HD:] = ones
+            for side, ref in enumerate(slab):
+                owner = core ^ side
+                for n in range(2):
+                    values = ref[at + n * block_rows : at + (n + 1) * block_rows, :]
+                    keys = values[:, :HD].astype(jnp.float32)
+                    values = values[:, HD:]
+                    ones = jnp.ones_like(values)
+                    to = side * block_rows
+                    if n:
+                        keep = (2 + owner) * block_rows + index < count
+                        keys = jnp.where(keep, keys, spare)
+                        values = jnp.where(keep, values.astype(jnp.float32), 0.0).astype(jnp.bfloat16)
+                        ones = jnp.where(keep, 1.0, 0.0).astype(jnp.bfloat16)
+                        to = block_rows if sides == 1 else (2 + owner) * block_rows
+                    to = pl.ds(pl.multiple_of(to, block_rows), block_rows)
+                    key_ref[x, :, to] = jnp.transpose(keys).astype(jnp.bfloat16)
+                    value_ref[x, to, :HD] = values
+                    value_ref[x, to, HD:] = ones
 
         @pl.loop(0, 4)
         def _(turn):
@@ -242,8 +222,7 @@
                     rows = []
                     for i in range(group):
                         lanes = slice((g * group + i) * HD, (g * group + i + 1) * HD)
-                        for t in range(2):
-                            rows.append(q_ref[4 * side + 2 * block + t, :, lanes])
+                        rows.append(q_ref[2 * side + block, :, lanes])
                     return jnp.dot(jnp.concatenate(rows, axis=0), keys, preferred_element_type=jnp.float32)
 
                 ready = scores(*chains[0])
@@ -286,17 +265,15 @@
                 result = (sums[:, :HD] / sums[:, HD:]).astype(jnp.bfloat16)
                 for i in range(group):
                     lanes = slice((g * group + i) * HD, (g * group + i + 1) * HD)
-                    for t in range(2):
-                        at = (2 * i + t) * piece
-                        done_ref[4 * side + 2 * block + t, :, lanes] = result[at : at + piece]
+                    done_ref[2 * side + block, :, lanes] = result[i * piece : (i + 1) * piece]
         for step, out_ref in enumerate(out_refs):
-            out_ref[...] = done_ref[sent_to(number, step)]
+            out_ref[...] = done_ref[peer_of(chip, this_core, step)]
 
 
 def attend(tables, q, state, slabs, backs, final, far_side=False):
     first = state is None
     piece = q.shape[1]
-    tall = GROUP * piece
+    tall = GROUP * piece // 2
     tokens = slabs[0][0].shape[0] * len(slabs[0]) // 2
     out_shape = [
         jax.ShapeDtypeStruct((2, 4, tall, 2 * HD), jnp.float32),
@@ -328,7 +305,8 @@
     def exchange(pieces):
         moved = [pieces[0]]
         for piece, step in zip(pieces[1:], STEPS[1:]):
-            moved.append(lax.ppermute(piece, ("span", "ctx"), [(f, f ^ step[f % 2]) for f in range(spans * ctx)]))
+            pairs = [(f, f ^ (2 * step[f % 2])) for f in range(spans * ctx)]
+            moved.append(lax.ppermute(piece, ("span", "ctx"), pairs))
         return moved
 
     def up(a, steps):

time: 62.2 us -> 61.6 us (level)
  the two profiles are of different devices: /device:TPU:25 before, /device:TPU:0 now
where the time goes in v5:
time: 61.6 us; the launch traced here: 61.3 us
  waiting for transfers between devices  31.1 us (50%)
  starting transfers between devices  14 us (23%)
  Pallas kernels  12.5 us (20%)
  local copies, waits for them, and re-layouts  3.62 us (6%)
    ppermute x3, waiting for transfers between devices, up(): lax.ppermute(a, 'span', [(s, (s + 2 * steps) % spans) for s in range(span...  15.2 us
    ppermute x6, waiting for transfers between devices, exchange(): moved.append(lax.ppermute(piece, ('span', 'ctx'), pairs))  15.2 us
    ppermute x6, starting transfers between devices, exchange(): moved.append(lax.ppermute(piece, ('span', 'ctx'), pairs))  8.15 us
    pallas_call x4, Pallas kernels, attend(): pl.pallas_call(functools.partial(attend_kernel, backs, len(slabs[0]), far...  7.64 us
    ppermute x3, starting transfers between devices, up(): lax.ppermute(a, 'span', [(s, (s + 2 * steps) % spans) for s in range(span...  5.28 us
    unnamed x10, local copies, waits for them, and re-layouts  3.62 us
    pallas_call x1, Pallas kernels, begin(): pl.pallas_call(begin_kernel, out_shape=[jax.ShapeDtypeStruct(shape, jnp.b...  2.29 us
    pallas_call x1, Pallas kernels, tabulate(): pl.pallas_call(functools.partial(table_kernel, planes), out_shape=[jax.Sh...  1.52 us
  transfers between devices with their start and end apart: 13, of which 8 were waited for; matrix products, arithmetic and copies ran while one was open for 0% of the time, Pallas kernels for 13%

profile of v5, /device:TPU:0, one launch (start us, length us, event | category | flops | bytes accessed | tf_op | source)
XLA Modules:
  0.0 61.3 jit_solution(7745223721114354591)
XLA Ops:
  0.0 2.3 %shard_map.73 = (bf16[128,1024]{1,0:T(8,128)(2,1)}, bf16[128,1024]{1,0:T(8,128)(2,1)}, bf16[128,1024]{1,0:T(8,128)(2,1)}, bf16[128,1024]{1,0:T(8,128)(2,1)}) custom-call(bf16[128,512]{1,0:T(8,128)(2,1)} %keys_ref.1, bf16[128,512]{1,0:T(8,128)(2,1)} %values_ref.1, bf16[128,3072]{1,0:T(8,128)(2,1)} %q_ref.1), custom_call_target="tpu_custom_call" | custom-call | tf_op jit(solution)/shard_map/pallas_call | solution.py:90
  2.3 4.0 %collective-permute-start = (bf16[128,1024]{1,0:T(8,128)(2,1)}, bf16[128,1024]{1,0:T(8,128)(2,1)S(1)}, u32[]{:S(2)}, u32[]{:S(2)}) collective-permute-start(bf16[128,1024]{1,0:T(8,128)(2,1)} %get-tuple-element.39), channel_id=1, source_target_pairs={{0,6},{1,7},{2,4},{3,5},{4,2},{5,3},{6,0},{7,1},{8,14},{9,15},{10,... | collective-permute-start | bytes 786440 | tf_op jit(solution)/shard_map/ppermute | solution.py:309
  6.3 0.5 collective-permute-start.1
  6.8 0.1 collective-permute-start.2
  6.9 0.0 copy-start
  6.9 0.9 %copy-done = bf16[128,1024]{1,0:T(8,128)(2,1)S(1)} copy-done((bf16[128,1024]{1,0:T(8,128)(2,1)S(1)}, bf16[128,1024]{1,0:T(8,128)(2,1)}, u32[]{:S(2)}) %copy-start) | copy-done | bytes 262168
  7.9 0.0 copy-start.1
  7.9 0.7 %copy-done.1 = f32[8,24]{1,0:T(8,128)S(1)} copy-done((f32[8,24]{1,0:T(8,128)S(1)}, f32[8,24]{1,0:T(8,128)}, u32[]{:S(2)}) %copy-start.1) | copy-done | bytes 792
  8.6 0.0 copy-start.2
  8.6 0.7 %copy-done.2 = s32[8,4]{0,1:T(4,128)S(1)} copy-done((s32[8,4]{0,1:T(4,128)S(1)}, s32[8,4]{0,1:T(4,128)}, u32[]{:S(2)}) %copy-start.2) | copy-done | bytes 152
  9.2 0.0 copy-start.3
  9.3 0.7 %copy-done.3 = s32[8]{0:T(128)S(1)} copy-done((s32[8]{0:T(128)S(1)}, s32[8]{0:T(128)}, u32[]{:S(2)}) %copy-start.3) | copy-done | bytes 56
  9.9 0.0 copy-start.4
  9.9 0.7 %copy-done.4 = s32[8]{0:T(128)S(1)} copy-done((s32[8]{0:T(128)S(1)}, s32[8]{0:T(128)}, u32[]{:S(2)}) %copy-start.4) | copy-done | bytes 56
  10.6 1.5 %shard_map.75 = (s32[16]{0:T(128)S(1)}, f32[12]{0:T(128)S(1)}) custom-call(s32[8]{0:T(128)S(1)} %copy-done.3, f32[8,24]{1,0:T(8,128)S(1)} %copy-done.1, s32[4,8]{1,0:T(4,128)S(1)} %bitcast.1, s32[8]{0:T(128)S(1)} %copy-done.4), custom_call_target="tpu_custom_call" | custom-call | tf_op jit(solution)/shard_map/pallas_call | solution.py:57
  12.1 1.6 %collective-permute-done.refs_1_ = bf16[128,1024]{1,0:T(8,128)(2,1)S(1)} collective-permute-done((bf16[128,1024]{1,0:T(8,128)(2,1)}, bf16[128,1024]{1,0:T(8,128)(2,1)S(1)}, u32[]{:S(2)}, u32[]{:S(2)}) %collective-permute-start) | collective-permute-done | bytes 262176 | tf_op jit(solution)/shard_map/ppermute | solution.py:309
  13.7 5.0 %collective-permute-done.1.refs_2_ = bf16[128,1024]{1,0:T(8,128)(2,1)S(1)} collective-permute-done((bf16[128,1024]{1,0:T(8,128)(2,1)}, bf16[128,1024]{1,0:T(8,128)(2,1)S(1)}, u32[]{:S(2)}, u32[]{:S(2)}) %collective-permute-start.1) | collective-permute-done | bytes 262176 | tf_op jit(solution)/shard_map/ppermute | solution.py:309
  18.7 0.0 collective-permute-done.2.refs_3_
  18.7 0.1 shard_map.76
  18.8 0.1 collective-permute-start.5
  18.9 3.7 %collective-permute-start.4 = (bf16[512,256]{1,0:T(8,128)(2,1)S(1)}, bf16[512,256]{1,0:T(8,128)(2,1)S(1)}, u32[]{:S(2)}, u32[]{:S(2)}) collective-permute-start(bf16[512,256]{1,0:T(8,128)(2,1)S(1)} %get-tuple-element.52.refs_1_), channel_id=1, source_target_pairs={{0,24},{4,28},{8,0},{12,4},{16,8},{20,12},{24,16},{28,20},{1,25},{... | collective-permute-start | bytes 786440 | tf_op jit(solution)/shard_map/ppermute | solution.py:313
  22.5 0.0 collective-permute-start.3
  22.5 0.0 collective-permute-done.5.refs_2_
  22.5 4.8 %shard_map.77 = (f32[2,4,384,256]{3,2,1,0:T(8,128)S(1)}, f32[2,4,384,128]{3,2,1,0:T(8,128)S(1)}) custom-call(s32[16]{0:T(128)S(1)} %get-tuple-element.45.table_ref, f32[12]{0:T(128)S(1)} %get-tuple-element.46.factor_ref, bf16[4,128,768]{2,1,0:T(8,128)(2,1)S(1)} %get-tuple-element.51.refs_0_, bf16[512,256]{1,0:T(8,128)(2,1)S(1)} %get-tuple-element.52.refs_1_, ...), custom_call_target="tpu_custom_call" | custom-call | flops 201326592 | bytes 1572864 | tf_op jit(solution)/shard_map/pallas_call | solution.py:289
  27.3 1.9 %collective-permute-done.4.refs_5_ = bf16[512,256]{1,0:T(8,128)(2,1)S(1)} collective-permute-done((bf16[512,256]{1,0:T(8,128)(2,1)S(1)}, bf16[512,256]{1,0:T(8,128)(2,1)S(1)}, u32[]{:S(2)}, u32[]{:S(2)}) %collective-permute-start.4) | collective-permute-done | bytes 262176 | tf_op jit(solution)/shard_map/ppermute | solution.py:313
  29.2 6.0 %collective-permute-done.3.refs_3_ = bf16[512,256]{1,0:T(8,128)(2,1)S(1)} collective-permute-done((bf16[512,256]{1,0:T(8,128)(2,1)S(1)}, bf16[512,256]{1,0:T(8,128)(2,1)S(1)}, u32[]{:S(2)}, u32[]{:S(2)}) %collective-permute-start.3) | collective-permute-done | bytes 262176 | tf_op jit(solution)/shard_map/ppermute | solution.py:313
  35.2 0.0 collective-permute-start.8
  35.2 0.5 collective-permute-start.7
  35.7 1.6 %collective-permute-start.6 = (bf16[512,256]{1,0:T(8,128)(2,1)S(1)}, bf16[512,256]{1,0:T(8,128)(2,1)S(1)}, u32[]{:S(2)}, u32[]{:S(2)}) collective-permute-start(bf16[512,256]{1,0:T(8,128)(2,1)S(1)} %collective-permute-done.3.refs_3_), channel_id=1, source_target_pairs={{0,8},{4,12},{8,16},{12,20},{16,24},{20,28},{24,0},{28,4},{1,9},{5... | collective-permute-start | bytes 786440 | tf_op jit(solution)/shard_map/ppermute | solution.py:313
  37.3 0.0 collective-permute-done.8.refs_6_
  37.3 0.0 collective-permute-done.7.refs_4_
  37.4 1.1 %shard_map.78 = (f32[2,4,384,256]{3,2,1,0:T(8,128)S(1)}, f32[2,4,384,128]{3,2,1,0:T(8,128)S(1)}) custom-call(s32[16]{0:T(128)S(1)} %get-tuple-element.45.table_ref, f32[12]{0:T(128)S(1)} %get-tuple-element.46.factor_ref, bf16[4,128,768]{2,1,0:T(8,128)(2,1)S(1)} %get-tuple-element.51.refs_0_, ...), custom_call_target="tpu_custom_call", output_to_operand_aliasing={{0}: (3, {}), {1}: (4, {})} | custom-call | flops 402653184 | bytes 1572864 | tf_op jit(solution)/shard_map/pallas_call | solution.py:289
  38.5 7.3 %collective-permute-done.6.refs_3_ = bf16[512,256]{1,0:T(8,128)(2,1)S(1)} collective-permute-done((bf16[512,256]{1,0:T(8,128)(2,1)S(1)}, bf16[512,256]{1,0:T(8,128)(2,1)S(1)}, u32[]{:S(2)}, u32[]{:S(2)}) %collective-permute-start.6) | collective-permute-done | bytes 262176 | tf_op jit(solution)/shard_map/ppermute | solution.py:313
  45.7 0.0 collective-permute-start.9
  45.7 0.7 %shard_map.79 = (f32[2,4,384,256]{3,2,1,0:T(8,128)S(1)}, f32[2,4,384,128]{3,2,1,0:T(8,128)S(1)}) custom-call(s32[16]{0:T(128)S(1)} %get-tuple-element.45.table_ref, f32[12]{0:T(128)S(1)} %get-tuple-element.46.factor_ref, bf16[4,128,768]{2,1,0:T(8,128)(2,1)S(1)} %get-tuple-element.51.refs_0_, ...), custom_call_target="tpu_custom_call", output_to_operand_aliasing={{0}: (3, {}), {1}: (4, {})} | custom-call | flops 100663296 | bytes 1572864 | tf_op jit(solution)/shard_map/pallas_call | solution.py:289
  46.5 0.8 %collective-permute-done.9.refs_3_ = bf16[512,256]{1,0:T(8,128)(2,1)S(1)} collective-permute-done((bf16[512,256]{1,0:T(8,128)(2,1)S(1)}, bf16[512,256]{1,0:T(8,128)(2,1)S(1)}, u32[]{:S(2)}, u32[]{:S(2)}) %collective-permute-start.9) | collective-permute-done | bytes 262176 | tf_op jit(solution)/shard_map/ppermute | solution.py:316
  47.3 1.0 %shard_map.80 = (bf16[128,768]{1,0:T(8,128)(2,1)S(1)}, bf16[128,768]{1,0:T(8,128)(2,1)S(1)}, bf16[128,768]{1,0:T(8,128)(2,1)S(1)}, bf16[128,768]{1,0:T(8,128)(2,...) custom-call(s32[16]{0:T(128)S(1)} %get-tuple-element.45.table_ref, ...), custom_call_target="tpu_custom_call", output_to_operand_aliasing={{4}: (3, {}), {5}: (4, {})} | custom-call | flops 100663296 | bytes 1572864 | tf_op jit(solution)/shard_map/pallas_call | solution.py:289
  48.3 1.7 %collective-permute-start.10 = (bf16[128,768]{1,0:T(8,128)(2,1)S(1)}, bf16[128,768]{1,0:T(8,128)(2,1)S(1)}, u32[]{:S(2)}, u32[]{:S(2)}) collective-permute-start(bf16[128,768]{1,0:T(8,128)(2,1)S(1)} %get-tuple-element.70), channel_id=1, source_target_pairs={{0,6},{1,7},{2,4},{3,5},{4,2},{5,3},{6,0},{7,1},{8,14},{9,15},{10,... | collective-permute-start | bytes 589832 | tf_op jit(solution)/shard_map/ppermute | solution.py:309
  50.0 1.2 %collective-permute-start.11 = (bf16[128,768]{1,0:T(8,128)(2,1)S(1)}, bf16[128,768]{1,0:T(8,128)(2,1)S(1)}, u32[]{:S(2)}, u32[]{:S(2)}) collective-permute-start(bf16[128,768]{1,0:T(8,128)(2,1)S(1)} %get-tuple-element.71), channel_id=1, source_target_pairs={{0,4},{1,3},{2,6},{3,1},{4,0},{5,7},{6,2},{7,5},{8,12},{9,11},{10,... | collective-permute-start | bytes 589832 | tf_op jit(solution)/shard_map/ppermute | solution.py:309
  51.3 0.6 collective-permute-start.12
  51.9 5.2 %collective-permute-done.10.refs_1_ = bf16[128,768]{1,0:T(8,128)(2,1)S(1)} collective-permute-done((bf16[128,768]{1,0:T(8,128)(2,1)S(1)}, bf16[128,768]{1,0:T(8,128)(2,1)S(1)}, u32[]{:S(2)}, u32[]{:S(2)}) %collective-permute-start.10) | collective-permute-done | bytes 196640 | tf_op jit(solution)/shard_map/ppermute | solution.py:309
  57.1 3.4 %collective-permute-done.11.refs_2_ = bf16[128,768]{1,0:T(8,128)(2,1)S(1)} collective-permute-done((bf16[128,768]{1,0:T(8,128)(2,1)S(1)}, bf16[128,768]{1,0:T(8,128)(2,1)S(1)}, u32[]{:S(2)}, u32[]{:S(2)}) %collective-permute-start.11) | collective-permute-done | bytes 196640 | tf_op jit(solution)/shard_map/ppermute | solution.py:309
  60.4 0.0 collective-permute-done.12.refs_3_
  60.4 0.9 %shard_map.81 = bf16[128,3072]{1,0:T(8,128)(2,1)} custom-call(bf16[128,768]{1,0:T(8,128)(2,1)S(1)} %get-tuple-element.69.refs_0_, bf16[128,768]{1,0:T(8,128)(2,1)S(1)} %collective-permute-done.10.refs_1_, bf16[128,768]{1,0:T(8,128)(2,1)S(1)} %collective-permute-done.11.refs_2_, bf16[128,768]{1,0:T(8,128)(2,1)S(1)} %collective-permute-done.12.refs_3_), custom_call_target="tpu_custom_call" | custom-call | tf_op jit(solution)/shard_map/pallas_call | solution.py:155
  (1 shorter events, 0.0 us)
Async XLA Ops:
  2.3 11.3 %collective-permute-start = (bf16[128,1024]{1,0:T(8,128)(2,1)}, bf16[128,1024]{1,0:T(8,128)(2,1)S(1)}, u32[]{:S(2)}, u32[]{:S(2)}) collective-permute-start(bf16[128,1024]{1,0:T(8,128)(2,1)} %get-tuple-element.39), channel_id=1, source_target_pairs={{0,6},{1,7},{2,4},{3,5},{4,2},{5,3},{6,0},{7,1},{8,14},{9,15},{10,... | collective-permute-start | bytes 786440 | tf_op jit(solution)/shard_map/ppermute | solution.py:309
  6.3 12.4 %collective-permute-start.1 = (bf16[128,1024]{1,0:T(8,128)(2,1)}, bf16[128,1024]{1,0:T(8,128)(2,1)S(1)}, u32[]{:S(2)}, u32[]{:S(2)}) collective-permute-start(bf16[128,1024]{1,0:T(8,128)(2,1)} %get-tuple-element.40), channel_id=1, source_target_pairs={{0,4},{1,3},{2,6},{3,1},{4,0},{5,7},{6,2},{7,5},{8,12},{9,11},{10,... | collective-permute-start | bytes 786440 | tf_op jit(solution)/shard_map/ppermute | solution.py:309
  6.8 11.9 %collective-permute-start.2 = (bf16[128,1024]{1,0:T(8,128)(2,1)}, bf16[128,1024]{1,0:T(8,128)(2,1)S(1)}, u32[]{:S(2)}, u32[]{:S(2)}) collective-permute-start(bf16[128,1024]{1,0:T(8,128)(2,1)} %get-tuple-element.41), channel_id=1, source_target_pairs={{0,2},{1,5},{2,0},{3,7},{4,6},{5,1},{6,4},{7,3},{8,10},{9,13},{10,... | collective-permute-start | bytes 786440 | tf_op jit(solution)/shard_map/ppermute | solution.py:309
  6.9 0.9 %copy-start = (bf16[128,1024]{1,0:T(8,128)(2,1)S(1)}, bf16[128,1024]{1,0:T(8,128)(2,1)}, u32[]{:S(2)}) copy-start(bf16[128,1024]{1,0:T(8,128)(2,1)} %get-tuple-element.42.piece_ref) | copy-start | bytes 786436
  7.9 0.7 %copy-start.1 = (f32[8,24]{1,0:T(8,128)S(1)}, f32[8,24]{1,0:T(8,128)}, u32[]{:S(2)}) copy-start(f32[8,24]{1,0:T(8,128)} %temps_ref.1) | copy-start | bytes 2308
  8.6 0.7 %copy-start.2 = (s32[8,4]{0,1:T(4,128)S(1)}, s32[8,4]{0,1:T(4,128)}, u32[]{:S(2)}) copy-start(s32[8,4]{0,1:T(4,128)} %param.12) | copy-start | bytes 388
  9.2 0.7 %copy-start.3 = (s32[8]{0:T(128)S(1)}, s32[8]{0:T(128)}, u32[]{:S(2)}) copy-start(s32[8]{0:T(128)} %levels_ref.1) | copy-start | bytes 100
  9.9 0.7 %copy-start.4 = (s32[8]{0:T(128)S(1)}, s32[8]{0:T(128)}, u32[]{:S(2)}) copy-start(s32[8]{0:T(128)} %counts_ref.1) | copy-start | bytes 100
  18.8 3.7 %collective-permute-start.5 = (bf16[512,256]{1,0:T(8,128)(2,1)S(1)}, bf16[512,256]{1,0:T(8,128)(2,1)S(1)}, u32[]{:S(2)}, u32[]{:S(2)}) collective-permute-start(bf16[512,256]{1,0:T(8,128)(2,1)S(1)} %get-tuple-element.52.refs_1_), channel_id=1, source_target_pairs={{0,1},{1,0},{2,3},{3,2},{4,5},{5,4},{6,7},{7,6},{8,9},{9,8},{10,11... | collective-permute-start | bytes 786440 | tf_op jit(solution)/shard_map/ppermute | solution.py:316
  18.9 10.3 %collective-permute-start.4 = (bf16[512,256]{1,0:T(8,128)(2,1)S(1)}, bf16[512,256]{1,0:T(8,128)(2,1)S(1)}, u32[]{:S(2)}, u32[]{:S(2)}) collective-permute-start(bf16[512,256]{1,0:T(8,128)(2,1)S(1)} %get-tuple-element.52.refs_1_), channel_id=1, source_target_pairs={{0,24},{4,28},{8,0},{12,4},{16,8},{20,12},{24,16},{28,20},{1,25},{... | collective-permute-start | bytes 786440 | tf_op jit(solution)/shard_map/ppermute | solution.py:313
  22.5 12.7 %collective-permute-start.3 = (bf16[512,256]{1,0:T(8,128)(2,1)S(1)}, bf16[512,256]{1,0:T(8,128)(2,1)S(1)}, u32[]{:S(2)}, u32[]{:S(2)}) collective-permute-start(bf16[512,256]{1,0:T(8,128)(2,1)S(1)} %get-tuple-element.52.refs_1_), channel_id=1, source_target_pairs={{0,8},{4,12},{8,16},{12,20},{16,24},{20,28},{24,0},{28,4},{1,9},{5... | collective-permute-start | bytes 786440 | tf_op jit(solution)/shard_map/ppermute | solution.py:313
  35.2 2.1 %collective-permute-start.8 = (bf16[512,256]{1,0:T(8,128)(2,1)S(1)}, bf16[512,256]{1,0:T(8,128)(2,1)S(1)}, u32[]{:S(2)}, u32[]{:S(2)}) collective-permute-start(bf16[512,256]{1,0:T(8,128)(2,1)S(1)} %collective-permute-done.4.refs_5_), channel_id=1, source_target_pairs={{0,1},{1,0},{2,3},{3,2},{4,5},{5,4},{6,7},{7,6},{8,9},{9,8},{10,11... | collective-permute-start | bytes 786440 | tf_op jit(solution)/shard_map/ppermute | solution.py:316
  35.2 2.1 %collective-permute-start.7 = (bf16[512,256]{1,0:T(8,128)(2,1)S(1)}, bf16[512,256]{1,0:T(8,128)(2,1)S(1)}, u32[]{:S(2)}, u32[]{:S(2)}) collective-permute-start(bf16[512,256]{1,0:T(8,128)(2,1)S(1)} %collective-permute-done.3.refs_3_), channel_id=1, source_target_pairs={{0,1},{1,0},{2,3},{3,2},{4,5},{5,4},{6,7},{7,6},{8,9},{9,8},{10,11... | collective-permute-start | bytes 786440 | tf_op jit(solution)/shard_map/ppermute | solution.py:316
  35.7 10.0 %collective-permute-start.6 = (bf16[512,256]{1,0:T(8,128)(2,1)S(1)}, bf16[512,256]{1,0:T(8,128)(2,1)S(1)}, u32[]{:S(2)}, u32[]{:S(2)}) collective-permute-start(bf16[512,256]{1,0:T(8,128)(2,1)S(1)} %collective-permute-done.3.refs_3_), channel_id=1, source_target_pairs={{0,8},{4,12},{8,16},{12,20},{16,24},{20,28},{24,0},{28,4},{1,9},{5... | collective-permute-start | bytes 786440 | tf_op jit(solution)/shard_map/ppermute | solution.py:313
  45.7 1.5 %collective-permute-start.9 = (bf16[512,256]{1,0:T(8,128)(2,1)S(1)}, bf16[512,256]{1,0:T(8,128)(2,1)S(1)}, u32[]{:S(2)}, u32[]{:S(2)}) collective-permute-start(bf16[512,256]{1,0:T(8,128)(2,1)S(1)} %collective-permute-done.6.refs_3_), channel_id=1, source_target_pairs={{0,1},{1,0},{2,3},{3,2},{4,5},{5,4},{6,7},{7,6},{8,9},{9,8},{10,11... | collective-permute-start | bytes 786440 | tf_op jit(solution)/shard_map/ppermute | solution.py:316
  48.3 8.8 %collective-permute-start.10 = (bf16[128,768]{1,0:T(8,128)(2,1)S(1)}, bf16[128,768]{1,0:T(8,128)(2,1)S(1)}, u32[]{:S(2)}, u32[]{:S(2)}) collective-permute-start(bf16[128,768]{1,0:T(8,128)(2,1)S(1)} %get-tuple-element.70), channel_id=1, source_target_pairs={{0,6},{1,7},{2,4},{3,5},{4,2},{5,3},{6,0},{7,1},{8,14},{9,15},{10,... | collective-permute-start | bytes 589832 | tf_op jit(solution)/shard_map/ppermute | solution.py:309
  50.0 10.4 %collective-permute-start.11 = (bf16[128,768]{1,0:T(8,128)(2,1)S(1)}, bf16[128,768]{1,0:T(8,128)(2,1)S(1)}, u32[]{:S(2)}, u32[]{:S(2)}) collective-permute-start(bf16[128,768]{1,0:T(8,128)(2,1)S(1)} %get-tuple-element.71), channel_id=1, source_target_pairs={{0,4},{1,3},{2,6},{3,1},{4,0},{5,7},{6,2},{7,5},{8,12},{9,11},{10,... | collective-permute-start | bytes 589832 | tf_op jit(solution)/shard_map/ppermute | solution.py:309
  51.3 9.2 %collective-permute-start.12 = (bf16[128,768]{1,0:T(8,128)(2,1)S(1)}, bf16[128,768]{1,0:T(8,128)(2,1)S(1)}, u32[]{:S(2)}, u32[]{:S(2)}) collective-permute-start(bf16[128,768]{1,0:T(8,128)(2,1)S(1)} %get-tuple-element.72), channel_id=1, source_target_pairs={{0,2},{1,5},{2,0},{3,7},{4,6},{5,1},{6,4},{7,3},{8,10},{9,13},{10,... | collective-permute-start | bytes 589832 | tf_op jit(solution)/shard_map/ppermute | solution.py:309

commit v6 on v5

--- a/solution.py
+++ b/solution.py
@@ -141,11 +141,11 @@
 
 def join_kernel(*refs):
     pieces, out_ref, sems = refs[:PEERS], refs[PEERS], refs[PEERS + 1]
-    _, chip, core = place()
+    _, chip, _ = place()
     copies = []
-    for step, piece in enumerate(pieces):
-        lanes = pl.ds(pl.multiple_of(peer_of(chip, core, step) * WIDE, HD), WIDE)
-        copies.append(pltpu.make_async_copy(piece, out_ref.at[:, lanes], sems.at[step]))
+    for flip, piece in enumerate(pieces):
+        lanes = pl.ds(pl.multiple_of((chip ^ flip) * WIDE, HD), WIDE)
+        copies.append(pltpu.make_async_copy(piece, out_ref.at[:, lanes], sems.at[flip]))
         copies[-1].start()
     for copy in copies:
         copy.wait()
@@ -162,16 +162,16 @@
     )(*pieces)
 
 
-def attend_kernel(backs, sides, far_side, first, final, table_ref, factor_ref, *refs):
+def attend_kernel(backs, first, final, table_ref, factor_ref, *refs):
     refs = list(refs)
     q_ref = refs.pop(0)
     if not first:
         del refs[:2]
-    slabs = [[refs.pop(0) for _ in range(sides)] for _ in backs]
-    out_refs = [refs.pop(0) for _ in range(PEERS)] if final else None
+    slabs = [(refs.pop(0), refs.pop(0)) for _ in backs]
+    out_refs = [refs.pop(0) for _ in range(2)] if final else None
     sums_ref, top_ref = refs.pop(0), refs.pop(0)
-    _, chip, this_core = place()
-    core = this_core ^ far_side
+    _, chip, core = place()
+    the_side = (chip >> 1) ^ (final == 1)
     if first:
         sums_ref[...] = jnp.zeros_like(sums_ref)
         top_ref[...] = jnp.full_like(top_ref, LOW)
@@ -201,18 +201,17 @@
                         keys = jnp.where(keep, keys, spare)
                         values = jnp.where(keep, values.astype(jnp.float32), 0.0).astype(jnp.bfloat16)
                         ones = jnp.where(keep, 1.0, 0.0).astype(jnp.bfloat16)
-                        to = block_rows if sides == 1 else (2 + owner) * block_rows
+                        to = (2 + owner) * block_rows
                     to = pl.ds(pl.multiple_of(to, block_rows), block_rows)
                     key_ref[x, :, to] = jnp.transpose(keys).astype(jnp.bfloat16)
                     value_ref[x, to, :HD] = values
                     value_ref[x, to, HD:] = ones
 
-        @pl.loop(0, 4)
+        @pl.loop(0, 2 if final else 4)
         def _(turn):
-            x = turn >> 1
-            side = turn & 1
-
-            count = table_ref[4 * back + turn]
+            x = turn if final else turn >> 1
+            side = the_side if final else turn & 1
+            count = table_ref[4 * back + 2 * x + side]
 
             def visit(width):
                 keys = key_ref[x, :, :width]
@@ -251,43 +250,40 @@
                     top_ref[side, chain] = top
 
             most = 3 * block_rows
-            if sides == 2:
-                pl.when((count > 0) & (count <= most))(lambda: visit(most))
-                pl.when(count > most)(lambda: visit(most + block_rows))
-            else:
-                pl.when(count > 0)(lambda: visit(2 * block_rows))
+            pl.when((count > 0) & (count <= most))(lambda: visit(most))
+            pl.when(count > most)(lambda: visit(most + block_rows))
 
     if final:
         done_ref = refs[2]
-        for side in range(2):
-            for block, g in chains:
-                sums = sums_ref[side, 2 * block + g]
-                result = (sums[:, :HD] / sums[:, HD:]).astype(jnp.bfloat16)
-                for i in range(group):
-                    lanes = slice((g * group + i) * HD, (g * group + i + 1) * HD)
-                    done_ref[2 * side + block, :, lanes] = result[i * piece : (i + 1) * piece]
-        for step, out_ref in enumerate(out_refs):
-            out_ref[...] = done_ref[peer_of(chip, this_core, step)]
-
-
-def attend(tables, q, state, slabs, backs, final, far_side=False):
+        for block, g in chains:
+            sums = sums_ref[the_side, 2 * block + g]
+            result = (sums[:, :HD] / sums[:, HD:]).astype(jnp.bfloat16)
+            for i in range(group):
+                lanes = slice((g * group + i) * HD, (g * group + i + 1) * HD)
+                done_ref[block, :, lanes] = result[i * piece : (i + 1) * piece]
+        for flip, out_ref in enumerate(out_refs):
+            out_ref[...] = done_ref[(chip & 1) ^ flip]
+
+
+def attend(tables, q, state, slabs, backs, final=0):
     first = state is None
     piece = q.shape[1]
     tall = GROUP * piece // 2
-    tokens = slabs[0][0].shape[0] * len(slabs[0]) // 2
+    tokens = slabs[0][0].shape[0]
     out_shape = [
         jax.ShapeDtypeStruct((2, 4, tall, 2 * HD), jnp.float32),
         jax.ShapeDtypeStruct((2, 4, tall, HD), jnp.float32),
     ]
     scratch = [pltpu.VMEM((2, HD, tokens), jnp.bfloat16), pltpu.VMEM((2, tokens, 2 * HD), jnp.bfloat16)]
     if final:
-        out_shape = [jax.ShapeDtypeStruct(q.shape[1:], jnp.bfloat16)] * PEERS + out_shape
-        scratch.append(pltpu.VMEM(q.shape, jnp.bfloat16))
+        out_shape = [jax.ShapeDtypeStruct(q.shape[1:], jnp.bfloat16)] * 2 + out_shape
+        scratch.append(pltpu.VMEM((2, *q.shape[1:]), jnp.bfloat16))
     work = len(backs) * PEERS * tall * tokens
     inputs = [q, *(state or ()), *[a for slab in slabs for a in slab]]
-    aliases = {} if first else {3: PEERS * final, 4: PEERS * final + 1}
-    return pl.pallas_call(
-        functools.partial(attend_kernel, backs, len(slabs[0]), far_side, first, final),
+    outs = len(out_shape) - 2
+    aliases = {} if first else {3: outs, 4: outs + 1}
+    return pl.pallas_call(
+        functools.partial(attend_kernel, backs, first, final),
         out_shape=out_shape,
         in_specs=[SMEM] * 2 + [VMEM] * len(inputs),
         out_specs=[VMEM] * len(out_shape),
@@ -302,12 +298,12 @@
     other_core = [(t, t ^ 1) for t in range(ctx)]
     last = spans // 2 - 1
 
+    def flip(piece, even, odd):
+        pairs = [(f, f ^ (2 * (odd if f % 2 else even))) for f in range(spans * ctx)]
+        return lax.ppermute(piece, ("span", "ctx"), pairs)
+
     def exchange(pieces):
-        moved = [pieces[0]]
-        for piece, step in zip(pieces[1:], STEPS[1:]):
-            pairs = [(f, f ^ (2 * step[f % 2])) for f in range(spans * ctx)]
-            moved.append(lax.ppermute(piece, ("span", "ctx"), pairs))
-        return moved
+        return [pieces[0]] + [flip(piece, *step) for piece, step in zip(pieces[1:], STEPS[1:])]
 
     def up(a, steps):
         return lax.ppermute(a, "span", [(s, (s + 2 * steps) % spans) for s in range(spans)])
@@ -320,21 +316,21 @@
     moved, mine, tables = lax.optimization_barrier((exchange(pieces)[1:], hold(pieces[0]), tables))
     own, q = gather([mine, *moved])
     slabs = {0: own, 1: up(own, 1), last: up(own, last)}
-    state = attend(tables, q, None, [(own, near(own))], [0], False)
+    state = attend(tables, q, None, [(own, near(own))], [0])
     slabs, state = lax.optimization_barrier((slabs, state))
     stage = [1, last]
     sides = [(slabs[b], near(slabs[b])) for b in stage]
     for back in range(2, last):
         slab = up(slabs[back - 1], 1)
-        state = attend(tables, q, state, sides, stage, False)
+        state = attend(tables, q, state, sides, stage)
         slabs[back], state = lax.optimization_barrier((slab, state))
         stage = [back]
         sides = [(slabs[back], near(slabs[back]))]
-    mine, other = sides[0]
-    state = attend(tables, q, state, [(mine,)], stage, False)
-    other, state = lax.optimization_barrier((other, state))
-    out = attend(tables, q, state, [(other,)], stage, True, True)
-    return join(exchange(out[:PEERS]))
+    beside, across, *state = attend(tables, q, state, sides, stage, 1)
+    across = flip(across, 3, 3)
+    mine, along, *_ = attend(tables, q, state, sides, stage, 2)
+    across, beside, mine, along = lax.optimization_barrier((across, beside, mine, along))
+    return join([mine, flip(along, 1, 1), flip(beside, 2, 2), across])
 
 
 def solution(mesh):

time: 61.6 us -> 64.7 us (1.050)
  waiting for transfers between devices: 31.1 us -> 33.6 us
    ppermute x6, waiting for transfers between devices: 15.2 us -> 16.9 us  [flip(): return lax.ppermute(piece, ('span', 'ctx'), pairs)]
    ppermute x4, waiting for transfers between devices: 0.81 us -> 1.54 us  [near(): return lax.ppermute(a, 'ctx', other_core)]
  transfers between devices with their start and end apart: 13 -> 13, of which waited for: 8 -> 9; matrix products, arithmetic and copies ran while one was open for 0% -> 0% of each run, Pallas kernels for 13% -> 13%
where the time goes in v6:
time: 64.7 us; the launch traced here: 64.5 us
  waiting for transfers between devices  33.6 us (52%)
  starting transfers between devices  14.4 us (22%)
  Pallas kernels  12.7 us (20%)
  local copies, waits for them, and re-layouts  3.62 us (6%)
    ppermute x6, waiting for transfers between devices, flip(): return lax.ppermute(piece, ('span', 'ctx'), pairs)  16.9 us
    ppermute x3, waiting for transfers between devices, up(): lax.ppermute(a, 'span', [(s, (s + 2 * steps) % spans) for s in range(span...  15.2 us
    ppermute x6, starting transfers between devices, flip(): return lax.ppermute(piece, ('span', 'ctx'), pairs)  8.52 us
    pallas_call x4, Pallas kernels, attend(): pl.pallas_call(functools.partial(attend_kernel, backs, first, final), out...  7.86 us
    ppermute x3, starting transfers between devices, up(): lax.ppermute(a, 'span', [(s, (s + 2 * steps) % spans) for s in range(span...  5.28 us
    unnamed x10, local copies, waits for them, and re-layouts  3.62 us
    pallas_call x1, Pallas kernels, begin(): pl.pallas_call(begin_kernel, out_shape=[jax.ShapeDtypeStruct(shape, jnp.b...  2.29 us
    ppermute x4, waiting for transfers between devices, near(): return lax.ppermute(a, 'ctx', other_core)  1.54 us
  transfers between devices with their start and end apart: 13, of which 9 were waited for; matrix products, arithmetic and copies ran while one was open for 0% of the time, Pallas kernels for 13%

profile of v6, /device:TPU:0, one launch (start us, length us, event | category | flops | bytes accessed | tf_op | source)
XLA Modules:
  0.0 64.5 jit_solution(17136329384071676617)
XLA Ops:
  0.0 2.3 %shard_map.73 = (bf16[128,1024]{1,0:T(8,128)(2,1)}, bf16[128,1024]{1,0:T(8,128)(2,1)}, bf16[128,1024]{1,0:T(8,128)(2,1)}, bf16[128,1024]{1,0:T(8,128)(2,1)}) custom-call(bf16[128,512]{1,0:T(8,128)(2,1)} %keys_ref.1, bf16[128,512]{1,0:T(8,128)(2,1)} %values_ref.1, bf16[128,3072]{1,0:T(8,128)(2,1)} %q_ref.1), custom_call_target="tpu_custom_call" | custom-call | tf_op jit(solution)/shard_map/pallas_call | solution.py:90
  2.3 4.0 %collective-permute-start = (bf16[128,1024]{1,0:T(8,128)(2,1)}, bf16[128,1024]{1,0:T(8,128)(2,1)S(1)}, u32[]{:S(2)}, u32[]{:S(2)}) collective-permute-start(bf16[128,1024]{1,0:T(8,128)(2,1)} %get-tuple-element.40), channel_id=1, source_target_pairs={{0,6},{1,7},{2,4},{3,5},{4,2},{5,3},{6,0},{7,1},{8,14},{9,15},{10,... | collective-permute-start | bytes 786440 | tf_op jit(solution)/shard_map/ppermute | solution.py:303
  6.3 0.5 collective-permute-start.1
  6.8 0.1 collective-permute-start.2
  6.9 0.0 copy-start
  6.9 0.9 %copy-done = bf16[128,1024]{1,0:T(8,128)(2,1)S(1)} copy-done((bf16[128,1024]{1,0:T(8,128)(2,1)S(1)}, bf16[128,1024]{1,0:T(8,128)(2,1)}, u32[]{:S(2)}) %copy-start) | copy-done | bytes 262168
  7.9 0.0 copy-start.1
  7.9 0.7 %copy-done.1 = f32[8,24]{1,0:T(8,128)S(1)} copy-done((f32[8,24]{1,0:T(8,128)S(1)}, f32[8,24]{1,0:T(8,128)}, u32[]{:S(2)}) %copy-start.1) | copy-done | bytes 792
  8.6 0.0 copy-start.2
  8.6 0.7 %copy-done.2 = s32[8,4]{0,1:T(4,128)S(1)} copy-done((s32[8,4]{0,1:T(4,128)S(1)}, s32[8,4]{0,1:T(4,128)}, u32[]{:S(2)}) %copy-start.2) | copy-done | bytes 152
  9.2 0.0 copy-start.3
  9.3 0.7 %copy-done.3 = s32[8]{0:T(128)S(1)} copy-done((s32[8]{0:T(128)S(1)}, s32[8]{0:T(128)}, u32[]{:S(2)}) %copy-start.3) | copy-done | bytes 56
  9.9 0.0 copy-start.4
  9.9 0.7 %copy-done.4 = s32[8]{0:T(128)S(1)} copy-done((s32[8]{0:T(128)S(1)}, s32[8]{0:T(128)}, u32[]{:S(2)}) %copy-start.4) | copy-done | bytes 56
  10.6 1.5 %shard_map.75 = (s32[16]{0:T(128)S(1)}, f32[12]{0:T(128)S(1)}) custom-call(s32[8]{0:T(128)S(1)} %copy-done.3, f32[8,24]{1,0:T(8,128)S(1)} %copy-done.1, s32[4,8]{1,0:T(4,128)S(1)} %bitcast.1, s32[8]{0:T(128)S(1)} %copy-done.4), custom_call_target="tpu_custom_call" | custom-call | tf_op jit(solution)/shard_map/pallas_call | solution.py:57
  12.1 1.6 %collective-permute-done.refs_1_ = bf16[128,1024]{1,0:T(8,128)(2,1)S(1)} collective-permute-done((bf16[128,1024]{1,0:T(8,128)(2,1)}, bf16[128,1024]{1,0:T(8,128)(2,1)S(1)}, u32[]{:S(2)}, u32[]{:S(2)}) %collective-permute-start) | collective-permute-done | bytes 262176 | tf_op jit(solution)/shard_map/ppermute | solution.py:303
  13.7 5.0 %collective-permute-done.1.refs_2_ = bf16[128,1024]{1,0:T(8,128)(2,1)S(1)} collective-permute-done((bf16[128,1024]{1,0:T(8,128)(2,1)}, bf16[128,1024]{1,0:T(8,128)(2,1)S(1)}, u32[]{:S(2)}, u32[]{:S(2)}) %collective-permute-start.1) | collective-permute-done | bytes 262176 | tf_op jit(solution)/shard_map/ppermute | solution.py:303
  18.7 0.0 collective-permute-done.2.refs_3_
  18.7 0.1 shard_map.76
  18.8 0.1 collective-permute-start.5
  18.9 3.7 %collective-permute-start.4 = (bf16[512,256]{1,0:T(8,128)(2,1)S(1)}, bf16[512,256]{1,0:T(8,128)(2,1)S(1)}, u32[]{:S(2)}, u32[]{:S(2)}) collective-permute-start(bf16[512,256]{1,0:T(8,128)(2,1)S(1)} %get-tuple-element.53.refs_1_), channel_id=1, source_target_pairs={{0,24},{4,28},{8,0},{12,4},{16,8},{20,12},{24,16},{28,20},{1,25},{... | collective-permute-start | bytes 786440 | tf_op jit(solution)/shard_map/ppermute | solution.py:309
  22.5 0.0 collective-permute-start.3
  22.5 0.0 collective-permute-done.5.refs_2_
  22.5 4.8 %shard_map.77 = (f32[2,4,384,256]{3,2,1,0:T(8,128)S(1)}, f32[2,4,384,128]{3,2,1,0:T(8,128)S(1)}) custom-call(s32[16]{0:T(128)S(1)} %get-tuple-element.46.table_ref, f32[12]{0:T(128)S(1)} %get-tuple-element.47.factor_ref, bf16[4,128,768]{2,1,0:T(8,128)(2,1)S(1)} %get-tuple-element.52.refs_0_, bf16[512,256]{1,0:T(8,128)(2,1)S(1)} %get-tuple-element.53.refs_1_, ...), custom_call_target="tpu_custom_call" | custom-call | flops 201326592 | bytes 1572864 | tf_op jit(solution)/shard_map/pallas_call | solution.py:285
  27.3 1.9 %collective-permute-done.4.refs_5_ = bf16[512,256]{1,0:T(8,128)(2,1)S(1)} collective-permute-done((bf16[512,256]{1,0:T(8,128)(2,1)S(1)}, bf16[512,256]{1,0:T(8,128)(2,1)S(1)}, u32[]{:S(2)}, u32[]{:S(2)}) %collective-permute-start.4) | collective-permute-done | bytes 262176 | tf_op jit(solution)/shard_map/ppermute | solution.py:309
  29.2 6.0 %collective-permute-done.3.refs_3_ = bf16[512,256]{1,0:T(8,128)(2,1)S(1)} collective-permute-done((bf16[512,256]{1,0:T(8,128)(2,1)S(1)}, bf16[512,256]{1,0:T(8,128)(2,1)S(1)}, u32[]{:S(2)}, u32[]{:S(2)}) %collective-permute-start.3) | collective-permute-done | bytes 262176 | tf_op jit(solution)/shard_map/ppermute | solution.py:309
  35.2 0.0 collective-permute-start.8
  35.2 0.5 collective-permute-start.7
  35.7 1.6 %collective-permute-start.6 = (bf16[512,256]{1,0:T(8,128)(2,1)S(1)}, bf16[512,256]{1,0:T(8,128)(2,1)S(1)}, u32[]{:S(2)}, u32[]{:S(2)}) collective-permute-start(bf16[512,256]{1,0:T(8,128)(2,1)S(1)} %collective-permute-done.3.refs_3_), channel_id=1, source_target_pairs={{0,8},{4,12},{8,16},{12,20},{16,24},{20,28},{24,0},{28,4},{1,9},{5... | collective-permute-start | bytes 786440 | tf_op jit(solution)/shard_map/ppermute | solution.py:309
  37.3 0.0 collective-permute-done.8.refs_6_
  37.3 0.0 collective-permute-done.7.refs_4_
  37.4 1.1 %shard_map.78 = (f32[2,4,384,256]{3,2,1,0:T(8,128)S(1)}, f32[2,4,384,128]{3,2,1,0:T(8,128)S(1)}) custom-call(s32[16]{0:T(128)S(1)} %get-tuple-element.46.table_ref, f32[12]{0:T(128)S(1)} %get-tuple-element.47.factor_ref, bf16[4,128,768]{2,1,0:T(8,128)(2,1)S(1)} %get-tuple-element.52.refs_0_, ...), custom_call_target="tpu_custom_call", output_to_operand_aliasing={{0}: (3, {}), {1}: (4, {})} | custom-call | flops 402653184 | bytes 1572864 | tf_op jit(solution)/shard_map/pallas_call | solution.py:285
  38.5 7.3 %collective-permute-done.6.refs_3_ = bf16[512,256]{1,0:T(8,128)(2,1)S(1)} collective-permute-done((bf16[512,256]{1,0:T(8,128)(2,1)S(1)}, bf16[512,256]{1,0:T(8,128)(2,1)S(1)}, u32[]{:S(2)}, u32[]{:S(2)}) %collective-permute-start.6) | collective-permute-done | bytes 262176 | tf_op jit(solution)/shard_map/ppermute | solution.py:309
  45.7 0.0 collective-permute-start.9
  45.7 1.5 %collective-permute-done.9.refs_4_ = bf16[512,256]{1,0:T(8,128)(2,1)S(1)} collective-permute-done((bf16[512,256]{1,0:T(8,128)(2,1)S(1)}, bf16[512,256]{1,0:T(8,128)(2,1)S(1)}, u32[]{:S(2)}, u32[]{:S(2)}) %collective-permute-start.9) | collective-permute-done | bytes 262176 | tf_op jit(solution)/shard_map/ppermute | solution.py:312
  47.3 1.0 %shard_map.79 = (bf16[128,768]{1,0:T(8,128)(2,1)S(1)}, bf16[128,768]{1,0:T(8,128)(2,1)S(1)}, f32[2,4,384,256]{3,2,1,0:T(8,128)S(1)}, f32[2,4,384,128]{3,2,1,0:T(8,128)S(1)}) custom-call(s32[16]{0:T(128)S(1)} %get-tuple-element.46.table_ref, f32[12]{0:T(128)S(1)} %get-tuple-element.47.factor_ref, ...), custom_call_target="tpu_custom_call", output_to_operand_aliasing={{2}: (3, {}), {3}: (4, {})} | custom-call | flops 201326592 | bytes 1572864 | tf_op jit(solution)/shard_map/pallas_call | solution.py:285
  48.3 1.7 %collective-permute-start.10 = (bf16[128,768]{1,0:T(8,128)(2,1)S(1)}, bf16[128,768]{1,0:T(8,128)(2,1)S(1)}, u32[]{:S(2)}, u32[]{:S(2)}) collective-permute-start(bf16[128,768]{1,0:T(8,128)(2,1)S(1)} %get-tuple-element.65), channel_id=1, source_target_pairs={{0,6},{1,7},{2,4},{3,5},{4,2},{5,3},{6,0},{7,1},{8,14},{9,15},{10,... | collective-permute-start | bytes 589832 | tf_op jit(solution)/shard_map/ppermute | solution.py:303
  50.0 1.0 %shard_map.80 = (bf16[128,768]{1,0:T(8,128)(2,1)S(1)}, bf16[128,768]{1,0:T(8,128)(2,1)S(1)}, f32[2,4,384,256]{3,2,1,0:T(8,128)S(1)}, f32[2,4,384,128]{3,2,1,0:T(8,128)S(1)}) custom-call(s32[16]{0:T(128)S(1)} %get-tuple-element.46.table_ref, f32[12]{0:T(128)S(1)} %get-tuple-element.47.factor_ref, ...), custom_call_target="tpu_custom_call", output_to_operand_aliasing={{2}: (3, {}), {3}: (4, {})} | custom-call | flops 201326592 | bytes 1572864 | tf_op jit(solution)/shard_map/pallas_call | solution.py:285
  50.9 5.2 %collective-permute-done.10.refs_3_ = bf16[128,768]{1,0:T(8,128)(2,1)S(1)} collective-permute-done((bf16[128,768]{1,0:T(8,128)(2,1)S(1)}, bf16[128,768]{1,0:T(8,128)(2,1)S(1)}, u32[]{:S(2)}, u32[]{:S(2)}) %collective-permute-start.10) | collective-permute-done | bytes 196640 | tf_op jit(solution)/shard_map/ppermute | solution.py:303
  56.2 1.4 %collective-permute-start.11 = (bf16[128,768]{1,0:T(8,128)(2,1)S(1)}, bf16[128,768]{1,0:T(8,128)(2,1)S(1)}, u32[]{:S(2)}, u32[]{:S(2)}) collective-permute-start(bf16[128,768]{1,0:T(8,128)(2,1)S(1)} %get-tuple-element.72), channel_id=1, source_target_pairs={{0,2},{1,3},{2,0},{3,1},{4,6},{5,7},{6,4},{7,5},{8,10},{9,11},{10,... | collective-permute-start | bytes 589832 | tf_op jit(solution)/shard_map/ppermute | solution.py:303
  57.6 0.8 %collective-permute-start.12 = (bf16[128,768]{1,0:T(8,128)(2,1)S(1)}, bf16[128,768]{1,0:T(8,128)(2,1)S(1)}, u32[]{:S(2)}, u32[]{:S(2)}) collective-permute-start(bf16[128,768]{1,0:T(8,128)(2,1)S(1)} %get-tuple-element.73), channel_id=1, source_target_pairs={{0,4},{1,5},{2,6},{3,7},{4,0},{5,1},{6,2},{7,3},{8,12},{9,13},{10,... | collective-permute-start | bytes 589832 | tf_op jit(solution)/shard_map/ppermute | solution.py:303
  58.4 3.9 %collective-permute-done.11.refs_1_ = bf16[128,768]{1,0:T(8,128)(2,1)S(1)} collective-permute-done((bf16[128,768]{1,0:T(8,128)(2,1)S(1)}, bf16[128,768]{1,0:T(8,128)(2,1)S(1)}, u32[]{:S(2)}, u32[]{:S(2)}) %collective-permute-start.11) | collective-permute-done | bytes 196640 | tf_op jit(solution)/shard_map/ppermute | solution.py:303
  62.3 1.1 %collective-permute-done.12.refs_2_ = bf16[128,768]{1,0:T(8,128)(2,1)S(1)} collective-permute-done((bf16[128,768]{1,0:T(8,128)(2,1)S(1)}, bf16[128,768]{1,0:T(8,128)(2,1)S(1)}, u32[]{:S(2)}, u32[]{:S(2)}) %collective-permute-start.12) | collective-permute-done | bytes 196640 | tf_op jit(solution)/shard_map/ppermute | solution.py:303
  63.4 0.9 %shard_map.81 = bf16[128,3072]{1,0:T(8,128)(2,1)} custom-call(bf16[128,768]{1,0:T(8,128)(2,1)S(1)} %get-tuple-element.71.refs_0_, bf16[128,768]{1,0:T(8,128)(2,1)S(1)} %collective-permute-done.11.refs_1_, bf16[128,768]{1,0:T(8,128)(2,1)S(1)} %collective-permute-done.12.refs_2_, bf16[128,768]{1,0:T(8,128)(2,1)S(1)} %collective-permute-done.10.refs_3_), custom_call_target="tpu_custom_call" | custom-call | tf_op jit(solution)/shard_map/pallas_call | solution.py:155
  (1 shorter events, 0.0 us)
Async XLA Ops:
  2.3 11.3 %collective-permute-start = (bf16[128,1024]{1,0:T(8,128)(2,1)}, bf16[128,1024]{1,0:T(8,128)(2,1)S(1)}, u32[]{:S(2)}, u32[]{:S(2)}) collective-permute-start(bf16[128,1024]{1,0:T(8,128)(2,1)} %get-tuple-element.40), channel_id=1, source_target_pairs={{0,6},{1,7},{2,4},{3,5},{4,2},{5,3},{6,0},{7,1},{8,14},{9,15},{10,... | collective-permute-start | bytes 786440 | tf_op jit(solution)/shard_map/ppermute | solution.py:303
  6.3 12.4 %collective-permute-start.1 = (bf16[128,1024]{1,0:T(8,128)(2,1)}, bf16[128,1024]{1,0:T(8,128)(2,1)S(1)}, u32[]{:S(2)}, u32[]{:S(2)}) collective-permute-start(bf16[128,1024]{1,0:T(8,128)(2,1)} %get-tuple-element.41), channel_id=1, source_target_pairs={{0,4},{1,3},{2,6},{3,1},{4,0},{5,7},{6,2},{7,5},{8,12},{9,11},{10,... | collective-permute-start | bytes 786440 | tf_op jit(solution)/shard_map/ppermute | solution.py:303
  6.8 11.9 %collective-permute-start.2 = (bf16[128,1024]{1,0:T(8,128)(2,1)}, bf16[128,1024]{1,0:T(8,128)(2,1)S(1)}, u32[]{:S(2)}, u32[]{:S(2)}) collective-permute-start(bf16[128,1024]{1,0:T(8,128)(2,1)} %get-tuple-element.42), channel_id=1, source_target_pairs={{0,2},{1,5},{2,0},{3,7},{4,6},{5,1},{6,4},{7,3},{8,10},{9,13},{10,... | collective-permute-start | bytes 786440 | tf_op jit(solution)/shard_map/ppermute | solution.py:303
  6.9 0.9 %copy-start = (bf16[128,1024]{1,0:T(8,128)(2,1)S(1)}, bf16[128,1024]{1,0:T(8,128)(2,1)}, u32[]{:S(2)}) copy-start(bf16[128,1024]{1,0:T(8,128)(2,1)} %get-tuple-element.43.piece_ref) | copy-start | bytes 786436
  7.9 0.7 %copy-start.1 = (f32[8,24]{1,0:T(8,128)S(1)}, f32[8,24]{1,0:T(8,128)}, u32[]{:S(2)}) copy-start(f32[8,24]{1,0:T(8,128)} %temps_ref.1) | copy-start | bytes 2308
  8.6 0.7 %copy-start.2 = (s32[8,4]{0,1:T(4,128)S(1)}, s32[8,4]{0,1:T(4,128)}, u32[]{:S(2)}) copy-start(s32[8,4]{0,1:T(4,128)} %param.12) | copy-start | bytes 388
  9.2 0.7 %copy-start.3 = (s32[8]{0:T(128)S(1)}, s32[8]{0:T(128)}, u32[]{:S(2)}) copy-start(s32[8]{0:T(128)} %levels_ref.1) | copy-start | bytes 100
  9.9 0.7 %copy-start.4 = (s32[8]{0:T(128)S(1)}, s32[8]{0:T(128)}, u32[]{:S(2)}) copy-start(s32[8]{0:T(128)} %counts_ref.1) | copy-start | bytes 100
  18.8 3.7 %collective-permute-start.5 = (bf16[512,256]{1,0:T(8,128)(2,1)S(1)}, bf16[512,256]{1,0:T(8,128)(2,1)S(1)}, u32[]{:S(2)}, u32[]{:S(2)}) collective-permute-start(bf16[512,256]{1,0:T(8,128)(2,1)S(1)} %get-tuple-element.53.refs_1_), channel_id=1, source_target_pairs={{0,1},{1,0},{2,3},{3,2},{4,5},{5,4},{6,7},{7,6},{8,9},{9,8},{10,11... | collective-permute-start | bytes 786440 | tf_op jit(solution)/shard_map/ppermute | solution.py:312
  18.9 10.3 %collective-permute-start.4 = (bf16[512,256]{1,0:T(8,128)(2,1)S(1)}, bf16[512,256]{1,0:T(8,128)(2,1)S(1)}, u32[]{:S(2)}, u32[]{:S(2)}) collective-permute-start(bf16[512,256]{1,0:T(8,128)(2,1)S(1)} %get-tuple-element.53.refs_1_), channel_id=1, source_target_pairs={{0,24},{4,28},{8,0},{12,4},{16,8},{20,12},{24,16},{28,20},{1,25},{... | collective-permute-start | bytes 786440 | tf_op jit(solution)/shard_map/ppermute | solution.py:309
  22.5 12.7 %collective-permute-start.3 = (bf16[512,256]{1,0:T(8,128)(2,1)S(1)}, bf16[512,256]{1,0:T(8,128)(2,1)S(1)}, u32[]{:S(2)}, u32[]{:S(2)}) collective-permute-start(bf16[512,256]{1,0:T(8,128)(2,1)S(1)} %get-tuple-element.53.refs_1_), channel_id=1, source_target_pairs={{0,8},{4,12},{8,16},{12,20},{16,24},{20,28},{24,0},{28,4},{1,9},{5... | collective-permute-start | bytes 786440 | tf_op jit(solution)/shard_map/ppermute | solution.py:309
  35.2 2.1 %collective-permute-start.8 = (bf16[512,256]{1,0:T(8,128)(2,1)S(1)}, bf16[512,256]{1,0:T(8,128)(2,1)S(1)}, u32[]{:S(2)}, u32[]{:S(2)}) collective-permute-start(bf16[512,256]{1,0:T(8,128)(2,1)S(1)} %collective-permute-done.4.refs_5_), channel_id=1, source_target_pairs={{0,1},{1,0},{2,3},{3,2},{4,5},{5,4},{6,7},{7,6},{8,9},{9,8},{10,11... | collective-permute-start | bytes 786440 | tf_op jit(solution)/shard_map/ppermute | solution.py:312
  35.2 2.1 %collective-permute-start.7 = (bf16[512,256]{1,0:T(8,128)(2,1)S(1)}, bf16[512,256]{1,0:T(8,128)(2,1)S(1)}, u32[]{:S(2)}, u32[]{:S(2)}) collective-permute-start(bf16[512,256]{1,0:T(8,128)(2,1)S(1)} %collective-permute-done.3.refs_3_), channel_id=1, source_target_pairs={{0,1},{1,0},{2,3},{3,2},{4,5},{5,4},{6,7},{7,6},{8,9},{9,8},{10,11... | collective-permute-start | bytes 786440 | tf_op jit(solution)/shard_map/ppermute | solution.py:312
  35.7 10.0 %collective-permute-start.6 = (bf16[512,256]{1,0:T(8,128)(2,1)S(1)}, bf16[512,256]{1,0:T(8,128)(2,1)S(1)}, u32[]{:S(2)}, u32[]{:S(2)}) collective-permute-start(bf16[512,256]{1,0:T(8,128)(2,1)S(1)} %collective-permute-done.3.refs_3_), channel_id=1, source_target_pairs={{0,8},{4,12},{8,16},{12,20},{16,24},{20,28},{24,0},{28,4},{1,9},{5... | collective-permute-start | bytes 786440 | tf_op jit(solution)/shard_map/ppermute | solution.py:309
  45.7 1.5 %collective-permute-start.9 = (bf16[512,256]{1,0:T(8,128)(2,1)S(1)}, bf16[512,256]{1,0:T(8,128)(2,1)S(1)}, u32[]{:S(2)}, u32[]{:S(2)}) collective-permute-start(bf16[512,256]{1,0:T(8,128)(2,1)S(1)} %collective-permute-done.6.refs_3_), channel_id=1, source_target_pairs={{0,1},{1,0},{2,3},{3,2},{4,5},{5,4},{6,7},{7,6},{8,9},{9,8},{10,11... | collective-permute-start | bytes 786440 | tf_op jit(solution)/shard_map/ppermute | solution.py:312
  48.3 7.9 %collective-permute-start.10 = (bf16[128,768]{1,0:T(8,128)(2,1)S(1)}, bf16[128,768]{1,0:T(8,128)(2,1)S(1)}, u32[]{:S(2)}, u32[]{:S(2)}) collective-permute-start(bf16[128,768]{1,0:T(8,128)(2,1)S(1)} %get-tuple-element.65), channel_id=1, source_target_pairs={{0,6},{1,7},{2,4},{3,5},{4,2},{5,3},{6,0},{7,1},{8,14},{9,15},{10,... | collective-permute-start | bytes 589832 | tf_op jit(solution)/shard_map/ppermute | solution.py:303
  56.2 6.1 %collective-permute-start.11 = (bf16[128,768]{1,0:T(8,128)(2,1)S(1)}, bf16[128,768]{1,0:T(8,128)(2,1)S(1)}, u32[]{:S(2)}, u32[]{:S(2)}) collective-permute-start(bf16[128,768]{1,0:T(8,128)(2,1)S(1)} %get-tuple-element.72), channel_id=1, source_target_pairs={{0,2},{1,3},{2,0},{3,1},{4,6},{5,7},{6,4},{7,5},{8,10},{9,11},{10,... | collective-permute-start | bytes 589832 | tf_op jit(solution)/shard_map/ppermute | solution.py:303
  57.6 5.8 %collective-permute-start.12 = (bf16[128,768]{1,0:T(8,128)(2,1)S(1)}, bf16[128,768]{1,0:T(8,128)(2,1)S(1)}, u32[]{:S(2)}, u32[]{:S(2)}) collective-permute-start(bf16[128,768]{1,0:T(8,128)(2,1)S(1)} %get-tuple-element.73), channel_id=1, source_target_pairs={{0,4},{1,5},{2,6},{3,7},{4,0},{5,1},{6,2},{7,3},{8,12},{9,13},{10,... | collective-permute-start | bytes 589832 | tf_op jit(solution)/shard_map/ppermute | solution.py:303

commit v7 on v5

--- a/solution.py
+++ b/solution.py
@@ -64,22 +64,25 @@
 
 
 def begin_kernel(keys_ref, values_ref, q_ref, *refs):
-    pieces, (source, q_source, target, sems) = refs[:PEERS], refs[PEERS:]
-    loads = [pltpu.make_async_copy(ref, source.at[i], sems.at[i]) for i, ref in enumerate((keys_ref, values_ref))]
-    loads.append(pltpu.make_async_copy(q_ref, q_source, sems.at[2]))
-    for load in loads:
-        load.start()
+    pieces, (target, sems, out_sems) = refs[:PEERS], refs[PEERS:]
     _, chip, core = place()
-    for load in loads:
-        load.wait()
+    steps = [*range(1, PEERS), 0]
+    loads = {}
+    for step in steps:
+        peer = peer_of(chip, core, step)
+        at = 0
+        for i, ref in enumerate((keys_ref, values_ref, q_ref)):
+            width = ref.shape[1] // KVH
+            lanes = pl.ds(pl.multiple_of(peer * width, HD), width)
+            load = pltpu.make_async_copy(ref.at[:, lanes], target.at[step, :, at : at + width], sems.at[step, i])
+            load.start()
+            loads[step, i] = load
+            at += width
     stores = []
-    for step in [*range(1, PEERS), 0]:
-        peer = peer_of(chip, core, step)
-        lanes = pl.ds(pl.multiple_of(peer * HD, HD), HD)
-        target[step, :, :HD] = source[0, :, lanes]
-        target[step, :, HD : 2 * HD] = source[1, :, lanes]
-        target[step, :, 2 * HD :] = q_source[:, pl.ds(pl.multiple_of(peer * WIDE, HD), WIDE)]
-        stores.append(pltpu.make_async_copy(target.at[step], pieces[step], sems.at[step]))
+    for step in steps:
+        for i in range(3):
+            loads[step, i].wait()
+        stores.append(pltpu.make_async_copy(target.at[step], pieces[step], out_sems.at[step]))
         stores[-1].start()
     for store in stores:
         store.wait()
@@ -93,9 +96,8 @@
         in_specs=[HBM] * 3,
         out_specs=[HBM] * PEERS,
         scratch_shapes=[
-            pltpu.VMEM((2, *keys.shape), jnp.bfloat16),
-            pltpu.VMEM(queries.shape, jnp.bfloat16),
             pltpu.VMEM((PEERS, *shape), jnp.bfloat16),
+            pltpu.SemaphoreType.DMA((PEERS, 3)),
             pltpu.SemaphoreType.DMA((PEERS,)),
         ],
     )(keys, values, queries)
@@ -162,16 +164,15 @@
     )(*pieces)
 
 
-def attend_kernel(backs, sides, far_side, first, final, table_ref, factor_ref, *refs):
+def attend_kernel(backs, first, final, table_ref, factor_ref, *refs):
     refs = list(refs)
     q_ref = refs.pop(0)
     if not first:
         del refs[:2]
-    slabs = [[refs.pop(0) for _ in range(sides)] for _ in backs]
+    slabs = [(refs.pop(0), refs.pop(0)) for _ in backs]
     out_refs = [refs.pop(0) for _ in range(PEERS)] if final else None
     sums_ref, top_ref = refs.pop(0), refs.pop(0)
-    _, chip, this_core = place()
-    core = this_core ^ far_side
+    _, chip, core = place()
     if first:
         sums_ref[...] = jnp.zeros_like(sums_ref)
         top_ref[...] = jnp.full_like(top_ref, LOW)
@@ -201,7 +202,7 @@
                         keys = jnp.where(keep, keys, spare)
                         values = jnp.where(keep, values.astype(jnp.float32), 0.0).astype(jnp.bfloat16)
                         ones = jnp.where(keep, 1.0, 0.0).astype(jnp.bfloat16)
-                        to = block_rows if sides == 1 else (2 + owner) * block_rows
+                        to = (2 + owner) * block_rows
                     to = pl.ds(pl.multiple_of(to, block_rows), block_rows)
                     key_ref[x, :, to] = jnp.transpose(keys).astype(jnp.bfloat16)
                     value_ref[x, to, :HD] = values
@@ -211,7 +212,6 @@
         def _(turn):
             x = turn >> 1
             side = turn & 1
-
             count = table_ref[4 * back + turn]
 
             def visit(width):
@@ -251,11 +251,8 @@
                     top_ref[side, chain] = top
 
             most = 3 * block_rows
-            if sides == 2:
-                pl.when((count > 0) & (count <= most))(lambda: visit(most))
-                pl.when(count > most)(lambda: visit(most + block_rows))
-            else:
-                pl.when(count > 0)(lambda: visit(2 * block_rows))
+            pl.when((count > 0) & (count <= most))(lambda: visit(most))
+            pl.when(count > most)(lambda: visit(most + block_rows))
 
     if final:
         done_ref = refs[2]
@@ -267,14 +264,14 @@
                     lanes = slice((g * group + i) * HD, (g * group + i + 1) * HD)
                     done_ref[2 * side + block, :, lanes] = result[i * piece : (i + 1) * piece]
         for step, out_ref in enumerate(out_refs):
-            out_ref[...] = done_ref[peer_of(chip, this_core, step)]
-
-
-def attend(tables, q, state, slabs, backs, final, far_side=False):
+            out_ref[...] = done_ref[peer_of(chip, core, step)]
+
+
+def attend(tables, q, state, slabs, backs, final=False):
     first = state is None
     piece = q.shape[1]
     tall = GROUP * piece // 2
-    tokens = slabs[0][0].shape[0] * len(slabs[0]) // 2
+    tokens = slabs[0][0].shape[0]
     out_shape = [
         jax.ShapeDtypeStruct((2, 4, tall, 2 * HD), jnp.float32),
         jax.ShapeDtypeStruct((2, 4, tall, HD), jnp.float32),
@@ -285,9 +282,10 @@
         scratch.append(pltpu.VMEM(q.shape, jnp.bfloat16))
     work = len(backs) * PEERS * tall * tokens
     inputs = [q, *(state or ()), *[a for slab in slabs for a in slab]]
-    aliases = {} if first else {3: PEERS * final, 4: PEERS * final + 1}
-    return pl.pallas_call(
-        functools.partial(attend_kernel, backs, len(slabs[0]), far_side, first, final),
+    outs = len(out_shape) - 2
+    aliases = {} if first else {3: outs, 4: outs + 1}
+    return pl.pallas_call(
+        functools.partial(attend_kernel, backs, first, final),
         out_shape=out_shape,
         in_specs=[SMEM] * 2 + [VMEM] * len(inputs),
         out_specs=[VMEM] * len(out_shape),
@@ -320,20 +318,17 @@
     moved, mine, tables = lax.optimization_barrier((exchange(pieces)[1:], hold(pieces[0]), tables))
     own, q = gather([mine, *moved])
     slabs = {0: own, 1: up(own, 1), last: up(own, last)}
-    state = attend(tables, q, None, [(own, near(own))], [0], False)
+    state = attend(tables, q, None, [(own, near(own))], [0])
     slabs, state = lax.optimization_barrier((slabs, state))
     stage = [1, last]
     sides = [(slabs[b], near(slabs[b])) for b in stage]
     for back in range(2, last):
         slab = up(slabs[back - 1], 1)
-        state = attend(tables, q, state, sides, stage, False)
+        state = attend(tables, q, state, sides, stage)
         slabs[back], state = lax.optimization_barrier((slab, state))
         stage = [back]
         sides = [(slabs[back], near(slabs[back]))]
-    mine, other = sides[0]
-    state = attend(tables, q, state, [(mine,)], stage, False)
-    other, state = lax.optimization_barrier((other, state))
-    out = attend(tables, q, state, [(other,)], stage, True, True)
+    out = attend(tables, q, state, sides, stage, True)
     return join(exchange(out[:PEERS]))
 
 

time: 61.6 us -> 61.5 us (level)
  Pallas kernels: 12.5 us -> 11.7 us
  waiting for transfers between devices: 31.1 us -> 31.9 us
    ppermute x4, waiting for transfers between devices: 0.81 us -> 1.54 us  [near(): return lax.ppermute(a, 'ctx', other_core)]
    pallas_call x4 -> x3, Pallas kernels: 7.64 us -> 7.02 us  [attend(): pl.pallas_call(functools.partial(attend_kernel, backs, first, final), out...]
  transfers between devices with their start and end apart: 13 -> 13, of which waited for: 8 -> 8; matrix products, arithmetic and copies ran while one was open for 0% -> 0% of each run, Pallas kernels for 13% -> 12%
where the time goes in v7:
time: 61.5 us; the launch traced here: 61.3 us
  waiting for transfers between devices  31.9 us (52%)
  starting transfers between devices  14 us (23%)
  Pallas kernels  11.7 us (19%)
  local copies, waits for them, and re-layouts  3.62 us (6%)
    ppermute x3, waiting for transfers between devices, up(): lax.ppermute(a, 'span', [(s, (s + 2 * steps) % spans) for s in range(span...  15.2 us
    ppermute x6, waiting for transfers between devices, exchange(): moved.append(lax.ppermute(piece, ('span', 'ctx'), pairs))  15.2 us
    ppermute x6, starting transfers between devices, exchange(): moved.append(lax.ppermute(piece, ('span', 'ctx'), pairs))  8.15 us
    pallas_call x3, Pallas kernels, attend(): pl.pallas_call(functools.partial(attend_kernel, backs, first, final), out...  7.02 us
    ppermute x3, starting transfers between devices, up(): lax.ppermute(a, 'span', [(s, (s + 2 * steps) % spans) for s in range(span...  5.28 us
    unnamed x10, local copies, waits for them, and re-layouts  3.62 us
    pallas_call x1, Pallas kernels, begin(): pl.pallas_call(begin_kernel, out_shape=[jax.ShapeDtypeStruct(shape, jnp.b...  2.15 us
    ppermute x4, waiting for transfers between devices, near(): return lax.ppermute(a, 'ctx', other_core)  1.54 us
  transfers between devices with their start and end apart: 13, of which 8 were waited for; matrix products, arithmetic and copies ran while one was open for 0% of the time, Pallas kernels for 12%

profile of v7, /device:TPU:0, one launch (start us, length us, event | category | flops | bytes accessed | tf_op | source)
XLA Modules:
  0.0 61.3 jit_solution(13713974453929531132)
XLA Ops:
  0.0 2.1 %shard_map.73 = (bf16[128,1024]{1,0:T(8,128)(2,1)}, bf16[128,1024]{1,0:T(8,128)(2,1)}, bf16[128,1024]{1,0:T(8,128)(2,1)}, bf16[128,1024]{1,0:T(8,128)(2,1)}) custom-call(bf16[128,512]{1,0:T(8,128)(2,1)} %keys_ref.1, bf16[128,512]{1,0:T(8,128)(2,1)} %values_ref.1, bf16[128,3072]{1,0:T(8,128)(2,1)} %q_ref.1), custom_call_target="tpu_custom_call" | custom-call | tf_op jit(solution)/shard_map/pallas_call | solution.py:93
  2.2 4.0 %collective-permute-start = (bf16[128,1024]{1,0:T(8,128)(2,1)}, bf16[128,1024]{1,0:T(8,128)(2,1)S(1)}, u32[]{:S(2)}, u32[]{:S(2)}) collective-permute-start(bf16[128,1024]{1,0:T(8,128)(2,1)} %get-tuple-element.34), channel_id=1, source_target_pairs={{0,6},{1,7},{2,4},{3,5},{4,2},{5,3},{6,0},{7,1},{8,14},{9,15},{10,... | collective-permute-start | bytes 786440 | tf_op jit(solution)/shard_map/ppermute | solution.py:307
  6.1 0.5 collective-permute-start.1
  6.7 0.1 collective-permute-start.2
  6.8 0.0 copy-start
  6.8 0.9 %copy-done = bf16[128,1024]{1,0:T(8,128)(2,1)S(1)} copy-done((bf16[128,1024]{1,0:T(8,128)(2,1)S(1)}, bf16[128,1024]{1,0:T(8,128)(2,1)}, u32[]{:S(2)}) %copy-start) | copy-done | bytes 262168
  7.7 0.0 copy-start.1
  7.7 0.7 %copy-done.1 = f32[8,24]{1,0:T(8,128)S(1)} copy-done((f32[8,24]{1,0:T(8,128)S(1)}, f32[8,24]{1,0:T(8,128)}, u32[]{:S(2)}) %copy-start.1) | copy-done | bytes 792
  8.4 0.0 copy-start.2
  8.4 0.7 %copy-done.2 = s32[8,4]{0,1:T(4,128)S(1)} copy-done((s32[8,4]{0,1:T(4,128)S(1)}, s32[8,4]{0,1:T(4,128)}, u32[]{:S(2)}) %copy-start.2) | copy-done | bytes 152
  9.1 0.0 copy-start.3
  9.1 0.7 %copy-done.3 = s32[8]{0:T(128)S(1)} copy-done((s32[8]{0:T(128)S(1)}, s32[8]{0:T(128)}, u32[]{:S(2)}) %copy-start.3) | copy-done | bytes 56
  9.8 0.0 copy-start.4
  9.8 0.7 %copy-done.4 = s32[8]{0:T(128)S(1)} copy-done((s32[8]{0:T(128)S(1)}, s32[8]{0:T(128)}, u32[]{:S(2)}) %copy-start.4) | copy-done | bytes 56
  10.4 1.5 %shard_map.75 = (s32[16]{0:T(128)S(1)}, f32[12]{0:T(128)S(1)}) custom-call(s32[8]{0:T(128)S(1)} %copy-done.3, f32[8,24]{1,0:T(8,128)S(1)} %copy-done.1, s32[4,8]{1,0:T(4,128)S(1)} %bitcast.1, s32[8]{0:T(128)S(1)} %copy-done.4), custom_call_target="tpu_custom_call" | custom-call | tf_op jit(solution)/shard_map/pallas_call | solution.py:57
  11.9 1.6 %collective-permute-done.refs_1_ = bf16[128,1024]{1,0:T(8,128)(2,1)S(1)} collective-permute-done((bf16[128,1024]{1,0:T(8,128)(2,1)}, bf16[128,1024]{1,0:T(8,128)(2,1)S(1)}, u32[]{:S(2)}, u32[]{:S(2)}) %collective-permute-start) | collective-permute-done | bytes 262176 | tf_op jit(solution)/shard_map/ppermute | solution.py:307
  13.5 5.0 %collective-permute-done.1.refs_2_ = bf16[128,1024]{1,0:T(8,128)(2,1)S(1)} collective-permute-done((bf16[128,1024]{1,0:T(8,128)(2,1)}, bf16[128,1024]{1,0:T(8,128)(2,1)S(1)}, u32[]{:S(2)}, u32[]{:S(2)}) %collective-permute-start.1) | collective-permute-done | bytes 262176 | tf_op jit(solution)/shard_map/ppermute | solution.py:307
  18.5 0.0 collective-permute-done.2.refs_3_
  18.5 0.1 shard_map.76
  18.6 0.1 collective-permute-start.5
  18.7 3.7 %collective-permute-start.4 = (bf16[512,256]{1,0:T(8,128)(2,1)S(1)}, bf16[512,256]{1,0:T(8,128)(2,1)S(1)}, u32[]{:S(2)}, u32[]{:S(2)}) collective-permute-start(bf16[512,256]{1,0:T(8,128)(2,1)S(1)} %get-tuple-element.47.refs_1_), channel_id=1, source_target_pairs={{0,24},{4,28},{8,0},{12,4},{16,8},{20,12},{24,16},{28,20},{1,25},{... | collective-permute-start | bytes 786440 | tf_op jit(solution)/shard_map/ppermute | solution.py:311
  22.4 0.0 collective-permute-start.3
  22.4 0.0 collective-permute-done.5.refs_2_
  22.4 4.8 %shard_map.77 = (f32[2,4,384,256]{3,2,1,0:T(8,128)S(1)}, f32[2,4,384,128]{3,2,1,0:T(8,128)S(1)}) custom-call(s32[16]{0:T(128)S(1)} %get-tuple-element.40.table_ref, f32[12]{0:T(128)S(1)} %get-tuple-element.41.factor_ref, bf16[4,128,768]{2,1,0:T(8,128)(2,1)S(1)} %get-tuple-element.46.refs_0_, bf16[512,256]{1,0:T(8,128)(2,1)S(1)} %get-tuple-element.47.refs_1_, ...), custom_call_target="tpu_custom_call" | custom-call | flops 201326592 | bytes 1572864 | tf_op jit(solution)/shard_map/pallas_call | solution.py:287
  27.2 1.9 %collective-permute-done.4.refs_5_ = bf16[512,256]{1,0:T(8,128)(2,1)S(1)} collective-permute-done((bf16[512,256]{1,0:T(8,128)(2,1)S(1)}, bf16[512,256]{1,0:T(8,128)(2,1)S(1)}, u32[]{:S(2)}, u32[]{:S(2)}) %collective-permute-start.4) | collective-permute-done | bytes 262176 | tf_op jit(solution)/shard_map/ppermute | solution.py:311
  29.0 6.0 %collective-permute-done.3.refs_3_ = bf16[512,256]{1,0:T(8,128)(2,1)S(1)} collective-permute-done((bf16[512,256]{1,0:T(8,128)(2,1)S(1)}, bf16[512,256]{1,0:T(8,128)(2,1)S(1)}, u32[]{:S(2)}, u32[]{:S(2)}) %collective-permute-start.3) | collective-permute-done | bytes 262176 | tf_op jit(solution)/shard_map/ppermute | solution.py:311
  35.1 0.0 collective-permute-start.8
  35.1 0.5 collective-permute-start.7
  35.6 1.6 %collective-permute-start.6 = (bf16[512,256]{1,0:T(8,128)(2,1)S(1)}, bf16[512,256]{1,0:T(8,128)(2,1)S(1)}, u32[]{:S(2)}, u32[]{:S(2)}) collective-permute-start(bf16[512,256]{1,0:T(8,128)(2,1)S(1)} %collective-permute-done.3.refs_3_), channel_id=1, source_target_pairs={{0,8},{4,12},{8,16},{12,20},{16,24},{20,28},{24,0},{28,4},{1,9},{5... | collective-permute-start | bytes 786440 | tf_op jit(solution)/shard_map/ppermute | solution.py:311
  37.2 0.0 collective-permute-done.8.refs_6_
  37.2 0.0 collective-permute-done.7.refs_4_
  37.2 1.1 %shard_map.78 = (f32[2,4,384,256]{3,2,1,0:T(8,128)S(1)}, f32[2,4,384,128]{3,2,1,0:T(8,128)S(1)}) custom-call(s32[16]{0:T(128)S(1)} %get-tuple-element.40.table_ref, f32[12]{0:T(128)S(1)} %get-tuple-element.41.factor_ref, bf16[4,128,768]{2,1,0:T(8,128)(2,1)S(1)} %get-tuple-element.46.refs_0_, ...), custom_call_target="tpu_custom_call", output_to_operand_aliasing={{0}: (3, {}), {1}: (4, {})} | custom-call | flops 402653184 | bytes 1572864 | tf_op jit(solution)/shard_map/pallas_call | solution.py:287
  38.3 7.3 %collective-permute-done.6.refs_3_ = bf16[512,256]{1,0:T(8,128)(2,1)S(1)} collective-permute-done((bf16[512,256]{1,0:T(8,128)(2,1)S(1)}, bf16[512,256]{1,0:T(8,128)(2,1)S(1)}, u32[]{:S(2)}, u32[]{:S(2)}) %collective-permute-start.6) | collective-permute-done | bytes 262176 | tf_op jit(solution)/shard_map/ppermute | solution.py:311
  45.6 0.0 collective-permute-start.9
  45.6 1.5 %collective-permute-done.9.refs_4_ = bf16[512,256]{1,0:T(8,128)(2,1)S(1)} collective-permute-done((bf16[512,256]{1,0:T(8,128)(2,1)S(1)}, bf16[512,256]{1,0:T(8,128)(2,1)S(1)}, u32[]{:S(2)}, u32[]{:S(2)}) %collective-permute-start.9) | collective-permute-done | bytes 262176 | tf_op jit(solution)/shard_map/ppermute | solution.py:314
  47.1 1.1 %shard_map.79 = (bf16[128,768]{1,0:T(8,128)(2,1)S(1)}, bf16[128,768]{1,0:T(8,128)(2,1)S(1)}, bf16[128,768]{1,0:T(8,128)(2,1)S(1)}, bf16[128,768]{1,0:T(8,128)(2,...) custom-call(s32[16]{0:T(128)S(1)} %get-tuple-element.40.table_ref, ...), custom_call_target="tpu_custom_call", output_to_operand_aliasing={{4}: (3, {}), {5}: (4, {})} | custom-call | flops 201326592 | bytes 1572864 | tf_op jit(solution)/shard_map/pallas_call | solution.py:287
  48.3 1.7 %collective-permute-start.10 = (bf16[128,768]{1,0:T(8,128)(2,1)S(1)}, bf16[128,768]{1,0:T(8,128)(2,1)S(1)}, u32[]{:S(2)}, u32[]{:S(2)}) collective-permute-start(bf16[128,768]{1,0:T(8,128)(2,1)S(1)} %get-tuple-element.60), channel_id=1, source_target_pairs={{0,6},{1,7},{2,4},{3,5},{4,2},{5,3},{6,0},{7,1},{8,14},{9,15},{10,... | collective-permute-start | bytes 589832 | tf_op jit(solution)/shard_map/ppermute | solution.py:307
  50.0 1.2 %collective-permute-start.11 = (bf16[128,768]{1,0:T(8,128)(2,1)S(1)}, bf16[128,768]{1,0:T(8,128)(2,1)S(1)}, u32[]{:S(2)}, u32[]{:S(2)}) collective-permute-start(bf16[128,768]{1,0:T(8,128)(2,1)S(1)} %get-tuple-element.61), channel_id=1, source_target_pairs={{0,4},{1,3},{2,6},{3,1},{4,0},{5,7},{6,2},{7,5},{8,12},{9,11},{10,... | collective-permute-start | bytes 589832 | tf_op jit(solution)/shard_map/ppermute | solution.py:307
  51.2 0.6 collective-permute-start.12
  51.8 5.2 %collective-permute-done.10.refs_1_ = bf16[128,768]{1,0:T(8,128)(2,1)S(1)} collective-permute-done((bf16[128,768]{1,0:T(8,128)(2,1)S(1)}, bf16[128,768]{1,0:T(8,128)(2,1)S(1)}, u32[]{:S(2)}, u32[]{:S(2)}) %collective-permute-start.10) | collective-permute-done | bytes 196640 | tf_op jit(solution)/shard_map/ppermute | solution.py:307
  57.0 3.4 %collective-permute-done.11.refs_2_ = bf16[128,768]{1,0:T(8,128)(2,1)S(1)} collective-permute-done((bf16[128,768]{1,0:T(8,128)(2,1)S(1)}, bf16[128,768]{1,0:T(8,128)(2,1)S(1)}, u32[]{:S(2)}, u32[]{:S(2)}) %collective-permute-start.11) | collective-permute-done | bytes 196640 | tf_op jit(solution)/shard_map/ppermute | solution.py:307
  60.4 0.0 collective-permute-done.12.refs_3_
  60.4 0.9 %shard_map.80 = bf16[128,3072]{1,0:T(8,128)(2,1)} custom-call(bf16[128,768]{1,0:T(8,128)(2,1)S(1)} %get-tuple-element.59.refs_0_, bf16[128,768]{1,0:T(8,128)(2,1)S(1)} %collective-permute-done.10.refs_1_, bf16[128,768]{1,0:T(8,128)(2,1)S(1)} %collective-permute-done.11.refs_2_, bf16[128,768]{1,0:T(8,128)(2,1)S(1)} %collective-permute-done.12.refs_3_), custom_call_target="tpu_custom_call" | custom-call | tf_op jit(solution)/shard_map/pallas_call | solution.py:157
  (1 shorter events, 0.0 us)
Async XLA Ops:
  2.2 11.3 %collective-permute-start = (bf16[128,1024]{1,0:T(8,128)(2,1)}, bf16[128,1024]{1,0:T(8,128)(2,1)S(1)}, u32[]{:S(2)}, u32[]{:S(2)}) collective-permute-start(bf16[128,1024]{1,0:T(8,128)(2,1)} %get-tuple-element.34), channel_id=1, source_target_pairs={{0,6},{1,7},{2,4},{3,5},{4,2},{5,3},{6,0},{7,1},{8,14},{9,15},{10,... | collective-permute-start | bytes 786440 | tf_op jit(solution)/shard_map/ppermute | solution.py:307
  6.1 12.4 %collective-permute-start.1 = (bf16[128,1024]{1,0:T(8,128)(2,1)}, bf16[128,1024]{1,0:T(8,128)(2,1)S(1)}, u32[]{:S(2)}, u32[]{:S(2)}) collective-permute-start(bf16[128,1024]{1,0:T(8,128)(2,1)} %get-tuple-element.35), channel_id=1, source_target_pairs={{0,4},{1,3},{2,6},{3,1},{4,0},{5,7},{6,2},{7,5},{8,12},{9,11},{10,... | collective-permute-start | bytes 786440 | tf_op jit(solution)/shard_map/ppermute | solution.py:307
  6.7 11.9 %collective-permute-start.2 = (bf16[128,1024]{1,0:T(8,128)(2,1)}, bf16[128,1024]{1,0:T(8,128)(2,1)S(1)}, u32[]{:S(2)}, u32[]{:S(2)}) collective-permute-start(bf16[128,1024]{1,0:T(8,128)(2,1)} %get-tuple-element.36), channel_id=1, source_target_pairs={{0,2},{1,5},{2,0},{3,7},{4,6},{5,1},{6,4},{7,3},{8,10},{9,13},{10,... | collective-permute-start | bytes 786440 | tf_op jit(solution)/shard_map/ppermute | solution.py:307
  6.8 0.9 %copy-start = (bf16[128,1024]{1,0:T(8,128)(2,1)S(1)}, bf16[128,1024]{1,0:T(8,128)(2,1)}, u32[]{:S(2)}) copy-start(bf16[128,1024]{1,0:T(8,128)(2,1)} %get-tuple-element.37.piece_ref) | copy-start | bytes 786436
  7.7 0.7 %copy-start.1 = (f32[8,24]{1,0:T(8,128)S(1)}, f32[8,24]{1,0:T(8,128)}, u32[]{:S(2)}) copy-start(f32[8,24]{1,0:T(8,128)} %temps_ref.1) | copy-start | bytes 2308
  8.4 0.7 %copy-start.2 = (s32[8,4]{0,1:T(4,128)S(1)}, s32[8,4]{0,1:T(4,128)}, u32[]{:S(2)}) copy-start(s32[8,4]{0,1:T(4,128)} %param.12) | copy-start | bytes 388
  9.1 0.7 %copy-start.3 = (s32[8]{0:T(128)S(1)}, s32[8]{0:T(128)}, u32[]{:S(2)}) copy-start(s32[8]{0:T(128)} %levels_ref.1) | copy-start | bytes 100
  9.8 0.7 %copy-start.4 = (s32[8]{0:T(128)S(1)}, s32[8]{0:T(128)}, u32[]{:S(2)}) copy-start(s32[8]{0:T(128)} %counts_ref.1) | copy-start | bytes 100
  18.6 3.7 %collective-permute-start.5 = (bf16[512,256]{1,0:T(8,128)(2,1)S(1)}, bf16[512,256]{1,0:T(8,128)(2,1)S(1)}, u32[]{:S(2)}, u32[]{:S(2)}) collective-permute-start(bf16[512,256]{1,0:T(8,128)(2,1)S(1)} %get-tuple-element.47.refs_1_), channel_id=1, source_target_pairs={{0,1},{1,0},{2,3},{3,2},{4,5},{5,4},{6,7},{7,6},{8,9},{9,8},{10,11... | collective-permute-start | bytes 786440 | tf_op jit(solution)/shard_map/ppermute | solution.py:314
  18.7 10.3 %collective-permute-start.4 = (bf16[512,256]{1,0:T(8,128)(2,1)S(1)}, bf16[512,256]{1,0:T(8,128)(2,1)S(1)}, u32[]{:S(2)}, u32[]{:S(2)}) collective-permute-start(bf16[512,256]{1,0:T(8,128)(2,1)S(1)} %get-tuple-element.47.refs_1_), channel_id=1, source_target_pairs={{0,24},{4,28},{8,0},{12,4},{16,8},{20,12},{24,16},{28,20},{1,25},{... | collective-permute-start | bytes 786440 | tf_op jit(solution)/shard_map/ppermute | solution.py:311
  22.4 12.7 %collective-permute-start.3 = (bf16[512,256]{1,0:T(8,128)(2,1)S(1)}, bf16[512,256]{1,0:T(8,128)(2,1)S(1)}, u32[]{:S(2)}, u32[]{:S(2)}) collective-permute-start(bf16[512,256]{1,0:T(8,128)(2,1)S(1)} %get-tuple-element.47.refs_1_), channel_id=1, source_target_pairs={{0,8},{4,12},{8,16},{12,20},{16,24},{20,28},{24,0},{28,4},{1,9},{5... | collective-permute-start | bytes 786440 | tf_op jit(solution)/shard_map/ppermute | solution.py:311
  35.1 2.1 %collective-permute-start.8 = (bf16[512,256]{1,0:T(8,128)(2,1)S(1)}, bf16[512,256]{1,0:T(8,128)(2,1)S(1)}, u32[]{:S(2)}, u32[]{:S(2)}) collective-permute-start(bf16[512,256]{1,0:T(8,128)(2,1)S(1)} %collective-permute-done.4.refs_5_), channel_id=1, source_target_pairs={{0,1},{1,0},{2,3},{3,2},{4,5},{5,4},{6,7},{7,6},{8,9},{9,8},{10,11... | collective-permute-start | bytes 786440 | tf_op jit(solution)/shard_map/ppermute | solution.py:314
  35.1 2.1 %collective-permute-start.7 = (bf16[512,256]{1,0:T(8,128)(2,1)S(1)}, bf16[512,256]{1,0:T(8,128)(2,1)S(1)}, u32[]{:S(2)}, u32[]{:S(2)}) collective-permute-start(bf16[512,256]{1,0:T(8,128)(2,1)S(1)} %collective-permute-done.3.refs_3_), channel_id=1, source_target_pairs={{0,1},{1,0},{2,3},{3,2},{4,5},{5,4},{6,7},{7,6},{8,9},{9,8},{10,11... | collective-permute-start | bytes 786440 | tf_op jit(solution)/shard_map/ppermute | solution.py:314
  35.6 10.0 %collective-permute-start.6 = (bf16[512,256]{1,0:T(8,128)(2,1)S(1)}, bf16[512,256]{1,0:T(8,128)(2,1)S(1)}, u32[]{:S(2)}, u32[]{:S(2)}) collective-permute-start(bf16[512,256]{1,0:T(8,128)(2,1)S(1)} %collective-permute-done.3.refs_3_), channel_id=1, source_target_pairs={{0,8},{4,12},{8,16},{12,20},{16,24},{20,28},{24,0},{28,4},{1,9},{5... | collective-permute-start | bytes 786440 | tf_op jit(solution)/shard_map/ppermute | solution.py:311
  45.6 1.5 %collective-permute-start.9 = (bf16[512,256]{1,0:T(8,128)(2,1)S(1)}, bf16[512,256]{1,0:T(8,128)(2,1)S(1)}, u32[]{:S(2)}, u32[]{:S(2)}) collective-permute-start(bf16[512,256]{1,0:T(8,128)(2,1)S(1)} %collective-permute-done.6.refs_3_), channel_id=1, source_target_pairs={{0,1},{1,0},{2,3},{3,2},{4,5},{5,4},{6,7},{7,6},{8,9},{9,8},{10,11... | collective-permute-start | bytes 786440 | tf_op jit(solution)/shard_map/ppermute | solution.py:314
  48.3 8.8 %collective-permute-start.10 = (bf16[128,768]{1,0:T(8,128)(2,1)S(1)}, bf16[128,768]{1,0:T(8,128)(2,1)S(1)}, u32[]{:S(2)}, u32[]{:S(2)}) collective-permute-start(bf16[128,768]{1,0:T(8,128)(2,1)S(1)} %get-tuple-element.60), channel_id=1, source_target_pairs={{0,6},{1,7},{2,4},{3,5},{4,2},{5,3},{6,0},{7,1},{8,14},{9,15},{10,... | collective-permute-start | bytes 589832 | tf_op jit(solution)/shard_map/ppermute | solution.py:307
  50.0 10.4 %collective-permute-start.11 = (bf16[128,768]{1,0:T(8,128)(2,1)S(1)}, bf16[128,768]{1,0:T(8,128)(2,1)S(1)}, u32[]{:S(2)}, u32[]{:S(2)}) collective-permute-start(bf16[128,768]{1,0:T(8,128)(2,1)S(1)} %get-tuple-element.61), channel_id=1, source_target_pairs={{0,4},{1,3},{2,6},{3,1},{4,0},{5,7},{6,2},{7,5},{8,12},{9,11},{10,... | collective-permute-start | bytes 589832 | tf_op jit(solution)/shard_map/ppermute | solution.py:307
  51.2 9.2 %collective-permute-start.12 = (bf16[128,768]{1,0:T(8,128)(2,1)S(1)}, bf16[128,768]{1,0:T(8,128)(2,1)S(1)}, u32[]{:S(2)}, u32[]{:S(2)}) collective-permute-start(bf16[128,768]{1,0:T(8,128)(2,1)S(1)} %get-tuple-element.62), channel_id=1, source_target_pairs={{0,2},{1,5},{2,0},{3,7},{4,6},{5,1},{6,4},{7,3},{8,10},{9,13},{10,... | collective-permute-start | bytes 589832 | tf_op jit(solution)/shard_map/ppermute | solution.py:307

commit v8 on v7

--- a/solution.py
+++ b/solution.py
@@ -64,43 +64,40 @@
 
 
 def begin_kernel(keys_ref, values_ref, q_ref, *refs):
-    pieces, (target, sems, out_sems) = refs[:PEERS], refs[PEERS:]
+    kv_pieces, q_pieces, (kv, q, sems, out_sems) = refs[:PEERS], refs[PEERS : 2 * PEERS], refs[2 * PEERS :]
     _, chip, core = place()
     steps = [*range(1, PEERS), 0]
     loads = {}
-    for step in steps:
-        peer = peer_of(chip, core, step)
-        at = 0
-        for i, ref in enumerate((keys_ref, values_ref, q_ref)):
-            width = ref.shape[1] // KVH
-            lanes = pl.ds(pl.multiple_of(peer * width, HD), width)
-            load = pltpu.make_async_copy(ref.at[:, lanes], target.at[step, :, at : at + width], sems.at[step, i])
-            load.start()
-            loads[step, i] = load
-            at += width
+    for i, ref in enumerate((keys_ref, values_ref, q_ref)):
+        width = ref.shape[1] // KVH
+        for step in steps:
+            lanes = pl.ds(pl.multiple_of(peer_of(chip, core, step) * width, HD), width)
+            target = q.at[step] if i == 2 else kv.at[step, :, i * HD : (i + 1) * HD]
+            loads[step, i] = pltpu.make_async_copy(ref.at[:, lanes], target, sems.at[step, i])
+            loads[step, i].start()
     stores = []
-    for step in steps:
-        for i in range(3):
-            loads[step, i].wait()
-        stores.append(pltpu.make_async_copy(target.at[step], pieces[step], out_sems.at[step]))
-        stores[-1].start()
+    for n, (source, pieces) in enumerate(((kv, kv_pieces), (q, q_pieces))):
+        for step in steps:
+            for i in (2,) if n else (0, 1):
+                loads[step, i].wait()
+            stores.append(pltpu.make_async_copy(source.at[step], pieces[step], out_sems.at[step, n]))
+            stores[-1].start()
     for store in stores:
         store.wait()
 
 
 def begin(keys, values, queries):
-    shape = (keys.shape[0], 2 * HD + WIDE)
-    return pl.pallas_call(
+    rows = keys.shape[0]
+    shapes = [(rows, 2 * HD), (rows, WIDE)]
+    out = pl.pallas_call(
         begin_kernel,
-        out_shape=[jax.ShapeDtypeStruct(shape, jnp.bfloat16)] * PEERS,
+        out_shape=[jax.ShapeDtypeStruct(shape, jnp.bfloat16) for shape in shapes for _ in range(PEERS)],
         in_specs=[HBM] * 3,
-        out_specs=[HBM] * PEERS,
-        scratch_shapes=[
-            pltpu.VMEM((PEERS, *shape), jnp.bfloat16),
-            pltpu.SemaphoreType.DMA((PEERS, 3)),
-            pltpu.SemaphoreType.DMA((PEERS,)),
-        ],
+        out_specs=[HBM] * (2 * PEERS),
+        scratch_shapes=[pltpu.VMEM((PEERS, *shape), jnp.bfloat16) for shape in shapes]
+        + [pltpu.SemaphoreType.DMA((PEERS, 3)), pltpu.SemaphoreType.DMA((PEERS, 2))],
     )(keys, values, queries)
+    return out[:PEERS], out[PEERS:]
 
 
 def hold_kernel(piece_ref, out_ref):
@@ -118,25 +115,18 @@
 
 
 def gather_kernel(*refs):
-    pieces, slab_ref, q_ref = refs[:PEERS], refs[PEERS], refs[PEERS + 1]
+    pieces, out_ref = refs[:PEERS], refs[PEERS]
     _, chip, core = place()
-    part = pieces[0].shape[0]
     for step, piece in enumerate(pieces):
-        peer = peer_of(chip, core, step)
-        slab_ref[pl.ds(pl.multiple_of(peer * part, part), part), :] = piece[:, : 2 * HD]
-        q_ref[peer] = piece[:, 2 * HD :]
+        out_ref[peer_of(chip, core, step)] = piece[...]
 
 
 def gather(pieces):
-    rows = pieces[0].shape[0]
     return pl.pallas_call(
         gather_kernel,
-        out_shape=[
-            jax.ShapeDtypeStruct((PEERS * rows, 2 * HD), jnp.bfloat16),
-            jax.ShapeDtypeStruct((PEERS, rows, WIDE), jnp.bfloat16),
-        ],
+        out_shape=jax.ShapeDtypeStruct((PEERS, *pieces[0].shape), jnp.bfloat16),
         in_specs=[VMEM] * PEERS,
-        out_specs=[VMEM] * 2,
+        out_specs=VMEM,
         compiler_params=SMALL,
     )(*pieces)
 
@@ -313,15 +303,17 @@
     def near(a):
         return lax.ppermute(a, "ctx", other_core)
 
-    pieces = begin(keys, values, queries)
+    kv_pieces, q_pieces = begin(keys, values, queries)
+    moved, mine = lax.optimization_barrier((exchange(kv_pieces)[1:], hold(kv_pieces[0])))
+    own = gather([mine, *moved]).reshape(-1, 2 * HD)
+    slabs = {0: own, 1: up(own, 1), last: up(own, last)}
+    other, q_pieces = lax.optimization_barrier((near(own), q_pieces))
     tables = tabulate(spans // 2, levels, temps, jnp.transpose(ctx_list), counts)
-    moved, mine, tables = lax.optimization_barrier((exchange(pieces)[1:], hold(pieces[0]), tables))
-    own, q = gather([mine, *moved])
-    slabs = {0: own, 1: up(own, 1), last: up(own, last)}
-    state = attend(tables, q, None, [(own, near(own))], [0])
-    slabs, state = lax.optimization_barrier((slabs, state))
-    stage = [1, last]
-    sides = [(slabs[b], near(slabs[b])) for b in stage]
+    slabs, moved, mine, tables = lax.optimization_barrier((slabs, exchange(q_pieces)[1:], hold(q_pieces[0]), tables))
+    q = gather([mine, *moved])
+    stage = [0, 1, last]
+    sides = [(slabs[b], near(slabs[b]) if b else other) for b in stage]
+    state = None
     for back in range(2, last):
         slab = up(slabs[back - 1], 1)
         state = attend(tables, q, state, sides, stage)

time: 61.5 us -> 57.4 us (0.933)
  the two profiles are of different devices: /device:TPU:0 before, /device:TPU:25 now
where the time goes in v8:
time: 57.4 us; the launch traced here: 56.3 us
  Pallas kernels  18.6 us (32%)
  waiting for transfers between devices  18.3 us (32%)
  starting transfers between devices  14.9 us (26%)
  local copies, waits for them, and re-layouts  4.44 us (8%)
    ppermute x9, waiting for transfers between devices, exchange(): moved.append(lax.ppermute(piece, ('span', 'ctx'), pairs))  14 us
    pallas_call x2, Pallas kernels, attend(): pl.pallas_call(functools.partial(attend_kernel, backs, first, final), out...  13.8 us
    ppermute x9, starting transfers between devices, exchange(): moved.append(lax.ppermute(piece, ('span', 'ctx'), pairs))  8.08 us
    unnamed x12, local copies, waits for them, and re-layouts  4.44 us
    ppermute x3, starting transfers between devices, up(): lax.ppermute(a, 'span', [(s, (s + 2 * steps) % spans) for s in range(span...  3.8 us
    ppermute x4, starting transfers between devices, near(): return lax.ppermute(a, 'ctx', other_core)  3.03 us
    ppermute x3, waiting for transfers between devices, up(): lax.ppermute(a, 'span', [(s, (s + 2 * steps) % spans) for s in range(span...  2.25 us
    pallas_call x1, Pallas kernels, begin(): pl.pallas_call(begin_kernel, out_shape=[jax.ShapeDtypeStruct(shape, jnp.b...  2.19 us
  transfers between devices with their start and end apart: 16, of which 10 were waited for; matrix products, arithmetic and copies ran while one was open for 0% of the time, Pallas kernels for 23%

profile of v8, /device:TPU:25, one launch (start us, length us, event | category | flops | bytes accessed | tf_op | source)
XLA Modules:
  0.0 56.3 jit_solution(1081386950855449440)
XLA Ops:
  0.0 2.2 %shard_map.73 = (bf16[128,256]{1,0:T(8,128)(2,1)}, bf16[128,256]{1,0:T(8,128)(2,1)}, bf16[128,256]{1,0:T(8,128)(2,1)}, bf16[128,256]{1,0:T(8,128)(2,1)}, bf16[12...) custom-call(bf16[128,512]{1,0:T(8,128)(2,1)} %keys_ref.1, ...), custom_call_target="tpu_custom_call" | custom-call | tf_op jit(solution)/shard_map/pallas_call | solution.py:92
  2.2 2.2 %collective-permute-start = (bf16[128,256]{1,0:T(8,128)(2,1)}, bf16[128,256]{1,0:T(8,128)(2,1)S(1)}, u32[]{:S(2)}, u32[]{:S(2)}) collective-permute-start(bf16[128,256]{1,0:T(8,128)(2,1)} %get-tuple-element.42), channel_id=1, source_target_pairs={{0,6},{1,7},{2,4},{3,5},{4,2},{5,3},{6,0},{7,1},{8,14},{9,15},{10,... | collective-permute-start | bytes 196616 | tf_op jit(solution)/shard_map/ppermute | solution.py:297
  4.4 0.2 collective-permute-start.1
  4.7 0.3 collective-permute-start.2
  4.9 0.0 copy-start.1
  4.9 0.8 %copy-done.1 = bf16[128,256]{1,0:T(8,128)(2,1)S(1)} copy-done((bf16[128,256]{1,0:T(8,128)(2,1)S(1)}, bf16[128,256]{1,0:T(8,128)(2,1)}, u32[]{:S(2)}) %copy-start.1) | copy-done | bytes 65560
  5.8 0.7 %collective-permute-done.refs_1_ = bf16[128,256]{1,0:T(8,128)(2,1)S(1)} collective-permute-done((bf16[128,256]{1,0:T(8,128)(2,1)}, bf16[128,256]{1,0:T(8,128)(2,1)S(1)}, u32[]{:S(2)}, u32[]{:S(2)}) %collective-permute-start) | collective-permute-done | bytes 65568 | tf_op jit(solution)/shard_map/ppermute | solution.py:297
  6.5 1.8 %collective-permute-done.1.refs_2_ = bf16[128,256]{1,0:T(8,128)(2,1)S(1)} collective-permute-done((bf16[128,256]{1,0:T(8,128)(2,1)}, bf16[128,256]{1,0:T(8,128)(2,1)S(1)}, u32[]{:S(2)}, u32[]{:S(2)}) %collective-permute-start.1) | collective-permute-done | bytes 65568 | tf_op jit(solution)/shard_map/ppermute | solution.py:297
  8.3 0.1 collective-permute-done.2.refs_3_
  8.4 2.1 %collective-permute-start.5 = (bf16[512,256]{1,0:T(8,128)(2,1)S(1)}, bf16[512,256]{1,0:T(8,128)(2,1)S(1)}, u32[]{:S(2)}, u32[]{:S(2)}) collective-permute-start(bf16[512,256]{1,0:T(8,128)(2,1)S(1)} %bitcast.2), channel_id=1, source_target_pairs={{0,1},{1,0},{2,3},{3,2},{4,5},{5,4},{6,7},{7,6},{8,9},{9,8},{10,11... | collective-permute-start | bytes 786440 | tf_op jit(solution)/shard_map/ppermute | solution.py:304
  10.5 0.2 collective-permute-start.4
  10.7 3.1 %collective-permute-start.3 = (bf16[512,256]{1,0:T(8,128)(2,1)S(1)}, bf16[512,256]{1,0:T(8,128)(2,1)S(1)}, u32[]{:S(2)}, u32[]{:S(2)}) collective-permute-start(bf16[512,256]{1,0:T(8,128)(2,1)S(1)} %bitcast.4), channel_id=1, source_target_pairs={{0,8},{4,12},{8,16},{12,20},{16,24},{20,28},{24,0},{28,4},{1,9},{5... | collective-permute-start | bytes 786440 | tf_op jit(solution)/shard_map/ppermute | solution.py:301
  13.8 0.0 collective-permute-done.5.refs_2_
  13.8 1.2 %collective-permute-start.6 = (bf16[128,768]{1,0:T(8,128)(2,1)}, bf16[128,768]{1,0:T(8,128)(2,1)S(1)}, u32[]{:S(2)}, u32[]{:S(2)}) collective-permute-start(bf16[128,768]{1,0:T(8,128)(2,1)} %get-tuple-element.54), channel_id=1, source_target_pairs={{0,6},{1,7},{2,4},{3,5},{4,2},{5,3},{6,0},{7,1},{8,14},{9,15},{10,... | collective-permute-start | bytes 589832 | tf_op jit(solution)/shard_map/ppermute | solution.py:297
  14.9 1.2 %collective-permute-start.7 = (bf16[128,768]{1,0:T(8,128)(2,1)}, bf16[128,768]{1,0:T(8,128)(2,1)S(1)}, u32[]{:S(2)}, u32[]{:S(2)}) collective-permute-start(bf16[128,768]{1,0:T(8,128)(2,1)} %get-tuple-element.55), channel_id=1, source_target_pairs={{0,4},{1,3},{2,6},{3,1},{4,0},{5,7},{6,2},{7,5},{8,12},{9,11},{10,... | collective-permute-start | bytes 589832 | tf_op jit(solution)/shard_map/ppermute | solution.py:297
  16.2 0.3 collective-permute-start.8
  16.4 0.0 copy-start.2
  16.4 0.7 %copy-done.2 = f32[8,24]{1,0:T(8,128)S(1)} copy-done((f32[8,24]{1,0:T(8,128)S(1)}, f32[8,24]{1,0:T(8,128)}, u32[]{:S(2)}) %copy-start.2) | copy-done | bytes 792
  17.1 0.0 copy-start.3
  17.1 0.7 %copy-done.3 = s32[8,4]{0,1:T(4,128)S(1)} copy-done((s32[8,4]{0,1:T(4,128)S(1)}, s32[8,4]{0,1:T(4,128)}, u32[]{:S(2)}) %copy-start.3) | copy-done | bytes 152
  17.8 0.0 copy-start.4
  17.8 0.7 %copy-done.4 = s32[8]{0:T(128)S(1)} copy-done((s32[8]{0:T(128)S(1)}, s32[8]{0:T(128)}, u32[]{:S(2)}) %copy-start.4) | copy-done | bytes 56
  18.4 0.0 copy-start.5
  18.4 0.7 %copy-done.5 = s32[8]{0:T(128)S(1)} copy-done((s32[8]{0:T(128)S(1)}, s32[8]{0:T(128)}, u32[]{:S(2)}) %copy-start.5) | copy-done | bytes 56
  19.1 1.5 %shard_map.77 = (s32[16]{0:T(128)S(1)}, f32[12]{0:T(128)S(1)}) custom-call(s32[8]{0:T(128)S(1)} %copy-done.4, f32[8,24]{1,0:T(8,128)S(1)} %copy-done.2, s32[4,8]{1,0:T(4,128)S(1)} %bitcast.6, s32[8]{0:T(128)S(1)} %copy-done.5), custom_call_target="tpu_custom_call" | custom-call | tf_op jit(solution)/shard_map/pallas_call | solution.py:57
  20.6 0.0 copy-start
  20.6 0.9 %copy-done = bf16[128,768]{1,0:T(8,128)(2,1)S(1)} copy-done((bf16[128,768]{1,0:T(8,128)(2,1)S(1)}, bf16[128,768]{1,0:T(8,128)(2,1)}, u32[]{:S(2)}) %copy-start) | copy-done | bytes 196632
  21.6 0.0 collective-permute-done.4.refs_5_
  21.6 2.2 %collective-permute-done.3.refs_3_ = bf16[512,256]{1,0:T(8,128)(2,1)S(1)} collective-permute-done((bf16[512,256]{1,0:T(8,128)(2,1)S(1)}, bf16[512,256]{1,0:T(8,128)(2,1)S(1)}, u32[]{:S(2)}, u32[]{:S(2)}) %collective-permute-start.3) | collective-permute-done | bytes 262176 | tf_op jit(solution)/shard_map/ppermute | solution.py:301
  23.8 0.0 collective-permute-done.6.refs_1_
  23.8 2.1 %collective-permute-done.7.refs_2_ = bf16[128,768]{1,0:T(8,128)(2,1)S(1)} collective-permute-done((bf16[128,768]{1,0:T(8,128)(2,1)}, bf16[128,768]{1,0:T(8,128)(2,1)S(1)}, u32[]{:S(2)}, u32[]{:S(2)}) %collective-permute-start.7) | collective-permute-done | bytes 196640 | tf_op jit(solution)/shard_map/ppermute | solution.py:297
  25.9 0.0 collective-permute-done.8.refs_3_
  25.9 0.5 collective-permute-start.11
  26.4 0.0 collective-permute-start.10
  26.4 0.5 collective-permute-start.9
  27.0 0.1 shard_map.78.refs_0_
  27.0 0.5 collective-permute-done.11.refs_6_
  27.6 0.4 collective-permute-done.10.refs_4_
  27.9 11.5 %shard_map.79 = (f32[2,4,384,256]{3,2,1,0:T(8,128)S(1)}, f32[2,4,384,128]{3,2,1,0:T(8,128)S(1)}) custom-call(s32[16]{0:T(128)S(1)} %get-tuple-element.60.table_ref, f32[12]{0:T(128)S(1)} %get-tuple-element.61.factor_ref, bf16[4,128,768]{2,1,0:T(8,128)(2,1)S(1)} %shard_map.78.refs_0_, bf16[512,256]{1,0:T(8,128)(2,1)S(1)} %bitcast.5, ...), custom_call_target="tpu_custom_call" | custom-call | flops 603979776 | bytes 1572864 | tf_op jit(solution)/shard_map/pallas_call | solution.py:277
  39.4 0.0 collective-permute-done.9.refs_3_
  39.4 0.4 collective-permute-start.12
  39.9 1.2 %collective-permute-done.12.refs_4_ = bf16[512,256]{1,0:T(8,128)(2,1)S(1)} collective-permute-done((bf16[512,256]{1,0:T(8,128)(2,1)S(1)}, bf16[512,256]{1,0:T(8,128)(2,1)S(1)}, u32[]{:S(2)}, u32[]{:S(2)}) %collective-permute-start.12) | collective-permute-done | bytes 262176 | tf_op jit(solution)/shard_map/ppermute | solution.py:304
  41.0 2.4 %shard_map.80 = (bf16[128,768]{1,0:T(8,128)(2,1)S(1)}, bf16[128,768]{1,0:T(8,128)(2,1)S(1)}, bf16[128,768]{1,0:T(8,128)(2,1)S(1)}, bf16[128,768]{1,0:T(8,128)(2,...) custom-call(s32[16]{0:T(128)S(1)} %get-tuple-element.60.table_ref, ...), custom_call_target="tpu_custom_call", output_to_operand_aliasing={{4}: (3, {}), {5}: (4, {})} | custom-call | flops 201326592 | bytes 1572864 | tf_op jit(solution)/shard_map/pallas_call | solution.py:277
  43.4 1.3 %collective-permute-start.13 = (bf16[128,768]{1,0:T(8,128)(2,1)S(1)}, bf16[128,768]{1,0:T(8,128)(2,1)S(1)}, u32[]{:S(2)}, u32[]{:S(2)}) collective-permute-start(bf16[128,768]{1,0:T(8,128)(2,1)S(1)} %get-tuple-element.76), channel_id=1, source_target_pairs={{0,6},{1,7},{2,4},{3,5},{4,2},{5,3},{6,0},{7,1},{8,14},{9,15},{10,... | collective-permute-start | bytes 589832 | tf_op jit(solution)/shard_map/ppermute | solution.py:297
  44.7 0.6 %collective-permute-start.14 = (bf16[128,768]{1,0:T(8,128)(2,1)S(1)}, bf16[128,768]{1,0:T(8,128)(2,1)S(1)}, u32[]{:S(2)}, u32[]{:S(2)}) collective-permute-start(bf16[128,768]{1,0:T(8,128)(2,1)S(1)} %get-tuple-element.77), channel_id=1, source_target_pairs={{0,4},{1,3},{2,6},{3,1},{4,0},{5,7},{6,2},{7,5},{8,12},{9,11},{10,... | collective-permute-start | bytes 589832 | tf_op jit(solution)/shard_map/ppermute | solution.py:297
  45.3 0.8 %collective-permute-start.15 = (bf16[128,768]{1,0:T(8,128)(2,1)S(1)}, bf16[128,768]{1,0:T(8,128)(2,1)S(1)}, u32[]{:S(2)}, u32[]{:S(2)}) collective-permute-start(bf16[128,768]{1,0:T(8,128)(2,1)S(1)} %get-tuple-element.78), channel_id=1, source_target_pairs={{0,2},{1,5},{2,0},{3,7},{4,6},{5,1},{6,4},{7,3},{8,10},{9,13},{10,... | collective-permute-start | bytes 589832 | tf_op jit(solution)/shard_map/ppermute | solution.py:297
  46.1 4.4 %collective-permute-done.13.refs_1_ = bf16[128,768]{1,0:T(8,128)(2,1)S(1)} collective-permute-done((bf16[128,768]{1,0:T(8,128)(2,1)S(1)}, bf16[128,768]{1,0:T(8,128)(2,1)S(1)}, u32[]{:S(2)}, u32[]{:S(2)}) %collective-permute-start.13) | collective-permute-done | bytes 196640 | tf_op jit(solution)/shard_map/ppermute | solution.py:297
  50.5 4.9 %collective-permute-done.14.refs_2_ = bf16[128,768]{1,0:T(8,128)(2,1)S(1)} collective-permute-done((bf16[128,768]{1,0:T(8,128)(2,1)S(1)}, bf16[128,768]{1,0:T(8,128)(2,1)S(1)}, u32[]{:S(2)}, u32[]{:S(2)}) %collective-permute-start.14) | collective-permute-done | bytes 196640 | tf_op jit(solution)/shard_map/ppermute | solution.py:297
  55.4 0.0 collective-permute-done.15.refs_3_
  55.4 0.9 %shard_map.81 = bf16[128,3072]{1,0:T(8,128)(2,1)} custom-call(bf16[128,768]{1,0:T(8,128)(2,1)S(1)} %get-tuple-element.75.refs_0_, bf16[128,768]{1,0:T(8,128)(2,1)S(1)} %collective-permute-done.13.refs_1_, bf16[128,768]{1,0:T(8,128)(2,1)S(1)} %collective-permute-done.14.refs_2_, bf16[128,768]{1,0:T(8,128)(2,1)S(1)} %collective-permute-done.15.refs_3_), custom_call_target="tpu_custom_call" | custom-call | tf_op jit(solution)/shard_map/pallas_call | solution.py:147
  (3 shorter events, 0.0 us)
Async XLA Ops:
  2.2 4.3 %collective-permute-start = (bf16[128,256]{1,0:T(8,128)(2,1)}, bf16[128,256]{1,0:T(8,128)(2,1)S(1)}, u32[]{:S(2)}, u32[]{:S(2)}) collective-permute-start(bf16[128,256]{1,0:T(8,128)(2,1)} %get-tuple-element.42), channel_id=1, source_target_pairs={{0,6},{1,7},{2,4},{3,5},{4,2},{5,3},{6,0},{7,1},{8,14},{9,15},{10,... | collective-permute-start | bytes 196616 | tf_op jit(solution)/shard_map/ppermute | solution.py:297
  4.4 3.9 %collective-permute-start.1 = (bf16[128,256]{1,0:T(8,128)(2,1)}, bf16[128,256]{1,0:T(8,128)(2,1)S(1)}, u32[]{:S(2)}, u32[]{:S(2)}) collective-permute-start(bf16[128,256]{1,0:T(8,128)(2,1)} %get-tuple-element.43), channel_id=1, source_target_pairs={{0,4},{1,3},{2,6},{3,1},{4,0},{5,7},{6,2},{7,5},{8,12},{9,11},{10,... | collective-permute-start | bytes 196616 | tf_op jit(solution)/shard_map/ppermute | solution.py:297
  4.7 3.7 %collective-permute-start.2 = (bf16[128,256]{1,0:T(8,128)(2,1)}, bf16[128,256]{1,0:T(8,128)(2,1)S(1)}, u32[]{:S(2)}, u32[]{:S(2)}) collective-permute-start(bf16[128,256]{1,0:T(8,128)(2,1)} %get-tuple-element.44), channel_id=1, source_target_pairs={{0,2},{1,5},{2,0},{3,7},{4,6},{5,1},{6,4},{7,3},{8,10},{9,13},{10,... | collective-permute-start | bytes 196616 | tf_op jit(solution)/shard_map/ppermute | solution.py:297
  4.9 0.8 %copy-start.1 = (bf16[128,256]{1,0:T(8,128)(2,1)S(1)}, bf16[128,256]{1,0:T(8,128)(2,1)}, u32[]{:S(2)}) copy-start(bf16[128,256]{1,0:T(8,128)(2,1)} %get-tuple-element.45.piece_ref) | copy-start | bytes 196612
  8.4 5.3 %collective-permute-start.5 = (bf16[512,256]{1,0:T(8,128)(2,1)S(1)}, bf16[512,256]{1,0:T(8,128)(2,1)S(1)}, u32[]{:S(2)}, u32[]{:S(2)}) collective-permute-start(bf16[512,256]{1,0:T(8,128)(2,1)S(1)} %bitcast.2), channel_id=1, source_target_pairs={{0,1},{1,0},{2,3},{3,2},{4,5},{5,4},{6,7},{7,6},{8,9},{9,8},{10,11... | collective-permute-start | bytes 786440 | tf_op jit(solution)/shard_map/ppermute | solution.py:304
  10.5 11.1 %collective-permute-start.4 = (bf16[512,256]{1,0:T(8,128)(2,1)S(1)}, bf16[512,256]{1,0:T(8,128)(2,1)S(1)}, u32[]{:S(2)}, u32[]{:S(2)}) collective-permute-start(bf16[512,256]{1,0:T(8,128)(2,1)S(1)} %bitcast.3), channel_id=1, source_target_pairs={{0,24},{4,28},{8,0},{12,4},{16,8},{20,12},{24,16},{28,20},{1,25},{... | collective-permute-start | bytes 786440 | tf_op jit(solution)/shard_map/ppermute | solution.py:301
  10.7 13.2 %collective-permute-start.3 = (bf16[512,256]{1,0:T(8,128)(2,1)S(1)}, bf16[512,256]{1,0:T(8,128)(2,1)S(1)}, u32[]{:S(2)}, u32[]{:S(2)}) collective-permute-start(bf16[512,256]{1,0:T(8,128)(2,1)S(1)} %bitcast.4), channel_id=1, source_target_pairs={{0,8},{4,12},{8,16},{12,20},{16,24},{20,28},{24,0},{28,4},{1,9},{5... | collective-permute-start | bytes 786440 | tf_op jit(solution)/shard_map/ppermute | solution.py:301
  13.8 10.1 %collective-permute-start.6 = (bf16[128,768]{1,0:T(8,128)(2,1)}, bf16[128,768]{1,0:T(8,128)(2,1)S(1)}, u32[]{:S(2)}, u32[]{:S(2)}) collective-permute-start(bf16[128,768]{1,0:T(8,128)(2,1)} %get-tuple-element.54), channel_id=1, source_target_pairs={{0,6},{1,7},{2,4},{3,5},{4,2},{5,3},{6,0},{7,1},{8,14},{9,15},{10,... | collective-permute-start | bytes 589832 | tf_op jit(solution)/shard_map/ppermute | solution.py:297
  14.9 11.0 %collective-permute-start.7 = (bf16[128,768]{1,0:T(8,128)(2,1)}, bf16[128,768]{1,0:T(8,128)(2,1)S(1)}, u32[]{:S(2)}, u32[]{:S(2)}) collective-permute-start(bf16[128,768]{1,0:T(8,128)(2,1)} %get-tuple-element.55), channel_id=1, source_target_pairs={{0,4},{1,3},{2,6},{3,1},{4,0},{5,7},{6,2},{7,5},{8,12},{9,11},{10,... | collective-permute-start | bytes 589832 | tf_op jit(solution)/shard_map/ppermute | solution.py:297
  16.2 9.8 %collective-permute-start.8 = (bf16[128,768]{1,0:T(8,128)(2,1)}, bf16[128,768]{1,0:T(8,128)(2,1)S(1)}, u32[]{:S(2)}, u32[]{:S(2)}) collective-permute-start(bf16[128,768]{1,0:T(8,128)(2,1)} %get-tuple-element.56), channel_id=1, source_target_pairs={{0,2},{1,5},{2,0},{3,7},{4,6},{5,1},{6,4},{7,3},{8,10},{9,13},{10,... | collective-permute-start | bytes 589832 | tf_op jit(solution)/shard_map/ppermute | solution.py:297
  16.4 0.7 %copy-start.2 = (f32[8,24]{1,0:T(8,128)S(1)}, f32[8,24]{1,0:T(8,128)}, u32[]{:S(2)}) copy-start(f32[8,24]{1,0:T(8,128)} %temps_ref.1) | copy-start | bytes 2308
  17.1 0.7 %copy-start.3 = (s32[8,4]{0,1:T(4,128)S(1)}, s32[8,4]{0,1:T(4,128)}, u32[]{:S(2)}) copy-start(s32[8,4]{0,1:T(4,128)} %param.12) | copy-start | bytes 388
  17.8 0.7 %copy-start.4 = (s32[8]{0:T(128)S(1)}, s32[8]{0:T(128)}, u32[]{:S(2)}) copy-start(s32[8]{0:T(128)} %levels_ref.1) | copy-start | bytes 100
  18.4 0.7 %copy-start.5 = (s32[8]{0:T(128)S(1)}, s32[8]{0:T(128)}, u32[]{:S(2)}) copy-start(s32[8]{0:T(128)} %counts_ref.1) | copy-start | bytes 100
  20.6 0.9 %copy-start = (bf16[128,768]{1,0:T(8,128)(2,1)S(1)}, bf16[128,768]{1,0:T(8,128)(2,1)}, u32[]{:S(2)}) copy-start(bf16[128,768]{1,0:T(8,128)(2,1)} %get-tuple-element.57.piece_ref) | copy-start | bytes 589828
  25.9 1.7 %collective-permute-start.11 = (bf16[512,256]{1,0:T(8,128)(2,1)S(1)}, bf16[512,256]{1,0:T(8,128)(2,1)S(1)}, u32[]{:S(2)}, u32[]{:S(2)}) collective-permute-start(bf16[512,256]{1,0:T(8,128)(2,1)S(1)} %collective-permute-done.4.refs_5_), channel_id=1, source_target_pairs={{0,1},{1,0},{2,3},{3,2},{4,5},{5,4},{6,7},{7,6},{8,9},{9,8},{10,11... | collective-permute-start | bytes 786440 | tf_op jit(solution)/shard_map/ppermute | solution.py:304
  26.4 1.5 %collective-permute-start.10 = (bf16[512,256]{1,0:T(8,128)(2,1)S(1)}, bf16[512,256]{1,0:T(8,128)(2,1)S(1)}, u32[]{:S(2)}, u32[]{:S(2)}) collective-permute-start(bf16[512,256]{1,0:T(8,128)(2,1)S(1)} %collective-permute-done.3.refs_3_), channel_id=1, source_target_pairs={{0,1},{1,0},{2,3},{3,2},{4,5},{5,4},{6,7},{7,6},{8,9},{9,8},{10,11... | collective-permute-start | bytes 786440 | tf_op jit(solution)/shard_map/ppermute | solution.py:304
  26.4 13.0 %collective-permute-start.9 = (bf16[512,256]{1,0:T(8,128)(2,1)S(1)}, bf16[512,256]{1,0:T(8,128)(2,1)S(1)}, u32[]{:S(2)}, u32[]{:S(2)}) collective-permute-start(bf16[512,256]{1,0:T(8,128)(2,1)S(1)} %collective-permute-done.3.refs_3_), channel_id=1, source_target_pairs={{0,8},{4,12},{8,16},{12,20},{16,24},{20,28},{24,0},{28,4},{1,9},{5... | collective-permute-start | bytes 786440 | tf_op jit(solution)/shard_map/ppermute | solution.py:301
  39.4 1.6 %collective-permute-start.12 = (bf16[512,256]{1,0:T(8,128)(2,1)S(1)}, bf16[512,256]{1,0:T(8,128)(2,1)S(1)}, u32[]{:S(2)}, u32[]{:S(2)}) collective-permute-start(bf16[512,256]{1,0:T(8,128)(2,1)S(1)} %collective-permute-done.9.refs_3_), channel_id=1, source_target_pairs={{0,1},{1,0},{2,3},{3,2},{4,5},{5,4},{6,7},{7,6},{8,9},{9,8},{10,11... | collective-permute-start | bytes 786440 | tf_op jit(solution)/shard_map/ppermute | solution.py:304
  43.4 7.1 %collective-permute-start.13 = (bf16[128,768]{1,0:T(8,128)(2,1)S(1)}, bf16[128,768]{1,0:T(8,128)(2,1)S(1)}, u32[]{:S(2)}, u32[]{:S(2)}) collective-permute-start(bf16[128,768]{1,0:T(8,128)(2,1)S(1)} %get-tuple-element.76), channel_id=1, source_target_pairs={{0,6},{1,7},{2,4},{3,5},{4,2},{5,3},{6,0},{7,1},{8,14},{9,15},{10,... | collective-permute-start | bytes 589832 | tf_op jit(solution)/shard_map/ppermute | solution.py:297
  44.7 10.7 %collective-permute-start.14 = (bf16[128,768]{1,0:T(8,128)(2,1)S(1)}, bf16[128,768]{1,0:T(8,128)(2,1)S(1)}, u32[]{:S(2)}, u32[]{:S(2)}) collective-permute-start(bf16[128,768]{1,0:T(8,128)(2,1)S(1)} %get-tuple-element.77), channel_id=1, source_target_pairs={{0,4},{1,3},{2,6},{3,1},{4,0},{5,7},{6,2},{7,5},{8,12},{9,11},{10,... | collective-permute-start | bytes 589832 | tf_op jit(solution)/shard_map/ppermute | solution.py:297
  45.3 10.1 %collective-permute-start.15 = (bf16[128,768]{1,0:T(8,128)(2,1)S(1)}, bf16[128,768]{1,0:T(8,128)(2,1)S(1)}, u32[]{:S(2)}, u32[]{:S(2)}) collective-permute-start(bf16[128,768]{1,0:T(8,128)(2,1)S(1)} %get-tuple-element.78), channel_id=1, source_target_pairs={{0,2},{1,5},{2,0},{3,7},{4,6},{5,1},{6,4},{7,3},{8,10},{9,13},{10,... | collective-permute-start | bytes 589832 | tf_op jit(solution)/shard_map/ppermute | solution.py:297

commit v9 on v8

--- a/solution.py
+++ b/solution.py
@@ -174,29 +174,32 @@
 
     block_rows = half // 2
     index = lax.broadcasted_iota(jnp.int32, (block_rows, HD), 0)
+    def prepare(slab, x, count):
+        at = x * half
+        spare = slab[0][at : at + 16, :HD].astype(jnp.float32)[0:1]
+        for side, ref in enumerate(slab):
+            owner = core ^ side
+            for n in range(2):
+                values = ref[at + n * block_rows : at + (n + 1) * block_rows, :]
+                keys = values[:, :HD].astype(jnp.float32)
+                values = values[:, HD:]
+                ones = jnp.ones_like(values)
+                to = side * block_rows
+                if n:
+                    keep = (2 + owner) * block_rows + index < count
+                    keys = jnp.where(keep, keys, spare)
+                    values = jnp.where(keep, values.astype(jnp.float32), 0.0).astype(jnp.bfloat16)
+                    ones = jnp.where(keep, 1.0, 0.0).astype(jnp.bfloat16)
+                    to = (2 + owner) * block_rows
+                to = pl.ds(pl.multiple_of(to, block_rows), block_rows)
+                key_ref[x, :, to] = jnp.transpose(keys).astype(jnp.bfloat16)
+                value_ref[x, to, :HD] = values
+                value_ref[x, to, HD:] = ones
+
     for slab, back in zip(slabs, backs):
         for x in range(2):
             count = jnp.maximum(table_ref[4 * back + 2 * x], table_ref[4 * back + 2 * x + 1])
-            at = x * half
-            spare = slab[0][at : at + 16, :HD].astype(jnp.float32)[0:1]
-            for side, ref in enumerate(slab):
-                owner = core ^ side
-                for n in range(2):
-                    values = ref[at + n * block_rows : at + (n + 1) * block_rows, :]
-                    keys = values[:, :HD].astype(jnp.float32)
-                    values = values[:, HD:]
-                    ones = jnp.ones_like(values)
-                    to = side * block_rows
-                    if n:
-                        keep = (2 + owner) * block_rows + index < count
-                        keys = jnp.where(keep, keys, spare)
-                        values = jnp.where(keep, values.astype(jnp.float32), 0.0).astype(jnp.bfloat16)
-                        ones = jnp.where(keep, 1.0, 0.0).astype(jnp.bfloat16)
-                        to = (2 + owner) * block_rows
-                    to = pl.ds(pl.multiple_of(to, block_rows), block_rows)
-                    key_ref[x, :, to] = jnp.transpose(keys).astype(jnp.bfloat16)
-                    value_ref[x, to, :HD] = values
-                    value_ref[x, to, HD:] = ones
+            pl.when(count > 0)(functools.partial(prepare, slab, x, count))
 
         @pl.loop(0, 4)
         def _(turn):
@@ -311,15 +314,20 @@
     tables = tabulate(spans // 2, levels, temps, jnp.transpose(ctx_list), counts)
     slabs, moved, mine, tables = lax.optimization_barrier((slabs, exchange(q_pieces)[1:], hold(q_pieces[0]), tables))
     q = gather([mine, *moved])
-    stage = [0, 1, last]
-    sides = [(slabs[b], near(slabs[b]) if b else other) for b in stage]
+    stage = [0, 1]
+    sides = [(own, other), (slabs[1], near(slabs[1]))]
+    farthest = [(slabs[last], near(slabs[last]))]
     state = None
     for back in range(2, last):
         slab = up(slabs[back - 1], 1)
         state = attend(tables, q, state, sides, stage)
         slabs[back], state = lax.optimization_barrier((slab, state))
+        other = near(slabs[back])
+        if back == 2:
+            state = attend(tables, q, state, farthest, [last])
+            other, state = lax.optimization_barrier((other, state))
         stage = [back]
-        sides = [(slabs[back], near(slabs[back]))]
+        sides = [(slabs[back], other)]
     out = attend(tables, q, state, sides, stage, True)
     return join(exchange(out[:PEERS]))
 

time: 57.4 us -> 54.4 us (0.948); the launches traced: 56.3 us -> 54 us
  Pallas kernels: 18.6 us -> 16.8 us
  waiting for transfers between devices: 18.3 us -> 17 us
  starting transfers between devices: 14.9 us -> 15.5 us
    ppermute x4, waiting for transfers between devices: 2.08 us -> 0.28 us  [near(): return lax.ppermute(a, 'ctx', other_core)]
    pallas_call x2 -> x3, Pallas kernels: 13.8 us -> 12.1 us  [attend(): pl.pallas_call(functools.partial(attend_kernel, backs, first, final), out...]
    ppermute x4, starting transfers between devices: 3.03 us -> 3.72 us  [near(): return lax.ppermute(a, 'ctx', other_core)]
  transfers between devices with their start and end apart: 16 -> 16, of which waited for: 10 -> 9; matrix products, arithmetic and copies ran while one was open for 0% -> 0% of each run, Pallas kernels for 23% -> 18%
where the time goes in v9:
time: 54.4 us; the launch traced here: 54 us
  waiting for transfers between devices  17 us (31%)
  Pallas kernels  16.8 us (31%)
  starting transfers between devices  15.5 us (28%)
  local copies, waits for them, and re-layouts  4.44 us (8%)
    ppermute x9, waiting for transfers between devices, exchange(): moved.append(lax.ppermute(piece, ('span', 'ctx'), pairs))  14 us
    pallas_call x3, Pallas kernels, attend(): pl.pallas_call(functools.partial(attend_kernel, backs, first, final), out...  12.1 us
    ppermute x9, starting transfers between devices, exchange(): moved.append(lax.ppermute(piece, ('span', 'ctx'), pairs))  8.08 us
    unnamed x12, local copies, waits for them, and re-layouts  4.44 us
    ppermute x3, starting transfers between devices, up(): lax.ppermute(a, 'span', [(s, (s + 2 * steps) % spans) for s in range(span...  3.74 us
    ppermute x4, starting transfers between devices, near(): return lax.ppermute(a, 'ctx', other_core)  3.72 us
    ppermute x3, waiting for transfers between devices, up(): lax.ppermute(a, 'span', [(s, (s + 2 * steps) % spans) for s in range(span...  2.7 us
    pallas_call x1, Pallas kernels, begin(): pl.pallas_call(begin_kernel, out_shape=[jax.ShapeDtypeStruct(shape, jnp.b...  2.19 us
  transfers between devices with their start and end apart: 16, of which 9 were waited for; matrix products, arithmetic and copies ran while one was open for 0% of the time, Pallas kernels for 18%

profile of v9, /device:TPU:25, one launch (start us, length us, event | category | flops | bytes accessed | tf_op | source)
XLA Modules:
  0.0 54.0 jit_solution(13355005643442507602)
XLA Ops:
  0.0 2.2 %shard_map.73 = (bf16[128,256]{1,0:T(8,128)(2,1)}, bf16[128,256]{1,0:T(8,128)(2,1)}, bf16[128,256]{1,0:T(8,128)(2,1)}, bf16[128,256]{1,0:T(8,128)(2,1)}, bf16[12...) custom-call(bf16[128,512]{1,0:T(8,128)(2,1)} %keys_ref.1, ...), custom_call_target="tpu_custom_call" | custom-call | tf_op jit(solution)/shard_map/pallas_call | solution.py:92
  2.2 2.2 %collective-permute-start = (bf16[128,256]{1,0:T(8,128)(2,1)}, bf16[128,256]{1,0:T(8,128)(2,1)S(1)}, u32[]{:S(2)}, u32[]{:S(2)}) collective-permute-start(bf16[128,256]{1,0:T(8,128)(2,1)} %get-tuple-element.46), channel_id=1, source_target_pairs={{0,6},{1,7},{2,4},{3,5},{4,2},{5,3},{6,0},{7,1},{8,14},{9,15},{10,... | collective-permute-start | bytes 196616 | tf_op jit(solution)/shard_map/ppermute | solution.py:300
  4.4 0.2 collective-permute-start.1
  4.7 0.3 collective-permute-start.2
  4.9 0.0 copy-start.1
  4.9 0.8 %copy-done.1 = bf16[128,256]{1,0:T(8,128)(2,1)S(1)} copy-done((bf16[128,256]{1,0:T(8,128)(2,1)S(1)}, bf16[128,256]{1,0:T(8,128)(2,1)}, u32[]{:S(2)}) %copy-start.1) | copy-done | bytes 65560
  5.8 0.7 %collective-permute-done.refs_1_ = bf16[128,256]{1,0:T(8,128)(2,1)S(1)} collective-permute-done((bf16[128,256]{1,0:T(8,128)(2,1)}, bf16[128,256]{1,0:T(8,128)(2,1)S(1)}, u32[]{:S(2)}, u32[]{:S(2)}) %collective-permute-start) | collective-permute-done | bytes 65568 | tf_op jit(solution)/shard_map/ppermute | solution.py:300
  6.5 1.8 %collective-permute-done.1.refs_2_ = bf16[128,256]{1,0:T(8,128)(2,1)S(1)} collective-permute-done((bf16[128,256]{1,0:T(8,128)(2,1)}, bf16[128,256]{1,0:T(8,128)(2,1)S(1)}, u32[]{:S(2)}, u32[]{:S(2)}) %collective-permute-start.1) | collective-permute-done | bytes 65568 | tf_op jit(solution)/shard_map/ppermute | solution.py:300
  8.3 0.1 collective-permute-done.2.refs_3_
  8.4 2.1 %collective-permute-start.5 = (bf16[512,256]{1,0:T(8,128)(2,1)S(1)}, bf16[512,256]{1,0:T(8,128)(2,1)S(1)}, u32[]{:S(2)}, u32[]{:S(2)}) collective-permute-start(bf16[512,256]{1,0:T(8,128)(2,1)S(1)} %bitcast.2), channel_id=1, source_target_pairs={{0,1},{1,0},{2,3},{3,2},{4,5},{5,4},{6,7},{7,6},{8,9},{9,8},{10,11... | collective-permute-start | bytes 786440 | tf_op jit(solution)/shard_map/ppermute | solution.py:307
  10.5 0.2 collective-permute-start.4
  10.7 3.1 %collective-permute-start.3 = (bf16[512,256]{1,0:T(8,128)(2,1)S(1)}, bf16[512,256]{1,0:T(8,128)(2,1)S(1)}, u32[]{:S(2)}, u32[]{:S(2)}) collective-permute-start(bf16[512,256]{1,0:T(8,128)(2,1)S(1)} %bitcast.4), channel_id=1, source_target_pairs={{0,8},{4,12},{8,16},{12,20},{16,24},{20,28},{24,0},{28,4},{1,9},{5... | collective-permute-start | bytes 786440 | tf_op jit(solution)/shard_map/ppermute | solution.py:304
  13.8 0.0 collective-permute-done.5.refs_2_
  13.8 1.2 %collective-permute-start.6 = (bf16[128,768]{1,0:T(8,128)(2,1)}, bf16[128,768]{1,0:T(8,128)(2,1)S(1)}, u32[]{:S(2)}, u32[]{:S(2)}) collective-permute-start(bf16[128,768]{1,0:T(8,128)(2,1)} %get-tuple-element.58), channel_id=1, source_target_pairs={{0,6},{1,7},{2,4},{3,5},{4,2},{5,3},{6,0},{7,1},{8,14},{9,15},{10,... | collective-permute-start | bytes 589832 | tf_op jit(solution)/shard_map/ppermute | solution.py:300
  14.9 1.2 %collective-permute-start.7 = (bf16[128,768]{1,0:T(8,128)(2,1)}, bf16[128,768]{1,0:T(8,128)(2,1)S(1)}, u32[]{:S(2)}, u32[]{:S(2)}) collective-permute-start(bf16[128,768]{1,0:T(8,128)(2,1)} %get-tuple-element.59), channel_id=1, source_target_pairs={{0,4},{1,3},{2,6},{3,1},{4,0},{5,7},{6,2},{7,5},{8,12},{9,11},{10,... | collective-permute-start | bytes 589832 | tf_op jit(solution)/shard_map/ppermute | solution.py:300
  16.2 0.3 collective-permute-start.8
  16.4 0.0 copy-start.2
  16.4 0.7 %copy-done.2 = f32[8,24]{1,0:T(8,128)S(1)} copy-done((f32[8,24]{1,0:T(8,128)S(1)}, f32[8,24]{1,0:T(8,128)}, u32[]{:S(2)}) %copy-start.2) | copy-done | bytes 792
  17.1 0.0 copy-start.3
  17.1 0.7 %copy-done.3 = s32[8,4]{0,1:T(4,128)S(1)} copy-done((s32[8,4]{0,1:T(4,128)S(1)}, s32[8,4]{0,1:T(4,128)}, u32[]{:S(2)}) %copy-start.3) | copy-done | bytes 152
  17.8 0.0 copy-start.4
  17.8 0.7 %copy-done.4 = s32[8]{0:T(128)S(1)} copy-done((s32[8]{0:T(128)S(1)}, s32[8]{0:T(128)}, u32[]{:S(2)}) %copy-start.4) | copy-done | bytes 56
  18.4 0.0 copy-start.5
  18.4 0.7 %copy-done.5 = s32[8]{0:T(128)S(1)} copy-done((s32[8]{0:T(128)S(1)}, s32[8]{0:T(128)}, u32[]{:S(2)}) %copy-start.5) | copy-done | bytes 56
  19.1 1.5 %shard_map.77 = (s32[16]{0:T(128)S(1)}, f32[12]{0:T(128)S(1)}) custom-call(s32[8]{0:T(128)S(1)} %copy-done.4, f32[8,24]{1,0:T(8,128)S(1)} %copy-done.2, s32[4,8]{1,0:T(4,128)S(1)} %bitcast.6, s32[8]{0:T(128)S(1)} %copy-done.5), custom_call_target="tpu_custom_call" | custom-call | tf_op jit(solution)/shard_map/pallas_call | solution.py:57
  20.6 0.0 copy-start
  20.6 0.9 %copy-done = bf16[128,768]{1,0:T(8,128)(2,1)S(1)} copy-done((bf16[128,768]{1,0:T(8,128)(2,1)S(1)}, bf16[128,768]{1,0:T(8,128)(2,1)}, u32[]{:S(2)}) %copy-start) | copy-done | bytes 196632
  21.6 0.0 collective-permute-done.4.refs_3_
  21.6 2.2 %collective-permute-done.3.refs_3_ = bf16[512,256]{1,0:T(8,128)(2,1)S(1)} collective-permute-done((bf16[512,256]{1,0:T(8,128)(2,1)S(1)}, bf16[512,256]{1,0:T(8,128)(2,1)S(1)}, u32[]{:S(2)}, u32[]{:S(2)}) %collective-permute-start.3) | collective-permute-done | bytes 262176 | tf_op jit(solution)/shard_map/ppermute | solution.py:304
  23.8 0.0 collective-permute-done.6.refs_1_
  23.8 2.1 %collective-permute-done.7.refs_2_ = bf16[128,768]{1,0:T(8,128)(2,1)S(1)} collective-permute-done((bf16[128,768]{1,0:T(8,128)(2,1)}, bf16[128,768]{1,0:T(8,128)(2,1)S(1)}, u32[]{:S(2)}, u32[]{:S(2)}) %collective-permute-start.7) | collective-permute-done | bytes 196640 | tf_op jit(solution)/shard_map/ppermute | solution.py:300
  25.9 0.0 collective-permute-done.8.refs_3_
  25.9 0.5 collective-permute-start.10
  26.4 0.5 collective-permute-start.9
  26.9 0.3 collective-permute-start.12
  27.2 0.1 shard_map.78.refs_0_
  27.3 0.3 collective-permute-done.10.refs_4_
  27.6 6.3 %shard_map.79 = (f32[2,4,384,256]{3,2,1,0:T(8,128)S(1)}, f32[2,4,384,128]{3,2,1,0:T(8,128)S(1)}) custom-call(s32[16]{0:T(128)S(1)} %get-tuple-element.64.table_ref, f32[12]{0:T(128)S(1)} %get-tuple-element.65.factor_ref, bf16[4,128,768]{2,1,0:T(8,128)(2,1)S(1)} %shard_map.78.refs_0_, bf16[512,256]{1,0:T(8,128)(2,1)S(1)} %bitcast.5, ...), custom_call_target="tpu_custom_call" | custom-call | flops 402653184 | bytes 1572864 | tf_op jit(solution)/shard_map/pallas_call | solution.py:280
  33.9 0.5 collective-permute-done.9.refs_3_
  34.3 0.8 %collective-permute-start.11 = (bf16[512,256]{1,0:T(8,128)(2,1)S(1)}, bf16[512,256]{1,0:T(8,128)(2,1)S(1)}, u32[]{:S(2)}, u32[]{:S(2)}) collective-permute-start(bf16[512,256]{1,0:T(8,128)(2,1)S(1)} %collective-permute-done.9.refs_3_), channel_id=1, source_target_pairs={{0,1},{1,0},{2,3},{3,2},{4,5},{5,4},{6,7},{7,6},{8,9},{9,8},{10,11... | collective-permute-start | bytes 786440 | tf_op jit(solution)/shard_map/ppermute | solution.py:307
  35.1 0.0 collective-permute-done.12.refs_4_
  35.1 2.0 %shard_map.80 = (f32[2,4,384,256]{3,2,1,0:T(8,128)S(1)}, f32[2,4,384,128]{3,2,1,0:T(8,128)S(1)}) custom-call(s32[16]{0:T(128)S(1)} %get-tuple-element.64.table_ref, f32[12]{0:T(128)S(1)} %get-tuple-element.65.factor_ref, bf16[4,128,768]{2,1,0:T(8,128)(2,1)S(1)} %shard_map.78.refs_0_, ...), custom_call_target="tpu_custom_call", output_to_operand_aliasing={{0}: (3, {}), {1}: (4, {})} | custom-call | flops 201326592 | bytes 1572864 | tf_op jit(solution)/shard_map/pallas_call | solution.py:280
  37.2 0.0 collective-permute-done.11.refs_4_
  37.2 3.8 %shard_map.81 = (bf16[128,768]{1,0:T(8,128)(2,1)S(1)}, bf16[128,768]{1,0:T(8,128)(2,1)S(1)}, bf16[128,768]{1,0:T(8,128)(2,1)S(1)}, bf16[128,768]{1,0:T(8,128)(2,...) custom-call(s32[16]{0:T(128)S(1)} %get-tuple-element.64.table_ref, ...), custom_call_target="tpu_custom_call", output_to_operand_aliasing={{4}: (3, {}), {5}: (4, {})} | custom-call | flops 201326592 | bytes 1572864 | tf_op jit(solution)/shard_map/pallas_call | solution.py:280
  41.0 1.3 %collective-permute-start.13 = (bf16[128,768]{1,0:T(8,128)(2,1)S(1)}, bf16[128,768]{1,0:T(8,128)(2,1)S(1)}, u32[]{:S(2)}, u32[]{:S(2)}) collective-permute-start(bf16[128,768]{1,0:T(8,128)(2,1)S(1)} %get-tuple-element.84), channel_id=1, source_target_pairs={{0,6},{1,7},{2,4},{3,5},{4,2},{5,3},{6,0},{7,1},{8,14},{9,15},{10,... | collective-permute-start | bytes 589832 | tf_op jit(solution)/shard_map/ppermute | solution.py:300
  42.3 0.4 collective-permute-start.14
  42.7 0.9 %collective-permute-start.15 = (bf16[128,768]{1,0:T(8,128)(2,1)S(1)}, bf16[128,768]{1,0:T(8,128)(2,1)S(1)}, u32[]{:S(2)}, u32[]{:S(2)}) collective-permute-start(bf16[128,768]{1,0:T(8,128)(2,1)S(1)} %get-tuple-element.86), channel_id=1, source_target_pairs={{0,2},{1,5},{2,0},{3,7},{4,6},{5,1},{6,4},{7,3},{8,10},{9,13},{10,... | collective-permute-start | bytes 589832 | tf_op jit(solution)/shard_map/ppermute | solution.py:300
  43.7 4.8 %collective-permute-done.13.refs_1_ = bf16[128,768]{1,0:T(8,128)(2,1)S(1)} collective-permute-done((bf16[128,768]{1,0:T(8,128)(2,1)S(1)}, bf16[128,768]{1,0:T(8,128)(2,1)S(1)}, u32[]{:S(2)}, u32[]{:S(2)}) %collective-permute-start.13) | collective-permute-done | bytes 196640 | tf_op jit(solution)/shard_map/ppermute | solution.py:300
  48.5 4.5 %collective-permute-done.14.refs_2_ = bf16[128,768]{1,0:T(8,128)(2,1)S(1)} collective-permute-done((bf16[128,768]{1,0:T(8,128)(2,1)S(1)}, bf16[128,768]{1,0:T(8,128)(2,1)S(1)}, u32[]{:S(2)}, u32[]{:S(2)}) %collective-permute-start.14) | collective-permute-done | bytes 196640 | tf_op jit(solution)/shard_map/ppermute | solution.py:300
  53.0 0.0 collective-permute-done.15.refs_3_
  53.0 0.9 %shard_map.82 = bf16[128,3072]{1,0:T(8,128)(2,1)} custom-call(bf16[128,768]{1,0:T(8,128)(2,1)S(1)} %get-tuple-element.83.refs_0_, bf16[128,768]{1,0:T(8,128)(2,1)S(1)} %collective-permute-done.13.refs_1_, bf16[128,768]{1,0:T(8,128)(2,1)S(1)} %collective-permute-done.14.refs_2_, bf16[128,768]{1,0:T(8,128)(2,1)S(1)} %collective-permute-done.15.refs_3_), custom_call_target="tpu_custom_call" | custom-call | tf_op jit(solution)/shard_map/pallas_call | solution.py:147
  (3 shorter events, 0.0 us)
Async XLA Ops:
  2.2 4.3 %collective-permute-start = (bf16[128,256]{1,0:T(8,128)(2,1)}, bf16[128,256]{1,0:T(8,128)(2,1)S(1)}, u32[]{:S(2)}, u32[]{:S(2)}) collective-permute-start(bf16[128,256]{1,0:T(8,128)(2,1)} %get-tuple-element.46), channel_id=1, source_target_pairs={{0,6},{1,7},{2,4},{3,5},{4,2},{5,3},{6,0},{7,1},{8,14},{9,15},{10,... | collective-permute-start | bytes 196616 | tf_op jit(solution)/shard_map/ppermute | solution.py:300
  4.4 3.9 %collective-permute-start.1 = (bf16[128,256]{1,0:T(8,128)(2,1)}, bf16[128,256]{1,0:T(8,128)(2,1)S(1)}, u32[]{:S(2)}, u32[]{:S(2)}) collective-permute-start(bf16[128,256]{1,0:T(8,128)(2,1)} %get-tuple-element.47), channel_id=1, source_target_pairs={{0,4},{1,3},{2,6},{3,1},{4,0},{5,7},{6,2},{7,5},{8,12},{9,11},{10,... | collective-permute-start | bytes 196616 | tf_op jit(solution)/shard_map/ppermute | solution.py:300
  4.7 3.7 %collective-permute-start.2 = (bf16[128,256]{1,0:T(8,128)(2,1)}, bf16[128,256]{1,0:T(8,128)(2,1)S(1)}, u32[]{:S(2)}, u32[]{:S(2)}) collective-permute-start(bf16[128,256]{1,0:T(8,128)(2,1)} %get-tuple-element.48), channel_id=1, source_target_pairs={{0,2},{1,5},{2,0},{3,7},{4,6},{5,1},{6,4},{7,3},{8,10},{9,13},{10,... | collective-permute-start | bytes 196616 | tf_op jit(solution)/shard_map/ppermute | solution.py:300
  4.9 0.8 %copy-start.1 = (bf16[128,256]{1,0:T(8,128)(2,1)S(1)}, bf16[128,256]{1,0:T(8,128)(2,1)}, u32[]{:S(2)}) copy-start(bf16[128,256]{1,0:T(8,128)(2,1)} %get-tuple-element.49.piece_ref) | copy-start | bytes 196612
  8.4 5.3 %collective-permute-start.5 = (bf16[512,256]{1,0:T(8,128)(2,1)S(1)}, bf16[512,256]{1,0:T(8,128)(2,1)S(1)}, u32[]{:S(2)}, u32[]{:S(2)}) collective-permute-start(bf16[512,256]{1,0:T(8,128)(2,1)S(1)} %bitcast.2), channel_id=1, source_target_pairs={{0,1},{1,0},{2,3},{3,2},{4,5},{5,4},{6,7},{7,6},{8,9},{9,8},{10,11... | collective-permute-start | bytes 786440 | tf_op jit(solution)/shard_map/ppermute | solution.py:307
  10.5 11.1 %collective-permute-start.4 = (bf16[512,256]{1,0:T(8,128)(2,1)S(1)}, bf16[512,256]{1,0:T(8,128)(2,1)S(1)}, u32[]{:S(2)}, u32[]{:S(2)}) collective-permute-start(bf16[512,256]{1,0:T(8,128)(2,1)S(1)} %bitcast.3), channel_id=1, source_target_pairs={{0,24},{4,28},{8,0},{12,4},{16,8},{20,12},{24,16},{28,20},{1,25},{... | collective-permute-start | bytes 786440 | tf_op jit(solution)/shard_map/ppermute | solution.py:304
  10.7 13.2 %collective-permute-start.3 = (bf16[512,256]{1,0:T(8,128)(2,1)S(1)}, bf16[512,256]{1,0:T(8,128)(2,1)S(1)}, u32[]{:S(2)}, u32[]{:S(2)}) collective-permute-start(bf16[512,256]{1,0:T(8,128)(2,1)S(1)} %bitcast.4), channel_id=1, source_target_pairs={{0,8},{4,12},{8,16},{12,20},{16,24},{20,28},{24,0},{28,4},{1,9},{5... | collective-permute-start | bytes 786440 | tf_op jit(solution)/shard_map/ppermute | solution.py:304
  13.8 10.1 %collective-permute-start.6 = (bf16[128,768]{1,0:T(8,128)(2,1)}, bf16[128,768]{1,0:T(8,128)(2,1)S(1)}, u32[]{:S(2)}, u32[]{:S(2)}) collective-permute-start(bf16[128,768]{1,0:T(8,128)(2,1)} %get-tuple-element.58), channel_id=1, source_target_pairs={{0,6},{1,7},{2,4},{3,5},{4,2},{5,3},{6,0},{7,1},{8,14},{9,15},{10,... | collective-permute-start | bytes 589832 | tf_op jit(solution)/shard_map/ppermute | solution.py:300
  14.9 11.0 %collective-permute-start.7 = (bf16[128,768]{1,0:T(8,128)(2,1)}, bf16[128,768]{1,0:T(8,128)(2,1)S(1)}, u32[]{:S(2)}, u32[]{:S(2)}) collective-permute-start(bf16[128,768]{1,0:T(8,128)(2,1)} %get-tuple-element.59), channel_id=1, source_target_pairs={{0,4},{1,3},{2,6},{3,1},{4,0},{5,7},{6,2},{7,5},{8,12},{9,11},{10,... | collective-permute-start | bytes 589832 | tf_op jit(solution)/shard_map/ppermute | solution.py:300
  16.2 9.8 %collective-permute-start.8 = (bf16[128,768]{1,0:T(8,128)(2,1)}, bf16[128,768]{1,0:T(8,128)(2,1)S(1)}, u32[]{:S(2)}, u32[]{:S(2)}) collective-permute-start(bf16[128,768]{1,0:T(8,128)(2,1)} %get-tuple-element.60), channel_id=1, source_target_pairs={{0,2},{1,5},{2,0},{3,7},{4,6},{5,1},{6,4},{7,3},{8,10},{9,13},{10,... | collective-permute-start | bytes 589832 | tf_op jit(solution)/shard_map/ppermute | solution.py:300
  16.4 0.7 %copy-start.2 = (f32[8,24]{1,0:T(8,128)S(1)}, f32[8,24]{1,0:T(8,128)}, u32[]{:S(2)}) copy-start(f32[8,24]{1,0:T(8,128)} %temps_ref.1) | copy-start | bytes 2308
  17.1 0.7 %copy-start.3 = (s32[8,4]{0,1:T(4,128)S(1)}, s32[8,4]{0,1:T(4,128)}, u32[]{:S(2)}) copy-start(s32[8,4]{0,1:T(4,128)} %param.12) | copy-start | bytes 388
  17.8 0.7 %copy-start.4 = (s32[8]{0:T(128)S(1)}, s32[8]{0:T(128)}, u32[]{:S(2)}) copy-start(s32[8]{0:T(128)} %levels_ref.1) | copy-start | bytes 100
  18.4 0.7 %copy-start.5 = (s32[8]{0:T(128)S(1)}, s32[8]{0:T(128)}, u32[]{:S(2)}) copy-start(s32[8]{0:T(128)} %counts_ref.1) | copy-start | bytes 100
  20.6 0.9 %copy-start = (bf16[128,768]{1,0:T(8,128)(2,1)S(1)}, bf16[128,768]{1,0:T(8,128)(2,1)}, u32[]{:S(2)}) copy-start(bf16[128,768]{1,0:T(8,128)(2,1)} %get-tuple-element.61.piece_ref) | copy-start | bytes 589828
  25.9 1.7 %collective-permute-start.10 = (bf16[512,256]{1,0:T(8,128)(2,1)S(1)}, bf16[512,256]{1,0:T(8,128)(2,1)S(1)}, u32[]{:S(2)}, u32[]{:S(2)}) collective-permute-start(bf16[512,256]{1,0:T(8,128)(2,1)S(1)} %collective-permute-done.3.refs_3_), channel_id=1, source_target_pairs={{0,1},{1,0},{2,3},{3,2},{4,5},{5,4},{6,7},{7,6},{8,9},{9,8},{10,11... | collective-permute-start | bytes 786440 | tf_op jit(solution)/shard_map/ppermute | solution.py:307
  26.4 7.9 %collective-permute-start.9 = (bf16[512,256]{1,0:T(8,128)(2,1)S(1)}, bf16[512,256]{1,0:T(8,128)(2,1)S(1)}, u32[]{:S(2)}, u32[]{:S(2)}) collective-permute-start(bf16[512,256]{1,0:T(8,128)(2,1)S(1)} %collective-permute-done.3.refs_3_), channel_id=1, source_target_pairs={{0,8},{4,12},{8,16},{12,20},{16,24},{20,28},{24,0},{28,4},{1,9},{5... | collective-permute-start | bytes 786440 | tf_op jit(solution)/shard_map/ppermute | solution.py:304
  26.9 8.2 %collective-permute-start.12 = (bf16[512,256]{1,0:T(8,128)(2,1)S(1)}, bf16[512,256]{1,0:T(8,128)(2,1)S(1)}, u32[]{:S(2)}, u32[]{:S(2)}) collective-permute-start(bf16[512,256]{1,0:T(8,128)(2,1)S(1)} %collective-permute-done.4.refs_3_), channel_id=1, source_target_pairs={{0,1},{1,0},{2,3},{3,2},{4,5},{5,4},{6,7},{7,6},{8,9},{9,8},{10,11... | collective-permute-start | bytes 786440 | tf_op jit(solution)/shard_map/ppermute | solution.py:307
  34.3 2.8 %collective-permute-start.11 = (bf16[512,256]{1,0:T(8,128)(2,1)S(1)}, bf16[512,256]{1,0:T(8,128)(2,1)S(1)}, u32[]{:S(2)}, u32[]{:S(2)}) collective-permute-start(bf16[512,256]{1,0:T(8,128)(2,1)S(1)} %collective-permute-done.9.refs_3_), channel_id=1, source_target_pairs={{0,1},{1,0},{2,3},{3,2},{4,5},{5,4},{6,7},{7,6},{8,9},{9,8},{10,11... | collective-permute-start | bytes 786440 | tf_op jit(solution)/shard_map/ppermute | solution.py:307
  41.0 7.5 %collective-permute-start.13 = (bf16[128,768]{1,0:T(8,128)(2,1)S(1)}, bf16[128,768]{1,0:T(8,128)(2,1)S(1)}, u32[]{:S(2)}, u32[]{:S(2)}) collective-permute-start(bf16[128,768]{1,0:T(8,128)(2,1)S(1)} %get-tuple-element.84), channel_id=1, source_target_pairs={{0,6},{1,7},{2,4},{3,5},{4,2},{5,3},{6,0},{7,1},{8,14},{9,15},{10,... | collective-permute-start | bytes 589832 | tf_op jit(solution)/shard_map/ppermute | solution.py:300
  42.3 10.7 %collective-permute-start.14 = (bf16[128,768]{1,0:T(8,128)(2,1)S(1)}, bf16[128,768]{1,0:T(8,128)(2,1)S(1)}, u32[]{:S(2)}, u32[]{:S(2)}) collective-permute-start(bf16[128,768]{1,0:T(8,128)(2,1)S(1)} %get-tuple-element.85), channel_id=1, source_target_pairs={{0,4},{1,3},{2,6},{3,1},{4,0},{5,7},{6,2},{7,5},{8,12},{9,11},{10,... | collective-permute-start | bytes 589832 | tf_op jit(solution)/shard_map/ppermute | solution.py:300
  42.7 10.2 %collective-permute-start.15 = (bf16[128,768]{1,0:T(8,128)(2,1)S(1)}, bf16[128,768]{1,0:T(8,128)(2,1)S(1)}, u32[]{:S(2)}, u32[]{:S(2)}) collective-permute-start(bf16[128,768]{1,0:T(8,128)(2,1)S(1)} %get-tuple-element.86), channel_id=1, source_target_pairs={{0,2},{1,5},{2,0},{3,7},{4,6},{5,1},{6,4},{7,3},{8,10},{9,13},{10,... | collective-permute-start | bytes 589832 | tf_op jit(solution)/shard_map/ppermute | solution.py:300
